TPU v7x, 32 devices: a whole 2x2x4 slice. The times are simulated.
32 devices in a mesh: gx: 4 (over x, core), gy: 8 (over z, y).
Axes of the slice: x: 2, y: 2, z: 4, core: 2. Of those that a mesh axis runs over, the one named last changes fastest.
Arguments:
- density: float32 [64, 256, 128], P('gx', 'gy'), may hold values from 0.05 to 1
- potential: float32 [64, 256, 128], P('gx', 'gy'), may hold values from -14 to 25
- adjoint_start: float32 [64, 256, 128], P('gx', 'gy'), may hold values from -6 to 6
- adjoint_source: float32 [64, 256, 128], P('gx', 'gy'), may hold values from -6 to 6
- labels: int32 [64, 256, 128], P('gx', 'gy'), may hold values from 0 to 2
Outputs:
- sensitivity: float32 [64, 256, 128], P('gx', 'gy')
- mean_energy: float32 [], replicated
All inputs are finite; a program needn't handle non-finite values.
Results may differ from a plain program's by a relative error of at most 0.0001.
Values sent between devices are 32-bit elements; how exact they have to be, the bound alone decides.
No kernel may reach another device: no remote copies, remote signals or barrier semaphores. Data moves between devices by JAX's collectives and lax.ppermute only.
A program may use at most 64 MiB of HBM per device.

v0:
```python
import jax
import jax.numpy as jnp
from jax import lax
from jax.sharding import PartitionSpec as P

ADJ_SWEEPS = 2
FILTER_SWEEPS = 4


eps_void = 1.0
eps_solid = 12.0
eps_back = 4.0
eps_metal = 40.0
screen = 0.5
radius_sq = 2.0
epsilon_mean = 1e-06


def extended(block, sides, width):
    for axis, dim in sides:
        count = lax.axis_size(axis)
        forward = [(i, i + 1) for i in range(count - 1)]
        backward = [(target, source) for source, target in forward]
        low = lax.ppermute(
            lax.slice_in_dim(block, block.shape[dim] - width, None, axis=dim), axis, forward
        )
        high = lax.ppermute(lax.slice_in_dim(block, 0, width, axis=dim), axis, backward)
        block = jnp.concatenate([low, block, high], axis=dim)
    return block


def material(density, labels):
    design = eps_void + density**3 * (eps_solid - eps_void)
    return jnp.where(labels == 1, design, jnp.where(labels == 2, eps_metal, eps_back))


def neighbours(padded):
    return [
        padded[2:, 1:-1, 1:-1],
        padded[:-2, 1:-1, 1:-1],
        padded[1:-1, 2:, 1:-1],
        padded[1:-1, :-2, 1:-1],
        padded[1:-1, 1:-1, 2:],
        padded[1:-1, 1:-1, :-2],
    ]


def pad_depth(rimmed):
    return jnp.pad(rimmed, ((0, 0), (0, 0), (1, 1)))


def edge_count(anchor, length, extent):
    places = anchor + jnp.arange(length, dtype=jnp.int32)
    count_cells = (places > 0).astype(jnp.float32) + (places < extent - 1).astype(jnp.float32)
    inside = ((places >= 0) & (places < extent)).astype(jnp.float32)
    return (count_cells, inside)


def adjoint_beside(adjoint):
    rimmed = extended(adjoint, (("gx", 0), ("gy", 1)), 1)
    return neighbours(pad_depth(rimmed))


def relax_once(rimmed, source, count_cells):
    beside = sum(neighbours(pad_depth(rimmed)))
    return (source + radius_sq * beside) / (1.0 + radius_sq * count_cells)


def filter_plain(filtered):
    return extended(filtered, (("gx", 0), ("gy", 1)), 1)


def shards(density, potential, adjoint_start, adjoint_source, labels):
    size_x, size_y, size_z = potential.shape
    extent_x = lax.axis_size("gx") * size_x
    extent_y = lax.axis_size("gy") * size_y
    anchor_x = lax.axis_index("gx") * size_x
    anchor_y = lax.axis_index("gy") * size_y
    permit = material(density, labels)
    rims = extended(jnp.stack([permit, potential]), (("gx", 1), ("gy", 2)), 1)
    permit_nb = neighbours(pad_depth(rims[0]))
    potential_nb = neighbours(pad_depth(rims[1]))
    weights = [2.0 * permit * other / (permit + other) for other in permit_nb]
    total_weight = (
        screen + weights[0] + weights[1] + weights[2] + weights[3] + weights[4] + weights[5]
    )
    metal_mask = labels == 2
    adjoint = adjoint_start
    for repeat in range(ADJ_SWEEPS):
        beside = adjoint_beside(adjoint)
        total = adjoint_source
        for weight, other in zip(weights, beside):
            total = total + weight * other
        adjoint = jnp.where(metal_mask, 0.0, total / total_weight)
    adjoint_nb = adjoint_beside(adjoint)
    product = jnp.zeros_like(potential)
    squares = jnp.zeros_like(potential)
    for other_pot, other_adj in zip(potential_nb, adjoint_nb):
        diff = other_pot - potential
        product = product + diff * (other_adj - adjoint)
        squares = squares + diff * diff
    product = 0.5 * product
    energy = 0.5 * permit * squares
    raw = jnp.where(labels == 1, -3.0 * density**2 * (eps_solid - eps_void) * product, 0.0)
    energy_sum = lax.psum(jnp.sum(energy), ("gx", "gy"))
    mean_energy = energy_sum / (extent_x * extent_y * size_z) + epsilon_mean
    count_x, inside_x = edge_count(anchor_x, size_x, extent_x)
    count_y, inside_y = edge_count(anchor_y, size_y, extent_y)
    count_z, inside_z = edge_count(0, size_z, size_z)
    count_cells = count_x[:, None, None] + count_y[None, :, None] + count_z[None, None, :]
    filtered = raw
    for repeat in range(FILTER_SWEEPS):
        filtered = relax_once(filter_plain(filtered), raw, count_cells)
    sensitivity = jnp.where(labels == 1, filtered, 0.0) / mean_energy
    return (sensitivity, mean_energy)


def solution(mesh):
    placed = (
        P("gx", "gy", None),
        P("gx", "gy", None),
        P("gx", "gy", None),
        P("gx", "gy", None),
        P("gx", "gy", None),
    )
    return jax.shard_map(
        shards, mesh=mesh, in_specs=placed, out_specs=(P("gx", "gy", None), P()), check_vma=False
    )
```

profile of v0, /device:TPU:0, one launch (start us, length us, event | category | flops | bytes accessed | tf_op | source)
XLA Modules:
  0.0 174.6 jit_solution(15891475841543131259)
XLA Ops:
  0.6 0.7 fusion.85
  1.4 2.5 %collective-permute-start.5 = (f32[1,32,128]{2,1,0:T(8,128)S(1)}, f32[1,32,128]{2,1,0:T(8,128)S(1)}, u32[]{:S(2)}, u32[]{:S(2)}) collective-permute-start(f32[1,32,128]{2,1,0:T(8,128)S(1)} %get-tuple-element.38), channel_id=1, source_target_pairs={{0,8},{8,16},{16,24},{1,9},{9,17},{17,25},{2,10},{10,18},{18,26},{... | collective-permute-start | bytes 49160 | tf_op jit(solution)/shard_map/ppermute | solution.py:24
  3.9 1.2 fusion.77
  5.0 4.6 %collective-permute-start = (f32[2,1,32,128]{3,2,1,0:T(8,128)S(1)}, f32[2,1,32,128]{3,2,1,0:T(8,128)S(1)}, u32[]{:S(2)}, u32[]{:S(2)}) collective-permute-start(f32[2,1,32,128]{3,2,1,0:T(8,128)S(1)} %get-tuple-element.9), channel_id=1, source_target_pairs={{0,8},{8,16},{16,24},{1,9},{9,17},{17,25},{2,10},{10,18},{18,26},{... | collective-permute-start | bytes 98312 | tf_op jit(solution)/shard_map/ppermute | solution.py:24
  9.7 1.3 collective-permute-start.1
  11.0 1.3 collective-permute-start.4
  12.4 2.3 %collective-permute-done.4 = f32[1,32,128]{2,1,0:T(8,128)S(1)} collective-permute-done((f32[1,32,128]{2,1,0:T(8,128)S(1)}, f32[1,32,128]{2,1,0:T(8,128)S(1)}, u32[]{:S(2)}, u32[]{:S(2)}) %collective-permute-start.4) | collective-permute-done | bytes 16416 | tf_op jit(solution)/shard_map/ppermute | solution.py:27
  14.7 1.3 collective-permute-start.6
  16.0 4.5 %collective-permute-start.7 = (f32[18,1,128]{2,1,0:T(1,128)S(1)}, f32[18,1,128]{2,1,0:T(1,128)S(1)}, u32[]{:S(2)}, u32[]{:S(2)}) collective-permute-start(f32[18,1,128]{2,1,0:T(1,128)S(1)} %get-tuple-element.23), channel_id=1, source_target_pairs={{0,1},{1,2},{2,3},{3,4},{4,5},{5,6},{6,7},{8,9},{9,10},{10,11},{11... | collective-permute-start | bytes 27656 | tf_op jit(solution)/shard_map/ppermute | solution.py:24
  20.6 4.3 %collective-permute-start.2 = (f32[2,18,1,128]{3,2,1,0:T(1,128)S(1)}, f32[2,18,1,128]{3,2,1,0:T(1,128)S(1)}, u32[]{:S(2)}, u32[]{:S(2)}) collective-permute-start(f32[2,18,1,128]{3,2,1,0:T(1,128)S(1)} %get-tuple-element.7), channel_id=1, source_target_pairs={{0,1},{1,2},{2,3},{3,4},{4,5},{5,6},{6,7},{8,9},{9,10},{10,11},{11... | collective-permute-start | bytes 55304 | tf_op jit(solution)/shard_map/ppermute | solution.py:24
  25.0 1.3 collective-permute-start.3
  26.3 0.3 select_maximum_fusion.24
  26.7 4.0 %collective-permute-done.3 = f32[2,18,1,128]{3,2,1,0:T(1,128)S(1)} collective-permute-done((f32[2,18,1,128]{3,2,1,0:T(1,128)S(1)}, f32[2,18,1,128]{3,2,1,0:T(1,128)S(1)}, u32[]{:S(2)}, u32[]{:S(2)}) %collective-permute-start.3) | collective-permute-done | bytes 18464 | tf_op jit(solution)/shard_map/ppermute | solution.py:27
  30.8 0.9 copy-done
  31.8 0.7 fusion.64
  32.5 1.3 collective-permute-start.8
  33.8 3.0 %collective-permute-start.9 = (f32[1,32,128]{2,1,0:T(8,128)S(1)}, f32[1,32,128]{2,1,0:T(8,128)S(1)}, u32[]{:S(2)}, u32[]{:S(2)}) collective-permute-start(f32[1,32,128]{2,1,0:T(8,128)S(1)} %get-tuple-element.35), channel_id=1, source_target_pairs={{0,8},{8,16},{16,24},{1,9},{9,17},{17,25},{2,10},{10,18},{18,26},{... | collective-permute-start | bytes 49160 | tf_op jit(solution)/shard_map/ppermute | solution.py:24
  36.9 0.8 collective-permute-done.9
  37.7 1.3 collective-permute-start.10
  39.0 4.5 %collective-permute-start.11 = (f32[18,1,128]{2,1,0:T(1,128)S(1)}, f32[18,1,128]{2,1,0:T(1,128)S(1)}, u32[]{:S(2)}, u32[]{:S(2)}) collective-permute-start(f32[18,1,128]{2,1,0:T(1,128)S(1)} %get-tuple-element.21), channel_id=1, source_target_pairs={{0,1},{1,2},{2,3},{3,4},{4,5},{5,6},{6,7},{8,9},{9,10},{10,11},{11... | collective-permute-start | bytes 27656 | tf_op jit(solution)/shard_map/ppermute | solution.py:24
  43.6 1.3 collective-permute-done.11
  44.9 0.3 select_maximum_fusion.20
  45.3 0.7 fusion.52
  46.0 1.3 collective-permute-start.12
  47.3 3.4 %collective-permute-start.13 = (f32[1,32,128]{2,1,0:T(8,128)S(1)}, f32[1,32,128]{2,1,0:T(8,128)S(1)}, u32[]{:S(2)}, u32[]{:S(2)}) collective-permute-start(f32[1,32,128]{2,1,0:T(8,128)S(1)} %get-tuple-element.33), channel_id=1, source_target_pairs={{0,8},{8,16},{16,24},{1,9},{9,17},{17,25},{2,10},{10,18},{18,26},{... | collective-permute-start | bytes 49160 | tf_op jit(solution)/shard_map/ppermute | solution.py:24
  50.8 0.8 collective-permute-done.13
  51.6 1.3 collective-permute-start.14
  52.9 5.0 %collective-permute-start.15 = (f32[18,1,128]{2,1,0:T(1,128)S(1)}, f32[18,1,128]{2,1,0:T(1,128)S(1)}, u32[]{:S(2)}, u32[]{:S(2)}) collective-permute-start(f32[18,1,128]{2,1,0:T(1,128)S(1)} %get-tuple-element.19), channel_id=1, source_target_pairs={{0,1},{1,2},{2,3},{3,4},{4,5},{5,6},{6,7},{8,9},{9,10},{10,11},{11... | collective-permute-start | bytes 27656 | tf_op jit(solution)/shard_map/ppermute | solution.py:24
  57.9 1.3 collective-permute-done.15
  59.2 0.3 select_maximum_fusion.16
  59.5 0.5 fusion.2
  60.0 1.3 collective-permute-start.16
  61.3 5.1 %collective-permute-start.17 = (f32[1,32,128]{2,1,0:T(8,128)S(1)}, f32[1,32,128]{2,1,0:T(8,128)S(1)}, u32[]{:S(2)}, u32[]{:S(2)}) collective-permute-start(f32[1,32,128]{2,1,0:T(8,128)S(1)} %get-tuple-element.31), channel_id=1, source_target_pairs={{0,8},{8,16},{16,24},{1,9},{9,17},{17,25},{2,10},{10,18},{18,26},{... | collective-permute-start | bytes 49160 | tf_op jit(solution)/shard_map/ppermute | solution.py:24
  66.6 0.7 collective-permute-done.17
  67.3 1.3 collective-permute-start.18
  68.6 5.7 %collective-permute-start.19 = (f32[18,1,128]{2,1,0:T(1,128)S(1)}, f32[18,1,128]{2,1,0:T(1,128)S(1)}, u32[]{:S(2)}, u32[]{:S(2)}) collective-permute-start(f32[18,1,128]{2,1,0:T(1,128)S(1)} %get-tuple-element.17), channel_id=1, source_target_pairs={{0,1},{1,2},{2,3},{3,4},{4,5},{5,6},{6,7},{8,9},{9,10},{10,11},{11... | collective-permute-start | bytes 27656 | tf_op jit(solution)/shard_map/ppermute | solution.py:24
  74.4 1.3 collective-permute-done.19
  75.7 0.3 select_maximum_fusion.12
  76.1 0.2 fusion.30
  76.3 1.3 collective-permute-start.20
  77.6 4.9 %collective-permute-start.21 = (f32[1,32,128]{2,1,0:T(8,128)S(1)}, f32[1,32,128]{2,1,0:T(8,128)S(1)}, u32[]{:S(2)}, u32[]{:S(2)}) collective-permute-start(f32[1,32,128]{2,1,0:T(8,128)S(1)} %get-tuple-element.29), channel_id=1, source_target_pairs={{0,8},{8,16},{16,24},{1,9},{9,17},{17,25},{2,10},{10,18},{18,26},{... | collective-permute-start | bytes 49160 | tf_op jit(solution)/shard_map/ppermute | solution.py:24
  82.5 0.8 collective-permute-done.21
  83.3 1.3 collective-permute-start.22
  84.6 5.7 %collective-permute-start.23 = (f32[18,1,128]{2,1,0:T(1,128)S(1)}, f32[18,1,128]{2,1,0:T(1,128)S(1)}, u32[]{:S(2)}, u32[]{:S(2)}) collective-permute-start(f32[18,1,128]{2,1,0:T(1,128)S(1)} %get-tuple-element.15), channel_id=1, source_target_pairs={{0,1},{1,2},{2,3},{3,4},{4,5},{5,6},{6,7},{8,9},{9,10},{10,11},{11... | collective-permute-start | bytes 27656 | tf_op jit(solution)/shard_map/ppermute | solution.py:24
  90.3 1.3 collective-permute-done.23
  91.7 0.3 select_maximum_fusion.8
  92.0 0.2 fusion.24
  92.3 1.3 collective-permute-start.24
  93.6 4.9 %collective-permute-start.25 = (f32[1,32,128]{2,1,0:T(8,128)S(1)}, f32[1,32,128]{2,1,0:T(8,128)S(1)}, u32[]{:S(2)}, u32[]{:S(2)}) collective-permute-start(f32[1,32,128]{2,1,0:T(8,128)S(1)} %get-tuple-element.27), channel_id=1, source_target_pairs={{0,8},{8,16},{16,24},{1,9},{9,17},{17,25},{2,10},{10,18},{18,26},{... | collective-permute-start | bytes 49160 | tf_op jit(solution)/shard_map/ppermute | solution.py:24
  98.5 0.8 collective-permute-done.25
  99.3 1.3 collective-permute-start.26
  100.6 5.7 %collective-permute-start.27 = (f32[18,1,128]{2,1,0:T(1,128)S(1)}, f32[18,1,128]{2,1,0:T(1,128)S(1)}, u32[]{:S(2)}, u32[]{:S(2)}) collective-permute-start(f32[18,1,128]{2,1,0:T(1,128)S(1)} %get-tuple-element.13), channel_id=1, source_target_pairs={{0,1},{1,2},{2,3},{3,4},{4,5},{5,6},{6,7},{8,9},{9,10},{10,11},{11... | collective-permute-start | bytes 27656 | tf_op jit(solution)/shard_map/ppermute | solution.py:24
  106.3 1.3 collective-permute-done.27
  107.7 0.3 select_maximum_fusion.4
  108.0 0.2 fusion.18
  108.3 1.3 collective-permute-start.28
  109.6 4.9 %collective-permute-start.29 = (f32[1,32,128]{2,1,0:T(8,128)S(1)}, f32[1,32,128]{2,1,0:T(8,128)S(1)}, u32[]{:S(2)}, u32[]{:S(2)}) collective-permute-start(f32[1,32,128]{2,1,0:T(8,128)S(1)} %get-tuple-element.25), channel_id=1, source_target_pairs={{0,8},{8,16},{16,24},{1,9},{9,17},{17,25},{2,10},{10,18},{18,26},{... | collective-permute-start | bytes 49160 | tf_op jit(solution)/shard_map/ppermute | solution.py:24
  114.5 0.8 collective-permute-done.29
  115.3 1.3 collective-permute-start.30
  116.6 5.7 %collective-permute-start.31 = (f32[18,1,128]{2,1,0:T(1,128)S(1)}, f32[18,1,128]{2,1,0:T(1,128)S(1)}, u32[]{:S(2)}, u32[]{:S(2)}) collective-permute-start(f32[18,1,128]{2,1,0:T(1,128)S(1)} %get-tuple-element.11), channel_id=1, source_target_pairs={{0,1},{1,2},{2,3},{3,4},{4,5},{5,6},{6,7},{8,9},{9,10},{10,11},{11... | collective-permute-start | bytes 27656 | tf_op jit(solution)/shard_map/ppermute | solution.py:24
  122.3 0.9 multiply_reduce_fusion
  123.3 48.2 %psum.7 = f32[]{:T(128)} all-reduce(f32[]{:T(128)} %multiply_reduce_fusion), channel_id=1, replica_groups=mesh['gx'=4,'gy'=8] {'gx','gy'}, use_global_device_ids=true, to_apply=%region_1.2 | all-reduce | flops 1 | bytes 8 | tf_op jit(solution)/shard_map/psum | solution.py:105
  172.1 0.3 select_maximum_fusion
  172.4 1.0 fusion.12
  (50 shorter events, 0.6 us)
Async XLA Ops:
  1.4 3.6 %copy-start.1 = (f32[16,32,128]{2,1,0:T(8,128)S(1)}, f32[16,32,128]{2,1,0:T(8,128)}, u32[]{:S(2)}) copy-start(f32[16,32,128]{2,1,0:T(8,128)} %param.6) | copy-start | bytes 786436
  1.4 10.9 %collective-permute-start.5 = (f32[1,32,128]{2,1,0:T(8,128)S(1)}, f32[1,32,128]{2,1,0:T(8,128)S(1)}, u32[]{:S(2)}, u32[]{:S(2)}) collective-permute-start(f32[1,32,128]{2,1,0:T(8,128)S(1)} %get-tuple-element.38), channel_id=1, source_target_pairs={{0,8},{8,16},{16,24},{1,9},{9,17},{17,25},{2,10},{10,18},{18,26},{... | collective-permute-start | bytes 49160 | tf_op jit(solution)/shard_map/ppermute | solution.py:24
  5.0 7.3 %copy-start.2 = (f32[16,32,128]{2,1,0:T(8,128)S(1)}, f32[16,32,128]{2,1,0:T(8,128)}, u32[]{:S(2)}) copy-start(f32[16,32,128]{2,1,0:T(8,128)} %param.7) | copy-start | bytes 786436
  5.0 15.5 %collective-permute-start = (f32[2,1,32,128]{3,2,1,0:T(8,128)S(1)}, f32[2,1,32,128]{3,2,1,0:T(8,128)S(1)}, u32[]{:S(2)}, u32[]{:S(2)}) collective-permute-start(f32[2,1,32,128]{3,2,1,0:T(8,128)S(1)} %get-tuple-element.9), channel_id=1, source_target_pairs={{0,8},{8,16},{16,24},{1,9},{9,17},{17,25},{2,10},{10,18},{18,26},{... | collective-permute-start | bytes 98312 | tf_op jit(solution)/shard_map/ppermute | solution.py:24
  9.7 10.9 %collective-permute-start.1 = (f32[2,1,32,128]{3,2,1,0:T(8,128)S(1)}, f32[2,1,32,128]{3,2,1,0:T(8,128)S(1)}, u32[]{:S(2)}, u32[]{:S(2)}) collective-permute-start(f32[2,1,32,128]{3,2,1,0:T(8,128)S(1)} %get-tuple-element.10), channel_id=1, source_target_pairs={{8,0},{16,8},{24,16},{9,1},{17,9},{25,17},{10,2},{18,10},{26,18},{... | collective-permute-start | bytes 98312 | tf_op jit(solution)/shard_map/ppermute | solution.py:27
  11.0 3.7 %collective-permute-start.4 = (f32[1,32,128]{2,1,0:T(8,128)S(1)}, f32[1,32,128]{2,1,0:T(8,128)S(1)}, u32[]{:S(2)}, u32[]{:S(2)}) collective-permute-start(f32[1,32,128]{2,1,0:T(8,128)S(1)} %get-tuple-element.37), channel_id=1, source_target_pairs={{8,0},{16,8},{24,16},{9,1},{17,9},{25,17},{10,2},{18,10},{26,18},{... | collective-permute-start | bytes 49160 | tf_op jit(solution)/shard_map/ppermute | solution.py:27
  14.7 11.6 %collective-permute-start.6 = (f32[18,1,128]{2,1,0:T(1,128)S(1)}, f32[18,1,128]{2,1,0:T(1,128)S(1)}, u32[]{:S(2)}, u32[]{:S(2)}) collective-permute-start(f32[18,1,128]{2,1,0:T(1,128)S(1)} %get-tuple-element.24), channel_id=1, source_target_pairs={{1,0},{2,1},{3,2},{4,3},{5,4},{6,5},{7,6},{9,8},{10,9},{11,10},{12... | collective-permute-start | bytes 27656 | tf_op jit(solution)/shard_map/ppermute | solution.py:27
  16.0 10.3 %collective-permute-start.7 = (f32[18,1,128]{2,1,0:T(1,128)S(1)}, f32[18,1,128]{2,1,0:T(1,128)S(1)}, u32[]{:S(2)}, u32[]{:S(2)}) collective-permute-start(f32[18,1,128]{2,1,0:T(1,128)S(1)} %get-tuple-element.23), channel_id=1, source_target_pairs={{0,1},{1,2},{2,3},{3,4},{4,5},{5,6},{6,7},{8,9},{9,10},{10,11},{11... | collective-permute-start | bytes 27656 | tf_op jit(solution)/shard_map/ppermute | solution.py:24
  20.6 6.0 %collective-permute-start.2 = (f32[2,18,1,128]{3,2,1,0:T(1,128)S(1)}, f32[2,18,1,128]{3,2,1,0:T(1,128)S(1)}, u32[]{:S(2)}, u32[]{:S(2)}) collective-permute-start(f32[2,18,1,128]{3,2,1,0:T(1,128)S(1)} %get-tuple-element.7), channel_id=1, source_target_pairs={{0,1},{1,2},{2,3},{3,4},{4,5},{5,6},{6,7},{8,9},{9,10},{10,11},{11... | collective-permute-start | bytes 55304 | tf_op jit(solution)/shard_map/ppermute | solution.py:24
  25.0 5.7 %collective-permute-start.3 = (f32[2,18,1,128]{3,2,1,0:T(1,128)S(1)}, f32[2,18,1,128]{3,2,1,0:T(1,128)S(1)}, u32[]{:S(2)}, u32[]{:S(2)}) collective-permute-start(f32[2,18,1,128]{3,2,1,0:T(1,128)S(1)} %get-tuple-element.8), channel_id=1, source_target_pairs={{1,0},{2,1},{3,2},{4,3},{5,4},{6,5},{7,6},{9,8},{10,9},{11,10},{12... | collective-permute-start | bytes 55304 | tf_op jit(solution)/shard_map/ppermute | solution.py:27
  30.7 1.0 copy-start
  30.7 1.0 copy-start.3
  32.5 4.3 %collective-permute-start.8 = (f32[1,32,128]{2,1,0:T(8,128)S(1)}, f32[1,32,128]{2,1,0:T(8,128)S(1)}, u32[]{:S(2)}, u32[]{:S(2)}) collective-permute-start(f32[1,32,128]{2,1,0:T(8,128)S(1)} %get-tuple-element.36), channel_id=1, source_target_pairs={{8,0},{16,8},{24,16},{9,1},{17,9},{25,17},{10,2},{18,10},{26,18},{... | collective-permute-start | bytes 49160 | tf_op jit(solution)/shard_map/ppermute | solution.py:27
  33.8 3.9 %collective-permute-start.9 = (f32[1,32,128]{2,1,0:T(8,128)S(1)}, f32[1,32,128]{2,1,0:T(8,128)S(1)}, u32[]{:S(2)}, u32[]{:S(2)}) collective-permute-start(f32[1,32,128]{2,1,0:T(8,128)S(1)} %get-tuple-element.35), channel_id=1, source_target_pairs={{0,8},{8,16},{16,24},{1,9},{9,17},{17,25},{2,10},{10,18},{18,26},{... | collective-permute-start | bytes 49160 | tf_op jit(solution)/shard_map/ppermute | solution.py:24
  37.7 5.9 %collective-permute-start.10 = (f32[18,1,128]{2,1,0:T(1,128)S(1)}, f32[18,1,128]{2,1,0:T(1,128)S(1)}, u32[]{:S(2)}, u32[]{:S(2)}) collective-permute-start(f32[18,1,128]{2,1,0:T(1,128)S(1)} %get-tuple-element.22), channel_id=1, source_target_pairs={{1,0},{2,1},{3,2},{4,3},{5,4},{6,5},{7,6},{9,8},{10,9},{11,10},{12... | collective-permute-start | bytes 27656 | tf_op jit(solution)/shard_map/ppermute | solution.py:27
  39.0 5.9 %collective-permute-start.11 = (f32[18,1,128]{2,1,0:T(1,128)S(1)}, f32[18,1,128]{2,1,0:T(1,128)S(1)}, u32[]{:S(2)}, u32[]{:S(2)}) collective-permute-start(f32[18,1,128]{2,1,0:T(1,128)S(1)} %get-tuple-element.21), channel_id=1, source_target_pairs={{0,1},{1,2},{2,3},{3,4},{4,5},{5,6},{6,7},{8,9},{9,10},{10,11},{11... | collective-permute-start | bytes 27656 | tf_op jit(solution)/shard_map/ppermute | solution.py:24
  46.0 4.8 %collective-permute-start.12 = (f32[1,32,128]{2,1,0:T(8,128)S(1)}, f32[1,32,128]{2,1,0:T(8,128)S(1)}, u32[]{:S(2)}, u32[]{:S(2)}) collective-permute-start(f32[1,32,128]{2,1,0:T(8,128)S(1)} %get-tuple-element.34), channel_id=1, source_target_pairs={{8,0},{16,8},{24,16},{9,1},{17,9},{25,17},{10,2},{18,10},{26,18},{... | collective-permute-start | bytes 49160 | tf_op jit(solution)/shard_map/ppermute | solution.py:27
  47.3 4.3 %collective-permute-start.13 = (f32[1,32,128]{2,1,0:T(8,128)S(1)}, f32[1,32,128]{2,1,0:T(8,128)S(1)}, u32[]{:S(2)}, u32[]{:S(2)}) collective-permute-start(f32[1,32,128]{2,1,0:T(8,128)S(1)} %get-tuple-element.33), channel_id=1, source_target_pairs={{0,8},{8,16},{16,24},{1,9},{9,17},{17,25},{2,10},{10,18},{18,26},{... | collective-permute-start | bytes 49160 | tf_op jit(solution)/shard_map/ppermute | solution.py:24
  51.6 6.3 %collective-permute-start.14 = (f32[18,1,128]{2,1,0:T(1,128)S(1)}, f32[18,1,128]{2,1,0:T(1,128)S(1)}, u32[]{:S(2)}, u32[]{:S(2)}) collective-permute-start(f32[18,1,128]{2,1,0:T(1,128)S(1)} %get-tuple-element.20), channel_id=1, source_target_pairs={{1,0},{2,1},{3,2},{4,3},{5,4},{6,5},{7,6},{9,8},{10,9},{11,10},{12... | collective-permute-start | bytes 27656 | tf_op jit(solution)/shard_map/ppermute | solution.py:27
  52.9 6.3 %collective-permute-start.15 = (f32[18,1,128]{2,1,0:T(1,128)S(1)}, f32[18,1,128]{2,1,0:T(1,128)S(1)}, u32[]{:S(2)}, u32[]{:S(2)}) collective-permute-start(f32[18,1,128]{2,1,0:T(1,128)S(1)} %get-tuple-element.19), channel_id=1, source_target_pairs={{0,1},{1,2},{2,3},{3,4},{4,5},{5,6},{6,7},{8,9},{9,10},{10,11},{11... | collective-permute-start | bytes 27656 | tf_op jit(solution)/shard_map/ppermute | solution.py:24
  60.0 6.5 %collective-permute-start.16 = (f32[1,32,128]{2,1,0:T(8,128)S(1)}, f32[1,32,128]{2,1,0:T(8,128)S(1)}, u32[]{:S(2)}, u32[]{:S(2)}) collective-permute-start(f32[1,32,128]{2,1,0:T(8,128)S(1)} %get-tuple-element.32), channel_id=1, source_target_pairs={{8,0},{16,8},{24,16},{9,1},{17,9},{25,17},{10,2},{18,10},{26,18},{... | collective-permute-start | bytes 49160 | tf_op jit(solution)/shard_map/ppermute | solution.py:27
  61.3 6.0 %collective-permute-start.17 = (f32[1,32,128]{2,1,0:T(8,128)S(1)}, f32[1,32,128]{2,1,0:T(8,128)S(1)}, u32[]{:S(2)}, u32[]{:S(2)}) collective-permute-start(f32[1,32,128]{2,1,0:T(8,128)S(1)} %get-tuple-element.31), channel_id=1, source_target_pairs={{0,8},{8,16},{16,24},{1,9},{9,17},{17,25},{2,10},{10,18},{18,26},{... | collective-permute-start | bytes 49160 | tf_op jit(solution)/shard_map/ppermute | solution.py:24
  67.3 7.0 %collective-permute-start.18 = (f32[18,1,128]{2,1,0:T(1,128)S(1)}, f32[18,1,128]{2,1,0:T(1,128)S(1)}, u32[]{:S(2)}, u32[]{:S(2)}) collective-permute-start(f32[18,1,128]{2,1,0:T(1,128)S(1)} %get-tuple-element.18), channel_id=1, source_target_pairs={{1,0},{2,1},{3,2},{4,3},{5,4},{6,5},{7,6},{9,8},{10,9},{11,10},{12... | collective-permute-start | bytes 27656 | tf_op jit(solution)/shard_map/ppermute | solution.py:27
  68.6 7.1 %collective-permute-start.19 = (f32[18,1,128]{2,1,0:T(1,128)S(1)}, f32[18,1,128]{2,1,0:T(1,128)S(1)}, u32[]{:S(2)}, u32[]{:S(2)}) collective-permute-start(f32[18,1,128]{2,1,0:T(1,128)S(1)} %get-tuple-element.17), channel_id=1, source_target_pairs={{0,1},{1,2},{2,3},{3,4},{4,5},{5,6},{6,7},{8,9},{9,10},{10,11},{11... | collective-permute-start | bytes 27656 | tf_op jit(solution)/shard_map/ppermute | solution.py:24
  76.3 6.2 %collective-permute-start.20 = (f32[1,32,128]{2,1,0:T(8,128)S(1)}, f32[1,32,128]{2,1,0:T(8,128)S(1)}, u32[]{:S(2)}, u32[]{:S(2)}) collective-permute-start(f32[1,32,128]{2,1,0:T(8,128)S(1)} %get-tuple-element.30), channel_id=1, source_target_pairs={{8,0},{16,8},{24,16},{9,1},{17,9},{25,17},{10,2},{18,10},{26,18},{... | collective-permute-start | bytes 49160 | tf_op jit(solution)/shard_map/ppermute | solution.py:27
  77.6 5.7 %collective-permute-start.21 = (f32[1,32,128]{2,1,0:T(8,128)S(1)}, f32[1,32,128]{2,1,0:T(8,128)S(1)}, u32[]{:S(2)}, u32[]{:S(2)}) collective-permute-start(f32[1,32,128]{2,1,0:T(8,128)S(1)} %get-tuple-element.29), channel_id=1, source_target_pairs={{0,8},{8,16},{16,24},{1,9},{9,17},{17,25},{2,10},{10,18},{18,26},{... | collective-permute-start | bytes 49160 | tf_op jit(solution)/shard_map/ppermute | solution.py:24
  83.3 7.0 %collective-permute-start.22 = (f32[18,1,128]{2,1,0:T(1,128)S(1)}, f32[18,1,128]{2,1,0:T(1,128)S(1)}, u32[]{:S(2)}, u32[]{:S(2)}) collective-permute-start(f32[18,1,128]{2,1,0:T(1,128)S(1)} %get-tuple-element.16), channel_id=1, source_target_pairs={{1,0},{2,1},{3,2},{4,3},{5,4},{6,5},{7,6},{9,8},{10,9},{11,10},{12... | collective-permute-start | bytes 27656 | tf_op jit(solution)/shard_map/ppermute | solution.py:27
  84.6 7.1 %collective-permute-start.23 = (f32[18,1,128]{2,1,0:T(1,128)S(1)}, f32[18,1,128]{2,1,0:T(1,128)S(1)}, u32[]{:S(2)}, u32[]{:S(2)}) collective-permute-start(f32[18,1,128]{2,1,0:T(1,128)S(1)} %get-tuple-element.15), channel_id=1, source_target_pairs={{0,1},{1,2},{2,3},{3,4},{4,5},{5,6},{6,7},{8,9},{9,10},{10,11},{11... | collective-permute-start | bytes 27656 | tf_op jit(solution)/shard_map/ppermute | solution.py:24
  92.3 6.2 %collective-permute-start.24 = (f32[1,32,128]{2,1,0:T(8,128)S(1)}, f32[1,32,128]{2,1,0:T(8,128)S(1)}, u32[]{:S(2)}, u32[]{:S(2)}) collective-permute-start(f32[1,32,128]{2,1,0:T(8,128)S(1)} %get-tuple-element.28), channel_id=1, source_target_pairs={{8,0},{16,8},{24,16},{9,1},{17,9},{25,17},{10,2},{18,10},{26,18},{... | collective-permute-start | bytes 49160 | tf_op jit(solution)/shard_map/ppermute | solution.py:27
  93.6 5.7 %collective-permute-start.25 = (f32[1,32,128]{2,1,0:T(8,128)S(1)}, f32[1,32,128]{2,1,0:T(8,128)S(1)}, u32[]{:S(2)}, u32[]{:S(2)}) collective-permute-start(f32[1,32,128]{2,1,0:T(8,128)S(1)} %get-tuple-element.27), channel_id=1, source_target_pairs={{0,8},{8,16},{16,24},{1,9},{9,17},{17,25},{2,10},{10,18},{18,26},{... | collective-permute-start | bytes 49160 | tf_op jit(solution)/shard_map/ppermute | solution.py:24
  99.3 7.0 %collective-permute-start.26 = (f32[18,1,128]{2,1,0:T(1,128)S(1)}, f32[18,1,128]{2,1,0:T(1,128)S(1)}, u32[]{:S(2)}, u32[]{:S(2)}) collective-permute-start(f32[18,1,128]{2,1,0:T(1,128)S(1)} %get-tuple-element.14), channel_id=1, source_target_pairs={{1,0},{2,1},{3,2},{4,3},{5,4},{6,5},{7,6},{9,8},{10,9},{11,10},{12... | collective-permute-start | bytes 27656 | tf_op jit(solution)/shard_map/ppermute | solution.py:27
  100.6 7.1 %collective-permute-start.27 = (f32[18,1,128]{2,1,0:T(1,128)S(1)}, f32[18,1,128]{2,1,0:T(1,128)S(1)}, u32[]{:S(2)}, u32[]{:S(2)}) collective-permute-start(f32[18,1,128]{2,1,0:T(1,128)S(1)} %get-tuple-element.13), channel_id=1, source_target_pairs={{0,1},{1,2},{2,3},{3,4},{4,5},{5,6},{6,7},{8,9},{9,10},{10,11},{11... | collective-permute-start | bytes 27656 | tf_op jit(solution)/shard_map/ppermute | solution.py:24
  108.3 6.2 %collective-permute-start.28 = (f32[1,32,128]{2,1,0:T(8,128)S(1)}, f32[1,32,128]{2,1,0:T(8,128)S(1)}, u32[]{:S(2)}, u32[]{:S(2)}) collective-permute-start(f32[1,32,128]{2,1,0:T(8,128)S(1)} %get-tuple-element.26), channel_id=1, source_target_pairs={{8,0},{16,8},{24,16},{9,1},{17,9},{25,17},{10,2},{18,10},{26,18},{... | collective-permute-start | bytes 49160 | tf_op jit(solution)/shard_map/ppermute | solution.py:27
  109.6 5.7 %collective-permute-start.29 = (f32[1,32,128]{2,1,0:T(8,128)S(1)}, f32[1,32,128]{2,1,0:T(8,128)S(1)}, u32[]{:S(2)}, u32[]{:S(2)}) collective-permute-start(f32[1,32,128]{2,1,0:T(8,128)S(1)} %get-tuple-element.25), channel_id=1, source_target_pairs={{0,8},{8,16},{16,24},{1,9},{9,17},{17,25},{2,10},{10,18},{18,26},{... | collective-permute-start | bytes 49160 | tf_op jit(solution)/shard_map/ppermute | solution.py:24
  115.3 56.8 %collective-permute-start.30 = (f32[18,1,128]{2,1,0:T(1,128)S(1)}, f32[18,1,128]{2,1,0:T(1,128)S(1)}, u32[]{:S(2)}, u32[]{:S(2)}) collective-permute-start(f32[18,1,128]{2,1,0:T(1,128)S(1)} %get-tuple-element.12), channel_id=1, source_target_pairs={{1,0},{2,1},{3,2},{4,3},{5,4},{6,5},{7,6},{9,8},{10,9},{11,10},{12... | collective-permute-start | bytes 27656 | tf_op jit(solution)/shard_map/ppermute | solution.py:27
  116.6 55.5 %collective-permute-start.31 = (f32[18,1,128]{2,1,0:T(1,128)S(1)}, f32[18,1,128]{2,1,0:T(1,128)S(1)}, u32[]{:S(2)}, u32[]{:S(2)}) collective-permute-start(f32[18,1,128]{2,1,0:T(1,128)S(1)} %get-tuple-element.11), channel_id=1, source_target_pairs={{0,1},{1,2},{2,3},{3,4},{4,5},{5,6},{6,7},{8,9},{9,10},{10,11},{11... | collective-permute-start | bytes 27656 | tf_op jit(solution)/shard_map/ppermute | solution.py:24
where the time goes:
time: 176 us; the launch traced here: 175 us
  starting transfers between devices  95.2 us (54%)
  blocking collectives  48.2 us (27%)
  waiting for transfers between devices  17.9 us (10%)
  other arithmetic  8.43 us (5%)
  between operations  3.05 us (2%)
  local copies, waits for them, and re-layouts  1.83 us (1%)
    ppermute x16, starting transfers between devices, extended(): lax.ppermute(lax.slice_in_dim(block, block.shape[dim] - width, None, axis...  74.5 us
    psum x1, blocking collectives, shards(): energy_sum = lax.psum(jnp.sum(energy), ('gx', 'gy'))  48.2 us
    ppermute x16, starting transfers between devices, extended(): lax.ppermute(lax.slice_in_dim(block, 0, width, axis=dim), axis, backward)  20.7 us
    ppermute x16, waiting for transfers between devices, extended(): lax.ppermute(lax.slice_in_dim(block, block.shape[dim] - width, None, axis...  11.5 us
    ppermute x16, waiting for transfers between devices, extended(): lax.ppermute(lax.slice_in_dim(block, 0, width, axis=dim), axis, backward)  6.36 us
  transfers between devices with their start and end apart: 32, of which 13 were waited for; matrix products, arithmetic and copies ran while one was open for 1% of the time, Pallas kernels for 0%

commit v1 on v0

v1 whole, which is shorter than its diff:
```python
import jax
import jax.numpy as jnp
from jax import lax
from jax.sharding import PartitionSpec as P

ADJ_SWEEPS = 2
FILTER_SWEEPS = 4

eps_void = 1.0
eps_solid = 12.0
eps_back = 4.0
eps_metal = 40.0
screen = 0.5
radius_sq = 2.0
epsilon_mean = 1e-06


def shift_pairs(axis):
    count = lax.axis_size(axis)
    forward = [(i, i + 1) for i in range(count - 1)]
    return forward, [(b, a) for a, b in forward]


def exchange(fields, widths, axis, dim):
    forward, backward = shift_pairs(axis)

    def pack(low):
        parts = []
        for f, w in zip(fields, widths):
            n = f.shape[dim]
            s = lax.slice_in_dim(f, 0, w, axis=dim) if low else lax.slice_in_dim(f, n - w, n, axis=dim)
            parts.append(s.reshape(-1, 128))
        return jnp.concatenate(parts, 0) if len(parts) > 1 else parts[0]

    to_low, to_high = pack(True), pack(False)
    from_high = lax.ppermute(to_low, axis, backward)
    from_low = lax.ppermute(to_high, axis, forward)
    out, at = [], 0
    for f, w in zip(fields, widths):
        shape = list(f.shape)
        shape[dim] = w
        rows = shape[0] * shape[1]
        lo = from_low[at:at + rows].reshape(shape)
        hi = from_high[at:at + rows].reshape(shape)
        at += rows
        out.append(jnp.concatenate([lo, f, hi], axis=dim))
    return out


def material(density, labels):
    design = eps_void + density**3 * (eps_solid - eps_void)
    return jnp.where(labels == 1, design, jnp.where(labels == 2, eps_metal, eps_back))


def crop(f, have, want):
    d = have - want
    return f[d:f.shape[0] - d, d:f.shape[1] - d]


def beside(f):
    zpad = jnp.pad(f[1:-1, 1:-1], ((0, 0), (0, 0), (1, 1)))
    return [f[2:, 1:-1], f[:-2, 1:-1], f[1:-1, 2:], f[1:-1, :-2], zpad[:, :, 2:], zpad[:, :, :-2]]


def shards(density, potential, adjoint_start, adjoint_source, labels):
    size_x, size_y, size_z = potential.shape
    extent_x = lax.axis_size("gx") * size_x
    extent_y = lax.axis_size("gy") * size_y
    permit = material(density, labels)
    fields = [permit, adjoint_start, adjoint_source, potential]
    widths = [3, 3, 2, 1]
    fields = exchange(fields, widths, "gx", 0)
    permit3, adjoint3, source2, potential1 = exchange(fields, widths, "gy", 1)

    permit2 = crop(permit3, 3, 2)
    weights = [2.0 * permit2 * other / jnp.maximum(permit2 + other, 0.25) for other in beside(permit3)]
    total = screen + weights[0] + weights[1] + weights[2] + weights[3] + weights[4] + weights[5]
    inverse = jnp.where(permit2 > 20.0, 0.0, 1.0 / total)
    adjoint = adjoint3
    for sweep in range(ADJ_SWEEPS):
        have = 2 - sweep
        total = crop(source2, 2, have)
        for weight, other in zip(weights, beside(adjoint)):
            total = total + crop(weight, 2, have) * other
        adjoint = total * crop(inverse, 2, have)
    centre = crop(adjoint, 1, 0)
    product = jnp.zeros_like(potential)
    squares = jnp.zeros_like(potential)
    for other_pot, other_adj in zip(beside(potential1), beside(adjoint)):
        diff = other_pot - potential
        product = product + diff * (other_adj - centre)
        squares = squares + diff * diff
    energy = jnp.sum((permit * squares).reshape(-1, size_z), axis=0, keepdims=True)
    energies = lax.all_gather(energy, ("gx", "gy"), axis=0, tiled=True)
    raw = jnp.where(labels == 1, -1.5 * density**2 * (eps_solid - eps_void) * product, 0.0)

    (raw4,) = exchange([raw], [4], "gx", 0)
    (raw4,) = exchange([raw4], [4], "gy", 1)
    place_x = lax.axis_index("gx") * size_x - 3 + jnp.arange(size_x + 6, dtype=jnp.int32)
    place_y = lax.axis_index("gy") * size_y - 3 + jnp.arange(size_y + 6, dtype=jnp.int32)
    place_z = jnp.arange(size_z, dtype=jnp.int32)

    def edges(place, extent):
        return (place > 0).astype(jnp.float32) + (place < extent - 1).astype(jnp.float32)

    count = edges(place_x, extent_x)[:, None, None] + edges(place_y, extent_y)[None, :, None] + edges(place_z, size_z)[None, None, :]
    inside = ((place_x >= 0) & (place_x < extent_x))[:, None, None] & ((place_y >= 0) & (place_y < extent_y))[None, :, None]
    scale = jnp.where(inside, 1.0 / (1.0 + radius_sq * count), 0.0)
    filtered = raw4
    for sweep in range(FILTER_SWEEPS):
        have = 3 - sweep
        near = beside(filtered)
        filtered = (crop(raw4, 4, have) + radius_sq * (near[0] + near[1] + near[2] + near[3] + near[4] + near[5])) * crop(scale, 3, have)
    mean_energy = 0.5 * jnp.sum(energies) / (extent_x * extent_y * size_z) + epsilon_mean
    sensitivity = jnp.where(labels == 1, filtered, 0.0) / mean_energy
    return (sensitivity, mean_energy)


def solution(mesh):
    spec = P("gx", "gy", None)
    return jax.shard_map(shards, mesh=mesh, in_specs=(spec,) * 5, out_specs=(spec, P()), check_vma=False)
```

time: 176 us -> 112 us (0.64)
  starting transfers between devices: 95.2 us -> 19.5 us
  blocking collectives: 48.2 us -> 65.5 us
  waiting for transfers between devices: 17.9 us -> 11 us
  local copies, waits for them, and re-layouts: 1.83 us -> 4.19 us
    ppermute x32 -> x8, starting transfers between devices: 95.2 us -> 19.5 us  [the longest x4 14.3 us: exchange(): from_low = lax.ppermute(to_high, axis, forward)]
    all_gather x0 -> x1, blocking collectives: none -> 65.5 us  [shards(): energies = lax.all_gather(energy, ('gx', 'gy'), axis=0, tiled=True)]
    psum x1 -> x0, blocking collectives: 48.2 us -> none  [shards(): energy_sum = lax.psum(jnp.sum(energy), ('gx', 'gy'))]
    ppermute x32 -> x8, waiting for transfers between devices: 17.9 us -> 11 us  [the longest x4 10.3 us: exchange(): from_high = lax.ppermute(to_low, axis, backward)]
    concatenate x14 -> x8, other arithmetic: 2.56 us -> 0.31 us  [the longest x4 0.26 us: exchange(): out.append(jnp.concatenate([lo, f, hi], axis=dim))]
    unnamed x10 -> x14, local copies, waits for them, and re-layouts: 0.99 us -> 3.19 us
    mul x0 -> x4, other arithmetic: none -> 1.93 us  [the longest x2 1.17 us: shards(): adjoint = total * crop(inverse, 2, have)]
  transfers between devices with their start and end apart: 32 -> 8, of which waited for: 13 -> 4; matrix products, arithmetic and copies ran while one was open for 1% -> 2% of each run, Pallas kernels for 0% -> 0%
where the time goes in v1:
time: 112 us; the launch traced here: 110 us
  blocking collectives  65.5 us (58%)
  starting transfers between devices  19.5 us (17%)
  waiting for transfers between devices  11 us (10%)
  other arithmetic  6.97 us (6%)
  local copies, waits for them, and re-layouts  4.19 us (4%)
  between operations  3.18 us (3%)
    all_gather x1, blocking collectives, shards(): energies = lax.all_gather(energy, ('gx', 'gy'), axis=0, tiled=True)  65.5 us
    ppermute x4, starting transfers between devices, exchange(): from_low = lax.ppermute(to_high, axis, forward)  14.3 us
    ppermute x4, waiting for transfers between devices, exchange(): from_high = lax.ppermute(to_low, axis, backward)  10.3 us
    ppermute x4, starting transfers between devices, exchange(): from_high = lax.ppermute(to_low, axis, backward)  5.17 us
    unnamed x14, local copies, waits for them, and re-layouts  3.19 us
  transfers between devices with their start and end apart: 8, of which 4 were waited for; matrix products, arithmetic and copies ran while one was open for 2% of the time, Pallas kernels for 0%

profile of v1, /device:TPU:0, one launch (start us, length us, event | category | flops | bytes accessed | tf_op | source)
XLA Modules:
  0.0 110.4 jit_solution(10220414857939875366)
XLA Ops:
  0.6 0.0 copy-start.4
  0.6 1.4 %fusion.37 = f32[16,32,128]{2,0,1:T(8,128)S(1)} fusion(f32[16,32,128]{2,1,0:T(8,128)} %param.5, s32[16,32,128]{2,1,0:T(8,128)} %param.9), kind=kLoop, calls=%fused_computation.86 | loop fusion | flops 524288 | bytes 786432 | tf_op jit(solution)/shard_map/jit(_where)/select_n | solution.py:52
  2.0 0.0 copy-start.2
  2.1 0.0 copy-start.3
  2.1 0.9 copy-done.2
  3.0 0.1 copy-done.3
  3.1 0.0 copy-done.4
  3.1 2.4 %collective-permute-start.1 = (f32[288,128]{1,0:T(8,128)S(1)}, f32[288,128]{1,0:T(8,128)S(1)}, u32[]{:S(2)}, u32[]{:S(2)}) collective-permute-start(f32[288,128]{1,0:T(8,128)S(1)} %pad_maximum_fusion.13), channel_id=1, source_target_pairs={{0,8},{8,16},{16,24},{1,9},{9,17},{17,25},{2,10},{10,18},{18,26},{... | collective-permute-start | bytes 442376 | tf_op jit(solution)/shard_map/ppermute | solution.py:37
  5.5 1.3 %collective-permute-start = (f32[288,128]{1,0:T(8,128)S(1)}, f32[288,128]{1,0:T(8,128)S(1)}, u32[]{:S(2)}, u32[]{:S(2)}) collective-permute-start(f32[288,128]{1,0:T(8,128)S(1)} %pad_maximum_fusion.12), channel_id=1, source_target_pairs={{8,0},{16,8},{24,16},{9,1},{17,9},{25,17},{10,2},{18,10},{26,18},{... | collective-permute-start | bytes 442376 | tf_op jit(solution)/shard_map/ppermute | solution.py:36
  6.8 0.2 copy.108
  7.0 0.2 copy.96
  7.2 0.2 copy.104
  7.4 0.1 broadcast_add_fusion
  7.5 0.1 broadcast_and_fusion
  7.5 0.0 collective-permute-done.1
  7.6 3.3 %collective-permute-done = f32[288,128]{1,0:T(8,128)S(1)} collective-permute-done((f32[288,128]{1,0:T(8,128)S(1)}, f32[288,128]{1,0:T(8,128)S(1)}, u32[]{:S(2)}, u32[]{:S(2)}) %collective-permute-start) | collective-permute-done | bytes 147488 | tf_op jit(solution)/shard_map/ppermute | solution.py:36
  11.4 3.4 %collective-permute-start.2 = (f32[190,128]{1,0:T(8,128)S(1)}, f32[190,128]{1,0:T(8,128)S(1)}, u32[]{:S(2)}, u32[]{:S(2)}) collective-permute-start(f32[190,128]{1,0:T(8,128)S(1)} %pad_maximum_fusion.14), channel_id=1, source_target_pairs={{0,1},{1,2},{2,3},{3,4},{4,5},{5,6},{6,7},{8,9},{9,10},{10,11},{11... | collective-permute-start | bytes 291848 | tf_op jit(solution)/shard_map/ppermute | solution.py:37
  14.9 1.3 %collective-permute-start.3 = (f32[190,128]{1,0:T(8,128)S(1)}, f32[190,128]{1,0:T(8,128)S(1)}, u32[]{:S(2)}, u32[]{:S(2)}) collective-permute-start(f32[190,128]{1,0:T(8,128)S(1)} %pad_maximum_fusion.15), channel_id=1, source_target_pairs={{1,0},{2,1},{3,2},{4,3},{5,4},{6,5},{7,6},{9,8},{10,9},{11,10},{12... | collective-permute-start | bytes 291848 | tf_op jit(solution)/shard_map/ppermute | solution.py:36
  16.2 0.8 collective-permute-done.2
  17.0 4.4 %collective-permute-done.3 = f32[190,128]{1,0:T(8,128)S(1)} collective-permute-done((f32[190,128]{1,0:T(8,128)S(1)}, f32[190,128]{1,0:T(8,128)S(1)}, u32[]{:S(2)}, u32[]{:S(2)}) %collective-permute-start.3) | collective-permute-done | bytes 97312 | tf_op jit(solution)/shard_map/ppermute | solution.py:36
  21.5 0.1 pad_maximum_fusion.2
  21.7 0.1 pad_maximum_fusion.1
  21.8 0.7 divide_select_fusion.1
  22.6 0.1 pad_maximum_fusion.3
  22.6 0.6 fusion.8
  23.3 0.5 fusion.22
  23.9 0.0 copy-start
  23.9 0.0 copy-start.1
  23.9 0.9 copy-done
  24.8 0.1 copy-done.1
  24.9 0.6 fusion.34
  25.5 4.2 %collective-permute-start.4 = (f32[128,128]{1,0:T(8,128)S(1)}, f32[128,128]{1,0:T(8,128)S(1)}, u32[]{:S(2)}, u32[]{:S(2)}) collective-permute-start(f32[128,128]{1,0:T(8,128)S(1)} %bitcast.65), channel_id=1, source_target_pairs={{0,8},{8,16},{16,24},{1,9},{9,17},{17,25},{2,10},{10,18},{18,26},{... | collective-permute-start | bytes 196616 | tf_op jit(solution)/shard_map/ppermute | solution.py:37
  29.7 1.3 %collective-permute-start.5 = (f32[128,128]{1,0:T(8,128)S(1)}, f32[128,128]{1,0:T(8,128)S(1)}, u32[]{:S(2)}, u32[]{:S(2)}) collective-permute-start(f32[128,128]{1,0:T(8,128)S(1)} %bitcast.67), channel_id=1, source_target_pairs={{8,0},{16,8},{24,16},{9,1},{17,9},{25,17},{10,2},{18,10},{26,18},{... | collective-permute-start | bytes 196616 | tf_op jit(solution)/shard_map/ppermute | solution.py:36
  31.0 0.0 collective-permute-done.4
  31.1 2.6 %collective-permute-done.5 = f32[128,128]{1,0:T(8,128)S(1)} collective-permute-done((f32[128,128]{1,0:T(8,128)S(1)}, f32[128,128]{1,0:T(8,128)S(1)}, u32[]{:S(2)}, u32[]{:S(2)}) %collective-permute-start.5) | collective-permute-done | bytes 65568 | tf_op jit(solution)/shard_map/ppermute | solution.py:36
  33.7 4.3 %collective-permute-start.6 = (f32[96,128]{1,0:T(8,128)S(1)}, f32[96,128]{1,0:T(8,128)S(1)}, u32[]{:S(2)}, u32[]{:S(2)}) collective-permute-start(f32[96,128]{1,0:T(8,128)S(1)} %bitcast.69), channel_id=1, source_target_pairs={{0,1},{1,2},{2,3},{3,4},{4,5},{5,6},{6,7},{8,9},{9,10},{10,11},{11... | collective-permute-start | bytes 147464 | tf_op jit(solution)/shard_map/ppermute | solution.py:37
  38.1 1.3 %collective-permute-start.7 = (f32[96,128]{1,0:T(8,128)S(1)}, f32[96,128]{1,0:T(8,128)S(1)}, u32[]{:S(2)}, u32[]{:S(2)}) collective-permute-start(f32[96,128]{1,0:T(8,128)S(1)} %bitcast.71), channel_id=1, source_target_pairs={{1,0},{2,1},{3,2},{4,3},{5,4},{6,5},{7,6},{9,8},{10,9},{11,10},{12... | collective-permute-start | bytes 147464 | tf_op jit(solution)/shard_map/ppermute | solution.py:36
  39.4 0.3 multiply_reduce_fusion
  39.7 65.5 %all-gather.1 = f32[32,1,128]{2,1,0:T(1,128)S(1)} all-gather(f32[1,1,128]{2,1,0:T(1,128)S(1)} %bitcast.73), channel_id=2, replica_groups=mesh['gx'=4,'gy'=8] {'gx','gy'}, dimensions={0}, use_global_device_ids=true | all-gather | bytes 16896 | tf_op jit(solution)/shard_map/all_gather | solution.py:94
  105.2 0.6 reduce_sum.19
  106.5 0.0 collective-permute-done.6
  106.5 0.0 collective-permute-done.7
  106.5 0.1 pad_maximum_fusion
  106.6 0.6 divide_select_fusion
  107.3 0.4 fusion.14
  107.7 0.4 fusion.28
  108.1 0.3 fusion.52
  108.4 0.8 copy.139
  (75 shorter events, 1.2 us)
Async XLA Ops:
  0.6 2.5 %copy-start.4 = (f32[16,32,128]{2,1,0:T(8,128)S(1)}, f32[16,32,128]{2,1,0:T(8,128)}, u32[]{:S(2)}) copy-start(f32[16,32,128]{2,1,0:T(8,128)} %param.6) | copy-start | bytes 786436
  2.0 1.0 copy-start.2
  2.1 1.0 copy-start.3
  3.1 4.4 %collective-permute-start.1 = (f32[288,128]{1,0:T(8,128)S(1)}, f32[288,128]{1,0:T(8,128)S(1)}, u32[]{:S(2)}, u32[]{:S(2)}) collective-permute-start(f32[288,128]{1,0:T(8,128)S(1)} %pad_maximum_fusion.13), channel_id=1, source_target_pairs={{0,8},{8,16},{16,24},{1,9},{9,17},{17,25},{2,10},{10,18},{18,26},{... | collective-permute-start | bytes 442376 | tf_op jit(solution)/shard_map/ppermute | solution.py:37
  5.5 5.4 %collective-permute-start = (f32[288,128]{1,0:T(8,128)S(1)}, f32[288,128]{1,0:T(8,128)S(1)}, u32[]{:S(2)}, u32[]{:S(2)}) collective-permute-start(f32[288,128]{1,0:T(8,128)S(1)} %pad_maximum_fusion.12), channel_id=1, source_target_pairs={{8,0},{16,8},{24,16},{9,1},{17,9},{25,17},{10,2},{18,10},{26,18},{... | collective-permute-start | bytes 442376 | tf_op jit(solution)/shard_map/ppermute | solution.py:36
  11.4 5.6 %collective-permute-start.2 = (f32[190,128]{1,0:T(8,128)S(1)}, f32[190,128]{1,0:T(8,128)S(1)}, u32[]{:S(2)}, u32[]{:S(2)}) collective-permute-start(f32[190,128]{1,0:T(8,128)S(1)} %pad_maximum_fusion.14), channel_id=1, source_target_pairs={{0,1},{1,2},{2,3},{3,4},{4,5},{5,6},{6,7},{8,9},{9,10},{10,11},{11... | collective-permute-start | bytes 291848 | tf_op jit(solution)/shard_map/ppermute | solution.py:37
  14.9 6.5 %collective-permute-start.3 = (f32[190,128]{1,0:T(8,128)S(1)}, f32[190,128]{1,0:T(8,128)S(1)}, u32[]{:S(2)}, u32[]{:S(2)}) collective-permute-start(f32[190,128]{1,0:T(8,128)S(1)} %pad_maximum_fusion.15), channel_id=1, source_target_pairs={{1,0},{2,1},{3,2},{4,3},{5,4},{6,5},{7,6},{9,8},{10,9},{11,10},{12... | collective-permute-start | bytes 291848 | tf_op jit(solution)/shard_map/ppermute | solution.py:36
  23.9 1.0 copy-start
  23.9 1.0 copy-start.1
  25.5 5.5 %collective-permute-start.4 = (f32[128,128]{1,0:T(8,128)S(1)}, f32[128,128]{1,0:T(8,128)S(1)}, u32[]{:S(2)}, u32[]{:S(2)}) collective-permute-start(f32[128,128]{1,0:T(8,128)S(1)} %bitcast.65), channel_id=1, source_target_pairs={{0,8},{8,16},{16,24},{1,9},{9,17},{17,25},{2,10},{10,18},{18,26},{... | collective-permute-start | bytes 196616 | tf_op jit(solution)/shard_map/ppermute | solution.py:37
  29.7 3.9 %collective-permute-start.5 = (f32[128,128]{1,0:T(8,128)S(1)}, f32[128,128]{1,0:T(8,128)S(1)}, u32[]{:S(2)}, u32[]{:S(2)}) collective-permute-start(f32[128,128]{1,0:T(8,128)S(1)} %bitcast.67), channel_id=1, source_target_pairs={{8,0},{16,8},{24,16},{9,1},{17,9},{25,17},{10,2},{18,10},{26,18},{... | collective-permute-start | bytes 196616 | tf_op jit(solution)/shard_map/ppermute | solution.py:36
  33.7 72.8 %collective-permute-start.6 = (f32[96,128]{1,0:T(8,128)S(1)}, f32[96,128]{1,0:T(8,128)S(1)}, u32[]{:S(2)}, u32[]{:S(2)}) collective-permute-start(f32[96,128]{1,0:T(8,128)S(1)} %bitcast.69), channel_id=1, source_target_pairs={{0,1},{1,2},{2,3},{3,4},{4,5},{5,6},{6,7},{8,9},{9,10},{10,11},{11... | collective-permute-start | bytes 147464 | tf_op jit(solution)/shard_map/ppermute | solution.py:37
  38.1 68.4 %collective-permute-start.7 = (f32[96,128]{1,0:T(8,128)S(1)}, f32[96,128]{1,0:T(8,128)S(1)}, u32[]{:S(2)}, u32[]{:S(2)}) collective-permute-start(f32[96,128]{1,0:T(8,128)S(1)} %bitcast.71), channel_id=1, source_target_pairs={{1,0},{2,1},{3,2},{4,3},{5,4},{6,5},{7,6},{9,8},{10,9},{11,10},{12... | collective-permute-start | bytes 147464 | tf_op jit(solution)/shard_map/ppermute | solution.py:36

commit v2 on v1

v2 whole, which is shorter than its diff:
```python
import functools

import jax
import jax.numpy as jnp
from jax import lax
from jax.experimental import pallas as pl
from jax.experimental.pallas import tpu as pltpu
from jax.sharding import PartitionSpec as P

ADJ_SWEEPS = 2
FILTER_SWEEPS = 4

eps_void = 1.0
eps_solid = 12.0
eps_back = 4.0
eps_metal = 40.0
screen = 0.5
radius_sq = 2.0
epsilon_mean = 1e-06

WIDTHS = (ADJ_SWEEPS + 1, ADJ_SWEEPS + 1, ADJ_SWEEPS, 1)
RIM = 4
VMEM_LIMIT = 24 * 1024 * 1024


def segments(widths, size_x):
    found, at = [], 0
    for field, width in enumerate(widths):
        for x in range(-width, size_x + width):
            rows = width - max(0, -x, x - size_x + 1)
            if rows > 0:
                found.append((field, x, rows, at))
                at += rows
    return found, -(-at // 8) * 8


def plane_starts(widths):
    starts, at = [], 0
    for width in widths:
        starts.append(at)
        at += width
    return starts, at


def material(density, labels):
    design = eps_void + density * density * density * (eps_solid - eps_void)
    return jnp.where(labels == 1, design, jnp.where(labels == 2, eps_metal, eps_back))


def call(body, outs, scratch=(), in_specs=None, cost=10000):
    kwargs = {} if in_specs is None else {"in_specs": in_specs, "grid": (1,)}
    return pl.pallas_call(
        body,
        out_shape=outs,
        scratch_shapes=list(scratch),
        compiler_params=pltpu.CompilerParams(vmem_limit_bytes=VMEM_LIMIT),
        cost_estimate=pl.CostEstimate(flops=cost, bytes_accessed=cost, transcendentals=0),
        **kwargs,
    )


def f32(*shape):
    return jax.ShapeDtypeStruct(shape, jnp.float32)


def pack_x(density, labels, adjoint, source, potential, low_out, high_out):
    size_x = density.shape[0]
    starts, _ = plane_starts(WIDTHS)
    for out, low in ((low_out, True), (high_out, False)):
        for field, width in enumerate(WIDTHS):
            span = pl.ds(0 if low else size_x - width, width)
            if field == 0:
                face = material(density[span], labels[span])
            else:
                face = (adjoint, source, potential)[field - 1][span]
            out[pl.ds(starts[field], width)] = face


def pack_y(size_x, from_low, from_high, density_l, labels_l, adjoint_l, source_l, potential_l,
           density_h, labels_h, adjoint_h, source_h, potential_h, low_out, high_out):
    starts, _ = plane_starts(WIDTHS)
    found, _ = segments(WIDTHS, size_x)
    size_y = from_low.shape[1]
    sides = (
        (low_out, (density_l, labels_l, adjoint_l, source_l, potential_l), True),
        (high_out, (density_h, labels_h, adjoint_h, source_h, potential_h), False),
    )
    for out, (density, labels, adjoint, source, potential), low in sides:
        for field, x, rows, at in found:
            own = slice(0, rows) if low else slice(8 - rows, 8)
            rim = slice(0, rows) if low else slice(size_y - rows, size_y)
            if x < 0:
                face = from_low[starts[field] + WIDTHS[field] + x, rim]
            elif x >= size_x:
                face = from_high[starts[field] + x - size_x, rim]
            elif field == 0:
                face = material(density[x, own], labels[x, own])
            else:
                face = (adjoint, source, potential)[field - 1][x, own]
            out[at:at + rows] = face


def shift(value, by, axis):
    return pltpu.roll(value, by % value.shape[axis], axis)


def adjoint_part(xlow, xhigh, ylow, yhigh, density, labels, adjoint_start, adjoint_source, potential,
                 raw_out, low_out, high_out, energy_out,
                 permit, start, source, poten, face_x, face_y, face_z, inverse, first, second):
    size_x, size_y, size_z = density.shape
    starts, _ = plane_starts(WIDTHS)
    found, _ = segments(WIDTHS, size_x)
    fields = (permit, start, source, poten)
    body = pl.ds(RIM, size_y)

    def fill(x, carry):
        permit[x + WIDTHS[0], body] = material(density[x], labels[x])
        start[x + WIDTHS[1], body] = adjoint_start[x]
        source[x + WIDTHS[2], body] = adjoint_source[x]
        poten[x + WIDTHS[3], body] = potential[x]
        return carry

    lax.fori_loop(0, size_x, fill, 0)
    for field, width in enumerate(WIDTHS):
        for k in range(width):
            fields[field][k, body] = xlow[starts[field] + k]
            fields[field][width + size_x + k, body] = xhigh[starts[field] + k]
    for field, x, rows, at in found:
        fields[field][x + WIDTHS[field], RIM - rows:RIM] = ylow[at:at + rows]
        fields[field][x + WIDTHS[field], RIM + size_y:RIM + size_y + rows] = yhigh[at:at + rows]

    wide = size_y + 2 * RIM
    lane = lax.broadcasted_iota(jnp.int32, (wide, size_z), 1)
    is_first = lane == 0
    is_last = lane == size_z - 1

    def harmonic(a, b):
        return 2.0 * a * b / jnp.maximum(a + b, 0.25)

    def faces_x(x, carry):
        face_x[x] = harmonic(permit[x], permit[x + 1])
        return carry

    lax.fori_loop(0, size_x + 5, faces_x, 0)

    def weigh(x, carry):
        p = permit[x + 1]
        fy = harmonic(p, shift(p, -1, 0))
        fz = jnp.where(is_last, 0.0, harmonic(p, shift(p, -1, 1)))
        face_y[x] = fy
        face_z[x] = fz
        total = screen + face_x[x] + face_x[x + 1] + fy + shift(fy, 1, 0) + fz + shift(fz, 1, 1)
        inverse[x] = jnp.where(p > 20.0, 0.0, 1.0 / total)
        return carry

    lax.fori_loop(0, size_x + 4, weigh, 0)

    def relax(x, a, a_low, a_high):
        fy, fz = face_y[x], face_z[x]
        total = source[x] + face_x[x + 1] * a_high + face_x[x] * a_low
        total = total + fy * shift(a, -1, 0) + shift(fy * a, 1, 0)
        total = total + fz * shift(a, -1, 1) + shift(fz * a, 1, 1)
        return total * inverse[x]

    def sweep_one(x, carry):
        first[x] = relax(x, start[x + 1], start[x], start[x + 2])
        return carry

    lax.fori_loop(0, size_x + 4, sweep_one, 0)

    def sweep_two(x, carry):
        second[x] = relax(x + 1, first[x + 1], first[x], first[x + 2])
        return carry

    lax.fori_loop(0, size_x + 2, sweep_two, 0)

    row = lax.broadcasted_iota(jnp.int32, (wide, size_z), 0)
    own = (row >= RIM) & (row < RIM + size_y)

    def finish(x, carry):
        v, a = poten[x + 1], second[x + 1]
        product = jnp.zeros_like(v)
        squares = jnp.zeros_like(v)
        for k in (0, 2):
            dv, da = poten[x + k] - v, second[x + k] - a
            product = product + dv * da
            squares = squares + dv * dv
        dv, da = shift(v, -1, 0) - v, shift(a, -1, 0) - a
        both, square = dv * da, dv * dv
        product = product + both + shift(both, 1, 0)
        squares = squares + square + shift(square, 1, 0)
        dv = jnp.where(is_last, 0.0, shift(v, -1, 1)) - v
        da = jnp.where(is_last, 0.0, shift(a, -1, 1)) - a
        both, square = dv * da, dv * dv
        product = product + both + jnp.where(is_first, v * a, shift(both, 1, 1))
        squares = squares + square + jnp.where(is_first, v * v, shift(square, 1, 1))
        energy = jnp.where(own, permit[x + 3] * squares, 0.0)
        d = density[x]
        gain = jnp.where(labels[x] == 1, -1.5 * (eps_solid - eps_void) * d * d, 0.0)
        raw_out[x] = gain * product[RIM:RIM + size_y]
        for k in range(wide // 8):
            carry = carry + energy[8 * k:8 * k + 8]
        return carry

    energy_out[...] = lax.fori_loop(0, size_x, finish, jnp.zeros((8, size_z), jnp.float32))
    low_out[...] = raw_out[pl.ds(0, FILTER_SWEEPS)]
    high_out[...] = raw_out[pl.ds(size_x - FILTER_SWEEPS, FILTER_SWEEPS)]


def pack_raw_y(from_low, from_high, raw, low_out, high_out):
    size_x, size_y, _ = raw.shape
    found, _ = segments((FILTER_SWEEPS,), size_x)
    for out, low in ((low_out, True), (high_out, False)):
        for _, x, rows, at in found:
            rim = slice(0, rows) if low else slice(size_y - rows, size_y)
            if x < 0:
                face = from_low[FILTER_SWEEPS + x, rim]
            elif x >= size_x:
                face = from_high[x - size_x, rim]
            else:
                face = raw[x, rim]
            out[at:at + rows] = face


def filter_part(xlow, xhigh, ylow, yhigh, raw_in, labels, out, raw, even, odd):
    size_x, size_y, size_z = raw_in.shape
    width = FILTER_SWEEPS
    found, _ = segments((width,), size_x)
    body = pl.ds(RIM, size_y)

    def fill(x, carry):
        raw[x + width, body] = raw_in[x]
        return carry

    lax.fori_loop(0, size_x, fill, 0)
    for k in range(width):
        raw[k, body] = xlow[k]
        raw[width + size_x + k, body] = xhigh[k]
    for _, x, rows, at in found:
        raw[x + width, RIM - rows:RIM] = ylow[at:at + rows]
        raw[x + width, RIM + size_y:RIM + size_y + rows] = yhigh[at:at + rows]

    wide = size_y + 2 * RIM
    extent_x = lax.axis_size("gx") * size_x
    extent_y = lax.axis_size("gy") * size_y
    base_x = lax.axis_index("gx") * size_x - width
    lane = lax.broadcasted_iota(jnp.int32, (wide, size_z), 1)
    place = lax.broadcasted_iota(jnp.int32, (wide, size_z), 0) + (lax.axis_index("gy") * size_y - RIM)
    is_first, is_last = lane == 0, lane == size_z - 1

    def edges(at, extent):
        return jnp.where(at > 0, 1.0, 0.0) + jnp.where(at < extent - 1, 1.0, 0.0)

    count = edges(place, extent_y) + edges(lane, size_z)
    inside = (place >= 0) & (place < extent_y)
    scale_two = jnp.where(inside, 1.0 / (1.0 + radius_sq * (count + 2.0)), 0.0)
    scale_one = jnp.where(inside, 1.0 / (1.0 + radius_sq * (count + 1.0)), 0.0)

    def relax(src, x):
        f = src[x]
        near = src[x - 1] + src[x + 1] + shift(f, 1, 0) + shift(f, -1, 0)
        near = near + jnp.where(is_first, 0.0, shift(f, 1, 1)) + jnp.where(is_last, 0.0, shift(f, -1, 1))
        at = base_x + x
        outside = (at < 0) | (at >= extent_x)
        border = (at == 0) | (at == extent_x - 1)
        scale = jnp.where(outside, 0.0, jnp.where(border, scale_one, scale_two))
        return (raw[x] + radius_sq * near) * scale

    src = raw
    for sweep in range(FILTER_SWEEPS - 1):
        dst = (even, odd)[sweep % 2]

        def step(x, carry, src=src, dst=dst):
            dst[x] = relax(src, x)
            return carry

        lax.fori_loop(sweep + 1, size_x + 2 * width - sweep - 1, step, 0)
        src = dst

    def last(x, carry):
        f = relax(src, x + width)
        out[x] = jnp.where(labels[x] == 1, f[RIM:RIM + size_y], 0.0)
        return carry

    lax.fori_loop(0, size_x, last, 0)


def rescale(voxels, filtered, mine, other, out, mean_out):
    total = jnp.sum(mine[...] + other[...])
    mean = 0.5 * total / voxels + epsilon_mean
    mean_out[0, 0] = mean
    out[...] = filtered[...] * (1.0 / jnp.full((1, 1, out.shape[2]), mean, jnp.float32))


def both_ways(low, high, axis):
    count = lax.axis_size(axis)
    forward = [(i, i + 1) for i in range(count - 1)]
    backward = [(b, a) for a, b in forward]
    from_high = lax.ppermute(low, axis, backward)
    from_low = lax.ppermute(high, axis, forward)
    return from_low, from_high


def partner(value, axis, bit):
    return lax.ppermute(value, axis, [(i, i ^ bit) for i in range(lax.axis_size(axis))])


def shards(density, potential, adjoint_start, adjoint_source, labels):
    size_x, size_y, size_z = potential.shape
    _, planes = plane_starts(WIDTHS)
    _, rows = segments(WIDTHS, size_x)
    own = (density, labels, adjoint_start, adjoint_source, potential)

    low, high = call(pack_x, (f32(planes, size_y, size_z),) * 2)(*own)
    xlow, xhigh = both_ways(low, high, "gx")
    top, end = (0, 0, 0), (0, size_y // 8 - 1, 0)
    whole = pl.BlockSpec((planes, size_y, size_z), lambda i: (0, 0, 0))
    low_spec = pl.BlockSpec((size_x, 8, size_z), lambda i: top)
    high_spec = pl.BlockSpec((size_x, 8, size_z), lambda i: end)
    low, high = call(
        functools.partial(pack_y, size_x),
        (f32(rows, size_z),) * 2,
        in_specs=[whole] * 2 + [low_spec] * 5 + [high_spec] * 5,
    )(xlow, xhigh, *own, *own)
    ylow, yhigh = both_ways(low, high, "gy")

    wide = size_y + 2 * RIM

    def room(extra):
        return pltpu.VMEM((size_x + extra, wide, size_z), jnp.float32)

    face = f32(FILTER_SWEEPS, size_y, size_z)
    raw, low, high, energy = call(
        adjoint_part,
        (f32(size_x, size_y, size_z), face, face, f32(8, size_z)),
        [room(6), room(6), room(4), room(2), room(5), room(4), room(4), room(4), room(4), room(2)],
    )(xlow, xhigh, ylow, yhigh, *own)

    xlow, xhigh = both_ways(low, high, "gx")
    stages = [("gx", 1 << k) for k in range((lax.axis_size("gx") - 1).bit_length())]
    stages += [("gy", 1 << k) for k in range((lax.axis_size("gy") - 1).bit_length())]
    other = partner(energy, *stages[0])
    _, rows = segments((FILTER_SWEEPS,), size_x)
    low, high = call(pack_raw_y, (f32(rows, size_z),) * 2)(xlow, xhigh, raw)
    ylow, yhigh = both_ways(low, high, "gy")
    for stage in stages[1:]:
        energy = energy + other
        other = partner(energy, *stage)
    filtered = call(
        filter_part,
        f32(size_x, size_y, size_z),
        [room(2 * FILTER_SWEEPS)] * 3,
    )(xlow, xhigh, ylow, yhigh, raw, labels)
    voxels = lax.axis_size("gx") * size_x * lax.axis_size("gy") * size_y * size_z
    sensitivity, mean_energy = pl.pallas_call(
        functools.partial(rescale, float(voxels)),
        out_shape=(f32(size_x, size_y, size_z), f32(1, 1)),
        out_specs=(pl.BlockSpec(memory_space=pltpu.VMEM), pl.BlockSpec(memory_space=pltpu.SMEM)),
        compiler_params=pltpu.CompilerParams(vmem_limit_bytes=VMEM_LIMIT),
    )(filtered, energy, other)
    return (sensitivity, mean_energy[0, 0])


def solution(mesh):
    spec = P("gx", "gy", None)
    return jax.shard_map(
        shards, mesh=mesh, in_specs=(spec,) * 5, out_specs=(spec, P()), check_vma=False
    )
```

time: 112 us -> 71.9 us (0.64); the launches traced: 110 us -> 71.4 us
  blocking collectives: 65.5 us -> 0 us
  Pallas kernels: 0 us -> 16.8 us
  starting transfers between devices: 19.5 us -> 30.3 us
  waiting for transfers between devices: 11 us -> 18.9 us
  other arithmetic: 6.97 us -> 0.01 us
  between operations: 3.18 us -> 0.78 us
    all_gather x1 -> x0, blocking collectives: 65.5 us -> none  [shards(): energies = lax.all_gather(energy, ('gx', 'gy'), axis=0, tiled=True)]
    pallas_call x0 -> x6, Pallas kernels: none -> 16.8 us  [the longest x1 9.29 us: shards(): call(adjoint_part, (f32(size_x, size_y, size_z), face, face, f32(8, size_...]
    ppermute x8 -> x13, starting transfers between devices: 19.5 us -> 30.3 us  [the longest x4 14.4 us: both_ways(): from_low = lax.ppermute(high, axis, forward)]
    ppermute x8 -> x13, waiting for transfers between devices: 11 us -> 18.9 us  [the longest x4 11 us: both_ways(): from_high = lax.ppermute(low, axis, backward)]
    select_n x4 -> x0, other arithmetic: 3.23 us -> none  [the longest x1 1.4 us: material(): jnp.where(labels == 1, design, jnp.where(labels == 2, eps_metal, eps_back))]
    mul x4 -> x0, other arithmetic: 1.93 us -> none  [the longest x2 1.17 us: shards(): adjoint = total * crop(inverse, 2, have)]
    unnamed x14 -> x12, local copies, waits for them, and re-layouts: 3.19 us -> 4.75 us
  transfers between devices with their start and end apart: 8 -> 13, of which waited for: 4 -> 8; matrix products, arithmetic and copies ran while one was open for 2% -> 0% of each run, Pallas kernels for 0% -> 9%
where the time goes in v2:
time: 71.9 us; the launch traced here: 71.4 us
  starting transfers between devices  30.3 us (42%)
  waiting for transfers between devices  18.9 us (26%)
  Pallas kernels  16.8 us (23%)
  local copies, waits for them, and re-layouts  4.75 us (7%)
  between operations  0.78 us (1%)
    ppermute x4, starting transfers between devices, both_ways(): from_low = lax.ppermute(high, axis, forward)  14.4 us
    ppermute x4, waiting for transfers between devices, both_ways(): from_high = lax.ppermute(low, axis, backward)  11 us
    ppermute x5, starting transfers between devices, partner(): lax.ppermute(value, axis, [(i, i ^ bit) for i in range(lax.axis_size(axis...  10.7 us
    pallas_call x1, Pallas kernels, shards(): call(adjoint_part, (f32(size_x, size_y, size_z), face, face, f32(8, size_...  9.29 us
    ppermute x5, waiting for transfers between devices, partner(): lax.ppermute(value, axis, [(i, i ^ bit) for i in range(lax.axis_size(axis...  7.13 us
    pallas_call x1, Pallas kernels, shards(): call(filter_part, f32(size_x, size_y, size_z), [room(2 * FILTER_SWEEPS)]...  6.45 us
    ppermute x4, starting transfers between devices, both_ways(): from_high = lax.ppermute(low, axis, backward)  5.17 us
    unnamed x12, local copies, waits for them, and re-layouts  4.75 us
  transfers between devices with their start and end apart: 13, of which 8 were waited for; matrix products, arithmetic and copies ran while one was open for 0% of the time, Pallas kernels for 9%

profile of v2, /device:TPU:0, one launch (start us, length us, event | category | flops | bytes accessed | tf_op | source)
XLA Modules:
  0.0 71.4 jit_solution(11287800071407604631)
XLA Ops:
  0.6 0.0 copy-start
  0.6 0.9 %copy-done = s32[16,32,128]{2,1,0:T(8,128)S(1)} copy-done((s32[16,32,128]{2,1,0:T(8,128)S(1)}, s32[16,32,128]{2,1,0:T(8,128)}, u32[]{:S(2)}) %copy-start) | copy-done | bytes 262168
  1.6 0.0 copy-start.2
  1.6 0.9 %copy-done.2 = f32[16,32,128]{2,1,0:T(8,128)S(1)} copy-done((f32[16,32,128]{2,1,0:T(8,128)S(1)}, f32[16,32,128]{2,1,0:T(8,128)}, u32[]{:S(2)}) %copy-start.2) | copy-done | bytes 262168
  2.5 0.0 copy-start.3
  2.5 0.9 %copy-done.3 = f32[16,32,128]{2,1,0:T(8,128)S(1)} copy-done((f32[16,32,128]{2,1,0:T(8,128)S(1)}, f32[16,32,128]{2,1,0:T(8,128)}, u32[]{:S(2)}) %copy-start.3) | copy-done | bytes 262168
  3.5 0.0 copy-start.4
  3.5 0.9 %copy-done.4 = f32[16,32,128]{2,1,0:T(8,128)S(1)} copy-done((f32[16,32,128]{2,1,0:T(8,128)S(1)}, f32[16,32,128]{2,1,0:T(8,128)}, u32[]{:S(2)}) %copy-start.4) | copy-done | bytes 262168
  4.4 0.0 copy-start.5
  4.4 0.9 %copy-done.5 = f32[16,32,128]{2,1,0:T(8,128)S(1)} copy-done((f32[16,32,128]{2,1,0:T(8,128)S(1)}, f32[16,32,128]{2,1,0:T(8,128)}, u32[]{:S(2)}) %copy-start.5) | copy-done | bytes 262168
  5.4 2.4 %collective-permute-start = (f32[9,32,128]{2,1,0:T(8,128)S(1)}, f32[9,32,128]{2,1,0:T(8,128)S(1)}, u32[]{:S(2)}, u32[]{:S(2)}) collective-permute-start(f32[9,32,128]{2,1,0:T(8,128)S(1)} %get-tuple-element.14), channel_id=1, source_target_pairs={{0,8},{8,16},{16,24},{1,9},{9,17},{17,25},{2,10},{10,18},{18,26},{... | collective-permute-start | bytes 442376 | tf_op jit(solution)/shard_map/ppermute | solution.py:300
  7.8 1.3 %collective-permute-start.1 = (f32[9,32,128]{2,1,0:T(8,128)S(1)}, f32[9,32,128]{2,1,0:T(8,128)S(1)}, u32[]{:S(2)}, u32[]{:S(2)}) collective-permute-start(f32[9,32,128]{2,1,0:T(8,128)S(1)} %get-tuple-element.15), channel_id=1, source_target_pairs={{8,0},{16,8},{24,16},{9,1},{17,9},{25,17},{10,2},{18,10},{26,18},{... | collective-permute-start | bytes 442376 | tf_op jit(solution)/shard_map/ppermute | solution.py:299
  9.1 0.0 collective-permute-done.from_low.xlow
  9.1 4.1 %collective-permute-done.1.from_high.xhigh = f32[9,32,128]{2,1,0:T(8,128)S(1)} collective-permute-done((f32[9,32,128]{2,1,0:T(8,128)S(1)}, f32[9,32,128]{2,1,0:T(8,128)S(1)}, u32[]{:S(2)}, u32[]{:S(2)}) %collective-permute-start.1) | collective-permute-done | bytes 147488 | tf_op jit(solution)/shard_map/ppermute | solution.py:299
  13.2 0.1 shard_map.69
  13.3 3.4 %collective-permute-start.2 = (f32[160,128]{1,0:T(8,128)S(1)}, f32[160,128]{1,0:T(8,128)S(1)}, u32[]{:S(2)}, u32[]{:S(2)}) collective-permute-start(f32[160,128]{1,0:T(8,128)S(1)} %get-tuple-element.16), channel_id=1, source_target_pairs={{0,1},{1,2},{2,3},{3,4},{4,5},{5,6},{6,7},{8,9},{9,10},{10,11},{11... | collective-permute-start | bytes 245768 | tf_op jit(solution)/shard_map/ppermute | solution.py:300
  16.7 1.3 %collective-permute-start.3 = (f32[160,128]{1,0:T(8,128)S(1)}, f32[160,128]{1,0:T(8,128)S(1)}, u32[]{:S(2)}, u32[]{:S(2)}) collective-permute-start(f32[160,128]{1,0:T(8,128)S(1)} %get-tuple-element.17), channel_id=1, source_target_pairs={{1,0},{2,1},{3,2},{4,3},{5,4},{6,5},{7,6},{9,8},{10,9},{11,10},{12... | collective-permute-start | bytes 245768 | tf_op jit(solution)/shard_map/ppermute | solution.py:299
  18.0 0.7 %collective-permute-done.2.ylow = f32[160,128]{1,0:T(8,128)S(1)} collective-permute-done((f32[160,128]{1,0:T(8,128)S(1)}, f32[160,128]{1,0:T(8,128)S(1)}, u32[]{:S(2)}, u32[]{:S(2)}) %collective-permute-start.2) | collective-permute-done | bytes 81952 | tf_op jit(solution)/shard_map/ppermute | solution.py:300
  18.8 4.3 %collective-permute-done.3.yhigh = f32[160,128]{1,0:T(8,128)S(1)} collective-permute-done((f32[160,128]{1,0:T(8,128)S(1)}, f32[160,128]{1,0:T(8,128)S(1)}, u32[]{:S(2)}, u32[]{:S(2)}) %collective-permute-start.3) | collective-permute-done | bytes 81952 | tf_op jit(solution)/shard_map/ppermute | solution.py:299
  23.1 9.3 %shard_map.70 = (f32[16,32,128]{2,1,0:T(8,128)S(1)}, f32[4,32,128]{2,1,0:T(8,128)S(1)}, f32[4,32,128]{2,1,0:T(8,128)S(1)}, f32[8,128]{1,0:T(8,128)S(1)}) custom-call(f32[9,32,128]{2,1,0:T(8,128)S(1)} %collective-permute-done.from_low.xlow, f32[9,32,128]{2,1,0:T(8,128)S(1)} %collective-permute-done.1.from_high.xhigh, ...), custom_call_target="tpu_custom_call" | custom-call | flops 10000 | bytes 10000 | tf_op jit(solution)/shard_map/pallas_call | solution.py:333
  32.4 0.0 copy-start.1
  32.4 4.3 %collective-permute-start.4 = (f32[4,32,128]{2,1,0:T(8,128)S(1)}, f32[4,32,128]{2,1,0:T(8,128)S(1)}, u32[]{:S(2)}, u32[]{:S(2)}) collective-permute-start(f32[4,32,128]{2,1,0:T(8,128)S(1)} %get-tuple-element.18), channel_id=1, source_target_pairs={{0,8},{8,16},{16,24},{1,9},{9,17},{17,25},{2,10},{10,18},{18,26},{... | collective-permute-start | bytes 196616 | tf_op jit(solution)/shard_map/ppermute | solution.py:300
  36.7 1.3 %collective-permute-start.5 = (f32[4,32,128]{2,1,0:T(8,128)S(1)}, f32[4,32,128]{2,1,0:T(8,128)S(1)}, u32[]{:S(2)}, u32[]{:S(2)}) collective-permute-start(f32[4,32,128]{2,1,0:T(8,128)S(1)} %get-tuple-element.19), channel_id=1, source_target_pairs={{8,0},{16,8},{24,16},{9,1},{17,9},{25,17},{10,2},{18,10},{26,18},{... | collective-permute-start | bytes 196616 | tf_op jit(solution)/shard_map/ppermute | solution.py:299
  38.0 0.0 collective-permute-done.4.from_low.xlow
  38.0 2.6 %collective-permute-done.5.from_high.xhigh = f32[4,32,128]{2,1,0:T(8,128)S(1)} collective-permute-done((f32[4,32,128]{2,1,0:T(8,128)S(1)}, f32[4,32,128]{2,1,0:T(8,128)S(1)}, u32[]{:S(2)}, u32[]{:S(2)}) %collective-permute-start.5) | collective-permute-done | bytes 65568 | tf_op jit(solution)/shard_map/ppermute | solution.py:299
  40.6 4.3 %collective-permute-start.6 = (f32[80,128]{1,0:T(8,128)S(1)}, f32[80,128]{1,0:T(8,128)S(1)}, u32[]{:S(2)}, u32[]{:S(2)}) collective-permute-start(f32[80,128]{1,0:T(8,128)S(1)} %get-tuple-element.21), channel_id=1, source_target_pairs={{0,1},{1,2},{2,3},{3,4},{4,5},{5,6},{6,7},{8,9},{9,10},{10,11},{11... | collective-permute-start | bytes 122888 | tf_op jit(solution)/shard_map/ppermute | solution.py:300
  45.0 1.3 %collective-permute-start.7 = (f32[80,128]{1,0:T(8,128)S(1)}, f32[80,128]{1,0:T(8,128)S(1)}, u32[]{:S(2)}, u32[]{:S(2)}) collective-permute-start(f32[80,128]{1,0:T(8,128)S(1)} %get-tuple-element.22), channel_id=1, source_target_pairs={{1,0},{2,1},{3,2},{4,3},{5,4},{6,5},{7,6},{9,8},{10,9},{11,10},{12... | collective-permute-start | bytes 122888 | tf_op jit(solution)/shard_map/ppermute | solution.py:299
  46.3 2.7 %collective-permute-start.8 = (f32[8,128]{1,0:T(8,128)S(1)}, f32[8,128]{1,0:T(8,128)S(1)}, u32[]{:S(2)}, u32[]{:S(2)}) collective-permute-start(f32[8,128]{1,0:T(8,128)S(1)} %get-tuple-element.23), channel_id=1, source_target_pairs={{0,8},{8,0},{16,24},{24,16},{1,9},{9,1},{17,25},{25,17},{2,10},{10... | collective-permute-start | bytes 12296 | tf_op jit(solution)/shard_map/ppermute | solution.py:305
  49.0 0.8 %collective-permute-done.8 = f32[8,128]{1,0:T(8,128)S(1)} collective-permute-done((f32[8,128]{1,0:T(8,128)S(1)}, f32[8,128]{1,0:T(8,128)S(1)}, u32[]{:S(2)}, u32[]{:S(2)}) %collective-permute-start.8) | collective-permute-done | bytes 4128 | tf_op jit(solution)/shard_map/ppermute | solution.py:305
  49.8 0.5 collective-permute-start.9
  50.3 3.1 %collective-permute-done.9 = f32[8,128]{1,0:T(8,128)S(1)} collective-permute-done((f32[8,128]{1,0:T(8,128)S(1)}, f32[8,128]{1,0:T(8,128)S(1)}, u32[]{:S(2)}, u32[]{:S(2)}) %collective-permute-start.9) | collective-permute-done | bytes 4128 | tf_op jit(solution)/shard_map/ppermute | solution.py:305
  53.4 2.4 %collective-permute-start.10 = (f32[8,128]{1,0:T(8,128)S(1)}, f32[8,128]{1,0:T(8,128)S(1)}, u32[]{:S(2)}, u32[]{:S(2)}) collective-permute-start(f32[8,128]{1,0:T(8,128)S(1)} %add.13), channel_id=1, source_target_pairs={{0,1},{1,0},{2,3},{3,2},{4,5},{5,4},{6,7},{7,6},{8,9},{9,8},{10,11... | collective-permute-start | bytes 12296 | tf_op jit(solution)/shard_map/ppermute | solution.py:305
  55.8 1.6 %collective-permute-done.10 = f32[8,128]{1,0:T(8,128)S(1)} collective-permute-done((f32[8,128]{1,0:T(8,128)S(1)}, f32[8,128]{1,0:T(8,128)S(1)}, u32[]{:S(2)}, u32[]{:S(2)}) %collective-permute-start.10) | collective-permute-done | bytes 4128 | tf_op jit(solution)/shard_map/ppermute | solution.py:305
  57.4 2.1 %collective-permute-start.11 = (f32[8,128]{1,0:T(8,128)S(1)}, f32[8,128]{1,0:T(8,128)S(1)}, u32[]{:S(2)}, u32[]{:S(2)}) collective-permute-start(f32[8,128]{1,0:T(8,128)S(1)} %add.14), channel_id=1, source_target_pairs={{0,2},{1,3},{2,0},{3,1},{4,6},{5,7},{6,4},{7,5},{8,10},{9,11},{10,... | collective-permute-start | bytes 12296 | tf_op jit(solution)/shard_map/ppermute | solution.py:305
  59.5 1.6 %collective-permute-done.11 = f32[8,128]{1,0:T(8,128)S(1)} collective-permute-done((f32[8,128]{1,0:T(8,128)S(1)}, f32[8,128]{1,0:T(8,128)S(1)}, u32[]{:S(2)}, u32[]{:S(2)}) %collective-permute-start.11) | collective-permute-done | bytes 4128 | tf_op jit(solution)/shard_map/ppermute | solution.py:305
  61.0 3.0 %collective-permute-start.12 = (f32[8,128]{1,0:T(8,128)S(1)}, f32[8,128]{1,0:T(8,128)S(1)}, u32[]{:S(2)}, u32[]{:S(2)}) collective-permute-start(f32[8,128]{1,0:T(8,128)S(1)} %add.15.mine), channel_id=1, source_target_pairs={{0,4},{1,5},{2,6},{3,7},{4,0},{5,1},{6,2},{7,3},{8,12},{9,13},{10,... | collective-permute-start | bytes 12296 | tf_op jit(solution)/shard_map/ppermute | solution.py:305
  64.1 0.0 collective-permute-done.6.ylow
  64.1 0.0 collective-permute-done.7.yhigh
  64.1 0.0 copy-done.1
  64.1 6.4 %shard_map.72.filtered = f32[16,32,128]{2,1,0:T(8,128)S(1)} custom-call(f32[4,32,128]{2,1,0:T(8,128)S(1)} %collective-permute-done.4.from_low.xlow, f32[4,32,128]{2,1,0:T(8,128)S(1)} %collective-permute-done.5.from_high.xhigh, f32[80,128]{1,0:T(8,128)S(1)} %collective-permute-done.6.ylow, f32[80,128]{1,0:T(8,128)S(1)} %collective-permute-done.7.yhigh, ...), custom_call_target="tpu_custom_call" | custom-call | flops 10000 | bytes 10000 | tf_op jit(solution)/shard_map/pallas_call | solution.py:349
  70.5 0.0 collective-permute-done.12.other
  70.6 0.9 %shard_map.73 = (f32[16,32,128]{2,1,0:T(8,128)}, f32[1,1]{1,0:T(1,128)}) custom-call(f32[16,32,128]{2,1,0:T(8,128)S(1)} %shard_map.72.filtered, f32[8,128]{1,0:T(8,128)S(1)} %add.15.mine, f32[8,128]{1,0:T(8,128)S(1)} %collective-permute-done.12.other), custom_call_target="tpu_custom_call" | custom-call | tf_op jit(solution)/shard_map/pallas_call | solution.py:355
  (6 shorter events, 0.1 us)
Async XLA Ops:
  0.6 1.0 %copy-start = (s32[16,32,128]{2,1,0:T(8,128)S(1)}, s32[16,32,128]{2,1,0:T(8,128)}, u32[]{:S(2)}) copy-start(s32[16,32,128]{2,1,0:T(8,128)} %labels.5) | copy-start | bytes 786436
  1.6 0.9 %copy-start.2 = (f32[16,32,128]{2,1,0:T(8,128)S(1)}, f32[16,32,128]{2,1,0:T(8,128)}, u32[]{:S(2)}) copy-start(f32[16,32,128]{2,1,0:T(8,128)} %density.3) | copy-start | bytes 786436
  2.5 0.9 %copy-start.3 = (f32[16,32,128]{2,1,0:T(8,128)S(1)}, f32[16,32,128]{2,1,0:T(8,128)}, u32[]{:S(2)}) copy-start(f32[16,32,128]{2,1,0:T(8,128)} %adjoint_start.1) | copy-start | bytes 786436
  3.5 0.9 %copy-start.4 = (f32[16,32,128]{2,1,0:T(8,128)S(1)}, f32[16,32,128]{2,1,0:T(8,128)}, u32[]{:S(2)}) copy-start(f32[16,32,128]{2,1,0:T(8,128)} %adjoint_source.1) | copy-start | bytes 786436
  4.4 0.9 %copy-start.5 = (f32[16,32,128]{2,1,0:T(8,128)S(1)}, f32[16,32,128]{2,1,0:T(8,128)}, u32[]{:S(2)}) copy-start(f32[16,32,128]{2,1,0:T(8,128)} %potential.3) | copy-start | bytes 786436
  5.4 3.7 %collective-permute-start = (f32[9,32,128]{2,1,0:T(8,128)S(1)}, f32[9,32,128]{2,1,0:T(8,128)S(1)}, u32[]{:S(2)}, u32[]{:S(2)}) collective-permute-start(f32[9,32,128]{2,1,0:T(8,128)S(1)} %get-tuple-element.14), channel_id=1, source_target_pairs={{0,8},{8,16},{16,24},{1,9},{9,17},{17,25},{2,10},{10,18},{18,26},{... | collective-permute-start | bytes 442376 | tf_op jit(solution)/shard_map/ppermute | solution.py:300
  7.8 5.4 %collective-permute-start.1 = (f32[9,32,128]{2,1,0:T(8,128)S(1)}, f32[9,32,128]{2,1,0:T(8,128)S(1)}, u32[]{:S(2)}, u32[]{:S(2)}) collective-permute-start(f32[9,32,128]{2,1,0:T(8,128)S(1)} %get-tuple-element.15), channel_id=1, source_target_pairs={{8,0},{16,8},{24,16},{9,1},{17,9},{25,17},{10,2},{18,10},{26,18},{... | collective-permute-start | bytes 442376 | tf_op jit(solution)/shard_map/ppermute | solution.py:299
  13.3 5.5 %collective-permute-start.2 = (f32[160,128]{1,0:T(8,128)S(1)}, f32[160,128]{1,0:T(8,128)S(1)}, u32[]{:S(2)}, u32[]{:S(2)}) collective-permute-start(f32[160,128]{1,0:T(8,128)S(1)} %get-tuple-element.16), channel_id=1, source_target_pairs={{0,1},{1,2},{2,3},{3,4},{4,5},{5,6},{6,7},{8,9},{9,10},{10,11},{11... | collective-permute-start | bytes 245768 | tf_op jit(solution)/shard_map/ppermute | solution.py:300
  16.7 6.3 %collective-permute-start.3 = (f32[160,128]{1,0:T(8,128)S(1)}, f32[160,128]{1,0:T(8,128)S(1)}, u32[]{:S(2)}, u32[]{:S(2)}) collective-permute-start(f32[160,128]{1,0:T(8,128)S(1)} %get-tuple-element.17), channel_id=1, source_target_pairs={{1,0},{2,1},{3,2},{4,3},{5,4},{6,5},{7,6},{9,8},{10,9},{11,10},{12... | collective-permute-start | bytes 245768 | tf_op jit(solution)/shard_map/ppermute | solution.py:299
  32.4 31.7 %copy-start.1 = (s32[16,32,128]{2,1,0:T(8,128)S(1)}, s32[16,32,128]{2,1,0:T(8,128)}, u32[]{:S(2)}) copy-start(s32[16,32,128]{2,1,0:T(8,128)} %labels.5) | copy-start | bytes 786436
  32.4 5.6 %collective-permute-start.4 = (f32[4,32,128]{2,1,0:T(8,128)S(1)}, f32[4,32,128]{2,1,0:T(8,128)S(1)}, u32[]{:S(2)}, u32[]{:S(2)}) collective-permute-start(f32[4,32,128]{2,1,0:T(8,128)S(1)} %get-tuple-element.18), channel_id=1, source_target_pairs={{0,8},{8,16},{16,24},{1,9},{9,17},{17,25},{2,10},{10,18},{18,26},{... | collective-permute-start | bytes 196616 | tf_op jit(solution)/shard_map/ppermute | solution.py:300
  36.7 3.9 %collective-permute-start.5 = (f32[4,32,128]{2,1,0:T(8,128)S(1)}, f32[4,32,128]{2,1,0:T(8,128)S(1)}, u32[]{:S(2)}, u32[]{:S(2)}) collective-permute-start(f32[4,32,128]{2,1,0:T(8,128)S(1)} %get-tuple-element.19), channel_id=1, source_target_pairs={{8,0},{16,8},{24,16},{9,1},{17,9},{25,17},{10,2},{18,10},{26,18},{... | collective-permute-start | bytes 196616 | tf_op jit(solution)/shard_map/ppermute | solution.py:299
  40.6 23.5 %collective-permute-start.6 = (f32[80,128]{1,0:T(8,128)S(1)}, f32[80,128]{1,0:T(8,128)S(1)}, u32[]{:S(2)}, u32[]{:S(2)}) collective-permute-start(f32[80,128]{1,0:T(8,128)S(1)} %get-tuple-element.21), channel_id=1, source_target_pairs={{0,1},{1,2},{2,3},{3,4},{4,5},{5,6},{6,7},{8,9},{9,10},{10,11},{11... | collective-permute-start | bytes 122888 | tf_op jit(solution)/shard_map/ppermute | solution.py:300
  45.0 19.1 %collective-permute-start.7 = (f32[80,128]{1,0:T(8,128)S(1)}, f32[80,128]{1,0:T(8,128)S(1)}, u32[]{:S(2)}, u32[]{:S(2)}) collective-permute-start(f32[80,128]{1,0:T(8,128)S(1)} %get-tuple-element.22), channel_id=1, source_target_pairs={{1,0},{2,1},{3,2},{4,3},{5,4},{6,5},{7,6},{9,8},{10,9},{11,10},{12... | collective-permute-start | bytes 122888 | tf_op jit(solution)/shard_map/ppermute | solution.py:299
  46.3 3.5 %collective-permute-start.8 = (f32[8,128]{1,0:T(8,128)S(1)}, f32[8,128]{1,0:T(8,128)S(1)}, u32[]{:S(2)}, u32[]{:S(2)}) collective-permute-start(f32[8,128]{1,0:T(8,128)S(1)} %get-tuple-element.23), channel_id=1, source_target_pairs={{0,8},{8,0},{16,24},{24,16},{1,9},{9,1},{17,25},{25,17},{2,10},{10... | collective-permute-start | bytes 12296 | tf_op jit(solution)/shard_map/ppermute | solution.py:305
  49.8 3.6 %collective-permute-start.9 = (f32[8,128]{1,0:T(8,128)S(1)}, f32[8,128]{1,0:T(8,128)S(1)}, u32[]{:S(2)}, u32[]{:S(2)}) collective-permute-start(f32[8,128]{1,0:T(8,128)S(1)} %add.12), channel_id=1, source_target_pairs={{0,16},{8,24},{16,0},{24,8},{1,17},{9,25},{17,1},{25,9},{2,18},{10... | collective-permute-start | bytes 12296 | tf_op jit(solution)/shard_map/ppermute | solution.py:305
  53.4 3.9 %collective-permute-start.10 = (f32[8,128]{1,0:T(8,128)S(1)}, f32[8,128]{1,0:T(8,128)S(1)}, u32[]{:S(2)}, u32[]{:S(2)}) collective-permute-start(f32[8,128]{1,0:T(8,128)S(1)} %add.13), channel_id=1, source_target_pairs={{0,1},{1,0},{2,3},{3,2},{4,5},{5,4},{6,7},{7,6},{8,9},{9,8},{10,11... | collective-permute-start | bytes 12296 | tf_op jit(solution)/shard_map/ppermute | solution.py:305
  57.4 3.7 %collective-permute-start.11 = (f32[8,128]{1,0:T(8,128)S(1)}, f32[8,128]{1,0:T(8,128)S(1)}, u32[]{:S(2)}, u32[]{:S(2)}) collective-permute-start(f32[8,128]{1,0:T(8,128)S(1)} %add.14), channel_id=1, source_target_pairs={{0,2},{1,3},{2,0},{3,1},{4,6},{5,7},{6,4},{7,5},{8,10},{9,11},{10,... | collective-permute-start | bytes 12296 | tf_op jit(solution)/shard_map/ppermute | solution.py:305
  61.0 9.5 %collective-permute-start.12 = (f32[8,128]{1,0:T(8,128)S(1)}, f32[8,128]{1,0:T(8,128)S(1)}, u32[]{:S(2)}, u32[]{:S(2)}) collective-permute-start(f32[8,128]{1,0:T(8,128)S(1)} %add.15.mine), channel_id=1, source_target_pairs={{0,4},{1,5},{2,6},{3,7},{4,0},{5,1},{6,2},{7,3},{8,12},{9,13},{10,... | collective-permute-start | bytes 12296 | tf_op jit(solution)/shard_map/ppermute | solution.py:305

commit v3 on v2

--- a/solution.py
+++ b/solution.py
@@ -63,17 +63,26 @@
     return jax.ShapeDtypeStruct(shape, jnp.float32)
 
 
-def pack_x(density, labels, adjoint, source, potential, low_out, high_out):
+def pack_x(density, labels, adjoint, source, potential, low_out, high_out, dense, label, sem):
     size_x = density.shape[0]
     starts, _ = plane_starts(WIDTHS)
-    for out, low in ((low_out, True), (high_out, False)):
-        for field, width in enumerate(WIDTHS):
-            span = pl.ds(0 if low else size_x - width, width)
-            if field == 0:
-                face = material(density[span], labels[span])
-            else:
-                face = (adjoint, source, potential)[field - 1][span]
-            out[pl.ds(starts[field], width)] = face
+    width = WIDTHS[0]
+    copies = []
+    for side, out in enumerate((low_out, high_out)):
+        def face(k):
+            return pl.ds(0 if side == 0 else size_x - k, k)
+
+        copies.append((density.at[face(width)], dense.at[side]))
+        copies.append((labels.at[face(width)], label.at[side]))
+        for array, start, count in zip((adjoint, source, potential), starts[1:], WIDTHS[1:]):
+            copies.append((array.at[face(count)], out.at[pl.ds(start, count)]))
+    copies = [pltpu.make_async_copy(a, b, sem.at[k]) for k, (a, b) in enumerate(copies)]
+    for copy in copies:
+        copy.start()
+    for copy in copies:
+        copy.wait()
+    low_out[pl.ds(0, width)] = material(dense[0], label[0])
+    high_out[pl.ds(0, width)] = material(dense[1], label[1])
 
 
 def pack_y(size_x, from_low, from_high, density_l, labels_l, adjoint_l, source_l, potential_l,
@@ -104,105 +113,115 @@
     return pltpu.roll(value, by % value.shape[axis], axis)
 
 
+def planes_loop(low, high, block, step):
+    count = high - low
+    block = max(k for k in range(1, block + 1) if count % k == 0)
+
+    def body(k, carry):
+        step(low + k * block, block)
+        return carry
+
+    lax.fori_loop(0, count // block, body, 0)
+
+
+def unpack_rows(fields, widths, low, high, size_x, size_y):
+    found, _ = segments(widths, size_x)
+    wide = size_y + 2 * RIM
+    for field, x, rows, at in found:
+        fields[field][x + widths[field], wide - rows:wide] = low[at:at + rows]
+        fields[field][x + widths[field], size_y:size_y + rows] = high[at:at + rows]
+
+
 def adjoint_part(xlow, xhigh, ylow, yhigh, density, labels, adjoint_start, adjoint_source, potential,
                  raw_out, low_out, high_out, energy_out,
                  permit, start, source, poten, face_x, face_y, face_z, inverse, first, second):
     size_x, size_y, size_z = density.shape
     starts, _ = plane_starts(WIDTHS)
-    found, _ = segments(WIDTHS, size_x)
     fields = (permit, start, source, poten)
-    body = pl.ds(RIM, size_y)
-
-    def fill(x, carry):
-        permit[x + WIDTHS[0], body] = material(density[x], labels[x])
-        start[x + WIDTHS[1], body] = adjoint_start[x]
-        source[x + WIDTHS[2], body] = adjoint_source[x]
-        poten[x + WIDTHS[3], body] = potential[x]
-        return carry
-
-    lax.fori_loop(0, size_x, fill, 0)
+    tile = pl.ds(0, size_y)
+
+    def fill(x, n):
+        span = pl.ds(x, n)
+        permit[pl.ds(x + WIDTHS[0], n), tile] = material(density[span], labels[span])
+        start[pl.ds(x + WIDTHS[1], n), tile] = adjoint_start[span]
+        source[pl.ds(x + WIDTHS[2], n), tile] = adjoint_source[span]
+        poten[pl.ds(x + WIDTHS[3], n), tile] = potential[span]
+
+    planes_loop(0, size_x, 4, fill)
     for field, width in enumerate(WIDTHS):
-        for k in range(width):
-            fields[field][k, body] = xlow[starts[field] + k]
-            fields[field][width + size_x + k, body] = xhigh[starts[field] + k]
-    for field, x, rows, at in found:
-        fields[field][x + WIDTHS[field], RIM - rows:RIM] = ylow[at:at + rows]
-        fields[field][x + WIDTHS[field], RIM + size_y:RIM + size_y + rows] = yhigh[at:at + rows]
+        fields[field][pl.ds(0, width), tile] = xlow[pl.ds(starts[field], width)]
+        fields[field][pl.ds(width + size_x, width), tile] = xhigh[pl.ds(starts[field], width)]
+    unpack_rows(fields, WIDTHS, ylow, yhigh, size_x, size_y)
 
     wide = size_y + 2 * RIM
-    lane = lax.broadcasted_iota(jnp.int32, (wide, size_z), 1)
+    lane = lax.broadcasted_iota(jnp.int32, (1, wide, size_z), 2)
     is_first = lane == 0
     is_last = lane == size_z - 1
 
     def harmonic(a, b):
         return 2.0 * a * b / jnp.maximum(a + b, 0.25)
 
-    def faces_x(x, carry):
-        face_x[x] = harmonic(permit[x], permit[x + 1])
-        return carry
-
-    lax.fori_loop(0, size_x + 5, faces_x, 0)
-
-    def weigh(x, carry):
-        p = permit[x + 1]
-        fy = harmonic(p, shift(p, -1, 0))
-        fz = jnp.where(is_last, 0.0, harmonic(p, shift(p, -1, 1)))
-        face_y[x] = fy
-        face_z[x] = fz
-        total = screen + face_x[x] + face_x[x + 1] + fy + shift(fy, 1, 0) + fz + shift(fz, 1, 1)
-        inverse[x] = jnp.where(p > 20.0, 0.0, 1.0 / total)
-        return carry
-
-    lax.fori_loop(0, size_x + 4, weigh, 0)
-
-    def relax(x, a, a_low, a_high):
-        fy, fz = face_y[x], face_z[x]
-        total = source[x] + face_x[x + 1] * a_high + face_x[x] * a_low
-        total = total + fy * shift(a, -1, 0) + shift(fy * a, 1, 0)
-        total = total + fz * shift(a, -1, 1) + shift(fz * a, 1, 1)
-        return total * inverse[x]
-
-    def sweep_one(x, carry):
-        first[x] = relax(x, start[x + 1], start[x], start[x + 2])
-        return carry
-
-    lax.fori_loop(0, size_x + 4, sweep_one, 0)
-
-    def sweep_two(x, carry):
-        second[x] = relax(x + 1, first[x + 1], first[x], first[x + 2])
-        return carry
-
-    lax.fori_loop(0, size_x + 2, sweep_two, 0)
-
-    row = lax.broadcasted_iota(jnp.int32, (wide, size_z), 0)
-    own = (row >= RIM) & (row < RIM + size_y)
-
-    def finish(x, carry):
-        v, a = poten[x + 1], second[x + 1]
+    def faces_x(x, n):
+        face_x[pl.ds(x, n)] = harmonic(permit[pl.ds(x, n)], permit[pl.ds(x + 1, n)])
+
+    planes_loop(0, size_x + 5, 4, faces_x)
+
+    def weigh(x, n):
+        span = pl.ds(x, n)
+        p = permit[pl.ds(x + 1, n)]
+        fy = harmonic(p, shift(p, -1, 1))
+        fz = jnp.where(is_last, 0.0, harmonic(p, shift(p, -1, 2)))
+        face_y[span] = fy
+        face_z[span] = fz
+        total = screen + face_x[span] + face_x[pl.ds(x + 1, n)] + fy + shift(fy, 1, 1) + fz + shift(fz, 1, 2)
+        inverse[span] = jnp.where(p > 20.0, 0.0, 1.0 / total)
+
+    planes_loop(0, size_x + 4, 4, weigh)
+
+    def relax(x, n, a, a_low, a_high):
+        span = pl.ds(x, n)
+        fy, fz = face_y[span], face_z[span]
+        total = source[span] + face_x[pl.ds(x + 1, n)] * a_high + face_x[span] * a_low
+        total = total + fy * shift(a, -1, 1) + shift(fy * a, 1, 1)
+        total = total + fz * shift(a, -1, 2) + shift(fz * a, 1, 2)
+        return total * inverse[span]
+
+    def sweep_one(x, n):
+        first[pl.ds(x, n)] = relax(x, n, start[pl.ds(x + 1, n)], start[pl.ds(x, n)], start[pl.ds(x + 2, n)])
+
+    planes_loop(0, size_x + 4, 4, sweep_one)
+
+    def sweep_two(x, n):
+        second[pl.ds(x, n)] = relax(x + 1, n, first[pl.ds(x + 1, n)], first[pl.ds(x, n)], first[pl.ds(x + 2, n)])
+
+    planes_loop(0, size_x + 2, 4, sweep_two)
+    energy_out[...] = jnp.zeros_like(energy_out)
+
+    def finish(x, n):
+        span = pl.ds(x, n)
+        v, a = poten[pl.ds(x + 1, n)], second[pl.ds(x + 1, n)]
         product = jnp.zeros_like(v)
         squares = jnp.zeros_like(v)
         for k in (0, 2):
-            dv, da = poten[x + k] - v, second[x + k] - a
+            dv, da = poten[pl.ds(x + k, n)] - v, second[pl.ds(x + k, n)] - a
             product = product + dv * da
             squares = squares + dv * dv
-        dv, da = shift(v, -1, 0) - v, shift(a, -1, 0) - a
+        dv, da = shift(v, -1, 1) - v, shift(a, -1, 1) - a
         both, square = dv * da, dv * dv
-        product = product + both + shift(both, 1, 0)
-        squares = squares + square + shift(square, 1, 0)
-        dv = jnp.where(is_last, 0.0, shift(v, -1, 1)) - v
-        da = jnp.where(is_last, 0.0, shift(a, -1, 1)) - a
+        product = product + both + shift(both, 1, 1)
+        squares = squares + square + shift(square, 1, 1)
+        dv = jnp.where(is_last, 0.0, shift(v, -1, 2)) - v
+        da = jnp.where(is_last, 0.0, shift(a, -1, 2)) - a
         both, square = dv * da, dv * dv
-        product = product + both + jnp.where(is_first, v * a, shift(both, 1, 1))
-        squares = squares + square + jnp.where(is_first, v * v, shift(square, 1, 1))
-        energy = jnp.where(own, permit[x + 3] * squares, 0.0)
-        d = density[x]
-        gain = jnp.where(labels[x] == 1, -1.5 * (eps_solid - eps_void) * d * d, 0.0)
-        raw_out[x] = gain * product[RIM:RIM + size_y]
-        for k in range(wide // 8):
-            carry = carry + energy[8 * k:8 * k + 8]
-        return carry
-
-    energy_out[...] = lax.fori_loop(0, size_x, finish, jnp.zeros((8, size_z), jnp.float32))
+        product = product + both + jnp.where(is_first, v * a, shift(both, 1, 2))
+        squares = squares + square + jnp.where(is_first, v * v, shift(square, 1, 2))
+        energy = (permit[pl.ds(x + 3, n)] * squares)[:, :size_y]
+        d = density[span]
+        gain = jnp.where(labels[span] == 1, -1.5 * (eps_solid - eps_void) * d * d, 0.0)
+        raw_out[span] = gain * product[:, :size_y]
+        energy_out[...] += jnp.sum(energy.reshape(-1, 8, size_z), axis=0)
+
+    planes_loop(0, size_x, 4, finish)
     low_out[...] = raw_out[pl.ds(0, FILTER_SWEEPS)]
     high_out[...] = raw_out[pl.ds(size_x - FILTER_SWEEPS, FILTER_SWEEPS)]
 
@@ -225,27 +244,23 @@
 def filter_part(xlow, xhigh, ylow, yhigh, raw_in, labels, out, raw, even, odd):
     size_x, size_y, size_z = raw_in.shape
     width = FILTER_SWEEPS
-    found, _ = segments((width,), size_x)
-    body = pl.ds(RIM, size_y)
-
-    def fill(x, carry):
-        raw[x + width, body] = raw_in[x]
-        return carry
-
-    lax.fori_loop(0, size_x, fill, 0)
-    for k in range(width):
-        raw[k, body] = xlow[k]
-        raw[width + size_x + k, body] = xhigh[k]
-    for _, x, rows, at in found:
-        raw[x + width, RIM - rows:RIM] = ylow[at:at + rows]
-        raw[x + width, RIM + size_y:RIM + size_y + rows] = yhigh[at:at + rows]
+    tile = pl.ds(0, size_y)
+
+    def fill(x, n):
+        raw[pl.ds(x + width, n), tile] = raw_in[pl.ds(x, n)]
+
+    planes_loop(0, size_x, 4, fill)
+    raw[pl.ds(0, width), tile] = xlow[...]
+    raw[pl.ds(width + size_x, width), tile] = xhigh[...]
+    unpack_rows((raw,), (width,), ylow, yhigh, size_x, size_y)
 
     wide = size_y + 2 * RIM
     extent_x = lax.axis_size("gx") * size_x
     extent_y = lax.axis_size("gy") * size_y
     base_x = lax.axis_index("gx") * size_x - width
-    lane = lax.broadcasted_iota(jnp.int32, (wide, size_z), 1)
-    place = lax.broadcasted_iota(jnp.int32, (wide, size_z), 0) + (lax.axis_index("gy") * size_y - RIM)
+    lane = lax.broadcasted_iota(jnp.int32, (1, wide, size_z), 2)
+    row = lax.broadcasted_iota(jnp.int32, (1, wide, size_z), 1)
+    place = lax.axis_index("gy") * size_y + jnp.where(row < size_y + RIM, row, row - wide)
     is_first, is_last = lane == 0, lane == size_z - 1
 
     def edges(at, extent):
@@ -256,33 +271,35 @@
     scale_two = jnp.where(inside, 1.0 / (1.0 + radius_sq * (count + 2.0)), 0.0)
     scale_one = jnp.where(inside, 1.0 / (1.0 + radius_sq * (count + 1.0)), 0.0)
 
-    def relax(src, x):
-        f = src[x]
-        near = src[x - 1] + src[x + 1] + shift(f, 1, 0) + shift(f, -1, 0)
-        near = near + jnp.where(is_first, 0.0, shift(f, 1, 1)) + jnp.where(is_last, 0.0, shift(f, -1, 1))
-        at = base_x + x
-        outside = (at < 0) | (at >= extent_x)
-        border = (at == 0) | (at == extent_x - 1)
-        scale = jnp.where(outside, 0.0, jnp.where(border, scale_one, scale_two))
-        return (raw[x] + radius_sq * near) * scale
+    def relax(src, x, n):
+        f = src[pl.ds(x, n)]
+        near = src[pl.ds(x - 1, n)] + src[pl.ds(x + 1, n)] + shift(f, 1, 1) + shift(f, -1, 1)
+        near = near + jnp.where(is_first, 0.0, shift(f, 1, 2)) + jnp.where(is_last, 0.0, shift(f, -1, 2))
+        total = raw[pl.ds(x, n)] + radius_sq * near
+        scaled = []
+        for k in range(n):
+            at = base_x + x + k
+            outside = (at < 0) | (at >= extent_x)
+            border = (at == 0) | (at == extent_x - 1)
+            scale = jnp.where(outside, 0.0, jnp.where(border, scale_one, scale_two))
+            scaled.append(total[k:k + 1] * scale)
+        return jnp.concatenate(scaled, axis=0)
 
     src = raw
     for sweep in range(FILTER_SWEEPS - 1):
         dst = (even, odd)[sweep % 2]
 
-        def step(x, carry, src=src, dst=dst):
-            dst[x] = relax(src, x)
-            return carry
-
-        lax.fori_loop(sweep + 1, size_x + 2 * width - sweep - 1, step, 0)
+        def step(x, n, src=src, dst=dst):
+            dst[pl.ds(x, n)] = relax(src, x, n)
+
+        planes_loop(sweep + 1, size_x + 2 * width - sweep - 1, 4, step)
         src = dst
 
-    def last(x, carry):
-        f = relax(src, x + width)
-        out[x] = jnp.where(labels[x] == 1, f[RIM:RIM + size_y], 0.0)
-        return carry
-
-    lax.fori_loop(0, size_x, last, 0)
+    def last(x, n):
+        f = relax(src, x + width, n)
+        out[pl.ds(x, n)] = jnp.where(labels[pl.ds(x, n)] == 1, f[:, :size_y], 0.0)
+
+    planes_loop(0, size_x, 4, last)
 
 
 def rescale(voxels, filtered, mine, other, out, mean_out):
@@ -311,7 +328,18 @@
     _, rows = segments(WIDTHS, size_x)
     own = (density, labels, adjoint_start, adjoint_source, potential)
 
-    low, high = call(pack_x, (f32(planes, size_y, size_z),) * 2)(*own)
+    depth = (2, WIDTHS[0], size_y, size_z)
+    low, high = pl.pallas_call(
+        pack_x,
+        out_shape=(f32(planes, size_y, size_z),) * 2,
+        in_specs=[pl.BlockSpec(memory_space=pltpu.HBM)] * 5,
+        scratch_shapes=[
+            pltpu.VMEM(depth, jnp.float32),
+            pltpu.VMEM(depth, jnp.int32),
+            pltpu.SemaphoreType.DMA((10,)),
+        ],
+        compiler_params=pltpu.CompilerParams(vmem_limit_bytes=VMEM_LIMIT),
+    )(*own)
     xlow, xhigh = both_ways(low, high, "gx")
     top, end = (0, 0, 0), (0, size_y // 8 - 1, 0)
     whole = pl.BlockSpec((planes, size_y, size_z), lambda i: (0, 0, 0))

time: 71.9 us -> 62.6 us (0.87)
  Pallas kernels: 16.8 us -> 7.46 us
    pallas_call x1, Pallas kernels: 9.29 us -> 3.17 us  [shards(): call(adjoint_part, (f32(size_x, size_y, size_z), face, face, f32(8, size_...]
    pallas_call x1, Pallas kernels: 6.45 us -> 2.69 us  [shards(): call(filter_part, f32(size_x, size_y, size_z), [room(2 * FILTER_SWEEPS)]...]
  transfers between devices with their start and end apart: 13 -> 13, of which waited for: 8 -> 8; matrix products, arithmetic and copies ran while one was open for 0% -> 0% of each run, Pallas kernels for 9% -> 4%
where the time goes in v3:
time: 62.6 us; the launch traced here: 62.1 us
  starting transfers between devices  30.3 us (48%)
  waiting for transfers between devices  18.9 us (30%)
  Pallas kernels  7.46 us (12%)
  local copies, waits for them, and re-layouts  4.75 us (8%)
  between operations  0.78 us (1%)
    ppermute x4, starting transfers between devices, both_ways(): from_low = lax.ppermute(high, axis, forward)  14.4 us
    ppermute x4, waiting for transfers between devices, both_ways(): from_high = lax.ppermute(low, axis, backward)  11 us
    ppermute x5, starting transfers between devices, partner(): lax.ppermute(value, axis, [(i, i ^ bit) for i in range(lax.axis_size(axis...  10.7 us
    ppermute x5, waiting for transfers between devices, partner(): lax.ppermute(value, axis, [(i, i ^ bit) for i in range(lax.axis_size(axis...  7.13 us
    ppermute x4, starting transfers between devices, both_ways(): from_high = lax.ppermute(low, axis, backward)  5.17 us
    unnamed x12, local copies, waits for them, and re-layouts  4.75 us
    pallas_call x1, Pallas kernels, shards(): call(adjoint_part, (f32(size_x, size_y, size_z), face, face, f32(8, size_...  3.17 us
    pallas_call x1, Pallas kernels, shards(): call(filter_part, f32(size_x, size_y, size_z), [room(2 * FILTER_SWEEPS)]...  2.69 us
  transfers between devices with their start and end apart: 13, of which 8 were waited for; matrix products, arithmetic and copies ran while one was open for 0% of the time, Pallas kernels for 4%

profile of v3, /device:TPU:0, one launch (start us, length us, event | category | flops | bytes accessed | tf_op | source)
XLA Modules:
  0.0 62.1 jit_solution(1295505418535480523)
XLA Ops:
  0.6 0.0 copy-start
  0.6 0.9 %copy-done = s32[16,32,128]{2,1,0:T(8,128)S(1)} copy-done((s32[16,32,128]{2,1,0:T(8,128)S(1)}, s32[16,32,128]{2,1,0:T(8,128)}, u32[]{:S(2)}) %copy-start) | copy-done | bytes 262168
  1.6 0.0 copy-start.2
  1.6 0.9 %copy-done.2 = f32[16,32,128]{2,1,0:T(8,128)S(1)} copy-done((f32[16,32,128]{2,1,0:T(8,128)S(1)}, f32[16,32,128]{2,1,0:T(8,128)}, u32[]{:S(2)}) %copy-start.2) | copy-done | bytes 262168
  2.5 0.0 copy-start.3
  2.5 0.9 %copy-done.3 = f32[16,32,128]{2,1,0:T(8,128)S(1)} copy-done((f32[16,32,128]{2,1,0:T(8,128)S(1)}, f32[16,32,128]{2,1,0:T(8,128)}, u32[]{:S(2)}) %copy-start.3) | copy-done | bytes 262168
  3.5 0.0 copy-start.4
  3.5 0.9 %copy-done.4 = f32[16,32,128]{2,1,0:T(8,128)S(1)} copy-done((f32[16,32,128]{2,1,0:T(8,128)S(1)}, f32[16,32,128]{2,1,0:T(8,128)}, u32[]{:S(2)}) %copy-start.4) | copy-done | bytes 262168
  4.4 0.0 copy-start.5
  4.4 0.9 %copy-done.5 = f32[16,32,128]{2,1,0:T(8,128)S(1)} copy-done((f32[16,32,128]{2,1,0:T(8,128)S(1)}, f32[16,32,128]{2,1,0:T(8,128)}, u32[]{:S(2)}) %copy-start.5) | copy-done | bytes 262168
  5.4 0.6 shard_map.68
  6.0 2.4 %collective-permute-start = (f32[9,32,128]{2,1,0:T(8,128)S(1)}, f32[9,32,128]{2,1,0:T(8,128)S(1)}, u32[]{:S(2)}, u32[]{:S(2)}) collective-permute-start(f32[9,32,128]{2,1,0:T(8,128)S(1)} %get-tuple-element.14), channel_id=1, source_target_pairs={{0,8},{8,16},{16,24},{1,9},{9,17},{17,25},{2,10},{10,18},{18,26},{... | collective-permute-start | bytes 442376 | tf_op jit(solution)/shard_map/ppermute | solution.py:317
  8.4 1.3 %collective-permute-start.1 = (f32[9,32,128]{2,1,0:T(8,128)S(1)}, f32[9,32,128]{2,1,0:T(8,128)S(1)}, u32[]{:S(2)}, u32[]{:S(2)}) collective-permute-start(f32[9,32,128]{2,1,0:T(8,128)S(1)} %get-tuple-element.15), channel_id=1, source_target_pairs={{8,0},{16,8},{24,16},{9,1},{17,9},{25,17},{10,2},{18,10},{26,18},{... | collective-permute-start | bytes 442376 | tf_op jit(solution)/shard_map/ppermute | solution.py:316
  9.7 0.0 collective-permute-done.from_low.xlow
  9.7 4.1 %collective-permute-done.1.from_high.xhigh = f32[9,32,128]{2,1,0:T(8,128)S(1)} collective-permute-done((f32[9,32,128]{2,1,0:T(8,128)S(1)}, f32[9,32,128]{2,1,0:T(8,128)S(1)}, u32[]{:S(2)}, u32[]{:S(2)}) %collective-permute-start.1) | collective-permute-done | bytes 147488 | tf_op jit(solution)/shard_map/ppermute | solution.py:316
  13.7 0.1 shard_map.69
  13.9 3.4 %collective-permute-start.2 = (f32[160,128]{1,0:T(8,128)S(1)}, f32[160,128]{1,0:T(8,128)S(1)}, u32[]{:S(2)}, u32[]{:S(2)}) collective-permute-start(f32[160,128]{1,0:T(8,128)S(1)} %get-tuple-element.16), channel_id=1, source_target_pairs={{0,1},{1,2},{2,3},{3,4},{4,5},{5,6},{6,7},{8,9},{9,10},{10,11},{11... | collective-permute-start | bytes 245768 | tf_op jit(solution)/shard_map/ppermute | solution.py:317
  17.3 1.3 %collective-permute-start.3 = (f32[160,128]{1,0:T(8,128)S(1)}, f32[160,128]{1,0:T(8,128)S(1)}, u32[]{:S(2)}, u32[]{:S(2)}) collective-permute-start(f32[160,128]{1,0:T(8,128)S(1)} %get-tuple-element.17), channel_id=1, source_target_pairs={{1,0},{2,1},{3,2},{4,3},{5,4},{6,5},{7,6},{9,8},{10,9},{11,10},{12... | collective-permute-start | bytes 245768 | tf_op jit(solution)/shard_map/ppermute | solution.py:316
  18.6 0.7 %collective-permute-done.2.ylow = f32[160,128]{1,0:T(8,128)S(1)} collective-permute-done((f32[160,128]{1,0:T(8,128)S(1)}, f32[160,128]{1,0:T(8,128)S(1)}, u32[]{:S(2)}, u32[]{:S(2)}) %collective-permute-start.2) | collective-permute-done | bytes 81952 | tf_op jit(solution)/shard_map/ppermute | solution.py:317
  19.3 4.3 %collective-permute-done.3.yhigh = f32[160,128]{1,0:T(8,128)S(1)} collective-permute-done((f32[160,128]{1,0:T(8,128)S(1)}, f32[160,128]{1,0:T(8,128)S(1)}, u32[]{:S(2)}, u32[]{:S(2)}) %collective-permute-start.3) | collective-permute-done | bytes 81952 | tf_op jit(solution)/shard_map/ppermute | solution.py:316
  23.6 3.2 %shard_map.70 = (f32[16,32,128]{2,1,0:T(8,128)S(1)}, f32[4,32,128]{2,1,0:T(8,128)S(1)}, f32[4,32,128]{2,1,0:T(8,128)S(1)}, f32[8,128]{1,0:T(8,128)S(1)}) custom-call(f32[9,32,128]{2,1,0:T(8,128)S(1)} %collective-permute-done.from_low.xlow, f32[9,32,128]{2,1,0:T(8,128)S(1)} %collective-permute-done.1.from_high.xhigh, ...), custom_call_target="tpu_custom_call" | custom-call | flops 10000 | bytes 10000 | tf_op jit(solution)/shard_map/pallas_call | solution.py:361
  26.8 0.0 copy-start.1
  26.8 4.3 %collective-permute-start.4 = (f32[4,32,128]{2,1,0:T(8,128)S(1)}, f32[4,32,128]{2,1,0:T(8,128)S(1)}, u32[]{:S(2)}, u32[]{:S(2)}) collective-permute-start(f32[4,32,128]{2,1,0:T(8,128)S(1)} %get-tuple-element.18), channel_id=1, source_target_pairs={{0,8},{8,16},{16,24},{1,9},{9,17},{17,25},{2,10},{10,18},{18,26},{... | collective-permute-start | bytes 196616 | tf_op jit(solution)/shard_map/ppermute | solution.py:317
  31.1 1.3 %collective-permute-start.5 = (f32[4,32,128]{2,1,0:T(8,128)S(1)}, f32[4,32,128]{2,1,0:T(8,128)S(1)}, u32[]{:S(2)}, u32[]{:S(2)}) collective-permute-start(f32[4,32,128]{2,1,0:T(8,128)S(1)} %get-tuple-element.19), channel_id=1, source_target_pairs={{8,0},{16,8},{24,16},{9,1},{17,9},{25,17},{10,2},{18,10},{26,18},{... | collective-permute-start | bytes 196616 | tf_op jit(solution)/shard_map/ppermute | solution.py:316
  32.4 0.0 collective-permute-done.4.from_low.xlow
  32.4 2.6 %collective-permute-done.5.from_high.xhigh = f32[4,32,128]{2,1,0:T(8,128)S(1)} collective-permute-done((f32[4,32,128]{2,1,0:T(8,128)S(1)}, f32[4,32,128]{2,1,0:T(8,128)S(1)}, u32[]{:S(2)}, u32[]{:S(2)}) %collective-permute-start.5) | collective-permute-done | bytes 65568 | tf_op jit(solution)/shard_map/ppermute | solution.py:316
  35.1 4.3 %collective-permute-start.6 = (f32[80,128]{1,0:T(8,128)S(1)}, f32[80,128]{1,0:T(8,128)S(1)}, u32[]{:S(2)}, u32[]{:S(2)}) collective-permute-start(f32[80,128]{1,0:T(8,128)S(1)} %get-tuple-element.21), channel_id=1, source_target_pairs={{0,1},{1,2},{2,3},{3,4},{4,5},{5,6},{6,7},{8,9},{9,10},{10,11},{11... | collective-permute-start | bytes 122888 | tf_op jit(solution)/shard_map/ppermute | solution.py:317
  39.4 1.3 %collective-permute-start.7 = (f32[80,128]{1,0:T(8,128)S(1)}, f32[80,128]{1,0:T(8,128)S(1)}, u32[]{:S(2)}, u32[]{:S(2)}) collective-permute-start(f32[80,128]{1,0:T(8,128)S(1)} %get-tuple-element.22), channel_id=1, source_target_pairs={{1,0},{2,1},{3,2},{4,3},{5,4},{6,5},{7,6},{9,8},{10,9},{11,10},{12... | collective-permute-start | bytes 122888 | tf_op jit(solution)/shard_map/ppermute | solution.py:316
  40.7 2.7 %collective-permute-start.8 = (f32[8,128]{1,0:T(8,128)S(1)}, f32[8,128]{1,0:T(8,128)S(1)}, u32[]{:S(2)}, u32[]{:S(2)}) collective-permute-start(f32[8,128]{1,0:T(8,128)S(1)} %get-tuple-element.23), channel_id=1, source_target_pairs={{0,8},{8,0},{16,24},{24,16},{1,9},{9,1},{17,25},{25,17},{2,10},{10... | collective-permute-start | bytes 12296 | tf_op jit(solution)/shard_map/ppermute | solution.py:322
  43.4 0.8 %collective-permute-done.8 = f32[8,128]{1,0:T(8,128)S(1)} collective-permute-done((f32[8,128]{1,0:T(8,128)S(1)}, f32[8,128]{1,0:T(8,128)S(1)}, u32[]{:S(2)}, u32[]{:S(2)}) %collective-permute-start.8) | collective-permute-done | bytes 4128 | tf_op jit(solution)/shard_map/ppermute | solution.py:322
  44.3 0.5 collective-permute-start.9
  44.7 3.1 %collective-permute-done.9 = f32[8,128]{1,0:T(8,128)S(1)} collective-permute-done((f32[8,128]{1,0:T(8,128)S(1)}, f32[8,128]{1,0:T(8,128)S(1)}, u32[]{:S(2)}, u32[]{:S(2)}) %collective-permute-start.9) | collective-permute-done | bytes 4128 | tf_op jit(solution)/shard_map/ppermute | solution.py:322
  47.9 2.4 %collective-permute-start.10 = (f32[8,128]{1,0:T(8,128)S(1)}, f32[8,128]{1,0:T(8,128)S(1)}, u32[]{:S(2)}, u32[]{:S(2)}) collective-permute-start(f32[8,128]{1,0:T(8,128)S(1)} %add.13), channel_id=1, source_target_pairs={{0,1},{1,0},{2,3},{3,2},{4,5},{5,4},{6,7},{7,6},{8,9},{9,8},{10,11... | collective-permute-start | bytes 12296 | tf_op jit(solution)/shard_map/ppermute | solution.py:322
  50.2 1.6 %collective-permute-done.10 = f32[8,128]{1,0:T(8,128)S(1)} collective-permute-done((f32[8,128]{1,0:T(8,128)S(1)}, f32[8,128]{1,0:T(8,128)S(1)}, u32[]{:S(2)}, u32[]{:S(2)}) %collective-permute-start.10) | collective-permute-done | bytes 4128 | tf_op jit(solution)/shard_map/ppermute | solution.py:322
  51.8 2.1 %collective-permute-start.11 = (f32[8,128]{1,0:T(8,128)S(1)}, f32[8,128]{1,0:T(8,128)S(1)}, u32[]{:S(2)}, u32[]{:S(2)}) collective-permute-start(f32[8,128]{1,0:T(8,128)S(1)} %add.14), channel_id=1, source_target_pairs={{0,2},{1,3},{2,0},{3,1},{4,6},{5,7},{6,4},{7,5},{8,10},{9,11},{10,... | collective-permute-start | bytes 12296 | tf_op jit(solution)/shard_map/ppermute | solution.py:322
  53.9 1.6 %collective-permute-done.11 = f32[8,128]{1,0:T(8,128)S(1)} collective-permute-done((f32[8,128]{1,0:T(8,128)S(1)}, f32[8,128]{1,0:T(8,128)S(1)}, u32[]{:S(2)}, u32[]{:S(2)}) %collective-permute-start.11) | collective-permute-done | bytes 4128 | tf_op jit(solution)/shard_map/ppermute | solution.py:322
  55.5 3.0 %collective-permute-start.12 = (f32[8,128]{1,0:T(8,128)S(1)}, f32[8,128]{1,0:T(8,128)S(1)}, u32[]{:S(2)}, u32[]{:S(2)}) collective-permute-start(f32[8,128]{1,0:T(8,128)S(1)} %add.15.mine), channel_id=1, source_target_pairs={{0,4},{1,5},{2,6},{3,7},{4,0},{5,1},{6,2},{7,3},{8,12},{9,13},{10,... | collective-permute-start | bytes 12296 | tf_op jit(solution)/shard_map/ppermute | solution.py:322
  58.5 0.0 collective-permute-done.6.ylow
  58.5 0.0 collective-permute-done.7.yhigh
  58.5 0.0 copy-done.1
  58.6 2.7 %shard_map.72.filtered = f32[16,32,128]{2,1,0:T(8,128)S(1)} custom-call(f32[4,32,128]{2,1,0:T(8,128)S(1)} %collective-permute-done.4.from_low.xlow, f32[4,32,128]{2,1,0:T(8,128)S(1)} %collective-permute-done.5.from_high.xhigh, f32[80,128]{1,0:T(8,128)S(1)} %collective-permute-done.6.ylow, f32[80,128]{1,0:T(8,128)S(1)} %collective-permute-done.7.yhigh, ...), custom_call_target="tpu_custom_call" | custom-call | flops 10000 | bytes 10000 | tf_op jit(solution)/shard_map/pallas_call | solution.py:377
  61.3 0.0 collective-permute-done.12.other
  61.3 0.9 %shard_map.73 = (f32[16,32,128]{2,1,0:T(8,128)}, f32[1,1]{1,0:T(1,128)}) custom-call(f32[16,32,128]{2,1,0:T(8,128)S(1)} %shard_map.72.filtered, f32[8,128]{1,0:T(8,128)S(1)} %add.15.mine, f32[8,128]{1,0:T(8,128)S(1)} %collective-permute-done.12.other), custom_call_target="tpu_custom_call" | custom-call | tf_op jit(solution)/shard_map/pallas_call | solution.py:383
  (5 shorter events, 0.0 us)
Async XLA Ops:
  0.6 1.0 %copy-start = (s32[16,32,128]{2,1,0:T(8,128)S(1)}, s32[16,32,128]{2,1,0:T(8,128)}, u32[]{:S(2)}) copy-start(s32[16,32,128]{2,1,0:T(8,128)} %labels.5) | copy-start | bytes 786436
  1.6 0.9 %copy-start.2 = (f32[16,32,128]{2,1,0:T(8,128)S(1)}, f32[16,32,128]{2,1,0:T(8,128)}, u32[]{:S(2)}) copy-start(f32[16,32,128]{2,1,0:T(8,128)} %density.3) | copy-start | bytes 786436
  2.5 0.9 %copy-start.3 = (f32[16,32,128]{2,1,0:T(8,128)S(1)}, f32[16,32,128]{2,1,0:T(8,128)}, u32[]{:S(2)}) copy-start(f32[16,32,128]{2,1,0:T(8,128)} %adjoint_start.1) | copy-start | bytes 786436
  3.5 0.9 %copy-start.4 = (f32[16,32,128]{2,1,0:T(8,128)S(1)}, f32[16,32,128]{2,1,0:T(8,128)}, u32[]{:S(2)}) copy-start(f32[16,32,128]{2,1,0:T(8,128)} %adjoint_source.1) | copy-start | bytes 786436
  4.4 0.9 %copy-start.5 = (f32[16,32,128]{2,1,0:T(8,128)S(1)}, f32[16,32,128]{2,1,0:T(8,128)}, u32[]{:S(2)}) copy-start(f32[16,32,128]{2,1,0:T(8,128)} %potential.3) | copy-start | bytes 786436
  6.0 3.7 %collective-permute-start = (f32[9,32,128]{2,1,0:T(8,128)S(1)}, f32[9,32,128]{2,1,0:T(8,128)S(1)}, u32[]{:S(2)}, u32[]{:S(2)}) collective-permute-start(f32[9,32,128]{2,1,0:T(8,128)S(1)} %get-tuple-element.14), channel_id=1, source_target_pairs={{0,8},{8,16},{16,24},{1,9},{9,17},{17,25},{2,10},{10,18},{18,26},{... | collective-permute-start | bytes 442376 | tf_op jit(solution)/shard_map/ppermute | solution.py:317
  8.4 5.4 %collective-permute-start.1 = (f32[9,32,128]{2,1,0:T(8,128)S(1)}, f32[9,32,128]{2,1,0:T(8,128)S(1)}, u32[]{:S(2)}, u32[]{:S(2)}) collective-permute-start(f32[9,32,128]{2,1,0:T(8,128)S(1)} %get-tuple-element.15), channel_id=1, source_target_pairs={{8,0},{16,8},{24,16},{9,1},{17,9},{25,17},{10,2},{18,10},{26,18},{... | collective-permute-start | bytes 442376 | tf_op jit(solution)/shard_map/ppermute | solution.py:316
  13.9 5.5 %collective-permute-start.2 = (f32[160,128]{1,0:T(8,128)S(1)}, f32[160,128]{1,0:T(8,128)S(1)}, u32[]{:S(2)}, u32[]{:S(2)}) collective-permute-start(f32[160,128]{1,0:T(8,128)S(1)} %get-tuple-element.16), channel_id=1, source_target_pairs={{0,1},{1,2},{2,3},{3,4},{4,5},{5,6},{6,7},{8,9},{9,10},{10,11},{11... | collective-permute-start | bytes 245768 | tf_op jit(solution)/shard_map/ppermute | solution.py:317
  17.3 6.3 %collective-permute-start.3 = (f32[160,128]{1,0:T(8,128)S(1)}, f32[160,128]{1,0:T(8,128)S(1)}, u32[]{:S(2)}, u32[]{:S(2)}) collective-permute-start(f32[160,128]{1,0:T(8,128)S(1)} %get-tuple-element.17), channel_id=1, source_target_pairs={{1,0},{2,1},{3,2},{4,3},{5,4},{6,5},{7,6},{9,8},{10,9},{11,10},{12... | collective-permute-start | bytes 245768 | tf_op jit(solution)/shard_map/ppermute | solution.py:316
  26.8 31.7 %copy-start.1 = (s32[16,32,128]{2,1,0:T(8,128)S(1)}, s32[16,32,128]{2,1,0:T(8,128)}, u32[]{:S(2)}) copy-start(s32[16,32,128]{2,1,0:T(8,128)} %labels.5) | copy-start | bytes 786436
  26.8 5.6 %collective-permute-start.4 = (f32[4,32,128]{2,1,0:T(8,128)S(1)}, f32[4,32,128]{2,1,0:T(8,128)S(1)}, u32[]{:S(2)}, u32[]{:S(2)}) collective-permute-start(f32[4,32,128]{2,1,0:T(8,128)S(1)} %get-tuple-element.18), channel_id=1, source_target_pairs={{0,8},{8,16},{16,24},{1,9},{9,17},{17,25},{2,10},{10,18},{18,26},{... | collective-permute-start | bytes 196616 | tf_op jit(solution)/shard_map/ppermute | solution.py:317
  31.1 3.9 %collective-permute-start.5 = (f32[4,32,128]{2,1,0:T(8,128)S(1)}, f32[4,32,128]{2,1,0:T(8,128)S(1)}, u32[]{:S(2)}, u32[]{:S(2)}) collective-permute-start(f32[4,32,128]{2,1,0:T(8,128)S(1)} %get-tuple-element.19), channel_id=1, source_target_pairs={{8,0},{16,8},{24,16},{9,1},{17,9},{25,17},{10,2},{18,10},{26,18},{... | collective-permute-start | bytes 196616 | tf_op jit(solution)/shard_map/ppermute | solution.py:316
  35.1 23.5 %collective-permute-start.6 = (f32[80,128]{1,0:T(8,128)S(1)}, f32[80,128]{1,0:T(8,128)S(1)}, u32[]{:S(2)}, u32[]{:S(2)}) collective-permute-start(f32[80,128]{1,0:T(8,128)S(1)} %get-tuple-element.21), channel_id=1, source_target_pairs={{0,1},{1,2},{2,3},{3,4},{4,5},{5,6},{6,7},{8,9},{9,10},{10,11},{11... | collective-permute-start | bytes 122888 | tf_op jit(solution)/shard_map/ppermute | solution.py:317
  39.4 19.1 %collective-permute-start.7 = (f32[80,128]{1,0:T(8,128)S(1)}, f32[80,128]{1,0:T(8,128)S(1)}, u32[]{:S(2)}, u32[]{:S(2)}) collective-permute-start(f32[80,128]{1,0:T(8,128)S(1)} %get-tuple-element.22), channel_id=1, source_target_pairs={{1,0},{2,1},{3,2},{4,3},{5,4},{6,5},{7,6},{9,8},{10,9},{11,10},{12... | collective-permute-start | bytes 122888 | tf_op jit(solution)/shard_map/ppermute | solution.py:316
  40.7 3.5 %collective-permute-start.8 = (f32[8,128]{1,0:T(8,128)S(1)}, f32[8,128]{1,0:T(8,128)S(1)}, u32[]{:S(2)}, u32[]{:S(2)}) collective-permute-start(f32[8,128]{1,0:T(8,128)S(1)} %get-tuple-element.23), channel_id=1, source_target_pairs={{0,8},{8,0},{16,24},{24,16},{1,9},{9,1},{17,25},{25,17},{2,10},{10... | collective-permute-start | bytes 12296 | tf_op jit(solution)/shard_map/ppermute | solution.py:322
  44.3 3.6 %collective-permute-start.9 = (f32[8,128]{1,0:T(8,128)S(1)}, f32[8,128]{1,0:T(8,128)S(1)}, u32[]{:S(2)}, u32[]{:S(2)}) collective-permute-start(f32[8,128]{1,0:T(8,128)S(1)} %add.12), channel_id=1, source_target_pairs={{0,16},{8,24},{16,0},{24,8},{1,17},{9,25},{17,1},{25,9},{2,18},{10... | collective-permute-start | bytes 12296 | tf_op jit(solution)/shard_map/ppermute | solution.py:322
  47.9 3.9 %collective-permute-start.10 = (f32[8,128]{1,0:T(8,128)S(1)}, f32[8,128]{1,0:T(8,128)S(1)}, u32[]{:S(2)}, u32[]{:S(2)}) collective-permute-start(f32[8,128]{1,0:T(8,128)S(1)} %add.13), channel_id=1, source_target_pairs={{0,1},{1,0},{2,3},{3,2},{4,5},{5,4},{6,7},{7,6},{8,9},{9,8},{10,11... | collective-permute-start | bytes 12296 | tf_op jit(solution)/shard_map/ppermute | solution.py:322
  51.8 3.7 %collective-permute-start.11 = (f32[8,128]{1,0:T(8,128)S(1)}, f32[8,128]{1,0:T(8,128)S(1)}, u32[]{:S(2)}, u32[]{:S(2)}) collective-permute-start(f32[8,128]{1,0:T(8,128)S(1)} %add.14), channel_id=1, source_target_pairs={{0,2},{1,3},{2,0},{3,1},{4,6},{5,7},{6,4},{7,5},{8,10},{9,11},{10,... | collective-permute-start | bytes 12296 | tf_op jit(solution)/shard_map/ppermute | solution.py:322
  55.5 5.8 %collective-permute-start.12 = (f32[8,128]{1,0:T(8,128)S(1)}, f32[8,128]{1,0:T(8,128)S(1)}, u32[]{:S(2)}, u32[]{:S(2)}) collective-permute-start(f32[8,128]{1,0:T(8,128)S(1)} %add.15.mine), channel_id=1, source_target_pairs={{0,4},{1,5},{2,6},{3,7},{4,0},{5,1},{6,2},{7,3},{8,12},{9,13},{10,... | collective-permute-start | bytes 12296 | tf_op jit(solution)/shard_map/ppermute | solution.py:322

commit v4 on v3

v4 whole, which is shorter than its diff:
```python
import functools

import jax
import jax.numpy as jnp
from jax import lax
from jax.experimental import pallas as pl
from jax.experimental.pallas import tpu as pltpu
from jax.sharding import PartitionSpec as P

ADJ_SWEEPS = 2
FILTER_SWEEPS = 4

eps_void = 1.0
eps_solid = 12.0
eps_back = 4.0
eps_metal = 40.0
screen = 0.5
radius_sq = 2.0
epsilon_mean = 1e-06

WIDTHS = (ADJ_SWEEPS + 1, ADJ_SWEEPS + 1, ADJ_SWEEPS, 1)
RIM = 4
VMEM_LIMIT = 24 * 1024 * 1024


def segments(widths, size_x):
    found, at = [], 0
    for field, width in enumerate(widths):
        for x in range(-width, size_x + width):
            rows = width - max(0, -x, x - size_x + 1)
            if rows > 0:
                found.append((field, x, rows, at))
                at += rows
    return found, -(-at // 8) * 8


def plane_starts(widths):
    starts, at = [], 0
    for width in widths:
        starts.append(at)
        at += width
    return starts, at


def material(density, labels):
    design = eps_void + density * density * density * (eps_solid - eps_void)
    return jnp.where(labels == 1, design, jnp.where(labels == 2, eps_metal, eps_back))


def call(body, outs, scratch=(), in_specs=None, cost=10000):
    kwargs = {} if in_specs is None else {"in_specs": in_specs, "grid": (1,)}
    return pl.pallas_call(
        body,
        out_shape=outs,
        scratch_shapes=list(scratch),
        compiler_params=pltpu.CompilerParams(vmem_limit_bytes=VMEM_LIMIT),
        cost_estimate=pl.CostEstimate(flops=cost, bytes_accessed=cost, transcendentals=0),
        **kwargs,
    )


def f32(*shape):
    return jax.ShapeDtypeStruct(shape, jnp.float32)


def odd_place(axis):
    return lax.rem(lax.axis_index(axis), 2) == 1


def pack_x(*refs):
    inputs, (even_out, odd_out), held, (sem,) = refs[:5], refs[5:7], refs[7:12], refs[12:]
    density, labels, adjoint, source, potential = held
    size_x = density.shape[0]
    starts, _ = plane_starts(WIDTHS)
    copies = [pltpu.make_async_copy(a, b, sem.at[k]) for k, (a, b) in enumerate(zip(inputs, held))]
    for copy in copies:
        copy.start()
    for copy in copies:
        copy.wait()
    low_first = odd_place("gx")
    for out, low in ((even_out, low_first), (odd_out, jnp.logical_not(low_first))):
        for field, width in enumerate(WIDTHS):
            span = pl.ds(jnp.where(low, 0, size_x - width), width)
            if field == 0:
                face = material(density[span], labels[span])
            else:
                face = (adjoint, source, potential)[field - 1][span]
            out[pl.ds(starts[field], width)] = face


def pack_y(x_even, x_odd, density, labels, adjoint, source, potential, even_out, odd_out):
    size_x, size_y, _ = density.shape
    starts, _ = plane_starts(WIDTHS)
    found, _ = segments(WIDTHS, size_x)
    x_swap, y_swap = odd_place("gx"), odd_place("gy")
    for field, x, rows, at in found:
        faces = []
        for rim in (slice(0, rows), slice(size_y - rows, size_y)):
            if x < 0:
                plane = starts[field] + WIDTHS[field] + x
                face = jnp.where(x_swap, x_even[plane, rim], x_odd[plane, rim])
            elif x >= size_x:
                plane = starts[field] + x - size_x
                face = jnp.where(x_swap, x_odd[plane, rim], x_even[plane, rim])
            elif field == 0:
                face = material(density[x, rim], labels[x, rim])
            else:
                face = (adjoint, source, potential)[field - 1][x, rim]
            faces.append(face)
        low, high = faces
        even_out[at:at + rows] = jnp.where(y_swap, low, high)
        odd_out[at:at + rows] = jnp.where(y_swap, high, low)


def shift(value, by, axis):
    return pltpu.roll(value, by % value.shape[axis], axis)


def planes_loop(low, high, block, step):
    count = high - low
    block = max(k for k in range(1, block + 1) if count % k == 0)

    def body(k, carry):
        step(low + k * block, block)
        return carry

    lax.fori_loop(0, count // block, body, 0)


def unpack_rows(fields, widths, even, odd, size_x, size_y, chosen=None):
    found, _ = segments(widths, size_x)
    wide = size_y + 2 * RIM
    swap = odd_place("gy")
    for field, x, rows, at in found:
        if chosen is not None and field not in chosen:
            continue
        a, b = even[at:at + rows], odd[at:at + rows]
        fields[field][x + widths[field], wide - rows:wide] = jnp.where(swap, a, b)
        fields[field][x + widths[field], size_y:size_y + rows] = jnp.where(swap, b, a)


def unpack_planes(field, width, even, odd, size_x, size_y):
    swap = odd_place("gx")
    tile = pl.ds(0, size_y)
    field[pl.ds(0, width), tile] = jnp.where(swap, even, odd)
    field[pl.ds(width + size_x, width), tile] = jnp.where(swap, odd, even)


def energy_part(x_even, x_odd, y_even, y_odd, density, labels, potential, energy_out, poten):
    size_x, size_y, size_z = density.shape
    starts, planes = plane_starts(WIDTHS)
    planes_loop(0, size_x, 4, lambda x, n: poten.__setitem__((pl.ds(x + 1, n), pl.ds(0, size_y)), potential[pl.ds(x, n)]))
    span = pl.ds(starts[3], 1)
    unpack_planes(poten, 1, x_even[span], x_odd[span], size_x, size_y)
    unpack_rows((None, None, None, poten), WIDTHS, y_even, y_odd, size_x, size_y, (3,))
    wide = size_y + 2 * RIM
    lane = lax.broadcasted_iota(jnp.int32, (1, wide, size_z), 2)
    is_first = lane == 0
    is_last = lane == size_z - 1
    energy_out[...] = jnp.zeros_like(energy_out)

    def step(x, n):
        span = pl.ds(x, n)
        v = poten[pl.ds(x + 1, n)]
        low, high = poten[pl.ds(x, n)] - v, poten[pl.ds(x + 2, n)] - v
        squares = low * low + high * high
        dv = shift(v, -1, 1) - v
        square = dv * dv
        squares = squares + square + shift(square, 1, 1)
        dv = jnp.where(is_last, 0.0, shift(v, -1, 2)) - v
        square = dv * dv
        squares = squares + square + jnp.where(is_first, v * v, shift(square, 1, 2))
        energy = material(density[span], labels[span]) * squares[:, :size_y]
        energy_out[...] += jnp.sum(energy.reshape(-1, 8, size_z), axis=0)

    planes_loop(0, size_x, 4, step)


def adjoint_part(x_even, x_odd, y_even, y_odd, density, labels, adjoint_start, adjoint_source, potential,
                 raw_out,
                 permit, start, source, poten, face_x, face_y, face_z, inverse, first, second):
    size_x, size_y, size_z = density.shape
    starts, _ = plane_starts(WIDTHS)
    fields = (permit, start, source, poten)
    tile = pl.ds(0, size_y)

    def fill(x, n):
        span = pl.ds(x, n)
        permit[pl.ds(x + WIDTHS[0], n), tile] = material(density[span], labels[span])
        start[pl.ds(x + WIDTHS[1], n), tile] = adjoint_start[span]
        source[pl.ds(x + WIDTHS[2], n), tile] = adjoint_source[span]
        poten[pl.ds(x + WIDTHS[3], n), tile] = potential[span]

    planes_loop(0, size_x, 4, fill)
    for field, width in enumerate(WIDTHS):
        span = pl.ds(starts[field], width)
        unpack_planes(fields[field], width, x_even[span], x_odd[span], size_x, size_y)
    unpack_rows(fields, WIDTHS, y_even, y_odd, size_x, size_y)

    wide = size_y + 2 * RIM
    lane = lax.broadcasted_iota(jnp.int32, (1, wide, size_z), 2)
    is_first = lane == 0
    is_last = lane == size_z - 1

    def harmonic(a, b):
        return 2.0 * a * b / jnp.maximum(a + b, 0.25)

    def faces_x(x, n):
        face_x[pl.ds(x, n)] = harmonic(permit[pl.ds(x, n)], permit[pl.ds(x + 1, n)])

    planes_loop(0, size_x + 5, 4, faces_x)

    def weigh(x, n):
        span = pl.ds(x, n)
        p = permit[pl.ds(x + 1, n)]
        fy = harmonic(p, shift(p, -1, 1))
        fz = jnp.where(is_last, 0.0, harmonic(p, shift(p, -1, 2)))
        face_y[span] = fy
        face_z[span] = fz
        total = screen + face_x[span] + face_x[pl.ds(x + 1, n)] + fy + shift(fy, 1, 1) + fz + shift(fz, 1, 2)
        inverse[span] = jnp.where(p > 20.0, 0.0, 1.0 / total)

    planes_loop(0, size_x + 4, 4, weigh)

    def relax(x, n, a, a_low, a_high):
        span = pl.ds(x, n)
        fy, fz = face_y[span], face_z[span]
        total = source[span] + face_x[pl.ds(x + 1, n)] * a_high + face_x[span] * a_low
        total = total + fy * shift(a, -1, 1) + shift(fy * a, 1, 1)
        total = total + fz * shift(a, -1, 2) + shift(fz * a, 1, 2)
        return total * inverse[span]

    def sweep_one(x, n):
        first[pl.ds(x, n)] = relax(x, n, start[pl.ds(x + 1, n)], start[pl.ds(x, n)], start[pl.ds(x + 2, n)])

    planes_loop(0, size_x + 4, 4, sweep_one)

    def sweep_two(x, n):
        second[pl.ds(x, n)] = relax(x + 1, n, first[pl.ds(x + 1, n)], first[pl.ds(x, n)], first[pl.ds(x + 2, n)])

    planes_loop(0, size_x + 2, 4, sweep_two)

    def finish(x, n):
        span = pl.ds(x, n)
        v, a = poten[pl.ds(x + 1, n)], second[pl.ds(x + 1, n)]
        product = (poten[pl.ds(x, n)] - v) * (second[pl.ds(x, n)] - a)
        product = product + (poten[pl.ds(x + 2, n)] - v) * (second[pl.ds(x + 2, n)] - a)
        both = (shift(v, -1, 1) - v) * (shift(a, -1, 1) - a)
        product = product + both + shift(both, 1, 1)
        both = (jnp.where(is_last, 0.0, shift(v, -1, 2)) - v) * (jnp.where(is_last, 0.0, shift(a, -1, 2)) - a)
        product = product + both + jnp.where(is_first, v * a, shift(both, 1, 2))
        d = density[span]
        gain = jnp.where(labels[span] == 1, -1.5 * (eps_solid - eps_void) * d * d, 0.0)
        raw_out[span] = gain * product[:, :size_y]

    planes_loop(0, size_x, 4, finish)


def pack_raw_x(raw, mine, other, even_out, odd_out, energy_out):
    size_x, size_y, size_z = raw.shape
    width = FILTER_SWEEPS
    low_first = odd_place("gx")
    energy = mine[...] + other[...]
    energy_out[...] = energy
    for out, low in ((even_out, low_first), (odd_out, jnp.logical_not(low_first))):
        out[pl.ds(0, width)] = raw[pl.ds(jnp.where(low, 0, size_x - width), width)]
    even_out[width, 0:8] = energy


def pack_raw_y(x_even, x_odd, raw, mine, other, even_out, odd_out, energy_out):
    size_x, size_y, _ = raw.shape
    width = FILTER_SWEEPS
    found, total = segments((width,), size_x)
    x_swap, y_swap = odd_place("gx"), odd_place("gy")
    energy = mine[...] + other[...]
    energy_out[...] = energy
    even_out[total:total + 8] = energy
    for _, x, rows, at in found:
        faces = []
        for rim in (slice(0, rows), slice(size_y - rows, size_y)):
            if x < 0:
                face = jnp.where(x_swap, x_even[width + x, rim], x_odd[width + x, rim])
            elif x >= size_x:
                face = jnp.where(x_swap, x_odd[x - size_x, rim], x_even[x - size_x, rim])
            else:
                face = raw[x, rim]
            faces.append(face)
        low, high = faces
        even_out[at:at + rows] = jnp.where(y_swap, low, high)
        odd_out[at:at + rows] = jnp.where(y_swap, high, low)


def filter_part(x_even, x_odd, y_even, y_odd, raw_in, labels, out, raw, even, odd):
    size_x, size_y, size_z = raw_in.shape
    width = FILTER_SWEEPS
    tile = pl.ds(0, size_y)

    def fill(x, n):
        raw[pl.ds(x + width, n), tile] = raw_in[pl.ds(x, n)]

    planes_loop(0, size_x, 4, fill)
    unpack_planes(raw, width, x_even[pl.ds(0, width)], x_odd[pl.ds(0, width)], size_x, size_y)
    unpack_rows((raw,), (width,), y_even, y_odd, size_x, size_y)

    wide = size_y + 2 * RIM
    extent_x = lax.axis_size("gx") * size_x
    extent_y = lax.axis_size("gy") * size_y
    base_x = lax.axis_index("gx") * size_x - width
    lane = lax.broadcasted_iota(jnp.int32, (1, wide, size_z), 2)
    row = lax.broadcasted_iota(jnp.int32, (1, wide, size_z), 1)
    place = lax.axis_index("gy") * size_y + jnp.where(row < size_y + RIM, row, row - wide)
    is_first, is_last = lane == 0, lane == size_z - 1

    def edges(at, extent):
        return jnp.where(at > 0, 1.0, 0.0) + jnp.where(at < extent - 1, 1.0, 0.0)

    count = edges(place, extent_y) + edges(lane, size_z)
    inside = (place >= 0) & (place < extent_y)
    scale_two = jnp.where(inside, 1.0 / (1.0 + radius_sq * (count + 2.0)), 0.0)
    scale_one = jnp.where(inside, 1.0 / (1.0 + radius_sq * (count + 1.0)), 0.0)

    def relax(src, x, n):
        f = src[pl.ds(x, n)]
        near = src[pl.ds(x - 1, n)] + src[pl.ds(x + 1, n)] + shift(f, 1, 1) + shift(f, -1, 1)
        near = near + jnp.where(is_first, 0.0, shift(f, 1, 2)) + jnp.where(is_last, 0.0, shift(f, -1, 2))
        total = raw[pl.ds(x, n)] + radius_sq * near
        scaled = []
        for k in range(n):
            at = base_x + x + k
            outside = (at < 0) | (at >= extent_x)
            border = (at == 0) | (at == extent_x - 1)
            scale = jnp.where(outside, 0.0, jnp.where(border, scale_one, scale_two))
            scaled.append(total[k:k + 1] * scale)
        return jnp.concatenate(scaled, axis=0)

    src = raw
    for sweep in range(FILTER_SWEEPS - 1):
        dst = (even, odd)[sweep % 2]

        def step(x, n, src=src, dst=dst):
            dst[pl.ds(x, n)] = relax(src, x, n)

        planes_loop(sweep + 1, size_x + 2 * width - sweep - 1, 4, step)
        src = dst

    def last(x, n):
        f = relax(src, x + width, n)
        out[pl.ds(x, n)] = jnp.where(labels[pl.ds(x, n)] == 1, f[:, :size_y], 0.0)

    planes_loop(0, size_x, 4, last)


def rescale(voxels, filtered, mine, other, out, mean_out):
    total = jnp.sum(mine[...] + other[...])
    mean = 0.5 * total / voxels + epsilon_mean
    mean_out[0, 0] = mean
    out[...] = filtered[...] * (1.0 / jnp.full((1, 1, out.shape[2]), mean, jnp.float32))


def swap_even(value, axis):
    return lax.ppermute(value, axis, [(i, i ^ 1) for i in range(lax.axis_size(axis))])


def swap_odd(value, axis):
    count = lax.axis_size(axis)
    up = [(i, i + 1) for i in range(1, count - 1, 2)]
    return lax.ppermute(value, axis, up + [(b, a) for a, b in up])


def partner(value, axis, bit):
    return lax.ppermute(value, axis, [(i, i ^ bit) for i in range(lax.axis_size(axis))])


def doubling(energy, stages):
    other = partner(energy, *stages[0])
    for stage in stages[1:]:
        energy = energy + other
        other = partner(energy, *stage)
    return energy, other


def shards(density, potential, adjoint_start, adjoint_source, labels):
    size_x, size_y, size_z = potential.shape
    _, planes = plane_starts(WIDTHS)
    _, rows = segments(WIDTHS, size_x)
    own = [
        pltpu.with_memory_space_constraint(array, pltpu.HBM)
        for array in (density, labels, adjoint_start, adjoint_source, potential)
    ]
    x_bits = [("gx", 1 << k) for k in range(1, (lax.axis_size("gx") - 1).bit_length())]
    y_bits = [("gy", 1 << k) for k in range(1, (lax.axis_size("gy") - 1).bit_length())]

    shape = (size_x, size_y, size_z)
    even, odd, *own = pl.pallas_call(
        pack_x,
        out_shape=(f32(planes, size_y, size_z),) * 2
        + (f32(*shape), jax.ShapeDtypeStruct(shape, jnp.int32)) + (f32(*shape),) * 3,
        in_specs=[pl.BlockSpec(memory_space=pltpu.HBM)] * 5,
        scratch_shapes=[pltpu.SemaphoreType.DMA((5,))],
        compiler_params=pltpu.CompilerParams(vmem_limit_bytes=VMEM_LIMIT),
    )(*own)
    x_odd = swap_odd(odd, "gx")
    x_even = swap_even(even, "gx")
    even, odd = call(pack_y, (f32(rows, size_z),) * 2)(x_even, x_odd, *own)
    y_odd = swap_odd(odd, "gy")
    y_even = swap_even(even, "gy")

    wide = size_y + 2 * RIM

    def room(extra):
        return pltpu.VMEM((size_x + extra, wide, size_z), jnp.float32)

    energy = call(energy_part, f32(8, size_z), [room(2)])(x_even, x_odd, y_even, y_odd, own[0], own[1], own[4])
    mine, other = doubling(energy, y_bits[1:])
    raw = call(
        adjoint_part,
        f32(*shape),
        [room(6), room(6), room(4), room(2), room(5), room(4), room(4), room(4), room(4), room(2)],
        cost=10000000,
    )(x_even, x_odd, y_even, y_odd, *own)

    face = f32(FILTER_SWEEPS, size_y, size_z)
    tall = f32(FILTER_SWEEPS + 1, size_y, size_z)
    even, odd, energy = call(pack_raw_x, (tall, face, f32(8, size_z)))(raw, mine, other)
    x_odd = swap_odd(odd, "gx")
    x_even = swap_even(even, "gx")
    energy = energy + x_even[FILTER_SWEEPS, 0:8]
    mine, other = doubling(energy, x_bits)
    _, rows = segments((FILTER_SWEEPS,), size_x)
    even, odd, energy = call(pack_raw_y, (f32(rows + 8, size_z), f32(rows, size_z), f32(8, size_z)))(
        x_even, x_odd, raw, mine, other)
    y_odd = swap_odd(odd, "gy")
    y_even = swap_even(even, "gy")
    energy = energy + y_even[rows:rows + 8]
    mine, other = doubling(energy, y_bits[:1])
    filtered = call(
        filter_part,
        f32(*shape),
        [room(2 * FILTER_SWEEPS)] * 3,
        cost=10000000,
    )(x_even, x_odd, y_even, y_odd, raw, own[1])
    voxels = lax.axis_size("gx") * size_x * lax.axis_size("gy") * size_y * size_z
    sensitivity, mean_energy = pl.pallas_call(
        functools.partial(rescale, float(voxels)),
        out_shape=(f32(*shape), f32(1, 1)),
        out_specs=(pl.BlockSpec(memory_space=pltpu.VMEM), pl.BlockSpec(memory_space=pltpu.SMEM)),
        compiler_params=pltpu.CompilerParams(vmem_limit_bytes=VMEM_LIMIT),
    )(filtered, mine, other)
    return (sensitivity, mean_energy[0, 0])


def solution(mesh):
    spec = P("gx", "gy", None)
    return jax.shard_map(
        shards, mesh=mesh, in_specs=(spec,) * 5, out_specs=(spec, P()), check_vma=False
    )
```

time: 62.6 us -> 40.9 us (0.65)
  waiting for transfers between devices: 18.9 us -> 7.43 us
  starting transfers between devices: 30.3 us -> 23.5 us
  local copies, waits for them, and re-layouts: 4.75 us -> 0 us
  Pallas kernels: 7.46 us -> 8.87 us
    ppermute x8, starting transfers between devices: 19.6 us -> 10.6 us  [the longest x4 7.94 us: swap_even(): lax.ppermute(value, axis, [(i, i ^ 1) for i in range(lax.axis_size(axis))])]
    ppermute x8, waiting for transfers between devices: 11.7 us -> 5.25 us  [the longest x4 5.24 us: swap_even(): lax.ppermute(value, axis, [(i, i ^ 1) for i in range(lax.axis_size(axis))])]
    ppermute x5 -> x3, waiting for transfers between devices: 7.13 us -> 2.17 us  [partner(): lax.ppermute(value, axis, [(i, i ^ bit) for i in range(lax.axis_size(axis...]
    unnamed x12 -> x0, local copies, waits for them, and re-layouts: 4.75 us -> none
    ppermute x5 -> x3, starting transfers between devices: 10.7 us -> 12.9 us  [partner(): lax.ppermute(value, axis, [(i, i ^ bit) for i in range(lax.axis_size(axis...]
    pallas_call x5 -> x7, Pallas kernels: 6.61 us -> 8.01 us  [the longest x1 3.17 us: shards(): call(adjoint_part, f32(*shape), [room(6), room(6), room(4), room(2), room...]
  transfers between devices with their start and end apart: 13 -> 11, of which waited for: 8 -> 5; matrix products, arithmetic and copies ran while one was open for 0% -> 0% of each run, Pallas kernels for 4% -> 14%
where the time goes in v4:
time: 40.9 us; the launch traced here: 40.5 us
  starting transfers between devices  23.5 us (57%)
  Pallas kernels  8.87 us (22%)
  waiting for transfers between devices  7.43 us (18%)
  between operations  0.73 us (2%)
    ppermute x3, starting transfers between devices, partner(): lax.ppermute(value, axis, [(i, i ^ bit) for i in range(lax.axis_size(axis...  12.9 us
    ppermute x4, starting transfers between devices, swap_even(): lax.ppermute(value, axis, [(i, i ^ 1) for i in range(lax.axis_size(axis))])  7.94 us
    ppermute x4, waiting for transfers between devices, swap_even(): lax.ppermute(value, axis, [(i, i ^ 1) for i in range(lax.axis_size(axis))])  5.24 us
    pallas_call x1, Pallas kernels, shards(): call(adjoint_part, f32(*shape), [room(6), room(6), room(4), room(2), room...  3.17 us
    pallas_call x1, Pallas kernels, shards(): call(filter_part, f32(*shape), [room(2 * FILTER_SWEEPS)] * 3, cost=10000000)  2.68 us
    ppermute x4, starting transfers between devices, swap_odd(): return lax.ppermute(value, axis, up + [(b, a) for a, b in up])  2.62 us
    ppermute x3, waiting for transfers between devices, partner(): lax.ppermute(value, axis, [(i, i ^ bit) for i in range(lax.axis_size(axis...  2.17 us
    pallas_call x1, Pallas kernels, shards(): pl.pallas_call(pack_x, out_shape=(f32(planes, size_y, size_z),) * 2 + (f3...  1.34 us
  transfers between devices with their start and end apart: 11, of which 5 were waited for; matrix products, arithmetic and copies ran while one was open for 0% of the time, Pallas kernels for 14%

profile of v4, /device:TPU:0, one launch (start us, length us, event | category | flops | bytes accessed | tf_op | source)
XLA Modules:
  0.0 40.5 jit_solution(17166395481252343027)
XLA Ops:
  0.6 1.3 %shard_map.68 = (f32[9,32,128]{2,1,0:T(8,128)S(1)}, f32[9,32,128]{2,1,0:T(8,128)S(1)}, f32[16,32,128]{2,1,0:T(8,128)S(1)}, s32[16,32,128]{2,1,0:T(8,128)S(1)}, f...) custom-call(f32[16,32,128]{2,1,0:T(8,128)} %refs_0_.1, s32[16,32,128]{2,1,0:T(8,128)} %refs_1_.1, ...), custom_call_target="tpu_custom_call" | custom-call | tf_op jit(solution)/shard_map/pallas_call | solution.py:394
  2.0 0.5 %collective-permute-start = (f32[9,32,128]{2,1,0:T(8,128)S(1)}, f32[9,32,128]{2,1,0:T(8,128)S(1)}, u32[]{:S(2)}, u32[]{:S(2)}) collective-permute-start(f32[9,32,128]{2,1,0:T(8,128)S(1)} %get-tuple-element.19), channel_id=1, source_target_pairs={{0,8},{8,0},{16,24},{24,16},{1,9},{9,1},{17,25},{25,17},{2,10},{10... | collective-permute-start | bytes 442376 | tf_op jit(solution)/shard_map/ppermute | solution.py:361
  2.5 0.7 %collective-permute-start.1 = (f32[9,32,128]{2,1,0:T(8,128)S(1)}, f32[9,32,128]{2,1,0:T(8,128)S(1)}, u32[]{:S(2)}, u32[]{:S(2)}) collective-permute-start(f32[9,32,128]{2,1,0:T(8,128)S(1)} %get-tuple-element.20), channel_id=1, source_target_pairs={{8,16},{16,8},{9,17},{17,9},{10,18},{18,10},{11,19},{19,11},{12,20... | collective-permute-start | bytes 442376 | tf_op jit(solution)/shard_map/ppermute | solution.py:367
  3.2 0.3 collective-permute-done.x_even
  3.5 0.0 collective-permute-done.1.x_odd
  3.5 0.1 shard_map.69
  3.6 2.9 %collective-permute-start.2 = (f32[160,128]{1,0:T(8,128)S(1)}, f32[160,128]{1,0:T(8,128)S(1)}, u32[]{:S(2)}, u32[]{:S(2)}) collective-permute-start(f32[160,128]{1,0:T(8,128)S(1)} %get-tuple-element.26), channel_id=1, source_target_pairs={{0,1},{1,0},{2,3},{3,2},{4,5},{5,4},{6,7},{7,6},{8,9},{9,8},{10,11... | collective-permute-start | bytes 245768 | tf_op jit(solution)/shard_map/ppermute | solution.py:361
  6.5 0.7 %collective-permute-start.3 = (f32[160,128]{1,0:T(8,128)S(1)}, f32[160,128]{1,0:T(8,128)S(1)}, u32[]{:S(2)}, u32[]{:S(2)}) collective-permute-start(f32[160,128]{1,0:T(8,128)S(1)} %get-tuple-element.27), channel_id=1, source_target_pairs={{1,2},{3,4},{5,6},{2,1},{4,3},{6,5},{9,10},{11,12},{13,14},{10,9},... | collective-permute-start | bytes 245768 | tf_op jit(solution)/shard_map/ppermute | solution.py:367
  7.2 1.8 %collective-permute-done.2.y_even = f32[160,128]{1,0:T(8,128)S(1)} collective-permute-done((f32[160,128]{1,0:T(8,128)S(1)}, f32[160,128]{1,0:T(8,128)S(1)}, u32[]{:S(2)}, u32[]{:S(2)}) %collective-permute-start.2) | collective-permute-done | bytes 81952 | tf_op jit(solution)/shard_map/ppermute | solution.py:361
  9.0 0.0 collective-permute-done.3.y_odd
  9.0 0.7 %shard_map.71.mine = f32[8,128]{1,0:T(8,128)S(1)} custom-call(f32[9,32,128]{2,1,0:T(8,128)S(1)} %collective-permute-done.x_even, f32[9,32,128]{2,1,0:T(8,128)S(1)} %collective-permute-done.1.x_odd, f32[160,128]{1,0:T(8,128)S(1)} %collective-permute-done.2.y_even, f32[160,128]{1,0:T(8,128)S(1)} %collective-permute-done.3.y_odd, ...), custom_call_target="tpu_custom_call" | custom-call | flops 10000 | bytes 10000 | tf_op jit(solution)/shard_map/pallas_call | solution.py:413
  9.7 7.5 %collective-permute-start.4 = (f32[8,128]{1,0:T(8,128)S(1)}, f32[8,128]{1,0:T(8,128)S(1)}, u32[]{:S(2)}, u32[]{:S(2)}) collective-permute-start(f32[8,128]{1,0:T(8,128)S(1)} %shard_map.71.mine), channel_id=1, source_target_pairs={{0,4},{1,5},{2,6},{3,7},{4,0},{5,1},{6,2},{7,3},{8,12},{9,13},{10,... | collective-permute-start | bytes 12296 | tf_op jit(solution)/shard_map/ppermute | solution.py:371
  17.2 3.2 %shard_map.70.raw.raw_in = f32[16,32,128]{2,1,0:T(8,128)S(1)} custom-call(f32[9,32,128]{2,1,0:T(8,128)S(1)} %collective-permute-done.x_even, f32[9,32,128]{2,1,0:T(8,128)S(1)} %collective-permute-done.1.x_odd, f32[160,128]{1,0:T(8,128)S(1)} %collective-permute-done.2.y_even, f32[160,128]{1,0:T(8,128)S(1)} %collective-permute-done.3.y_odd, ...), custom_call_target="tpu_custom_call" | custom-call | flops 10000000 | bytes 10000000 | tf_op jit(solution)/shard_map/pallas_call | solution.py:415
  20.3 0.0 collective-permute-done.4.other
  20.4 3.9 %collective-permute-start.5 = (f32[5,32,128]{2,1,0:T(8,128)S(1)}, f32[5,32,128]{2,1,0:T(8,128)S(1)}, u32[]{:S(2)}, u32[]{:S(2)}) collective-permute-start(f32[5,32,128]{2,1,0:T(8,128)S(1)} %get-tuple-element.28), channel_id=1, source_target_pairs={{0,8},{8,0},{16,24},{24,16},{1,9},{9,1},{17,25},{25,17},{2,10},{10... | collective-permute-start | bytes 245768 | tf_op jit(solution)/shard_map/ppermute | solution.py:361
  24.3 0.7 %collective-permute-start.6 = (f32[4,32,128]{2,1,0:T(8,128)S(1)}, f32[4,32,128]{2,1,0:T(8,128)S(1)}, u32[]{:S(2)}, u32[]{:S(2)}) collective-permute-start(f32[4,32,128]{2,1,0:T(8,128)S(1)} %get-tuple-element.29), channel_id=1, source_target_pairs={{8,16},{16,8},{9,17},{17,9},{10,18},{18,10},{11,19},{19,11},{12,20... | collective-permute-start | bytes 196616 | tf_op jit(solution)/shard_map/ppermute | solution.py:367
  24.9 0.3 collective-permute-done.5.x_even
  25.2 3.8 %collective-permute-start.7 = (f32[8,128]{1,0:T(8,128)S(1)}, f32[8,128]{1,0:T(8,128)S(1)}, u32[]{:S(2)}, u32[]{:S(2)}) collective-permute-start(f32[8,128]{1,0:T(8,128)S(1)} %fusion.mine), channel_id=1, source_target_pairs={{0,16},{8,24},{16,0},{24,8},{1,17},{9,25},{17,1},{25,9},{2,18},{10... | collective-permute-start | bytes 12296 | tf_op jit(solution)/shard_map/ppermute | solution.py:371
  29.0 0.0 collective-permute-done.6.x_odd
  29.0 2.2 %collective-permute-done.7.other = f32[8,128]{1,0:T(8,128)S(1)} collective-permute-done((f32[8,128]{1,0:T(8,128)S(1)}, f32[8,128]{1,0:T(8,128)S(1)}, u32[]{:S(2)}, u32[]{:S(2)}) %collective-permute-start.7) | collective-permute-done | bytes 4128 | tf_op jit(solution)/shard_map/ppermute | solution.py:371
  31.2 0.6 %collective-permute-start.8 = (f32[88,128]{1,0:T(8,128)S(1)}, f32[88,128]{1,0:T(8,128)S(1)}, u32[]{:S(2)}, u32[]{:S(2)}) collective-permute-start(f32[88,128]{1,0:T(8,128)S(1)} %get-tuple-element.31), channel_id=1, source_target_pairs={{0,1},{1,0},{2,3},{3,2},{4,5},{5,4},{6,7},{7,6},{8,9},{9,8},{10,11... | collective-permute-start | bytes 135176 | tf_op jit(solution)/shard_map/ppermute | solution.py:361
  31.8 0.7 %collective-permute-start.9 = (f32[80,128]{1,0:T(8,128)S(1)}, f32[80,128]{1,0:T(8,128)S(1)}, u32[]{:S(2)}, u32[]{:S(2)}) collective-permute-start(f32[80,128]{1,0:T(8,128)S(1)} %get-tuple-element.32), channel_id=1, source_target_pairs={{1,2},{3,4},{5,6},{2,1},{4,3},{6,5},{9,10},{11,12},{13,14},{10,9},... | collective-permute-start | bytes 122888 | tf_op jit(solution)/shard_map/ppermute | solution.py:367
  32.5 2.9 %collective-permute-done.8.y_even = f32[88,128]{1,0:T(8,128)S(1)} collective-permute-done((f32[88,128]{1,0:T(8,128)S(1)}, f32[88,128]{1,0:T(8,128)S(1)}, u32[]{:S(2)}, u32[]{:S(2)}) %collective-permute-start.8) | collective-permute-done | bytes 45088 | tf_op jit(solution)/shard_map/ppermute | solution.py:361
  35.4 1.6 %collective-permute-start.10 = (f32[8,128]{1,0:T(8,128)S(1)}, f32[8,128]{1,0:T(8,128)S(1)}, u32[]{:S(2)}, u32[]{:S(2)}) collective-permute-start(f32[8,128]{1,0:T(8,128)S(1)} %slice_add_fusion.mine), channel_id=1, source_target_pairs={{0,2},{1,3},{2,0},{3,1},{4,6},{5,7},{6,4},{7,5},{8,10},{9,11},{10,... | collective-permute-start | bytes 12296 | tf_op jit(solution)/shard_map/ppermute | solution.py:371
  36.9 0.0 collective-permute-done.9.y_odd
  36.9 2.7 %shard_map.74.filtered = f32[16,32,128]{2,1,0:T(8,128)S(1)} custom-call(f32[5,32,128]{2,1,0:T(8,128)S(1)} %collective-permute-done.5.x_even, f32[4,32,128]{2,1,0:T(8,128)S(1)} %collective-permute-done.6.x_odd, f32[88,128]{1,0:T(8,128)S(1)} %collective-permute-done.8.y_even, f32[80,128]{1,0:T(8,128)S(1)} %collective-permute-done.9.y_odd, ...), custom_call_target="tpu_custom_call" | custom-call | flops 10000000 | bytes 10000000 | tf_op jit(solution)/shard_map/pallas_call | solution.py:436
  39.6 0.0 collective-permute-done.10.other
  39.6 0.9 %shard_map.75 = (f32[16,32,128]{2,1,0:T(8,128)}, f32[1,1]{1,0:T(1,128)}) custom-call(f32[16,32,128]{2,1,0:T(8,128)S(1)} %shard_map.74.filtered, f32[8,128]{1,0:T(8,128)S(1)} %slice_add_fusion.mine, f32[8,128]{1,0:T(8,128)S(1)} %collective-permute-done.10.other), custom_call_target="tpu_custom_call" | custom-call | tf_op jit(solution)/shard_map/pallas_call | solution.py:443
  (4 shorter events, 0.1 us)
Async XLA Ops:
  2.0 1.5 %collective-permute-start = (f32[9,32,128]{2,1,0:T(8,128)S(1)}, f32[9,32,128]{2,1,0:T(8,128)S(1)}, u32[]{:S(2)}, u32[]{:S(2)}) collective-permute-start(f32[9,32,128]{2,1,0:T(8,128)S(1)} %get-tuple-element.19), channel_id=1, source_target_pairs={{0,8},{8,0},{16,24},{24,16},{1,9},{9,1},{17,25},{25,17},{2,10},{10... | collective-permute-start | bytes 442376 | tf_op jit(solution)/shard_map/ppermute | solution.py:361
  2.5 1.0 %collective-permute-start.1 = (f32[9,32,128]{2,1,0:T(8,128)S(1)}, f32[9,32,128]{2,1,0:T(8,128)S(1)}, u32[]{:S(2)}, u32[]{:S(2)}) collective-permute-start(f32[9,32,128]{2,1,0:T(8,128)S(1)} %get-tuple-element.20), channel_id=1, source_target_pairs={{8,16},{16,8},{9,17},{17,9},{10,18},{18,10},{11,19},{19,11},{12,20... | collective-permute-start | bytes 442376 | tf_op jit(solution)/shard_map/ppermute | solution.py:367
  3.6 5.4 %collective-permute-start.2 = (f32[160,128]{1,0:T(8,128)S(1)}, f32[160,128]{1,0:T(8,128)S(1)}, u32[]{:S(2)}, u32[]{:S(2)}) collective-permute-start(f32[160,128]{1,0:T(8,128)S(1)} %get-tuple-element.26), channel_id=1, source_target_pairs={{0,1},{1,0},{2,3},{3,2},{4,5},{5,4},{6,7},{7,6},{8,9},{9,8},{10,11... | collective-permute-start | bytes 245768 | tf_op jit(solution)/shard_map/ppermute | solution.py:361
  6.5 2.4 %collective-permute-start.3 = (f32[160,128]{1,0:T(8,128)S(1)}, f32[160,128]{1,0:T(8,128)S(1)}, u32[]{:S(2)}, u32[]{:S(2)}) collective-permute-start(f32[160,128]{1,0:T(8,128)S(1)} %get-tuple-element.27), channel_id=1, source_target_pairs={{1,2},{3,4},{5,6},{2,1},{4,3},{6,5},{9,10},{11,12},{13,14},{10,9},... | collective-permute-start | bytes 245768 | tf_op jit(solution)/shard_map/ppermute | solution.py:367
  9.7 10.7 %collective-permute-start.4 = (f32[8,128]{1,0:T(8,128)S(1)}, f32[8,128]{1,0:T(8,128)S(1)}, u32[]{:S(2)}, u32[]{:S(2)}) collective-permute-start(f32[8,128]{1,0:T(8,128)S(1)} %shard_map.71.mine), channel_id=1, source_target_pairs={{0,4},{1,5},{2,6},{3,7},{4,0},{5,1},{6,2},{7,3},{8,12},{9,13},{10,... | collective-permute-start | bytes 12296 | tf_op jit(solution)/shard_map/ppermute | solution.py:371
  20.4 4.8 %collective-permute-start.5 = (f32[5,32,128]{2,1,0:T(8,128)S(1)}, f32[5,32,128]{2,1,0:T(8,128)S(1)}, u32[]{:S(2)}, u32[]{:S(2)}) collective-permute-start(f32[5,32,128]{2,1,0:T(8,128)S(1)} %get-tuple-element.28), channel_id=1, source_target_pairs={{0,8},{8,0},{16,24},{24,16},{1,9},{9,1},{17,25},{25,17},{2,10},{10... | collective-permute-start | bytes 245768 | tf_op jit(solution)/shard_map/ppermute | solution.py:361
  24.3 4.7 %collective-permute-start.6 = (f32[4,32,128]{2,1,0:T(8,128)S(1)}, f32[4,32,128]{2,1,0:T(8,128)S(1)}, u32[]{:S(2)}, u32[]{:S(2)}) collective-permute-start(f32[4,32,128]{2,1,0:T(8,128)S(1)} %get-tuple-element.29), channel_id=1, source_target_pairs={{8,16},{16,8},{9,17},{17,9},{10,18},{18,10},{11,19},{19,11},{12,20... | collective-permute-start | bytes 196616 | tf_op jit(solution)/shard_map/ppermute | solution.py:367
  25.2 6.0 %collective-permute-start.7 = (f32[8,128]{1,0:T(8,128)S(1)}, f32[8,128]{1,0:T(8,128)S(1)}, u32[]{:S(2)}, u32[]{:S(2)}) collective-permute-start(f32[8,128]{1,0:T(8,128)S(1)} %fusion.mine), channel_id=1, source_target_pairs={{0,16},{8,24},{16,0},{24,8},{1,17},{9,25},{17,1},{25,9},{2,18},{10... | collective-permute-start | bytes 12296 | tf_op jit(solution)/shard_map/ppermute | solution.py:371
  31.2 4.1 %collective-permute-start.8 = (f32[88,128]{1,0:T(8,128)S(1)}, f32[88,128]{1,0:T(8,128)S(1)}, u32[]{:S(2)}, u32[]{:S(2)}) collective-permute-start(f32[88,128]{1,0:T(8,128)S(1)} %get-tuple-element.31), channel_id=1, source_target_pairs={{0,1},{1,0},{2,3},{3,2},{4,5},{5,4},{6,7},{7,6},{8,9},{9,8},{10,11... | collective-permute-start | bytes 135176 | tf_op jit(solution)/shard_map/ppermute | solution.py:361
  31.8 5.1 %collective-permute-start.9 = (f32[80,128]{1,0:T(8,128)S(1)}, f32[80,128]{1,0:T(8,128)S(1)}, u32[]{:S(2)}, u32[]{:S(2)}) collective-permute-start(f32[80,128]{1,0:T(8,128)S(1)} %get-tuple-element.32), channel_id=1, source_target_pairs={{1,2},{3,4},{5,6},{2,1},{4,3},{6,5},{9,10},{11,12},{13,14},{10,9},... | collective-permute-start | bytes 122888 | tf_op jit(solution)/shard_map/ppermute | solution.py:367
  35.4 4.3 %collective-permute-start.10 = (f32[8,128]{1,0:T(8,128)S(1)}, f32[8,128]{1,0:T(8,128)S(1)}, u32[]{:S(2)}, u32[]{:S(2)}) collective-permute-start(f32[8,128]{1,0:T(8,128)S(1)} %slice_add_fusion.mine), channel_id=1, source_target_pairs={{0,2},{1,3},{2,0},{3,1},{4,6},{5,7},{6,4},{7,5},{8,10},{9,11},{10,... | collective-permute-start | bytes 12296 | tf_op jit(solution)/shard_map/ppermute | solution.py:371

commit v5 on v4

--- a/solution.py
+++ b/solution.py
@@ -1,5 +1,3 @@
-import functools
-
 import jax
 import jax.numpy as jnp
 from jax import lax
@@ -88,7 +86,7 @@
             out[pl.ds(starts[field], width)] = face
 
 
-def pack_y(x_even, x_odd, density, labels, adjoint, source, potential, even_out, odd_out):
+def pack_y(x_odd, x_even, density, labels, adjoint, source, potential, even_out, odd_out):
     size_x, size_y, _ = density.shape
     starts, _ = plane_starts(WIDTHS)
     found, _ = segments(WIDTHS, size_x)
@@ -146,7 +144,7 @@
     field[pl.ds(width + size_x, width), tile] = jnp.where(swap, odd, even)
 
 
-def energy_part(x_even, x_odd, y_even, y_odd, density, labels, potential, energy_out, poten):
+def energy_part(x_odd, x_even, y_odd, y_even, density, labels, potential, energy_out, poten):
     size_x, size_y, size_z = density.shape
     starts, planes = plane_starts(WIDTHS)
     planes_loop(0, size_x, 4, lambda x, n: poten.__setitem__((pl.ds(x + 1, n), pl.ds(0, size_y)), potential[pl.ds(x, n)]))
@@ -176,7 +174,7 @@
     planes_loop(0, size_x, 4, step)
 
 
-def adjoint_part(x_even, x_odd, y_even, y_odd, density, labels, adjoint_start, adjoint_source, potential,
+def adjoint_part(x_odd, x_even, y_odd, y_even, density, labels, adjoint_start, adjoint_source, potential,
                  raw_out,
                  permit, start, source, poten, face_x, face_y, face_z, inverse, first, second):
     size_x, size_y, size_z = density.shape
@@ -208,7 +206,7 @@
     def faces_x(x, n):
         face_x[pl.ds(x, n)] = harmonic(permit[pl.ds(x, n)], permit[pl.ds(x + 1, n)])
 
-    planes_loop(0, size_x + 5, 4, faces_x)
+    planes_loop(0, size_x + 5, 7, faces_x)
 
     def weigh(x, n):
         span = pl.ds(x, n)
@@ -220,7 +218,7 @@
         total = screen + face_x[span] + face_x[pl.ds(x + 1, n)] + fy + shift(fy, 1, 1) + fz + shift(fz, 1, 2)
         inverse[span] = jnp.where(p > 20.0, 0.0, 1.0 / total)
 
-    planes_loop(0, size_x + 4, 4, weigh)
+    planes_loop(0, size_x + 4, 5, weigh)
 
     def relax(x, n, a, a_low, a_high):
         span = pl.ds(x, n)
@@ -233,12 +231,12 @@
     def sweep_one(x, n):
         first[pl.ds(x, n)] = relax(x, n, start[pl.ds(x + 1, n)], start[pl.ds(x, n)], start[pl.ds(x + 2, n)])
 
-    planes_loop(0, size_x + 4, 4, sweep_one)
+    planes_loop(0, size_x + 4, 10, sweep_one)
 
     def sweep_two(x, n):
         second[pl.ds(x, n)] = relax(x + 1, n, first[pl.ds(x + 1, n)], first[pl.ds(x, n)], first[pl.ds(x + 2, n)])
 
-    planes_loop(0, size_x + 2, 4, sweep_two)
+    planes_loop(0, size_x + 2, 9, sweep_two)
 
     def finish(x, n):
         span = pl.ds(x, n)
@@ -253,7 +251,7 @@
         gain = jnp.where(labels[span] == 1, -1.5 * (eps_solid - eps_void) * d * d, 0.0)
         raw_out[span] = gain * product[:, :size_y]
 
-    planes_loop(0, size_x, 4, finish)
+    planes_loop(0, size_x, 8, finish)
 
 
 def pack_raw_x(raw, mine, other, even_out, odd_out, energy_out):
@@ -267,7 +265,7 @@
     even_out[width, 0:8] = energy
 
 
-def pack_raw_y(x_even, x_odd, raw, mine, other, even_out, odd_out, energy_out):
+def pack_raw_y(x_odd, x_even, raw, mine, other, even_out, odd_out, energy_out):
     size_x, size_y, _ = raw.shape
     width = FILTER_SWEEPS
     found, total = segments((width,), size_x)
@@ -290,7 +288,7 @@
         odd_out[at:at + rows] = jnp.where(y_swap, high, low)
 
 
-def filter_part(x_even, x_odd, y_even, y_odd, raw_in, labels, out, raw, even, odd):
+def filter_part(x_odd, x_even, y_odd, y_even, raw_in, labels, mine, other, out, mean_out, raw, even, odd, held, sem):
     size_x, size_y, size_z = raw_in.shape
     width = FILTER_SWEEPS
     tile = pl.ds(0, size_y)
@@ -340,21 +338,23 @@
         def step(x, n, src=src, dst=dst):
             dst[pl.ds(x, n)] = relax(src, x, n)
 
-        planes_loop(sweep + 1, size_x + 2 * width - sweep - 1, 4, step)
+        planes_loop(sweep + 1, size_x + 2 * width - sweep - 1, 11, step)
         src = dst
 
-    def last(x, n):
-        f = relax(src, x + width, n)
-        out[pl.ds(x, n)] = jnp.where(labels[pl.ds(x, n)] == 1, f[:, :size_y], 0.0)
-
-    planes_loop(0, size_x, 4, last)
-
-
-def rescale(voxels, filtered, mine, other, out, mean_out):
     total = jnp.sum(mine[...] + other[...])
-    mean = 0.5 * total / voxels + epsilon_mean
+    mean = 0.5 * total / (extent_x * extent_y * size_z) + epsilon_mean
     mean_out[0, 0] = mean
-    out[...] = filtered[...] * (1.0 / jnp.full((1, 1, out.shape[2]), mean, jnp.float32))
+    inverse = 1.0 / jnp.full((1, 1, size_z), mean, jnp.float32)
+    block = size_x // 2
+    copies = []
+    for k in range(2):
+        span = pl.ds(k * block, block)
+        f = relax(src, k * block + width, block)[:, :size_y]
+        held[span] = jnp.where(labels[span] == 1, f * inverse, 0.0)
+        copies.append(pltpu.make_async_copy(held.at[span], out.at[span], sem.at[k]))
+        copies[k].start()
+    for copy in copies:
+        copy.wait()
 
 
 def swap_even(value, axis):
@@ -399,53 +399,47 @@
         scratch_shapes=[pltpu.SemaphoreType.DMA((5,))],
         compiler_params=pltpu.CompilerParams(vmem_limit_bytes=VMEM_LIMIT),
     )(*own)
+    x_even = swap_even(even, "gx")
     x_odd = swap_odd(odd, "gx")
-    x_even = swap_even(even, "gx")
-    even, odd = call(pack_y, (f32(rows, size_z),) * 2)(x_even, x_odd, *own)
+    even, odd = call(pack_y, (f32(rows, size_z),) * 2)(x_odd, x_even, *own)
+    y_even = swap_even(even, "gy")
     y_odd = swap_odd(odd, "gy")
-    y_even = swap_even(even, "gy")
 
     wide = size_y + 2 * RIM
 
     def room(extra):
         return pltpu.VMEM((size_x + extra, wide, size_z), jnp.float32)
 
-    energy = call(energy_part, f32(8, size_z), [room(2)])(x_even, x_odd, y_even, y_odd, own[0], own[1], own[4])
+    energy = call(energy_part, f32(8, size_z), [room(2)])(x_odd, x_even, y_odd, y_even, own[0], own[1], own[4])
     mine, other = doubling(energy, y_bits[1:])
     raw = call(
         adjoint_part,
         f32(*shape),
         [room(6), room(6), room(4), room(2), room(5), room(4), room(4), room(4), room(4), room(2)],
         cost=10000000,
-    )(x_even, x_odd, y_even, y_odd, *own)
+    )(x_odd, x_even, y_odd, y_even, *own)
 
     face = f32(FILTER_SWEEPS, size_y, size_z)
     tall = f32(FILTER_SWEEPS + 1, size_y, size_z)
     even, odd, energy = call(pack_raw_x, (tall, face, f32(8, size_z)))(raw, mine, other)
+    x_even = swap_even(even, "gx")
     x_odd = swap_odd(odd, "gx")
-    x_even = swap_even(even, "gx")
     energy = energy + x_even[FILTER_SWEEPS, 0:8]
     mine, other = doubling(energy, x_bits)
     _, rows = segments((FILTER_SWEEPS,), size_x)
     even, odd, energy = call(pack_raw_y, (f32(rows + 8, size_z), f32(rows, size_z), f32(8, size_z)))(
-        x_even, x_odd, raw, mine, other)
+        x_odd, x_even, raw, mine, other)
+    y_even = swap_even(even, "gy")
     y_odd = swap_odd(odd, "gy")
-    y_even = swap_even(even, "gy")
     energy = energy + y_even[rows:rows + 8]
     mine, other = doubling(energy, y_bits[:1])
-    filtered = call(
+    sensitivity, mean_energy = pl.pallas_call(
         filter_part,
-        f32(*shape),
-        [room(2 * FILTER_SWEEPS)] * 3,
-        cost=10000000,
-    )(x_even, x_odd, y_even, y_odd, raw, own[1])
-    voxels = lax.axis_size("gx") * size_x * lax.axis_size("gy") * size_y * size_z
-    sensitivity, mean_energy = pl.pallas_call(
-        functools.partial(rescale, float(voxels)),
         out_shape=(f32(*shape), f32(1, 1)),
-        out_specs=(pl.BlockSpec(memory_space=pltpu.VMEM), pl.BlockSpec(memory_space=pltpu.SMEM)),
+        out_specs=(pl.BlockSpec(memory_space=pl.ANY), pl.BlockSpec(memory_space=pltpu.SMEM)),
+        scratch_shapes=[room(2 * FILTER_SWEEPS)] * 3 + [pltpu.VMEM(shape, jnp.float32), pltpu.SemaphoreType.DMA((2,))],
         compiler_params=pltpu.CompilerParams(vmem_limit_bytes=VMEM_LIMIT),
-    )(filtered, mine, other)
+    )(x_odd, x_even, y_odd, y_even, raw, own[1], mine, other)
     return (sensitivity, mean_energy[0, 0])
 
 

time: 40.9 us -> 40.6 us (level)
  waiting for transfers between devices: 7.43 us -> 11.5 us
  starting transfers between devices: 23.5 us -> 21.1 us
  Pallas kernels: 8.87 us -> 7.14 us
    ppermute x3, starting transfers between devices: 12.9 us -> 8.04 us  [partner(): lax.ppermute(value, axis, [(i, i ^ bit) for i in range(lax.axis_size(axis...]
    ppermute x4, starting transfers between devices: 7.94 us -> 10.4 us  [swap_even(): lax.ppermute(value, axis, [(i, i ^ 1) for i in range(lax.axis_size(axis))])]
    ppermute x4, waiting for transfers between devices: 5.24 us -> 7.3 us  [swap_even(): lax.ppermute(value, axis, [(i, i ^ 1) for i in range(lax.axis_size(axis))])]
    ppermute x3, waiting for transfers between devices: 2.17 us -> 4.2 us  [partner(): lax.ppermute(value, axis, [(i, i ^ bit) for i in range(lax.axis_size(axis...]
    pallas_call x3 -> x2, Pallas kernels: 3.62 us -> 2.68 us  [the longest x1 2.6 us: shards(): pl.pallas_call(filter_part, out_shape=(f32(*shape), f32(1, 1)), out_specs...]
    pallas_call x1, Pallas kernels: 3.17 us -> 2.38 us  [shards(): call(adjoint_part, f32(*shape), [room(6), room(6), room(4), room(2), room...]
  transfers between devices with their start and end apart: 11 -> 11, of which waited for: 5 -> 6; matrix products, arithmetic and copies ran while one was open for 0% -> 0% of each run, Pallas kernels for 14% -> 6%
where the time goes in v5:
time: 40.6 us; the launch traced here: 40.4 us
  starting transfers between devices  21.1 us (52%)
  waiting for transfers between devices  11.5 us (28%)
  Pallas kernels  7.14 us (18%)
  between operations  0.72 us (2%)
    ppermute x4, starting transfers between devices, swap_even(): lax.ppermute(value, axis, [(i, i ^ 1) for i in range(lax.axis_size(axis))])  10.4 us
    ppermute x3, starting transfers between devices, partner(): lax.ppermute(value, axis, [(i, i ^ bit) for i in range(lax.axis_size(axis...  8.04 us
    ppermute x4, waiting for transfers between devices, swap_even(): lax.ppermute(value, axis, [(i, i ^ 1) for i in range(lax.axis_size(axis))])  7.3 us
    ppermute x3, waiting for transfers between devices, partner(): lax.ppermute(value, axis, [(i, i ^ bit) for i in range(lax.axis_size(axis...  4.2 us
    ppermute x4, starting transfers between devices, swap_odd(): return lax.ppermute(value, axis, up + [(b, a) for a, b in up])  2.65 us
    pallas_call x1, Pallas kernels, shards(): pl.pallas_call(filter_part, out_shape=(f32(*shape), f32(1, 1)), out_specs...  2.6 us
    pallas_call x1, Pallas kernels, shards(): call(adjoint_part, f32(*shape), [room(6), room(6), room(4), room(2), room...  2.38 us
    pallas_call x1, Pallas kernels, shards(): pl.pallas_call(pack_x, out_shape=(f32(planes, size_y, size_z),) * 2 + (f3...  1.34 us
  transfers between devices with their start and end apart: 11, of which 6 were waited for; matrix products, arithmetic and copies ran while one was open for 0% of the time, Pallas kernels for 6%

profile of v5, /device:TPU:0, one launch (start us, length us, event | category | flops | bytes accessed | tf_op | source)
XLA Modules:
  0.0 40.4 jit_solution(17001492555907065853)
XLA Ops:
  0.6 1.3 %shard_map.68 = (f32[9,32,128]{2,1,0:T(8,128)S(1)}, f32[9,32,128]{2,1,0:T(8,128)S(1)}, f32[16,32,128]{2,1,0:T(8,128)S(1)}, s32[16,32,128]{2,1,0:T(8,128)S(1)}, f...) custom-call(f32[16,32,128]{2,1,0:T(8,128)} %refs_0_.1, s32[16,32,128]{2,1,0:T(8,128)} %refs_1_.1, ...), custom_call_target="tpu_custom_call" | custom-call | tf_op jit(solution)/shard_map/pallas_call | solution.py:394
  2.0 0.7 %collective-permute-start = (f32[9,32,128]{2,1,0:T(8,128)S(1)}, f32[9,32,128]{2,1,0:T(8,128)S(1)}, u32[]{:S(2)}, u32[]{:S(2)}) collective-permute-start(f32[9,32,128]{2,1,0:T(8,128)S(1)} %get-tuple-element.19), channel_id=1, source_target_pairs={{8,16},{16,8},{9,17},{17,9},{10,18},{18,10},{11,19},{19,11},{12,20... | collective-permute-start | bytes 442376 | tf_op jit(solution)/shard_map/ppermute | solution.py:367
  2.7 4.4 %collective-permute-start.1 = (f32[9,32,128]{2,1,0:T(8,128)S(1)}, f32[9,32,128]{2,1,0:T(8,128)S(1)}, u32[]{:S(2)}, u32[]{:S(2)}) collective-permute-start(f32[9,32,128]{2,1,0:T(8,128)S(1)} %get-tuple-element.20), channel_id=1, source_target_pairs={{0,8},{8,0},{16,24},{24,16},{1,9},{9,1},{17,25},{25,17},{2,10},{10... | collective-permute-start | bytes 442376 | tf_op jit(solution)/shard_map/ppermute | solution.py:361
  7.0 0.0 collective-permute-done.x_odd
  7.0 1.0 %collective-permute-done.1.x_even = f32[9,32,128]{2,1,0:T(8,128)S(1)} collective-permute-done((f32[9,32,128]{2,1,0:T(8,128)S(1)}, f32[9,32,128]{2,1,0:T(8,128)S(1)}, u32[]{:S(2)}, u32[]{:S(2)}) %collective-permute-start.1) | collective-permute-done | bytes 147488 | tf_op jit(solution)/shard_map/ppermute | solution.py:361
  8.0 0.1 shard_map.69
  8.1 0.7 %collective-permute-start.2 = (f32[160,128]{1,0:T(8,128)S(1)}, f32[160,128]{1,0:T(8,128)S(1)}, u32[]{:S(2)}, u32[]{:S(2)}) collective-permute-start(f32[160,128]{1,0:T(8,128)S(1)} %get-tuple-element.26), channel_id=1, source_target_pairs={{1,2},{3,4},{5,6},{2,1},{4,3},{6,5},{9,10},{11,12},{13,14},{10,9},... | collective-permute-start | bytes 245768 | tf_op jit(solution)/shard_map/ppermute | solution.py:367
  8.8 4.3 %collective-permute-start.3 = (f32[160,128]{1,0:T(8,128)S(1)}, f32[160,128]{1,0:T(8,128)S(1)}, u32[]{:S(2)}, u32[]{:S(2)}) collective-permute-start(f32[160,128]{1,0:T(8,128)S(1)} %get-tuple-element.27), channel_id=1, source_target_pairs={{0,1},{1,0},{2,3},{3,2},{4,5},{5,4},{6,7},{7,6},{8,9},{9,8},{10,11... | collective-permute-start | bytes 245768 | tf_op jit(solution)/shard_map/ppermute | solution.py:361
  13.1 0.0 collective-permute-done.2.y_odd
  13.1 3.8 %collective-permute-done.3.y_even = f32[160,128]{1,0:T(8,128)S(1)} collective-permute-done((f32[160,128]{1,0:T(8,128)S(1)}, f32[160,128]{1,0:T(8,128)S(1)}, u32[]{:S(2)}, u32[]{:S(2)}) %collective-permute-start.3) | collective-permute-done | bytes 81952 | tf_op jit(solution)/shard_map/ppermute | solution.py:361
  17.0 0.7 %shard_map.71.mine = f32[8,128]{1,0:T(8,128)S(1)} custom-call(f32[9,32,128]{2,1,0:T(8,128)S(1)} %collective-permute-done.x_odd, f32[9,32,128]{2,1,0:T(8,128)S(1)} %collective-permute-done.1.x_even, f32[160,128]{1,0:T(8,128)S(1)} %collective-permute-done.2.y_odd, f32[160,128]{1,0:T(8,128)S(1)} %collective-permute-done.3.y_even, ...), custom_call_target="tpu_custom_call" | custom-call | flops 10000 | bytes 10000 | tf_op jit(solution)/shard_map/pallas_call | solution.py:413
  17.7 3.6 %collective-permute-start.4 = (f32[8,128]{1,0:T(8,128)S(1)}, f32[8,128]{1,0:T(8,128)S(1)}, u32[]{:S(2)}, u32[]{:S(2)}) collective-permute-start(f32[8,128]{1,0:T(8,128)S(1)} %shard_map.71.mine), channel_id=1, source_target_pairs={{0,4},{1,5},{2,6},{3,7},{4,0},{5,1},{6,2},{7,3},{8,12},{9,13},{10,... | collective-permute-start | bytes 12296 | tf_op jit(solution)/shard_map/ppermute | solution.py:371
  21.3 2.4 %shard_map.70.raw.raw_in = f32[16,32,128]{2,1,0:T(8,128)S(1)} custom-call(f32[9,32,128]{2,1,0:T(8,128)S(1)} %collective-permute-done.x_odd, f32[9,32,128]{2,1,0:T(8,128)S(1)} %collective-permute-done.1.x_even, f32[160,128]{1,0:T(8,128)S(1)} %collective-permute-done.2.y_odd, f32[160,128]{1,0:T(8,128)S(1)} %collective-permute-done.3.y_even, ...), custom_call_target="tpu_custom_call" | custom-call | flops 10000000 | bytes 10000000 | tf_op jit(solution)/shard_map/pallas_call | solution.py:415
  23.7 0.0 collective-permute-done.4.other
  23.7 0.1 collective-permute-start.6
  23.8 0.7 %collective-permute-start.5 = (f32[4,32,128]{2,1,0:T(8,128)S(1)}, f32[4,32,128]{2,1,0:T(8,128)S(1)}, u32[]{:S(2)}, u32[]{:S(2)}) collective-permute-start(f32[4,32,128]{2,1,0:T(8,128)S(1)} %get-tuple-element.28), channel_id=1, source_target_pairs={{8,16},{16,8},{9,17},{17,9},{10,18},{18,10},{11,19},{19,11},{12,20... | collective-permute-start | bytes 196616 | tf_op jit(solution)/shard_map/ppermute | solution.py:367
  24.5 0.6 %collective-permute-done.6.x_even = f32[5,32,128]{2,1,0:T(8,128)S(1)} collective-permute-done((f32[5,32,128]{2,1,0:T(8,128)S(1)}, f32[5,32,128]{2,1,0:T(8,128)S(1)}, u32[]{:S(2)}, u32[]{:S(2)}) %collective-permute-start.6) | collective-permute-done | bytes 81952 | tf_op jit(solution)/shard_map/ppermute | solution.py:361
  25.1 2.9 %collective-permute-start.7 = (f32[8,128]{1,0:T(8,128)S(1)}, f32[8,128]{1,0:T(8,128)S(1)}, u32[]{:S(2)}, u32[]{:S(2)}) collective-permute-start(f32[8,128]{1,0:T(8,128)S(1)} %fusion.mine), channel_id=1, source_target_pairs={{0,16},{8,24},{16,0},{24,8},{1,17},{9,25},{17,1},{25,9},{2,18},{10... | collective-permute-start | bytes 12296 | tf_op jit(solution)/shard_map/ppermute | solution.py:371
  27.9 0.0 collective-permute-done.5.x_odd
  27.9 2.2 %collective-permute-done.7.other = f32[8,128]{1,0:T(8,128)S(1)} collective-permute-done((f32[8,128]{1,0:T(8,128)S(1)}, f32[8,128]{1,0:T(8,128)S(1)}, u32[]{:S(2)}, u32[]{:S(2)}) %collective-permute-start.7) | collective-permute-done | bytes 4128 | tf_op jit(solution)/shard_map/ppermute | solution.py:371
  30.1 1.6 %collective-permute-start.9 = (f32[88,128]{1,0:T(8,128)S(1)}, f32[88,128]{1,0:T(8,128)S(1)}, u32[]{:S(2)}, u32[]{:S(2)}) collective-permute-start(f32[88,128]{1,0:T(8,128)S(1)} %get-tuple-element.32), channel_id=1, source_target_pairs={{0,1},{1,0},{2,3},{3,2},{4,5},{5,4},{6,7},{7,6},{8,9},{9,8},{10,11... | collective-permute-start | bytes 135176 | tf_op jit(solution)/shard_map/ppermute | solution.py:361
  31.7 0.7 %collective-permute-start.8 = (f32[80,128]{1,0:T(8,128)S(1)}, f32[80,128]{1,0:T(8,128)S(1)}, u32[]{:S(2)}, u32[]{:S(2)}) collective-permute-start(f32[80,128]{1,0:T(8,128)S(1)} %get-tuple-element.31), channel_id=1, source_target_pairs={{1,2},{3,4},{5,6},{2,1},{4,3},{6,5},{9,10},{11,12},{13,14},{10,9},... | collective-permute-start | bytes 122888 | tf_op jit(solution)/shard_map/ppermute | solution.py:367
  32.4 1.9 %collective-permute-done.9.y_even = f32[88,128]{1,0:T(8,128)S(1)} collective-permute-done((f32[88,128]{1,0:T(8,128)S(1)}, f32[88,128]{1,0:T(8,128)S(1)}, u32[]{:S(2)}, u32[]{:S(2)}) %collective-permute-start.9) | collective-permute-done | bytes 45088 | tf_op jit(solution)/shard_map/ppermute | solution.py:361
  34.2 1.6 %collective-permute-start.10 = (f32[8,128]{1,0:T(8,128)S(1)}, f32[8,128]{1,0:T(8,128)S(1)}, u32[]{:S(2)}, u32[]{:S(2)}) collective-permute-start(f32[8,128]{1,0:T(8,128)S(1)} %slice_add_fusion.mine), channel_id=1, source_target_pairs={{0,2},{1,3},{2,0},{3,1},{4,6},{5,7},{6,4},{7,5},{8,10},{9,11},{10,... | collective-permute-start | bytes 12296 | tf_op jit(solution)/shard_map/ppermute | solution.py:371
  35.8 0.0 collective-permute-done.8.y_odd
  35.8 2.0 %collective-permute-done.10.other = f32[8,128]{1,0:T(8,128)S(1)} collective-permute-done((f32[8,128]{1,0:T(8,128)S(1)}, f32[8,128]{1,0:T(8,128)S(1)}, u32[]{:S(2)}, u32[]{:S(2)}) %collective-permute-start.10) | collective-permute-done | bytes 4128 | tf_op jit(solution)/shard_map/ppermute | solution.py:371
  37.8 2.6 %shard_map.74 = (f32[16,32,128]{2,1,0:T(8,128)}, f32[1,1]{1,0:T(1,128)}) custom-call(f32[4,32,128]{2,1,0:T(8,128)S(1)} %collective-permute-done.5.x_odd, f32[5,32,128]{2,1,0:T(8,128)S(1)} %collective-permute-done.6.x_even, f32[80,128]{1,0:T(8,128)S(1)} %collective-permute-done.8.y_odd, f32[88,128]{1,0:T(8,128)S(1)} %collective-permute-done.9.y_even, ...), custom_call_target="tpu_custom_call" | custom-call | tf_op jit(solution)/shard_map/pallas_call | solution.py:436
  (4 shorter events, 0.1 us)
Async XLA Ops:
  2.0 5.0 %collective-permute-start = (f32[9,32,128]{2,1,0:T(8,128)S(1)}, f32[9,32,128]{2,1,0:T(8,128)S(1)}, u32[]{:S(2)}, u32[]{:S(2)}) collective-permute-start(f32[9,32,128]{2,1,0:T(8,128)S(1)} %get-tuple-element.19), channel_id=1, source_target_pairs={{8,16},{16,8},{9,17},{17,9},{10,18},{18,10},{11,19},{19,11},{12,20... | collective-permute-start | bytes 442376 | tf_op jit(solution)/shard_map/ppermute | solution.py:367
  2.7 5.4 %collective-permute-start.1 = (f32[9,32,128]{2,1,0:T(8,128)S(1)}, f32[9,32,128]{2,1,0:T(8,128)S(1)}, u32[]{:S(2)}, u32[]{:S(2)}) collective-permute-start(f32[9,32,128]{2,1,0:T(8,128)S(1)} %get-tuple-element.20), channel_id=1, source_target_pairs={{0,8},{8,0},{16,24},{24,16},{1,9},{9,1},{17,25},{25,17},{2,10},{10... | collective-permute-start | bytes 442376 | tf_op jit(solution)/shard_map/ppermute | solution.py:361
  8.1 5.0 %collective-permute-start.2 = (f32[160,128]{1,0:T(8,128)S(1)}, f32[160,128]{1,0:T(8,128)S(1)}, u32[]{:S(2)}, u32[]{:S(2)}) collective-permute-start(f32[160,128]{1,0:T(8,128)S(1)} %get-tuple-element.26), channel_id=1, source_target_pairs={{1,2},{3,4},{5,6},{2,1},{4,3},{6,5},{9,10},{11,12},{13,14},{10,9},... | collective-permute-start | bytes 245768 | tf_op jit(solution)/shard_map/ppermute | solution.py:367
  8.8 8.2 %collective-permute-start.3 = (f32[160,128]{1,0:T(8,128)S(1)}, f32[160,128]{1,0:T(8,128)S(1)}, u32[]{:S(2)}, u32[]{:S(2)}) collective-permute-start(f32[160,128]{1,0:T(8,128)S(1)} %get-tuple-element.27), channel_id=1, source_target_pairs={{0,1},{1,0},{2,3},{3,2},{4,5},{5,4},{6,7},{7,6},{8,9},{9,8},{10,11... | collective-permute-start | bytes 245768 | tf_op jit(solution)/shard_map/ppermute | solution.py:361
  17.7 6.0 %collective-permute-start.4 = (f32[8,128]{1,0:T(8,128)S(1)}, f32[8,128]{1,0:T(8,128)S(1)}, u32[]{:S(2)}, u32[]{:S(2)}) collective-permute-start(f32[8,128]{1,0:T(8,128)S(1)} %shard_map.71.mine), channel_id=1, source_target_pairs={{0,4},{1,5},{2,6},{3,7},{4,0},{5,1},{6,2},{7,3},{8,12},{9,13},{10,... | collective-permute-start | bytes 12296 | tf_op jit(solution)/shard_map/ppermute | solution.py:371
  23.7 1.3 %collective-permute-start.6 = (f32[5,32,128]{2,1,0:T(8,128)S(1)}, f32[5,32,128]{2,1,0:T(8,128)S(1)}, u32[]{:S(2)}, u32[]{:S(2)}) collective-permute-start(f32[5,32,128]{2,1,0:T(8,128)S(1)} %get-tuple-element.29), channel_id=1, source_target_pairs={{0,8},{8,0},{16,24},{24,16},{1,9},{9,1},{17,25},{25,17},{2,10},{10... | collective-permute-start | bytes 245768 | tf_op jit(solution)/shard_map/ppermute | solution.py:361
  23.8 4.1 %collective-permute-start.5 = (f32[4,32,128]{2,1,0:T(8,128)S(1)}, f32[4,32,128]{2,1,0:T(8,128)S(1)}, u32[]{:S(2)}, u32[]{:S(2)}) collective-permute-start(f32[4,32,128]{2,1,0:T(8,128)S(1)} %get-tuple-element.28), channel_id=1, source_target_pairs={{8,16},{16,8},{9,17},{17,9},{10,18},{18,10},{11,19},{19,11},{12,20... | collective-permute-start | bytes 196616 | tf_op jit(solution)/shard_map/ppermute | solution.py:367
  25.1 5.0 %collective-permute-start.7 = (f32[8,128]{1,0:T(8,128)S(1)}, f32[8,128]{1,0:T(8,128)S(1)}, u32[]{:S(2)}, u32[]{:S(2)}) collective-permute-start(f32[8,128]{1,0:T(8,128)S(1)} %fusion.mine), channel_id=1, source_target_pairs={{0,16},{8,24},{16,0},{24,8},{1,17},{9,25},{17,1},{25,9},{2,18},{10... | collective-permute-start | bytes 12296 | tf_op jit(solution)/shard_map/ppermute | solution.py:371
  30.1 4.1 %collective-permute-start.9 = (f32[88,128]{1,0:T(8,128)S(1)}, f32[88,128]{1,0:T(8,128)S(1)}, u32[]{:S(2)}, u32[]{:S(2)}) collective-permute-start(f32[88,128]{1,0:T(8,128)S(1)} %get-tuple-element.32), channel_id=1, source_target_pairs={{0,1},{1,0},{2,3},{3,2},{4,5},{5,4},{6,7},{7,6},{8,9},{9,8},{10,11... | collective-permute-start | bytes 135176 | tf_op jit(solution)/shard_map/ppermute | solution.py:361
  31.7 4.1 %collective-permute-start.8 = (f32[80,128]{1,0:T(8,128)S(1)}, f32[80,128]{1,0:T(8,128)S(1)}, u32[]{:S(2)}, u32[]{:S(2)}) collective-permute-start(f32[80,128]{1,0:T(8,128)S(1)} %get-tuple-element.31), channel_id=1, source_target_pairs={{1,2},{3,4},{5,6},{2,1},{4,3},{6,5},{9,10},{11,12},{13,14},{10,9},... | collective-permute-start | bytes 122888 | tf_op jit(solution)/shard_map/ppermute | solution.py:367
  34.2 3.6 %collective-permute-start.10 = (f32[8,128]{1,0:T(8,128)S(1)}, f32[8,128]{1,0:T(8,128)S(1)}, u32[]{:S(2)}, u32[]{:S(2)}) collective-permute-start(f32[8,128]{1,0:T(8,128)S(1)} %slice_add_fusion.mine), channel_id=1, source_target_pairs={{0,2},{1,3},{2,0},{3,1},{4,6},{5,7},{6,4},{7,5},{8,10},{9,11},{10,... | collective-permute-start | bytes 12296 | tf_op jit(solution)/shard_map/ppermute | solution.py:371

commit v6 on v5

--- a/solution.py
+++ b/solution.py
@@ -1,3 +1,5 @@
+import functools
+
 import jax
 import jax.numpy as jnp
 from jax import lax
@@ -21,12 +23,12 @@
 VMEM_LIMIT = 24 * 1024 * 1024
 
 
-def segments(widths, size_x):
+def segments(widths, size_x, beside=True, beyond=True):
     found, at = [], 0
     for field, width in enumerate(widths):
         for x in range(-width, size_x + width):
             rows = width - max(0, -x, x - size_x + 1)
-            if rows > 0:
+            if rows > 0 and (beside if 0 <= x < size_x else beyond):
                 found.append((field, x, rows, at))
                 at += rows
     return found, -(-at // 8) * 8
@@ -65,10 +67,10 @@
     return lax.rem(lax.axis_index(axis), 2) == 1
 
 
-def pack_x(*refs):
-    inputs, (even_out, odd_out), held, (sem,) = refs[:5], refs[5:7], refs[7:12], refs[12:]
+def pack_own(*refs):
+    inputs, (x_odd_out, x_even_out, y_even_out, y_odd_out), held, sem = refs[:5], refs[5:9], refs[9:14], refs[14]
     density, labels, adjoint, source, potential = held
-    size_x = density.shape[0]
+    size_x, size_y, _ = density.shape
     starts, _ = plane_starts(WIDTHS)
     copies = [pltpu.make_async_copy(a, b, sem.at[k]) for k, (a, b) in enumerate(zip(inputs, held))]
     for copy in copies:
@@ -76,7 +78,7 @@
     for copy in copies:
         copy.wait()
     low_first = odd_place("gx")
-    for out, low in ((even_out, low_first), (odd_out, jnp.logical_not(low_first))):
+    for out, low in ((x_even_out, low_first), (x_odd_out, jnp.logical_not(low_first))):
         for field, width in enumerate(WIDTHS):
             span = pl.ds(jnp.where(low, 0, size_x - width), width)
             if field == 0:
@@ -84,26 +86,32 @@
             else:
                 face = (adjoint, source, potential)[field - 1][span]
             out[pl.ds(starts[field], width)] = face
-
-
-def pack_y(x_odd, x_even, density, labels, adjoint, source, potential, even_out, odd_out):
-    size_x, size_y, _ = density.shape
+    y_swap = odd_place("gy")
+    for field, x, rows, at in segments(WIDTHS, size_x, beyond=False)[0]:
+        faces = []
+        for rim in (slice(0, rows), slice(size_y - rows, size_y)):
+            if field == 0:
+                faces.append(material(density[x, rim], labels[x, rim]))
+            else:
+                faces.append((adjoint, source, potential)[field - 1][x, rim])
+        low, high = faces
+        y_even_out[at:at + rows] = jnp.where(y_swap, low, high)
+        y_odd_out[at:at + rows] = jnp.where(y_swap, high, low)
+
+
+def pack_corners(size_x, x_odd, x_even, even_out, odd_out):
+    size_y = x_odd.shape[1]
     starts, _ = plane_starts(WIDTHS)
-    found, _ = segments(WIDTHS, size_x)
     x_swap, y_swap = odd_place("gx"), odd_place("gy")
-    for field, x, rows, at in found:
+    for field, x, rows, at in segments(WIDTHS, size_x, beside=False)[0]:
         faces = []
         for rim in (slice(0, rows), slice(size_y - rows, size_y)):
             if x < 0:
                 plane = starts[field] + WIDTHS[field] + x
                 face = jnp.where(x_swap, x_even[plane, rim], x_odd[plane, rim])
-            elif x >= size_x:
+            else:
                 plane = starts[field] + x - size_x
                 face = jnp.where(x_swap, x_odd[plane, rim], x_even[plane, rim])
-            elif field == 0:
-                face = material(density[x, rim], labels[x, rim])
-            else:
-                face = (adjoint, source, potential)[field - 1][x, rim]
             faces.append(face)
         low, high = faces
         even_out[at:at + rows] = jnp.where(y_swap, low, high)
@@ -125,12 +133,11 @@
     lax.fori_loop(0, count // block, body, 0)
 
 
-def unpack_rows(fields, widths, even, odd, size_x, size_y, chosen=None):
-    found, _ = segments(widths, size_x)
+def unpack_rows(fields, widths, found, even, odd, size_y):
     wide = size_y + 2 * RIM
     swap = odd_place("gy")
     for field, x, rows, at in found:
-        if chosen is not None and field not in chosen:
+        if fields[field] is None:
             continue
         a, b = even[at:at + rows], odd[at:at + rows]
         fields[field][x + widths[field], wide - rows:wide] = jnp.where(swap, a, b)
@@ -144,13 +151,14 @@
     field[pl.ds(width + size_x, width), tile] = jnp.where(swap, odd, even)
 
 
-def energy_part(x_odd, x_even, y_odd, y_even, density, labels, potential, energy_out, poten):
+def energy_part(x_odd, x_even, y_even, y_odd, density, labels, potential, energy_out, poten):
     size_x, size_y, size_z = density.shape
     starts, planes = plane_starts(WIDTHS)
     planes_loop(0, size_x, 4, lambda x, n: poten.__setitem__((pl.ds(x + 1, n), pl.ds(0, size_y)), potential[pl.ds(x, n)]))
     span = pl.ds(starts[3], 1)
     unpack_planes(poten, 1, x_even[span], x_odd[span], size_x, size_y)
-    unpack_rows((None, None, None, poten), WIDTHS, y_even, y_odd, size_x, size_y, (3,))
+    found, _ = segments(WIDTHS, size_x, beyond=False)
+    unpack_rows((None, None, None, poten), WIDTHS, found, y_even, y_odd, size_y)
     wide = size_y + 2 * RIM
     lane = lax.broadcasted_iota(jnp.int32, (1, wide, size_z), 2)
     is_first = lane == 0
@@ -174,7 +182,7 @@
     planes_loop(0, size_x, 4, step)
 
 
-def adjoint_part(x_odd, x_even, y_odd, y_even, density, labels, adjoint_start, adjoint_source, potential,
+def adjoint_part(x_odd, x_even, y_even, y_odd, corner_even, corner_odd, density, labels, adjoint_start, adjoint_source, potential,
                  raw_out,
                  permit, start, source, poten, face_x, face_y, face_z, inverse, first, second):
     size_x, size_y, size_z = density.shape
@@ -193,7 +201,8 @@
     for field, width in enumerate(WIDTHS):
         span = pl.ds(starts[field], width)
         unpack_planes(fields[field], width, x_even[span], x_odd[span], size_x, size_y)
-    unpack_rows(fields, WIDTHS, y_even, y_odd, size_x, size_y)
+    unpack_rows(fields, WIDTHS, segments(WIDTHS, size_x, beyond=False)[0], y_even, y_odd, size_y)
+    unpack_rows(fields, WIDTHS, segments(WIDTHS, size_x, beside=False)[0], corner_even, corner_odd, size_y)
 
     wide = size_y + 2 * RIM
     lane = lax.broadcasted_iota(jnp.int32, (1, wide, size_z), 2)
@@ -298,7 +307,7 @@
 
     planes_loop(0, size_x, 4, fill)
     unpack_planes(raw, width, x_even[pl.ds(0, width)], x_odd[pl.ds(0, width)], size_x, size_y)
-    unpack_rows((raw,), (width,), y_even, y_odd, size_x, size_y)
+    unpack_rows((raw,), (width,), segments((width,), size_x)[0], y_even, y_odd, size_y)
 
     wide = size_y + 2 * RIM
     extent_x = lax.axis_size("gx") * size_x
@@ -382,7 +391,8 @@
 def shards(density, potential, adjoint_start, adjoint_source, labels):
     size_x, size_y, size_z = potential.shape
     _, planes = plane_starts(WIDTHS)
-    _, rows = segments(WIDTHS, size_x)
+    _, rows = segments(WIDTHS, size_x, beyond=False)
+    _, corners = segments(WIDTHS, size_x, beside=False)
     own = [
         pltpu.with_memory_space_constraint(array, pltpu.HBM)
         for array in (density, labels, adjoint_start, adjoint_source, potential)
@@ -391,9 +401,9 @@
     y_bits = [("gy", 1 << k) for k in range(1, (lax.axis_size("gy") - 1).bit_length())]
 
     shape = (size_x, size_y, size_z)
-    even, odd, *own = pl.pallas_call(
-        pack_x,
-        out_shape=(f32(planes, size_y, size_z),) * 2
+    odd, even, tile_even, tile_odd, *own = pl.pallas_call(
+        pack_own,
+        out_shape=(f32(planes, size_y, size_z),) * 2 + (f32(rows, size_z),) * 2
         + (f32(*shape), jax.ShapeDtypeStruct(shape, jnp.int32)) + (f32(*shape),) * 3,
         in_specs=[pl.BlockSpec(memory_space=pltpu.HBM)] * 5,
         scratch_shapes=[pltpu.SemaphoreType.DMA((5,))],
@@ -401,23 +411,25 @@
     )(*own)
     x_even = swap_even(even, "gx")
     x_odd = swap_odd(odd, "gx")
-    even, odd = call(pack_y, (f32(rows, size_z),) * 2)(x_odd, x_even, *own)
-    y_even = swap_even(even, "gy")
-    y_odd = swap_odd(odd, "gy")
+    y_even = swap_even(tile_even, "gy")
+    y_odd = swap_odd(tile_odd, "gy")
+    even, odd = call(functools.partial(pack_corners, size_x), (f32(corners, size_z),) * 2)(x_odd, x_even)
+    corner_even = swap_even(even, "gy")
+    corner_odd = swap_odd(odd, "gy")
 
     wide = size_y + 2 * RIM
 
     def room(extra):
         return pltpu.VMEM((size_x + extra, wide, size_z), jnp.float32)
 
-    energy = call(energy_part, f32(8, size_z), [room(2)])(x_odd, x_even, y_odd, y_even, own[0], own[1], own[4])
+    energy = call(energy_part, f32(8, size_z), [room(2)])(x_odd, x_even, y_even, y_odd, own[0], own[1], own[4])
     mine, other = doubling(energy, y_bits[1:])
     raw = call(
         adjoint_part,
         f32(*shape),
         [room(6), room(6), room(4), room(2), room(5), room(4), room(4), room(4), room(4), room(2)],
         cost=10000000,
-    )(x_odd, x_even, y_odd, y_even, *own)
+    )(x_odd, x_even, y_even, y_odd, corner_even, corner_odd, *own)
 
     face = f32(FILTER_SWEEPS, size_y, size_z)
     tall = f32(FILTER_SWEEPS + 1, size_y, size_z)

time: 40.6 us -> 39 us (0.961)
  waiting for transfers between devices: 11.5 us -> 5.73 us
  starting transfers between devices: 21.1 us -> 25.1 us
    ppermute x4 -> x5, waiting for transfers between devices: 7.3 us -> 1.97 us  [swap_even(): lax.ppermute(value, axis, [(i, i ^ 1) for i in range(lax.axis_size(axis))])]
    ppermute x4 -> x5, starting transfers between devices: 10.4 us -> 12.7 us  [swap_even(): lax.ppermute(value, axis, [(i, i ^ 1) for i in range(lax.axis_size(axis))])]
    ppermute x3, starting transfers between devices: 8.04 us -> 9.16 us  [partner(): lax.ppermute(value, axis, [(i, i ^ bit) for i in range(lax.axis_size(axis...]
    ppermute x4 -> x5, starting transfers between devices: 2.65 us -> 3.29 us  [swap_odd(): return lax.ppermute(value, axis, up + [(b, a) for a, b in up])]
    ppermute x3, waiting for transfers between devices: 4.2 us -> 3.75 us  [partner(): lax.ppermute(value, axis, [(i, i ^ bit) for i in range(lax.axis_size(axis...]
  transfers between devices with their start and end apart: 11 -> 13, of which waited for: 6 -> 4; matrix products, arithmetic and copies ran while one was open for 0% -> 0% of each run, Pallas kernels for 6% -> 8%
where the time goes in v6:
time: 39 us; the launch traced here: 38.8 us
  starting transfers between devices  25.1 us (64%)
  Pallas kernels  7.16 us (18%)
  waiting for transfers between devices  5.73 us (15%)
  between operations  0.77 us (2%)
    ppermute x5, starting transfers between devices, swap_even(): lax.ppermute(value, axis, [(i, i ^ 1) for i in range(lax.axis_size(axis))])  12.7 us
    ppermute x3, starting transfers between devices, partner(): lax.ppermute(value, axis, [(i, i ^ bit) for i in range(lax.axis_size(axis...  9.16 us
    ppermute x3, waiting for transfers between devices, partner(): lax.ppermute(value, axis, [(i, i ^ bit) for i in range(lax.axis_size(axis...  3.75 us
    ppermute x5, starting transfers between devices, swap_odd(): return lax.ppermute(value, axis, up + [(b, a) for a, b in up])  3.29 us
    pallas_call x1, Pallas kernels, shards(): pl.pallas_call(filter_part, out_shape=(f32(*shape), f32(1, 1)), out_specs...  2.6 us
    pallas_call x1, Pallas kernels, shards(): call(adjoint_part, f32(*shape), [room(6), room(6), room(4), room(2), room...  2.38 us
    ppermute x5, waiting for transfers between devices, swap_even(): lax.ppermute(value, axis, [(i, i ^ 1) for i in range(lax.axis_size(axis))])  1.97 us
    pallas_call x1, Pallas kernels, shards(): pl.pallas_call(pack_own, out_shape=(f32(planes, size_y, size_z),) * 2 + (...  1.41 us
  transfers between devices with their start and end apart: 13, of which 4 were waited for; matrix products, arithmetic and copies ran while one was open for 0% of the time, Pallas kernels for 8%

profile of v6, /device:TPU:0, one launch (start us, length us, event | category | flops | bytes accessed | tf_op | source)
XLA Modules:
  0.0 38.8 jit_solution(14825388951487469001)
XLA Ops:
  0.6 1.4 %shard_map.68 = (f32[9,32,128]{2,1,0:T(8,128)S(1)}, f32[9,32,128]{2,1,0:T(8,128)S(1)}, f32[144,128]{1,0:T(8,128)S(1)}, f32[144,128]{1,0:T(8,128)S(1)}, f32[16,32...) custom-call(f32[16,32,128]{2,1,0:T(8,128)} %refs_0_.1, ...), custom_call_target="tpu_custom_call" | custom-call | tf_op jit(solution)/shard_map/pallas_call | solution.py:404
  2.0 0.7 %collective-permute-start = (f32[9,32,128]{2,1,0:T(8,128)S(1)}, f32[9,32,128]{2,1,0:T(8,128)S(1)}, u32[]{:S(2)}, u32[]{:S(2)}) collective-permute-start(f32[9,32,128]{2,1,0:T(8,128)S(1)} %get-tuple-element.21), channel_id=1, source_target_pairs={{8,16},{16,8},{9,17},{17,9},{10,18},{18,10},{11,19},{19,11},{12,20... | collective-permute-start | bytes 442376 | tf_op jit(solution)/shard_map/ppermute | solution.py:376
  2.7 4.4 %collective-permute-start.1 = (f32[9,32,128]{2,1,0:T(8,128)S(1)}, f32[9,32,128]{2,1,0:T(8,128)S(1)}, u32[]{:S(2)}, u32[]{:S(2)}) collective-permute-start(f32[9,32,128]{2,1,0:T(8,128)S(1)} %get-tuple-element.22), channel_id=1, source_target_pairs={{0,8},{8,0},{16,24},{24,16},{1,9},{9,1},{17,25},{25,17},{2,10},{10... | collective-permute-start | bytes 442376 | tf_op jit(solution)/shard_map/ppermute | solution.py:370
  7.1 1.5 %collective-permute-start.2 = (f32[144,128]{1,0:T(8,128)S(1)}, f32[144,128]{1,0:T(8,128)S(1)}, u32[]{:S(2)}, u32[]{:S(2)}) collective-permute-start(f32[144,128]{1,0:T(8,128)S(1)} %get-tuple-element.23), channel_id=1, source_target_pairs={{0,1},{1,0},{2,3},{3,2},{4,5},{5,4},{6,7},{7,6},{8,9},{9,8},{10,11... | collective-permute-start | bytes 221192 | tf_op jit(solution)/shard_map/ppermute | solution.py:370
  8.6 0.7 %collective-permute-start.3 = (f32[144,128]{1,0:T(8,128)S(1)}, f32[144,128]{1,0:T(8,128)S(1)}, u32[]{:S(2)}, u32[]{:S(2)}) collective-permute-start(f32[144,128]{1,0:T(8,128)S(1)} %get-tuple-element.24), channel_id=1, source_target_pairs={{1,2},{3,4},{5,6},{2,1},{4,3},{6,5},{9,10},{11,12},{13,14},{10,9},... | collective-permute-start | bytes 221192 | tf_op jit(solution)/shard_map/ppermute | solution.py:376
  9.3 0.0 collective-permute-done.x_odd
  9.3 0.0 collective-permute-done.1.x_even
  9.3 4.3 %collective-permute-start.4 = (f32[16,128]{1,0:T(8,128)S(1)}, f32[16,128]{1,0:T(8,128)S(1)}, u32[]{:S(2)}, u32[]{:S(2)}) collective-permute-start(f32[16,128]{1,0:T(8,128)S(1)} %get-tuple-element.25), channel_id=1, source_target_pairs={{0,1},{1,0},{2,3},{3,2},{4,5},{5,4},{6,7},{7,6},{8,9},{9,8},{10,11... | collective-permute-start | bytes 24584 | tf_op jit(solution)/shard_map/ppermute | solution.py:370
  13.7 0.6 %collective-permute-start.5 = (f32[16,128]{1,0:T(8,128)S(1)}, f32[16,128]{1,0:T(8,128)S(1)}, u32[]{:S(2)}, u32[]{:S(2)}) collective-permute-start(f32[16,128]{1,0:T(8,128)S(1)} %get-tuple-element.26), channel_id=1, source_target_pairs={{1,2},{3,4},{5,6},{2,1},{4,3},{6,5},{9,10},{11,12},{13,14},{10,9},... | collective-permute-start | bytes 24584 | tf_op jit(solution)/shard_map/ppermute | solution.py:376
  14.3 0.0 collective-permute-done.2.y_even
  14.3 0.0 collective-permute-done.3.y_odd
  14.3 0.7 %shard_map.71.mine = f32[8,128]{1,0:T(8,128)S(1)} custom-call(f32[9,32,128]{2,1,0:T(8,128)S(1)} %collective-permute-done.x_odd, f32[9,32,128]{2,1,0:T(8,128)S(1)} %collective-permute-done.1.x_even, f32[144,128]{1,0:T(8,128)S(1)} %collective-permute-done.2.y_even, f32[144,128]{1,0:T(8,128)S(1)} %collective-permute-done.3.y_odd, ...), custom_call_target="tpu_custom_call" | custom-call | flops 10000 | bytes 10000 | tf_op jit(solution)/shard_map/pallas_call | solution.py:425
  15.0 4.1 %collective-permute-start.6 = (f32[8,128]{1,0:T(8,128)S(1)}, f32[8,128]{1,0:T(8,128)S(1)}, u32[]{:S(2)}, u32[]{:S(2)}) collective-permute-start(f32[8,128]{1,0:T(8,128)S(1)} %shard_map.71.mine), channel_id=1, source_target_pairs={{0,4},{1,5},{2,6},{3,7},{4,0},{5,1},{6,2},{7,3},{8,12},{9,13},{10,... | collective-permute-start | bytes 12296 | tf_op jit(solution)/shard_map/ppermute | solution.py:380
  19.1 0.0 collective-permute-done.4.corner_even
  19.1 0.0 collective-permute-done.5.corner_odd
  19.1 2.4 %shard_map.70.raw.raw_in = f32[16,32,128]{2,1,0:T(8,128)S(1)} custom-call(f32[9,32,128]{2,1,0:T(8,128)S(1)} %collective-permute-done.x_odd, f32[9,32,128]{2,1,0:T(8,128)S(1)} %collective-permute-done.1.x_even, f32[144,128]{1,0:T(8,128)S(1)} %collective-permute-done.2.y_even, f32[144,128]{1,0:T(8,128)S(1)} %collective-permute-done.3.y_odd, ...), custom_call_target="tpu_custom_call" | custom-call | flops 10000000 | bytes 10000000 | tf_op jit(solution)/shard_map/pallas_call | solution.py:427
  21.5 0.0 collective-permute-done.6.other
  21.6 0.1 collective-permute-start.8
  21.7 0.7 %collective-permute-start.7 = (f32[4,32,128]{2,1,0:T(8,128)S(1)}, f32[4,32,128]{2,1,0:T(8,128)S(1)}, u32[]{:S(2)}, u32[]{:S(2)}) collective-permute-start(f32[4,32,128]{2,1,0:T(8,128)S(1)} %get-tuple-element.32), channel_id=1, source_target_pairs={{8,16},{16,8},{9,17},{17,9},{10,18},{18,10},{11,19},{19,11},{12,20... | collective-permute-start | bytes 196616 | tf_op jit(solution)/shard_map/ppermute | solution.py:376
  22.3 0.6 %collective-permute-done.8.x_even = f32[5,32,128]{2,1,0:T(8,128)S(1)} collective-permute-done((f32[5,32,128]{2,1,0:T(8,128)S(1)}, f32[5,32,128]{2,1,0:T(8,128)S(1)}, u32[]{:S(2)}, u32[]{:S(2)}) %collective-permute-start.8) | collective-permute-done | bytes 81952 | tf_op jit(solution)/shard_map/ppermute | solution.py:370
  22.9 2.9 %collective-permute-start.9 = (f32[8,128]{1,0:T(8,128)S(1)}, f32[8,128]{1,0:T(8,128)S(1)}, u32[]{:S(2)}, u32[]{:S(2)}) collective-permute-start(f32[8,128]{1,0:T(8,128)S(1)} %fusion.mine), channel_id=1, source_target_pairs={{0,16},{8,24},{16,0},{24,8},{1,17},{9,25},{17,1},{25,9},{2,18},{10... | collective-permute-start | bytes 12296 | tf_op jit(solution)/shard_map/ppermute | solution.py:380
  25.8 0.0 collective-permute-done.7.x_odd
  25.8 2.2 %collective-permute-done.9.other = f32[8,128]{1,0:T(8,128)S(1)} collective-permute-done((f32[8,128]{1,0:T(8,128)S(1)}, f32[8,128]{1,0:T(8,128)S(1)}, u32[]{:S(2)}, u32[]{:S(2)}) %collective-permute-start.9) | collective-permute-done | bytes 4128 | tf_op jit(solution)/shard_map/ppermute | solution.py:380
  28.0 2.4 %collective-permute-start.11 = (f32[88,128]{1,0:T(8,128)S(1)}, f32[88,128]{1,0:T(8,128)S(1)}, u32[]{:S(2)}, u32[]{:S(2)}) collective-permute-start(f32[88,128]{1,0:T(8,128)S(1)} %get-tuple-element.36), channel_id=1, source_target_pairs={{0,1},{1,0},{2,3},{3,2},{4,5},{5,4},{6,7},{7,6},{8,9},{9,8},{10,11... | collective-permute-start | bytes 135176 | tf_op jit(solution)/shard_map/ppermute | solution.py:370
  30.4 0.7 %collective-permute-start.10 = (f32[80,128]{1,0:T(8,128)S(1)}, f32[80,128]{1,0:T(8,128)S(1)}, u32[]{:S(2)}, u32[]{:S(2)}) collective-permute-start(f32[80,128]{1,0:T(8,128)S(1)} %get-tuple-element.35), channel_id=1, source_target_pairs={{1,2},{3,4},{5,6},{2,1},{4,3},{6,5},{9,10},{11,12},{13,14},{10,9},... | collective-permute-start | bytes 122888 | tf_op jit(solution)/shard_map/ppermute | solution.py:376
  31.0 1.4 %collective-permute-done.11.y_even = f32[88,128]{1,0:T(8,128)S(1)} collective-permute-done((f32[88,128]{1,0:T(8,128)S(1)}, f32[88,128]{1,0:T(8,128)S(1)}, u32[]{:S(2)}, u32[]{:S(2)}) %collective-permute-start.11) | collective-permute-done | bytes 45088 | tf_op jit(solution)/shard_map/ppermute | solution.py:370
  32.4 2.2 %collective-permute-start.12 = (f32[8,128]{1,0:T(8,128)S(1)}, f32[8,128]{1,0:T(8,128)S(1)}, u32[]{:S(2)}, u32[]{:S(2)}) collective-permute-start(f32[8,128]{1,0:T(8,128)S(1)} %slice_add_fusion.mine), channel_id=1, source_target_pairs={{0,2},{1,3},{2,0},{3,1},{4,6},{5,7},{6,4},{7,5},{8,10},{9,11},{10,... | collective-permute-start | bytes 12296 | tf_op jit(solution)/shard_map/ppermute | solution.py:380
  34.6 0.0 collective-permute-done.10.y_odd
  34.6 1.6 %collective-permute-done.12.other = f32[8,128]{1,0:T(8,128)S(1)} collective-permute-done((f32[8,128]{1,0:T(8,128)S(1)}, f32[8,128]{1,0:T(8,128)S(1)}, u32[]{:S(2)}, u32[]{:S(2)}) %collective-permute-start.12) | collective-permute-done | bytes 4128 | tf_op jit(solution)/shard_map/ppermute | solution.py:380
  36.2 2.6 %shard_map.74 = (f32[16,32,128]{2,1,0:T(8,128)}, f32[1,1]{1,0:T(1,128)}) custom-call(f32[4,32,128]{2,1,0:T(8,128)S(1)} %collective-permute-done.7.x_odd, f32[5,32,128]{2,1,0:T(8,128)S(1)} %collective-permute-done.8.x_even, f32[80,128]{1,0:T(8,128)S(1)} %collective-permute-done.10.y_odd, f32[88,128]{1,0:T(8,128)S(1)} %collective-permute-done.11.y_even, ...), custom_call_target="tpu_custom_call" | custom-call | tf_op jit(solution)/shard_map/pallas_call | solution.py:448
  (5 shorter events, 0.1 us)
Async XLA Ops:
  2.0 7.2 %collective-permute-start = (f32[9,32,128]{2,1,0:T(8,128)S(1)}, f32[9,32,128]{2,1,0:T(8,128)S(1)}, u32[]{:S(2)}, u32[]{:S(2)}) collective-permute-start(f32[9,32,128]{2,1,0:T(8,128)S(1)} %get-tuple-element.21), channel_id=1, source_target_pairs={{8,16},{16,8},{9,17},{17,9},{10,18},{18,10},{11,19},{19,11},{12,20... | collective-permute-start | bytes 442376 | tf_op jit(solution)/shard_map/ppermute | solution.py:376
  2.7 6.6 %collective-permute-start.1 = (f32[9,32,128]{2,1,0:T(8,128)S(1)}, f32[9,32,128]{2,1,0:T(8,128)S(1)}, u32[]{:S(2)}, u32[]{:S(2)}) collective-permute-start(f32[9,32,128]{2,1,0:T(8,128)S(1)} %get-tuple-element.22), channel_id=1, source_target_pairs={{0,8},{8,0},{16,24},{24,16},{1,9},{9,1},{17,25},{25,17},{2,10},{10... | collective-permute-start | bytes 442376 | tf_op jit(solution)/shard_map/ppermute | solution.py:370
  7.1 7.2 %collective-permute-start.2 = (f32[144,128]{1,0:T(8,128)S(1)}, f32[144,128]{1,0:T(8,128)S(1)}, u32[]{:S(2)}, u32[]{:S(2)}) collective-permute-start(f32[144,128]{1,0:T(8,128)S(1)} %get-tuple-element.23), channel_id=1, source_target_pairs={{0,1},{1,0},{2,3},{3,2},{4,5},{5,4},{6,7},{7,6},{8,9},{9,8},{10,11... | collective-permute-start | bytes 221192 | tf_op jit(solution)/shard_map/ppermute | solution.py:370
  8.6 5.7 %collective-permute-start.3 = (f32[144,128]{1,0:T(8,128)S(1)}, f32[144,128]{1,0:T(8,128)S(1)}, u32[]{:S(2)}, u32[]{:S(2)}) collective-permute-start(f32[144,128]{1,0:T(8,128)S(1)} %get-tuple-element.24), channel_id=1, source_target_pairs={{1,2},{3,4},{5,6},{2,1},{4,3},{6,5},{9,10},{11,12},{13,14},{10,9},... | collective-permute-start | bytes 221192 | tf_op jit(solution)/shard_map/ppermute | solution.py:376
  9.3 9.8 %collective-permute-start.4 = (f32[16,128]{1,0:T(8,128)S(1)}, f32[16,128]{1,0:T(8,128)S(1)}, u32[]{:S(2)}, u32[]{:S(2)}) collective-permute-start(f32[16,128]{1,0:T(8,128)S(1)} %get-tuple-element.25), channel_id=1, source_target_pairs={{0,1},{1,0},{2,3},{3,2},{4,5},{5,4},{6,7},{7,6},{8,9},{9,8},{10,11... | collective-permute-start | bytes 24584 | tf_op jit(solution)/shard_map/ppermute | solution.py:370
  13.7 5.5 %collective-permute-start.5 = (f32[16,128]{1,0:T(8,128)S(1)}, f32[16,128]{1,0:T(8,128)S(1)}, u32[]{:S(2)}, u32[]{:S(2)}) collective-permute-start(f32[16,128]{1,0:T(8,128)S(1)} %get-tuple-element.26), channel_id=1, source_target_pairs={{1,2},{3,4},{5,6},{2,1},{4,3},{6,5},{9,10},{11,12},{13,14},{10,9},... | collective-permute-start | bytes 24584 | tf_op jit(solution)/shard_map/ppermute | solution.py:376
  15.0 6.5 %collective-permute-start.6 = (f32[8,128]{1,0:T(8,128)S(1)}, f32[8,128]{1,0:T(8,128)S(1)}, u32[]{:S(2)}, u32[]{:S(2)}) collective-permute-start(f32[8,128]{1,0:T(8,128)S(1)} %shard_map.71.mine), channel_id=1, source_target_pairs={{0,4},{1,5},{2,6},{3,7},{4,0},{5,1},{6,2},{7,3},{8,12},{9,13},{10,... | collective-permute-start | bytes 12296 | tf_op jit(solution)/shard_map/ppermute | solution.py:380
  21.6 1.3 %collective-permute-start.8 = (f32[5,32,128]{2,1,0:T(8,128)S(1)}, f32[5,32,128]{2,1,0:T(8,128)S(1)}, u32[]{:S(2)}, u32[]{:S(2)}) collective-permute-start(f32[5,32,128]{2,1,0:T(8,128)S(1)} %get-tuple-element.33), channel_id=1, source_target_pairs={{0,8},{8,0},{16,24},{24,16},{1,9},{9,1},{17,25},{25,17},{2,10},{10... | collective-permute-start | bytes 245768 | tf_op jit(solution)/shard_map/ppermute | solution.py:370
  21.7 4.1 %collective-permute-start.7 = (f32[4,32,128]{2,1,0:T(8,128)S(1)}, f32[4,32,128]{2,1,0:T(8,128)S(1)}, u32[]{:S(2)}, u32[]{:S(2)}) collective-permute-start(f32[4,32,128]{2,1,0:T(8,128)S(1)} %get-tuple-element.32), channel_id=1, source_target_pairs={{8,16},{16,8},{9,17},{17,9},{10,18},{18,10},{11,19},{19,11},{12,20... | collective-permute-start | bytes 196616 | tf_op jit(solution)/shard_map/ppermute | solution.py:376
  22.9 5.0 %collective-permute-start.9 = (f32[8,128]{1,0:T(8,128)S(1)}, f32[8,128]{1,0:T(8,128)S(1)}, u32[]{:S(2)}, u32[]{:S(2)}) collective-permute-start(f32[8,128]{1,0:T(8,128)S(1)} %fusion.mine), channel_id=1, source_target_pairs={{0,16},{8,24},{16,0},{24,8},{1,17},{9,25},{17,1},{25,9},{2,18},{10... | collective-permute-start | bytes 12296 | tf_op jit(solution)/shard_map/ppermute | solution.py:380
  28.0 4.4 %collective-permute-start.11 = (f32[88,128]{1,0:T(8,128)S(1)}, f32[88,128]{1,0:T(8,128)S(1)}, u32[]{:S(2)}, u32[]{:S(2)}) collective-permute-start(f32[88,128]{1,0:T(8,128)S(1)} %get-tuple-element.36), channel_id=1, source_target_pairs={{0,1},{1,0},{2,3},{3,2},{4,5},{5,4},{6,7},{7,6},{8,9},{9,8},{10,11... | collective-permute-start | bytes 135176 | tf_op jit(solution)/shard_map/ppermute | solution.py:370
  30.4 4.2 %collective-permute-start.10 = (f32[80,128]{1,0:T(8,128)S(1)}, f32[80,128]{1,0:T(8,128)S(1)}, u32[]{:S(2)}, u32[]{:S(2)}) collective-permute-start(f32[80,128]{1,0:T(8,128)S(1)} %get-tuple-element.35), channel_id=1, source_target_pairs={{1,2},{3,4},{5,6},{2,1},{4,3},{6,5},{9,10},{11,12},{13,14},{10,9},... | collective-permute-start | bytes 122888 | tf_op jit(solution)/shard_map/ppermute | solution.py:376
  32.4 3.8 %collective-permute-start.12 = (f32[8,128]{1,0:T(8,128)S(1)}, f32[8,128]{1,0:T(8,128)S(1)}, u32[]{:S(2)}, u32[]{:S(2)}) collective-permute-start(f32[8,128]{1,0:T(8,128)S(1)} %slice_add_fusion.mine), channel_id=1, source_target_pairs={{0,2},{1,3},{2,0},{3,1},{4,6},{5,7},{6,4},{7,5},{8,10},{9,11},{10,... | collective-permute-start | bytes 12296 | tf_op jit(solution)/shard_map/ppermute | solution.py:380

commit v7 on v6

--- a/solution.py
+++ b/solution.py
@@ -264,14 +264,11 @@
 
 
 def pack_raw_x(raw, mine, other, even_out, odd_out, energy_out):
-    size_x, size_y, size_z = raw.shape
-    width = FILTER_SWEEPS
+    size_x = raw.shape[0]
+    energy_out[...] = mine[...] + other[...]
     low_first = odd_place("gx")
-    energy = mine[...] + other[...]
-    energy_out[...] = energy
     for out, low in ((even_out, low_first), (odd_out, jnp.logical_not(low_first))):
-        out[pl.ds(0, width)] = raw[pl.ds(jnp.where(low, 0, size_x - width), width)]
-    even_out[width, 0:8] = energy
+        out[...] = raw[pl.ds(jnp.where(low, 0, size_x - FILTER_SWEEPS), FILTER_SWEEPS)]
 
 
 def pack_raw_y(x_odd, x_even, raw, mine, other, even_out, odd_out, energy_out):
@@ -297,18 +294,8 @@
         odd_out[at:at + rows] = jnp.where(y_swap, high, low)
 
 
-def filter_part(x_odd, x_even, y_odd, y_even, raw_in, labels, mine, other, out, mean_out, raw, even, odd, held, sem):
-    size_x, size_y, size_z = raw_in.shape
+def relaxation(raw, size_x, size_y, size_z):
     width = FILTER_SWEEPS
-    tile = pl.ds(0, size_y)
-
-    def fill(x, n):
-        raw[pl.ds(x + width, n), tile] = raw_in[pl.ds(x, n)]
-
-    planes_loop(0, size_x, 4, fill)
-    unpack_planes(raw, width, x_even[pl.ds(0, width)], x_odd[pl.ds(0, width)], size_x, size_y)
-    unpack_rows((raw,), (width,), segments((width,), size_x)[0], y_even, y_odd, size_y)
-
     wide = size_y + 2 * RIM
     extent_x = lax.axis_size("gx") * size_x
     extent_y = lax.axis_size("gy") * size_y
@@ -340,9 +327,24 @@
             scaled.append(total[k:k + 1] * scale)
         return jnp.concatenate(scaled, axis=0)
 
+    return relax
+
+
+def filter_first(x_odd, x_even, y_odd, y_even, raw_in, raw, odd, even):
+    size_x, size_y, size_z = raw_in.shape
+    width = FILTER_SWEEPS
+    tile = pl.ds(0, size_y)
+
+    def fill(x, n):
+        raw[pl.ds(x + width, n), tile] = raw_in[pl.ds(x, n)]
+
+    planes_loop(0, size_x, 4, fill)
+    unpack_planes(raw, width, x_even[...], x_odd[...], size_x, size_y)
+    unpack_rows((raw,), (width,), segments((width,), size_x)[0], y_even, y_odd, size_y)
+    relax = relaxation(raw, size_x, size_y, size_z)
     src = raw
     for sweep in range(FILTER_SWEEPS - 1):
-        dst = (even, odd)[sweep % 2]
+        dst = (odd, even)[(FILTER_SWEEPS - sweep) % 2]
 
         def step(x, n, src=src, dst=dst):
             dst[pl.ds(x, n)] = relax(src, x, n)
@@ -350,15 +352,19 @@
         planes_loop(sweep + 1, size_x + 2 * width - sweep - 1, 11, step)
         src = dst
 
-    total = jnp.sum(mine[...] + other[...])
-    mean = 0.5 * total / (extent_x * extent_y * size_z) + epsilon_mean
+
+def filter_last(raw, src, labels, mine, other, out, mean_out, held, sem):
+    size_x, size_y, size_z = labels.shape
+    relax = relaxation(raw, size_x, size_y, size_z)
+    voxels = lax.axis_size("gx") * size_x * lax.axis_size("gy") * size_y * size_z
+    mean = 0.5 * jnp.sum(mine[...] + other[...]) / voxels + epsilon_mean
     mean_out[0, 0] = mean
     inverse = 1.0 / jnp.full((1, 1, size_z), mean, jnp.float32)
     block = size_x // 2
     copies = []
     for k in range(2):
         span = pl.ds(k * block, block)
-        f = relax(src, k * block + width, block)[:, :size_y]
+        f = relax(src, k * block + FILTER_SWEEPS, block)[:, :size_y]
         held[span] = jnp.where(labels[span] == 1, f * inverse, 0.0)
         copies.append(pltpu.make_async_copy(held.at[span], out.at[span], sem.at[k]))
         copies[k].start()
@@ -432,11 +438,16 @@
     )(x_odd, x_even, y_even, y_odd, corner_even, corner_odd, *own)
 
     face = f32(FILTER_SWEEPS, size_y, size_z)
-    tall = f32(FILTER_SWEEPS + 1, size_y, size_z)
-    even, odd, energy = call(pack_raw_x, (tall, face, f32(8, size_z)))(raw, mine, other)
+    raw = call(
+        adjoint_part,
+        f32(*shape),
+        [room(6), room(6), room(4), room(2), room(5), room(4), room(4), room(4), room(4), room(2)],
+        cost=10000000,
+    )(x_odd, x_even, y_even, y_odd, corner_even, corner_odd, *own)
+
+    even, odd, energy = call(pack_raw_x, (face, face, f32(8, size_z)))(raw, mine, other)
     x_even = swap_even(even, "gx")
     x_odd = swap_odd(odd, "gx")
-    energy = energy + x_even[FILTER_SWEEPS, 0:8]
     mine, other = doubling(energy, x_bits)
     _, rows = segments((FILTER_SWEEPS,), size_x)
     even, odd, energy = call(pack_raw_y, (f32(rows + 8, size_z), f32(rows, size_z), f32(8, size_z)))(
@@ -444,14 +455,21 @@
     y_even = swap_even(even, "gy")
     y_odd = swap_odd(odd, "gy")
     energy = energy + y_even[rows:rows + 8]
-    mine, other = doubling(energy, y_bits[:1])
+    mine, other = doubling(energy, y_bits[:1] + [("gx", 1)])
+    padded = f32(size_x + 2 * FILTER_SWEEPS, wide, size_z)
+    raw, filtered = call(
+        filter_first,
+        (padded, padded),
+        [pltpu.VMEM(padded.shape, jnp.float32)],
+        cost=10000000,
+    )(x_odd, x_even, y_odd, y_even, raw)
     sensitivity, mean_energy = pl.pallas_call(
-        filter_part,
+        filter_last,
         out_shape=(f32(*shape), f32(1, 1)),
         out_specs=(pl.BlockSpec(memory_space=pl.ANY), pl.BlockSpec(memory_space=pltpu.SMEM)),
-        scratch_shapes=[room(2 * FILTER_SWEEPS)] * 3 + [pltpu.VMEM(shape, jnp.float32), pltpu.SemaphoreType.DMA((2,))],
+        scratch_shapes=[pltpu.VMEM(shape, jnp.float32), pltpu.SemaphoreType.DMA((2,))],
         compiler_params=pltpu.CompilerParams(vmem_limit_bytes=VMEM_LIMIT),
-    )(x_odd, x_even, y_odd, y_even, raw, own[1], mine, other)
+    )(raw, filtered, own[1], mine, other)
     return (sensitivity, mean_energy[0, 0])
 
 

time: 39 us -> 38.9 us (level); the launches traced: 38.8 us -> 38.2 us
  starting transfers between devices: 25.1 us -> 24 us
  waiting for transfers between devices: 5.73 us -> 6.22 us
    ppermute x3 -> x4, starting transfers between devices: 9.16 us -> 6.67 us  [partner(): lax.ppermute(value, axis, [(i, i ^ bit) for i in range(lax.axis_size(axis...]
    ppermute x5, starting transfers between devices: 12.7 us -> 14 us  [swap_even(): lax.ppermute(value, axis, [(i, i ^ 1) for i in range(lax.axis_size(axis))])]
    ppermute x3 -> x4, waiting for transfers between devices: 3.75 us -> 4.83 us  [partner(): lax.ppermute(value, axis, [(i, i ^ bit) for i in range(lax.axis_size(axis...]
    ppermute x5, waiting for transfers between devices: 1.97 us -> 1.38 us  [swap_even(): lax.ppermute(value, axis, [(i, i ^ 1) for i in range(lax.axis_size(axis))])]
    pallas_call x2 -> x3, Pallas kernels: 2.63 us -> 2.65 us  [the longest x1 1.45 us: shards(): pl.pallas_call(filter_last, out_shape=(f32(*shape), f32(1, 1)), out_specs...]
  transfers between devices with their start and end apart: 13 -> 14, of which waited for: 4 -> 3; matrix products, arithmetic and copies ran while one was open for 0% -> 0% of each run, Pallas kernels for 8% -> 11%
where the time goes in v7:
time: 38.9 us; the launch traced here: 38.2 us
  starting transfers between devices  24 us (62%)
  Pallas kernels  7.19 us (18%)
  waiting for transfers between devices  6.22 us (16%)
  between operations  0.78 us (2%)
    ppermute x5, starting transfers between devices, swap_even(): lax.ppermute(value, axis, [(i, i ^ 1) for i in range(lax.axis_size(axis))])  14 us
    ppermute x4, starting transfers between devices, partner(): lax.ppermute(value, axis, [(i, i ^ bit) for i in range(lax.axis_size(axis...  6.67 us
    ppermute x4, waiting for transfers between devices, partner(): lax.ppermute(value, axis, [(i, i ^ bit) for i in range(lax.axis_size(axis...  4.83 us
    ppermute x5, starting transfers between devices, swap_odd(): return lax.ppermute(value, axis, up + [(b, a) for a, b in up])  3.29 us
    pallas_call x1, Pallas kernels, shards(): call(adjoint_part, f32(*shape), [room(6), room(6), room(4), room(2), room...  2.38 us
    pallas_call x1, Pallas kernels, shards(): pl.pallas_call(filter_last, out_shape=(f32(*shape), f32(1, 1)), out_specs...  1.45 us
    pallas_call x1, Pallas kernels, shards(): pl.pallas_call(pack_own, out_shape=(f32(planes, size_y, size_z),) * 2 + (...  1.41 us
    ppermute x5, waiting for transfers between devices, swap_even(): lax.ppermute(value, axis, [(i, i ^ 1) for i in range(lax.axis_size(axis))])  1.38 us
  transfers between devices with their start and end apart: 14, of which 3 were waited for; matrix products, arithmetic and copies ran while one was open for 0% of the time, Pallas kernels for 11%

profile of v7, /device:TPU:0, one launch (start us, length us, event | category | flops | bytes accessed | tf_op | source)
XLA Modules:
  0.0 38.2 jit_solution(18369669355037619493)
XLA Ops:
  0.6 1.4 %shard_map.68 = (f32[9,32,128]{2,1,0:T(8,128)S(1)}, f32[9,32,128]{2,1,0:T(8,128)S(1)}, f32[144,128]{1,0:T(8,128)S(1)}, f32[144,128]{1,0:T(8,128)S(1)}, f32[16,32...) custom-call(f32[16,32,128]{2,1,0:T(8,128)} %refs_0_.1, ...), custom_call_target="tpu_custom_call" | custom-call | tf_op jit(solution)/shard_map/pallas_call | solution.py:410
  2.0 0.7 %collective-permute-start = (f32[9,32,128]{2,1,0:T(8,128)S(1)}, f32[9,32,128]{2,1,0:T(8,128)S(1)}, u32[]{:S(2)}, u32[]{:S(2)}) collective-permute-start(f32[9,32,128]{2,1,0:T(8,128)S(1)} %get-tuple-element.23), channel_id=1, source_target_pairs={{8,16},{16,8},{9,17},{17,9},{10,18},{18,10},{11,19},{19,11},{12,20... | collective-permute-start | bytes 442376 | tf_op jit(solution)/shard_map/ppermute | solution.py:382
  2.7 4.4 %collective-permute-start.1 = (f32[9,32,128]{2,1,0:T(8,128)S(1)}, f32[9,32,128]{2,1,0:T(8,128)S(1)}, u32[]{:S(2)}, u32[]{:S(2)}) collective-permute-start(f32[9,32,128]{2,1,0:T(8,128)S(1)} %get-tuple-element.24), channel_id=1, source_target_pairs={{0,8},{8,0},{16,24},{24,16},{1,9},{9,1},{17,25},{25,17},{2,10},{10... | collective-permute-start | bytes 442376 | tf_op jit(solution)/shard_map/ppermute | solution.py:376
  7.1 1.5 %collective-permute-start.2 = (f32[144,128]{1,0:T(8,128)S(1)}, f32[144,128]{1,0:T(8,128)S(1)}, u32[]{:S(2)}, u32[]{:S(2)}) collective-permute-start(f32[144,128]{1,0:T(8,128)S(1)} %get-tuple-element.25), channel_id=1, source_target_pairs={{0,1},{1,0},{2,3},{3,2},{4,5},{5,4},{6,7},{7,6},{8,9},{9,8},{10,11... | collective-permute-start | bytes 221192 | tf_op jit(solution)/shard_map/ppermute | solution.py:376
  8.6 0.7 %collective-permute-start.3 = (f32[144,128]{1,0:T(8,128)S(1)}, f32[144,128]{1,0:T(8,128)S(1)}, u32[]{:S(2)}, u32[]{:S(2)}) collective-permute-start(f32[144,128]{1,0:T(8,128)S(1)} %get-tuple-element.26), channel_id=1, source_target_pairs={{1,2},{3,4},{5,6},{2,1},{4,3},{6,5},{9,10},{11,12},{13,14},{10,9},... | collective-permute-start | bytes 221192 | tf_op jit(solution)/shard_map/ppermute | solution.py:382
  9.3 0.0 collective-permute-done.x_odd
  9.3 0.0 collective-permute-done.1.x_even
  9.3 4.3 %collective-permute-start.4 = (f32[16,128]{1,0:T(8,128)S(1)}, f32[16,128]{1,0:T(8,128)S(1)}, u32[]{:S(2)}, u32[]{:S(2)}) collective-permute-start(f32[16,128]{1,0:T(8,128)S(1)} %get-tuple-element.27), channel_id=1, source_target_pairs={{0,1},{1,0},{2,3},{3,2},{4,5},{5,4},{6,7},{7,6},{8,9},{9,8},{10,11... | collective-permute-start | bytes 24584 | tf_op jit(solution)/shard_map/ppermute | solution.py:376
  13.7 0.6 %collective-permute-start.5 = (f32[16,128]{1,0:T(8,128)S(1)}, f32[16,128]{1,0:T(8,128)S(1)}, u32[]{:S(2)}, u32[]{:S(2)}) collective-permute-start(f32[16,128]{1,0:T(8,128)S(1)} %get-tuple-element.28), channel_id=1, source_target_pairs={{1,2},{3,4},{5,6},{2,1},{4,3},{6,5},{9,10},{11,12},{13,14},{10,9},... | collective-permute-start | bytes 24584 | tf_op jit(solution)/shard_map/ppermute | solution.py:382
  14.3 0.0 collective-permute-done.2.y_even
  14.3 0.0 collective-permute-done.3.y_odd
  14.3 0.7 %shard_map.71.mine = f32[8,128]{1,0:T(8,128)S(1)} custom-call(f32[9,32,128]{2,1,0:T(8,128)S(1)} %collective-permute-done.x_odd, f32[9,32,128]{2,1,0:T(8,128)S(1)} %collective-permute-done.1.x_even, f32[144,128]{1,0:T(8,128)S(1)} %collective-permute-done.2.y_even, f32[144,128]{1,0:T(8,128)S(1)} %collective-permute-done.3.y_odd, ...), custom_call_target="tpu_custom_call" | custom-call | flops 10000 | bytes 10000 | tf_op jit(solution)/shard_map/pallas_call | solution.py:431
  15.0 4.1 %collective-permute-start.6 = (f32[8,128]{1,0:T(8,128)S(1)}, f32[8,128]{1,0:T(8,128)S(1)}, u32[]{:S(2)}, u32[]{:S(2)}) collective-permute-start(f32[8,128]{1,0:T(8,128)S(1)} %shard_map.71.mine), channel_id=1, source_target_pairs={{0,4},{1,5},{2,6},{3,7},{4,0},{5,1},{6,2},{7,3},{8,12},{9,13},{10,... | collective-permute-start | bytes 12296 | tf_op jit(solution)/shard_map/ppermute | solution.py:386
  19.1 0.0 collective-permute-done.4.corner_even
  19.1 0.0 collective-permute-done.5.corner_odd
  19.1 2.4 %shard_map.70.raw.raw_in = f32[16,32,128]{2,1,0:T(8,128)S(1)} custom-call(f32[9,32,128]{2,1,0:T(8,128)S(1)} %collective-permute-done.x_odd, f32[9,32,128]{2,1,0:T(8,128)S(1)} %collective-permute-done.1.x_even, f32[144,128]{1,0:T(8,128)S(1)} %collective-permute-done.2.y_even, f32[144,128]{1,0:T(8,128)S(1)} %collective-permute-done.3.y_odd, ...), custom_call_target="tpu_custom_call" | custom-call | flops 10000000 | bytes 10000000 | tf_op jit(solution)/shard_map/pallas_call | solution.py:441
  21.5 0.0 collective-permute-done.6.other
  21.6 0.7 %collective-permute-start.7 = (f32[4,32,128]{2,1,0:T(8,128)S(1)}, f32[4,32,128]{2,1,0:T(8,128)S(1)}, u32[]{:S(2)}, u32[]{:S(2)}) collective-permute-start(f32[4,32,128]{2,1,0:T(8,128)S(1)} %get-tuple-element.34), channel_id=1, source_target_pairs={{8,16},{16,8},{9,17},{17,9},{10,18},{18,10},{11,19},{19,11},{12,20... | collective-permute-start | bytes 196616 | tf_op jit(solution)/shard_map/ppermute | solution.py:382
  22.3 1.4 %collective-permute-start.8 = (f32[4,32,128]{2,1,0:T(8,128)S(1)}, f32[4,32,128]{2,1,0:T(8,128)S(1)}, u32[]{:S(2)}, u32[]{:S(2)}) collective-permute-start(f32[4,32,128]{2,1,0:T(8,128)S(1)} %get-tuple-element.35), channel_id=1, source_target_pairs={{0,8},{8,0},{16,24},{24,16},{1,9},{9,1},{17,25},{25,17},{2,10},{10... | collective-permute-start | bytes 196616 | tf_op jit(solution)/shard_map/ppermute | solution.py:376
  23.7 0.4 collective-permute-start.9
  24.0 3.2 %collective-permute-done.9.other = f32[8,128]{1,0:T(8,128)S(1)} collective-permute-done((f32[8,128]{1,0:T(8,128)S(1)}, f32[8,128]{1,0:T(8,128)S(1)}, u32[]{:S(2)}, u32[]{:S(2)}) %collective-permute-start.9) | collective-permute-done | bytes 4128 | tf_op jit(solution)/shard_map/ppermute | solution.py:386
  27.3 0.0 collective-permute-done.7.x_odd
  27.3 0.0 collective-permute-done.8.x_even
  27.3 2.4 %collective-permute-start.11 = (f32[88,128]{1,0:T(8,128)S(1)}, f32[88,128]{1,0:T(8,128)S(1)}, u32[]{:S(2)}, u32[]{:S(2)}) collective-permute-start(f32[88,128]{1,0:T(8,128)S(1)} %get-tuple-element.38), channel_id=1, source_target_pairs={{0,1},{1,0},{2,3},{3,2},{4,5},{5,4},{6,7},{7,6},{8,9},{9,8},{10,11... | collective-permute-start | bytes 135176 | tf_op jit(solution)/shard_map/ppermute | solution.py:376
  29.7 0.7 %collective-permute-start.10 = (f32[80,128]{1,0:T(8,128)S(1)}, f32[80,128]{1,0:T(8,128)S(1)}, u32[]{:S(2)}, u32[]{:S(2)}) collective-permute-start(f32[80,128]{1,0:T(8,128)S(1)} %get-tuple-element.37), channel_id=1, source_target_pairs={{1,2},{3,4},{5,6},{2,1},{4,3},{6,5},{9,10},{11,12},{13,14},{10,9},... | collective-permute-start | bytes 122888 | tf_op jit(solution)/shard_map/ppermute | solution.py:382
  30.4 1.4 %collective-permute-done.11.y_even = f32[88,128]{1,0:T(8,128)S(1)} collective-permute-done((f32[88,128]{1,0:T(8,128)S(1)}, f32[88,128]{1,0:T(8,128)S(1)}, u32[]{:S(2)}, u32[]{:S(2)}) %collective-permute-start.11) | collective-permute-done | bytes 45088 | tf_op jit(solution)/shard_map/ppermute | solution.py:376
  31.7 2.2 %collective-permute-start.12 = (f32[8,128]{1,0:T(8,128)S(1)}, f32[8,128]{1,0:T(8,128)S(1)}, u32[]{:S(2)}, u32[]{:S(2)}) collective-permute-start(f32[8,128]{1,0:T(8,128)S(1)} %slice_add_fusion), channel_id=1, source_target_pairs={{0,2},{1,3},{2,0},{3,1},{4,6},{5,7},{6,4},{7,5},{8,10},{9,11},{10,... | collective-permute-start | bytes 12296 | tf_op jit(solution)/shard_map/ppermute | solution.py:386
  33.9 1.6 %collective-permute-done.12 = f32[8,128]{1,0:T(8,128)S(1)} collective-permute-done((f32[8,128]{1,0:T(8,128)S(1)}, f32[8,128]{1,0:T(8,128)S(1)}, u32[]{:S(2)}, u32[]{:S(2)}) %collective-permute-start.12) | collective-permute-done | bytes 4128 | tf_op jit(solution)/shard_map/ppermute | solution.py:386
  35.5 0.0 collective-permute-start.13
  35.5 0.0 collective-permute-done.10.y_odd
  35.5 1.2 %shard_map.74 = (f32[24,40,128]{2,1,0:T(8,128)S(1)}, f32[24,40,128]{2,1,0:T(8,128)S(1)}) custom-call(f32[4,32,128]{2,1,0:T(8,128)S(1)} %collective-permute-done.7.x_odd, f32[4,32,128]{2,1,0:T(8,128)S(1)} %collective-permute-done.8.x_even, f32[80,128]{1,0:T(8,128)S(1)} %collective-permute-done.10.y_odd, f32[88,128]{1,0:T(8,128)S(1)} %collective-permute-done.11.y_even, ...), custom_call_target="tpu_custom_call" | custom-call | flops 10000000 | bytes 10000000 | tf_op jit(solution)/shard_map/pallas_call | solution.py:460
  36.7 0.0 collective-permute-done.13.other
  36.7 1.5 %shard_map.75 = (f32[16,32,128]{2,1,0:T(8,128)}, f32[1,1]{1,0:T(1,128)}) custom-call(f32[24,40,128]{2,1,0:T(8,128)S(1)} %get-tuple-element.39.raw, f32[24,40,128]{2,1,0:T(8,128)S(1)} %get-tuple-element.40.src, s32[16,32,128]{2,1,0:T(8,128)S(1)} %get-tuple-element.30.labels, f32[8,128]{1,0:T(8,128)S(1)} %add.7.mine, f32[8,128]{1,0:T(8,128)S(1)} %collective-permute-done.13.other), custom_call_target="tpu_custom_call" | custom-call | tf_op jit(solution)/shard_map/pallas_call | solution.py:466
  (5 shorter events, 0.1 us)
Async XLA Ops:
  2.0 7.2 %collective-permute-start = (f32[9,32,128]{2,1,0:T(8,128)S(1)}, f32[9,32,128]{2,1,0:T(8,128)S(1)}, u32[]{:S(2)}, u32[]{:S(2)}) collective-permute-start(f32[9,32,128]{2,1,0:T(8,128)S(1)} %get-tuple-element.23), channel_id=1, source_target_pairs={{8,16},{16,8},{9,17},{17,9},{10,18},{18,10},{11,19},{19,11},{12,20... | collective-permute-start | bytes 442376 | tf_op jit(solution)/shard_map/ppermute | solution.py:382
  2.7 6.6 %collective-permute-start.1 = (f32[9,32,128]{2,1,0:T(8,128)S(1)}, f32[9,32,128]{2,1,0:T(8,128)S(1)}, u32[]{:S(2)}, u32[]{:S(2)}) collective-permute-start(f32[9,32,128]{2,1,0:T(8,128)S(1)} %get-tuple-element.24), channel_id=1, source_target_pairs={{0,8},{8,0},{16,24},{24,16},{1,9},{9,1},{17,25},{25,17},{2,10},{10... | collective-permute-start | bytes 442376 | tf_op jit(solution)/shard_map/ppermute | solution.py:376
  7.1 7.2 %collective-permute-start.2 = (f32[144,128]{1,0:T(8,128)S(1)}, f32[144,128]{1,0:T(8,128)S(1)}, u32[]{:S(2)}, u32[]{:S(2)}) collective-permute-start(f32[144,128]{1,0:T(8,128)S(1)} %get-tuple-element.25), channel_id=1, source_target_pairs={{0,1},{1,0},{2,3},{3,2},{4,5},{5,4},{6,7},{7,6},{8,9},{9,8},{10,11... | collective-permute-start | bytes 221192 | tf_op jit(solution)/shard_map/ppermute | solution.py:376
  8.6 5.7 %collective-permute-start.3 = (f32[144,128]{1,0:T(8,128)S(1)}, f32[144,128]{1,0:T(8,128)S(1)}, u32[]{:S(2)}, u32[]{:S(2)}) collective-permute-start(f32[144,128]{1,0:T(8,128)S(1)} %get-tuple-element.26), channel_id=1, source_target_pairs={{1,2},{3,4},{5,6},{2,1},{4,3},{6,5},{9,10},{11,12},{13,14},{10,9},... | collective-permute-start | bytes 221192 | tf_op jit(solution)/shard_map/ppermute | solution.py:382
  9.3 9.8 %collective-permute-start.4 = (f32[16,128]{1,0:T(8,128)S(1)}, f32[16,128]{1,0:T(8,128)S(1)}, u32[]{:S(2)}, u32[]{:S(2)}) collective-permute-start(f32[16,128]{1,0:T(8,128)S(1)} %get-tuple-element.27), channel_id=1, source_target_pairs={{0,1},{1,0},{2,3},{3,2},{4,5},{5,4},{6,7},{7,6},{8,9},{9,8},{10,11... | collective-permute-start | bytes 24584 | tf_op jit(solution)/shard_map/ppermute | solution.py:376
  13.7 5.5 %collective-permute-start.5 = (f32[16,128]{1,0:T(8,128)S(1)}, f32[16,128]{1,0:T(8,128)S(1)}, u32[]{:S(2)}, u32[]{:S(2)}) collective-permute-start(f32[16,128]{1,0:T(8,128)S(1)} %get-tuple-element.28), channel_id=1, source_target_pairs={{1,2},{3,4},{5,6},{2,1},{4,3},{6,5},{9,10},{11,12},{13,14},{10,9},... | collective-permute-start | bytes 24584 | tf_op jit(solution)/shard_map/ppermute | solution.py:382
  15.0 6.5 %collective-permute-start.6 = (f32[8,128]{1,0:T(8,128)S(1)}, f32[8,128]{1,0:T(8,128)S(1)}, u32[]{:S(2)}, u32[]{:S(2)}) collective-permute-start(f32[8,128]{1,0:T(8,128)S(1)} %shard_map.71.mine), channel_id=1, source_target_pairs={{0,4},{1,5},{2,6},{3,7},{4,0},{5,1},{6,2},{7,3},{8,12},{9,13},{10,... | collective-permute-start | bytes 12296 | tf_op jit(solution)/shard_map/ppermute | solution.py:386
  21.6 5.7 %collective-permute-start.7 = (f32[4,32,128]{2,1,0:T(8,128)S(1)}, f32[4,32,128]{2,1,0:T(8,128)S(1)}, u32[]{:S(2)}, u32[]{:S(2)}) collective-permute-start(f32[4,32,128]{2,1,0:T(8,128)S(1)} %get-tuple-element.34), channel_id=1, source_target_pairs={{8,16},{16,8},{9,17},{17,9},{10,18},{18,10},{11,19},{19,11},{12,20... | collective-permute-start | bytes 196616 | tf_op jit(solution)/shard_map/ppermute | solution.py:382
  22.3 5.0 %collective-permute-start.8 = (f32[4,32,128]{2,1,0:T(8,128)S(1)}, f32[4,32,128]{2,1,0:T(8,128)S(1)}, u32[]{:S(2)}, u32[]{:S(2)}) collective-permute-start(f32[4,32,128]{2,1,0:T(8,128)S(1)} %get-tuple-element.35), channel_id=1, source_target_pairs={{0,8},{8,0},{16,24},{24,16},{1,9},{9,1},{17,25},{25,17},{2,10},{10... | collective-permute-start | bytes 196616 | tf_op jit(solution)/shard_map/ppermute | solution.py:376
  23.7 3.6 %collective-permute-start.9 = (f32[8,128]{1,0:T(8,128)S(1)}, f32[8,128]{1,0:T(8,128)S(1)}, u32[]{:S(2)}, u32[]{:S(2)}) collective-permute-start(f32[8,128]{1,0:T(8,128)S(1)} %get-tuple-element.36.mine), channel_id=1, source_target_pairs={{0,16},{8,24},{16,0},{24,8},{1,17},{9,25},{17,1},{25,9},{2,18},{10... | collective-permute-start | bytes 12296 | tf_op jit(solution)/shard_map/ppermute | solution.py:386
  27.3 4.4 %collective-permute-start.11 = (f32[88,128]{1,0:T(8,128)S(1)}, f32[88,128]{1,0:T(8,128)S(1)}, u32[]{:S(2)}, u32[]{:S(2)}) collective-permute-start(f32[88,128]{1,0:T(8,128)S(1)} %get-tuple-element.38), channel_id=1, source_target_pairs={{0,1},{1,0},{2,3},{3,2},{4,5},{5,4},{6,7},{7,6},{8,9},{9,8},{10,11... | collective-permute-start | bytes 135176 | tf_op jit(solution)/shard_map/ppermute | solution.py:376
  29.7 5.8 %collective-permute-start.10 = (f32[80,128]{1,0:T(8,128)S(1)}, f32[80,128]{1,0:T(8,128)S(1)}, u32[]{:S(2)}, u32[]{:S(2)}) collective-permute-start(f32[80,128]{1,0:T(8,128)S(1)} %get-tuple-element.37), channel_id=1, source_target_pairs={{1,2},{3,4},{5,6},{2,1},{4,3},{6,5},{9,10},{11,12},{13,14},{10,9},... | collective-permute-start | bytes 122888 | tf_op jit(solution)/shard_map/ppermute | solution.py:382
  31.7 3.8 %collective-permute-start.12 = (f32[8,128]{1,0:T(8,128)S(1)}, f32[8,128]{1,0:T(8,128)S(1)}, u32[]{:S(2)}, u32[]{:S(2)}) collective-permute-start(f32[8,128]{1,0:T(8,128)S(1)} %slice_add_fusion), channel_id=1, source_target_pairs={{0,2},{1,3},{2,0},{3,1},{4,6},{5,7},{6,4},{7,5},{8,10},{9,11},{10,... | collective-permute-start | bytes 12296 | tf_op jit(solution)/shard_map/ppermute | solution.py:386
  35.5 1.2 %collective-permute-start.13 = (f32[8,128]{1,0:T(8,128)S(1)}, f32[8,128]{1,0:T(8,128)S(1)}, u32[]{:S(2)}, u32[]{:S(2)}) collective-permute-start(f32[8,128]{1,0:T(8,128)S(1)} %add.7.mine), channel_id=1, source_target_pairs={{0,8},{8,0},{16,24},{24,16},{1,9},{9,1},{17,25},{25,17},{2,10},{10... | collective-permute-start | bytes 12296 | tf_op jit(solution)/shard_map/ppermute | solution.py:386

commit v8 on v7

--- a/solution.py
+++ b/solution.py
@@ -151,7 +151,7 @@
     field[pl.ds(width + size_x, width), tile] = jnp.where(swap, odd, even)
 
 
-def energy_part(x_odd, x_even, y_even, y_odd, density, labels, potential, energy_out, poten):
+def energy_part(x_odd, x_even, y_odd, y_even, density, labels, potential, energy_out, poten):
     size_x, size_y, size_z = density.shape
     starts, planes = plane_starts(WIDTHS)
     planes_loop(0, size_x, 4, lambda x, n: poten.__setitem__((pl.ds(x + 1, n), pl.ds(0, size_y)), potential[pl.ds(x, n)]))
@@ -182,7 +182,7 @@
     planes_loop(0, size_x, 4, step)
 
 
-def adjoint_part(x_odd, x_even, y_even, y_odd, corner_even, corner_odd, density, labels, adjoint_start, adjoint_source, potential,
+def adjoint_part(x_odd, x_even, y_odd, y_even, corner_odd, corner_even, density, labels, adjoint_start, adjoint_source, potential,
                  raw_out,
                  permit, start, source, poten, face_x, face_y, face_z, inverse, first, second):
     size_x, size_y, size_z = density.shape
@@ -428,22 +428,15 @@
     def room(extra):
         return pltpu.VMEM((size_x + extra, wide, size_z), jnp.float32)
 
-    energy = call(energy_part, f32(8, size_z), [room(2)])(x_odd, x_even, y_even, y_odd, own[0], own[1], own[4])
+    energy = call(energy_part, f32(8, size_z), [room(2)])(x_odd, x_even, y_odd, y_even, own[0], own[1], own[4])
     mine, other = doubling(energy, y_bits[1:])
-    raw = call(
-        adjoint_part,
-        f32(*shape),
-        [room(6), room(6), room(4), room(2), room(5), room(4), room(4), room(4), room(4), room(2)],
-        cost=10000000,
-    )(x_odd, x_even, y_even, y_odd, corner_even, corner_odd, *own)
-
     face = f32(FILTER_SWEEPS, size_y, size_z)
     raw = call(
         adjoint_part,
         f32(*shape),
         [room(6), room(6), room(4), room(2), room(5), room(4), room(4), room(4), room(4), room(2)],
         cost=10000000,
-    )(x_odd, x_even, y_even, y_odd, corner_even, corner_odd, *own)
+    )(x_odd, x_even, y_odd, y_even, corner_odd, corner_even, *own)
 
     even, odd, energy = call(pack_raw_x, (face, face, f32(8, size_z)))(raw, mine, other)
     x_even = swap_even(even, "gx")

time: 38.9 us -> 38.8 us (level); the launches traced: 38.2 us -> 38.5 us
  waiting for transfers between devices: 6.22 us -> 8.82 us
  starting transfers between devices: 24 us -> 21.8 us
    ppermute x4, starting transfers between devices: 6.67 us -> 3.01 us  [partner(): lax.ppermute(value, axis, [(i, i ^ bit) for i in range(lax.axis_size(axis...]
    ppermute x4, waiting for transfers between devices: 4.83 us -> 6.38 us  [partner(): lax.ppermute(value, axis, [(i, i ^ bit) for i in range(lax.axis_size(axis...]
    ppermute x5, starting transfers between devices: 14 us -> 15.4 us  [swap_even(): lax.ppermute(value, axis, [(i, i ^ 1) for i in range(lax.axis_size(axis))])]
    ppermute x5, waiting for transfers between devices: 1.38 us -> 2.43 us  [swap_even(): lax.ppermute(value, axis, [(i, i ^ 1) for i in range(lax.axis_size(axis))])]
  transfers between devices with their start and end apart: 14 -> 14, of which waited for: 3 -> 4; matrix products, arithmetic and copies ran while one was open for 0% -> 0% of each run, Pallas kernels for 11% -> 11%
where the time goes in v8:
time: 38.8 us; the launch traced here: 38.5 us
  starting transfers between devices  21.8 us (56%)
  waiting for transfers between devices  8.82 us (23%)
  Pallas kernels  7.16 us (18%)
  between operations  0.74 us (2%)
    ppermute x5, starting transfers between devices, swap_even(): lax.ppermute(value, axis, [(i, i ^ 1) for i in range(lax.axis_size(axis))])  15.4 us
    ppermute x4, waiting for transfers between devices, partner(): lax.ppermute(value, axis, [(i, i ^ bit) for i in range(lax.axis_size(axis...  6.38 us
    ppermute x5, starting transfers between devices, swap_odd(): return lax.ppermute(value, axis, up + [(b, a) for a, b in up])  3.3 us
    ppermute x4, starting transfers between devices, partner(): lax.ppermute(value, axis, [(i, i ^ bit) for i in range(lax.axis_size(axis...  3.01 us
    ppermute x5, waiting for transfers between devices, swap_even(): lax.ppermute(value, axis, [(i, i ^ 1) for i in range(lax.axis_size(axis))])  2.43 us
    pallas_call x1, Pallas kernels, shards(): call(adjoint_part, f32(*shape), [room(6), room(6), room(4), room(2), room...  2.38 us
    pallas_call x1, Pallas kernels, shards(): pl.pallas_call(filter_last, out_shape=(f32(*shape), f32(1, 1)), out_specs...  1.45 us
    pallas_call x1, Pallas kernels, shards(): pl.pallas_call(pack_own, out_shape=(f32(planes, size_y, size_z),) * 2 + (...  1.41 us
  transfers between devices with their start and end apart: 14, of which 4 were waited for; matrix products, arithmetic and copies ran while one was open for 0% of the time, Pallas kernels for 11%

profile of v8, /device:TPU:0, one launch (start us, length us, event | category | flops | bytes accessed | tf_op | source)
XLA Modules:
  0.0 38.5 jit_solution(17458630811428330288)
XLA Ops:
  0.6 1.4 %shard_map.68 = (f32[9,32,128]{2,1,0:T(8,128)S(1)}, f32[9,32,128]{2,1,0:T(8,128)S(1)}, f32[144,128]{1,0:T(8,128)S(1)}, f32[144,128]{1,0:T(8,128)S(1)}, f32[16,32...) custom-call(f32[16,32,128]{2,1,0:T(8,128)} %refs_0_.1, ...), custom_call_target="tpu_custom_call" | custom-call | tf_op jit(solution)/shard_map/pallas_call | solution.py:410
  2.0 0.7 %collective-permute-start = (f32[9,32,128]{2,1,0:T(8,128)S(1)}, f32[9,32,128]{2,1,0:T(8,128)S(1)}, u32[]{:S(2)}, u32[]{:S(2)}) collective-permute-start(f32[9,32,128]{2,1,0:T(8,128)S(1)} %get-tuple-element.23), channel_id=1, source_target_pairs={{8,16},{16,8},{9,17},{17,9},{10,18},{18,10},{11,19},{19,11},{12,20... | collective-permute-start | bytes 442376 | tf_op jit(solution)/shard_map/ppermute | solution.py:382
  2.7 4.4 %collective-permute-start.1 = (f32[9,32,128]{2,1,0:T(8,128)S(1)}, f32[9,32,128]{2,1,0:T(8,128)S(1)}, u32[]{:S(2)}, u32[]{:S(2)}) collective-permute-start(f32[9,32,128]{2,1,0:T(8,128)S(1)} %get-tuple-element.24), channel_id=1, source_target_pairs={{0,8},{8,0},{16,24},{24,16},{1,9},{9,1},{17,25},{25,17},{2,10},{10... | collective-permute-start | bytes 442376 | tf_op jit(solution)/shard_map/ppermute | solution.py:376
  7.1 0.7 %collective-permute-start.2 = (f32[144,128]{1,0:T(8,128)S(1)}, f32[144,128]{1,0:T(8,128)S(1)}, u32[]{:S(2)}, u32[]{:S(2)}) collective-permute-start(f32[144,128]{1,0:T(8,128)S(1)} %get-tuple-element.25), channel_id=1, source_target_pairs={{1,2},{3,4},{5,6},{2,1},{4,3},{6,5},{9,10},{11,12},{13,14},{10,9},... | collective-permute-start | bytes 221192 | tf_op jit(solution)/shard_map/ppermute | solution.py:382
  7.7 4.3 %collective-permute-start.3 = (f32[144,128]{1,0:T(8,128)S(1)}, f32[144,128]{1,0:T(8,128)S(1)}, u32[]{:S(2)}, u32[]{:S(2)}) collective-permute-start(f32[144,128]{1,0:T(8,128)S(1)} %get-tuple-element.26), channel_id=1, source_target_pairs={{0,1},{1,0},{2,3},{3,2},{4,5},{5,4},{6,7},{7,6},{8,9},{9,8},{10,11... | collective-permute-start | bytes 221192 | tf_op jit(solution)/shard_map/ppermute | solution.py:376
  12.1 0.0 collective-permute-done.x_odd
  12.1 0.0 collective-permute-done.1.x_even
  12.1 0.7 %collective-permute-start.4 = (f32[16,128]{1,0:T(8,128)S(1)}, f32[16,128]{1,0:T(8,128)S(1)}, u32[]{:S(2)}, u32[]{:S(2)}) collective-permute-start(f32[16,128]{1,0:T(8,128)S(1)} %get-tuple-element.27), channel_id=1, source_target_pairs={{1,2},{3,4},{5,6},{2,1},{4,3},{6,5},{9,10},{11,12},{13,14},{10,9},... | collective-permute-start | bytes 24584 | tf_op jit(solution)/shard_map/ppermute | solution.py:382
  12.8 4.4 %collective-permute-start.5 = (f32[16,128]{1,0:T(8,128)S(1)}, f32[16,128]{1,0:T(8,128)S(1)}, u32[]{:S(2)}, u32[]{:S(2)}) collective-permute-start(f32[16,128]{1,0:T(8,128)S(1)} %get-tuple-element.28), channel_id=1, source_target_pairs={{0,1},{1,0},{2,3},{3,2},{4,5},{5,4},{6,7},{7,6},{8,9},{9,8},{10,11... | collective-permute-start | bytes 24584 | tf_op jit(solution)/shard_map/ppermute | solution.py:376
  17.1 0.0 collective-permute-done.2.y_odd
  17.2 0.0 collective-permute-done.3.y_even
  17.2 0.7 %shard_map.71.mine = f32[8,128]{1,0:T(8,128)S(1)} custom-call(f32[9,32,128]{2,1,0:T(8,128)S(1)} %collective-permute-done.x_odd, f32[9,32,128]{2,1,0:T(8,128)S(1)} %collective-permute-done.1.x_even, f32[144,128]{1,0:T(8,128)S(1)} %collective-permute-done.2.y_odd, f32[144,128]{1,0:T(8,128)S(1)} %collective-permute-done.3.y_even, ...), custom_call_target="tpu_custom_call" | custom-call | flops 10000 | bytes 10000 | tf_op jit(solution)/shard_map/pallas_call | solution.py:431
  17.8 1.1 %collective-permute-start.6 = (f32[8,128]{1,0:T(8,128)S(1)}, f32[8,128]{1,0:T(8,128)S(1)}, u32[]{:S(2)}, u32[]{:S(2)}) collective-permute-start(f32[8,128]{1,0:T(8,128)S(1)} %shard_map.71.mine), channel_id=1, source_target_pairs={{0,4},{1,5},{2,6},{3,7},{4,0},{5,1},{6,2},{7,3},{8,12},{9,13},{10,... | collective-permute-start | bytes 12296 | tf_op jit(solution)/shard_map/ppermute | solution.py:386
  19.0 0.0 collective-permute-done.4.corner_odd
  19.0 0.0 collective-permute-done.5.corner_even
  19.0 2.4 %shard_map.70.raw.raw_in = f32[16,32,128]{2,1,0:T(8,128)S(1)} custom-call(f32[9,32,128]{2,1,0:T(8,128)S(1)} %collective-permute-done.x_odd, f32[9,32,128]{2,1,0:T(8,128)S(1)} %collective-permute-done.1.x_even, f32[144,128]{1,0:T(8,128)S(1)} %collective-permute-done.2.y_odd, f32[144,128]{1,0:T(8,128)S(1)} %collective-permute-done.3.y_even, ...), custom_call_target="tpu_custom_call" | custom-call | flops 10000000 | bytes 10000000 | tf_op jit(solution)/shard_map/pallas_call | solution.py:434
  21.4 1.0 %collective-permute-done.6.other = f32[8,128]{1,0:T(8,128)S(1)} collective-permute-done((f32[8,128]{1,0:T(8,128)S(1)}, f32[8,128]{1,0:T(8,128)S(1)}, u32[]{:S(2)}, u32[]{:S(2)}) %collective-permute-start.6) | collective-permute-done | bytes 4128 | tf_op jit(solution)/shard_map/ppermute | solution.py:386
  22.4 0.7 %collective-permute-start.7 = (f32[4,32,128]{2,1,0:T(8,128)S(1)}, f32[4,32,128]{2,1,0:T(8,128)S(1)}, u32[]{:S(2)}, u32[]{:S(2)}) collective-permute-start(f32[4,32,128]{2,1,0:T(8,128)S(1)} %get-tuple-element.34), channel_id=1, source_target_pairs={{8,16},{16,8},{9,17},{17,9},{10,18},{18,10},{11,19},{19,11},{12,20... | collective-permute-start | bytes 196616 | tf_op jit(solution)/shard_map/ppermute | solution.py:382
  23.1 1.3 %collective-permute-start.8 = (f32[4,32,128]{2,1,0:T(8,128)S(1)}, f32[4,32,128]{2,1,0:T(8,128)S(1)}, u32[]{:S(2)}, u32[]{:S(2)}) collective-permute-start(f32[4,32,128]{2,1,0:T(8,128)S(1)} %get-tuple-element.35), channel_id=1, source_target_pairs={{0,8},{8,0},{16,24},{24,16},{1,9},{9,1},{17,25},{25,17},{2,10},{10... | collective-permute-start | bytes 196616 | tf_op jit(solution)/shard_map/ppermute | solution.py:376
  24.5 0.3 collective-permute-start.9
  24.7 3.3 %collective-permute-done.9.other = f32[8,128]{1,0:T(8,128)S(1)} collective-permute-done((f32[8,128]{1,0:T(8,128)S(1)}, f32[8,128]{1,0:T(8,128)S(1)}, u32[]{:S(2)}, u32[]{:S(2)}) %collective-permute-start.9) | collective-permute-done | bytes 4128 | tf_op jit(solution)/shard_map/ppermute | solution.py:386
  28.1 0.0 collective-permute-done.7.x_odd
  28.1 0.0 collective-permute-done.8.x_even
  28.1 1.0 %collective-permute-start.11 = (f32[88,128]{1,0:T(8,128)S(1)}, f32[88,128]{1,0:T(8,128)S(1)}, u32[]{:S(2)}, u32[]{:S(2)}) collective-permute-start(f32[88,128]{1,0:T(8,128)S(1)} %get-tuple-element.38), channel_id=1, source_target_pairs={{0,1},{1,0},{2,3},{3,2},{4,5},{5,4},{6,7},{7,6},{8,9},{9,8},{10,11... | collective-permute-start | bytes 135176 | tf_op jit(solution)/shard_map/ppermute | solution.py:376
  29.1 0.7 %collective-permute-start.10 = (f32[80,128]{1,0:T(8,128)S(1)}, f32[80,128]{1,0:T(8,128)S(1)}, u32[]{:S(2)}, u32[]{:S(2)}) collective-permute-start(f32[80,128]{1,0:T(8,128)S(1)} %get-tuple-element.37), channel_id=1, source_target_pairs={{1,2},{3,4},{5,6},{2,1},{4,3},{6,5},{9,10},{11,12},{13,14},{10,9},... | collective-permute-start | bytes 122888 | tf_op jit(solution)/shard_map/ppermute | solution.py:382
  29.8 2.4 %collective-permute-done.11.y_even = f32[88,128]{1,0:T(8,128)S(1)} collective-permute-done((f32[88,128]{1,0:T(8,128)S(1)}, f32[88,128]{1,0:T(8,128)S(1)}, u32[]{:S(2)}, u32[]{:S(2)}) %collective-permute-start.11) | collective-permute-done | bytes 45088 | tf_op jit(solution)/shard_map/ppermute | solution.py:376
  32.2 1.6 %collective-permute-start.12 = (f32[8,128]{1,0:T(8,128)S(1)}, f32[8,128]{1,0:T(8,128)S(1)}, u32[]{:S(2)}, u32[]{:S(2)}) collective-permute-start(f32[8,128]{1,0:T(8,128)S(1)} %slice_add_fusion), channel_id=1, source_target_pairs={{0,2},{1,3},{2,0},{3,1},{4,6},{5,7},{6,4},{7,5},{8,10},{9,11},{10,... | collective-permute-start | bytes 12296 | tf_op jit(solution)/shard_map/ppermute | solution.py:386
  33.8 2.0 %collective-permute-done.12 = f32[8,128]{1,0:T(8,128)S(1)} collective-permute-done((f32[8,128]{1,0:T(8,128)S(1)}, f32[8,128]{1,0:T(8,128)S(1)}, u32[]{:S(2)}, u32[]{:S(2)}) %collective-permute-start.12) | collective-permute-done | bytes 4128 | tf_op jit(solution)/shard_map/ppermute | solution.py:386
  35.8 0.0 collective-permute-start.13
  35.8 0.0 collective-permute-done.10.y_odd
  35.8 1.2 %shard_map.74 = (f32[24,40,128]{2,1,0:T(8,128)S(1)}, f32[24,40,128]{2,1,0:T(8,128)S(1)}) custom-call(f32[4,32,128]{2,1,0:T(8,128)S(1)} %collective-permute-done.7.x_odd, f32[4,32,128]{2,1,0:T(8,128)S(1)} %collective-permute-done.8.x_even, f32[80,128]{1,0:T(8,128)S(1)} %collective-permute-done.10.y_odd, f32[88,128]{1,0:T(8,128)S(1)} %collective-permute-done.11.y_even, ...), custom_call_target="tpu_custom_call" | custom-call | flops 10000000 | bytes 10000000 | tf_op jit(solution)/shard_map/pallas_call | solution.py:453
  37.0 0.0 collective-permute-done.13.other
  37.0 1.5 %shard_map.75 = (f32[16,32,128]{2,1,0:T(8,128)}, f32[1,1]{1,0:T(1,128)}) custom-call(f32[24,40,128]{2,1,0:T(8,128)S(1)} %get-tuple-element.39.raw, f32[24,40,128]{2,1,0:T(8,128)S(1)} %get-tuple-element.40.src, s32[16,32,128]{2,1,0:T(8,128)S(1)} %get-tuple-element.30.labels, f32[8,128]{1,0:T(8,128)S(1)} %add.7.mine, f32[8,128]{1,0:T(8,128)S(1)} %collective-permute-done.13.other), custom_call_target="tpu_custom_call" | custom-call | tf_op jit(solution)/shard_map/pallas_call | solution.py:459
  (5 shorter events, 0.1 us)
Async XLA Ops:
  2.0 10.0 %collective-permute-start = (f32[9,32,128]{2,1,0:T(8,128)S(1)}, f32[9,32,128]{2,1,0:T(8,128)S(1)}, u32[]{:S(2)}, u32[]{:S(2)}) collective-permute-start(f32[9,32,128]{2,1,0:T(8,128)S(1)} %get-tuple-element.23), channel_id=1, source_target_pairs={{8,16},{16,8},{9,17},{17,9},{10,18},{18,10},{11,19},{19,11},{12,20... | collective-permute-start | bytes 442376 | tf_op jit(solution)/shard_map/ppermute | solution.py:382
  2.7 9.4 %collective-permute-start.1 = (f32[9,32,128]{2,1,0:T(8,128)S(1)}, f32[9,32,128]{2,1,0:T(8,128)S(1)}, u32[]{:S(2)}, u32[]{:S(2)}) collective-permute-start(f32[9,32,128]{2,1,0:T(8,128)S(1)} %get-tuple-element.24), channel_id=1, source_target_pairs={{0,8},{8,0},{16,24},{24,16},{1,9},{9,1},{17,25},{25,17},{2,10},{10... | collective-permute-start | bytes 442376 | tf_op jit(solution)/shard_map/ppermute | solution.py:376
  7.1 10.1 %collective-permute-start.2 = (f32[144,128]{1,0:T(8,128)S(1)}, f32[144,128]{1,0:T(8,128)S(1)}, u32[]{:S(2)}, u32[]{:S(2)}) collective-permute-start(f32[144,128]{1,0:T(8,128)S(1)} %get-tuple-element.25), channel_id=1, source_target_pairs={{1,2},{3,4},{5,6},{2,1},{4,3},{6,5},{9,10},{11,12},{13,14},{10,9},... | collective-permute-start | bytes 221192 | tf_op jit(solution)/shard_map/ppermute | solution.py:382
  7.7 9.4 %collective-permute-start.3 = (f32[144,128]{1,0:T(8,128)S(1)}, f32[144,128]{1,0:T(8,128)S(1)}, u32[]{:S(2)}, u32[]{:S(2)}) collective-permute-start(f32[144,128]{1,0:T(8,128)S(1)} %get-tuple-element.26), channel_id=1, source_target_pairs={{0,1},{1,0},{2,3},{3,2},{4,5},{5,4},{6,7},{7,6},{8,9},{9,8},{10,11... | collective-permute-start | bytes 221192 | tf_op jit(solution)/shard_map/ppermute | solution.py:376
  12.1 6.9 %collective-permute-start.4 = (f32[16,128]{1,0:T(8,128)S(1)}, f32[16,128]{1,0:T(8,128)S(1)}, u32[]{:S(2)}, u32[]{:S(2)}) collective-permute-start(f32[16,128]{1,0:T(8,128)S(1)} %get-tuple-element.27), channel_id=1, source_target_pairs={{1,2},{3,4},{5,6},{2,1},{4,3},{6,5},{9,10},{11,12},{13,14},{10,9},... | collective-permute-start | bytes 24584 | tf_op jit(solution)/shard_map/ppermute | solution.py:382
  12.8 6.2 %collective-permute-start.5 = (f32[16,128]{1,0:T(8,128)S(1)}, f32[16,128]{1,0:T(8,128)S(1)}, u32[]{:S(2)}, u32[]{:S(2)}) collective-permute-start(f32[16,128]{1,0:T(8,128)S(1)} %get-tuple-element.28), channel_id=1, source_target_pairs={{0,1},{1,0},{2,3},{3,2},{4,5},{5,4},{6,7},{7,6},{8,9},{9,8},{10,11... | collective-permute-start | bytes 24584 | tf_op jit(solution)/shard_map/ppermute | solution.py:376
  17.8 4.6 %collective-permute-start.6 = (f32[8,128]{1,0:T(8,128)S(1)}, f32[8,128]{1,0:T(8,128)S(1)}, u32[]{:S(2)}, u32[]{:S(2)}) collective-permute-start(f32[8,128]{1,0:T(8,128)S(1)} %shard_map.71.mine), channel_id=1, source_target_pairs={{0,4},{1,5},{2,6},{3,7},{4,0},{5,1},{6,2},{7,3},{8,12},{9,13},{10,... | collective-permute-start | bytes 12296 | tf_op jit(solution)/shard_map/ppermute | solution.py:386
  22.4 5.6 %collective-permute-start.7 = (f32[4,32,128]{2,1,0:T(8,128)S(1)}, f32[4,32,128]{2,1,0:T(8,128)S(1)}, u32[]{:S(2)}, u32[]{:S(2)}) collective-permute-start(f32[4,32,128]{2,1,0:T(8,128)S(1)} %get-tuple-element.34), channel_id=1, source_target_pairs={{8,16},{16,8},{9,17},{17,9},{10,18},{18,10},{11,19},{19,11},{12,20... | collective-permute-start | bytes 196616 | tf_op jit(solution)/shard_map/ppermute | solution.py:382
  23.1 5.0 %collective-permute-start.8 = (f32[4,32,128]{2,1,0:T(8,128)S(1)}, f32[4,32,128]{2,1,0:T(8,128)S(1)}, u32[]{:S(2)}, u32[]{:S(2)}) collective-permute-start(f32[4,32,128]{2,1,0:T(8,128)S(1)} %get-tuple-element.35), channel_id=1, source_target_pairs={{0,8},{8,0},{16,24},{24,16},{1,9},{9,1},{17,25},{25,17},{2,10},{10... | collective-permute-start | bytes 196616 | tf_op jit(solution)/shard_map/ppermute | solution.py:376
  24.5 3.6 %collective-permute-start.9 = (f32[8,128]{1,0:T(8,128)S(1)}, f32[8,128]{1,0:T(8,128)S(1)}, u32[]{:S(2)}, u32[]{:S(2)}) collective-permute-start(f32[8,128]{1,0:T(8,128)S(1)} %get-tuple-element.36.mine), channel_id=1, source_target_pairs={{0,16},{8,24},{16,0},{24,8},{1,17},{9,25},{17,1},{25,9},{2,18},{10... | collective-permute-start | bytes 12296 | tf_op jit(solution)/shard_map/ppermute | solution.py:386
  28.1 4.1 %collective-permute-start.11 = (f32[88,128]{1,0:T(8,128)S(1)}, f32[88,128]{1,0:T(8,128)S(1)}, u32[]{:S(2)}, u32[]{:S(2)}) collective-permute-start(f32[88,128]{1,0:T(8,128)S(1)} %get-tuple-element.38), channel_id=1, source_target_pairs={{0,1},{1,0},{2,3},{3,2},{4,5},{5,4},{6,7},{7,6},{8,9},{9,8},{10,11... | collective-permute-start | bytes 135176 | tf_op jit(solution)/shard_map/ppermute | solution.py:376
  29.1 6.7 %collective-permute-start.10 = (f32[80,128]{1,0:T(8,128)S(1)}, f32[80,128]{1,0:T(8,128)S(1)}, u32[]{:S(2)}, u32[]{:S(2)}) collective-permute-start(f32[80,128]{1,0:T(8,128)S(1)} %get-tuple-element.37), channel_id=1, source_target_pairs={{1,2},{3,4},{5,6},{2,1},{4,3},{6,5},{9,10},{11,12},{13,14},{10,9},... | collective-permute-start | bytes 122888 | tf_op jit(solution)/shard_map/ppermute | solution.py:382
  32.2 3.6 %collective-permute-start.12 = (f32[8,128]{1,0:T(8,128)S(1)}, f32[8,128]{1,0:T(8,128)S(1)}, u32[]{:S(2)}, u32[]{:S(2)}) collective-permute-start(f32[8,128]{1,0:T(8,128)S(1)} %slice_add_fusion), channel_id=1, source_target_pairs={{0,2},{1,3},{2,0},{3,1},{4,6},{5,7},{6,4},{7,5},{8,10},{9,11},{10,... | collective-permute-start | bytes 12296 | tf_op jit(solution)/shard_map/ppermute | solution.py:386
  35.8 1.2 %collective-permute-start.13 = (f32[8,128]{1,0:T(8,128)S(1)}, f32[8,128]{1,0:T(8,128)S(1)}, u32[]{:S(2)}, u32[]{:S(2)}) collective-permute-start(f32[8,128]{1,0:T(8,128)S(1)} %add.7.mine), channel_id=1, source_target_pairs={{0,8},{8,0},{16,24},{24,16},{1,9},{9,1},{17,25},{25,17},{2,10},{10... | collective-permute-start | bytes 12296 | tf_op jit(solution)/shard_map/ppermute | solution.py:386

commit v9 on v8

--- a/solution.py
+++ b/solution.py
@@ -263,22 +263,18 @@
     planes_loop(0, size_x, 8, finish)
 
 
-def pack_raw_x(raw, mine, other, even_out, odd_out, energy_out):
+def pack_raw_x(raw, even_out, odd_out):
     size_x = raw.shape[0]
-    energy_out[...] = mine[...] + other[...]
     low_first = odd_place("gx")
     for out, low in ((even_out, low_first), (odd_out, jnp.logical_not(low_first))):
         out[...] = raw[pl.ds(jnp.where(low, 0, size_x - FILTER_SWEEPS), FILTER_SWEEPS)]
 
 
-def pack_raw_y(x_odd, x_even, raw, mine, other, even_out, odd_out, energy_out):
+def pack_raw_y(x_odd, x_even, raw, even_out, odd_out):
     size_x, size_y, _ = raw.shape
     width = FILTER_SWEEPS
-    found, total = segments((width,), size_x)
+    found, _ = segments((width,), size_x)
     x_swap, y_swap = odd_place("gx"), odd_place("gy")
-    energy = mine[...] + other[...]
-    energy_out[...] = energy
-    even_out[total:total + 8] = energy
     for _, x, rows, at in found:
         faces = []
         for rim in (slice(0, rows), slice(size_y - rows, size_y)):
@@ -353,11 +349,11 @@
         src = dst
 
 
-def filter_last(raw, src, labels, mine, other, out, mean_out, held, sem):
+def filter_last(raw, src, labels, energies, out, mean_out, held, sem):
     size_x, size_y, size_z = labels.shape
     relax = relaxation(raw, size_x, size_y, size_z)
     voxels = lax.axis_size("gx") * size_x * lax.axis_size("gy") * size_y * size_z
-    mean = 0.5 * jnp.sum(mine[...] + other[...]) / voxels + epsilon_mean
+    mean = 0.5 * jnp.sum(jnp.sum(energies[...], axis=0)) / voxels + epsilon_mean
     mean_out[0, 0] = mean
     inverse = 1.0 / jnp.full((1, 1, size_z), mean, jnp.float32)
     block = size_x // 2
@@ -382,18 +378,6 @@
     return lax.ppermute(value, axis, up + [(b, a) for a, b in up])
 
 
-def partner(value, axis, bit):
-    return lax.ppermute(value, axis, [(i, i ^ bit) for i in range(lax.axis_size(axis))])
-
-
-def doubling(energy, stages):
-    other = partner(energy, *stages[0])
-    for stage in stages[1:]:
-        energy = energy + other
-        other = partner(energy, *stage)
-    return energy, other
-
-
 def shards(density, potential, adjoint_start, adjoint_source, labels):
     size_x, size_y, size_z = potential.shape
     _, planes = plane_starts(WIDTHS)
@@ -403,8 +387,6 @@
         pltpu.with_memory_space_constraint(array, pltpu.HBM)
         for array in (density, labels, adjoint_start, adjoint_source, potential)
     ]
-    x_bits = [("gx", 1 << k) for k in range(1, (lax.axis_size("gx") - 1).bit_length())]
-    y_bits = [("gy", 1 << k) for k in range(1, (lax.axis_size("gy") - 1).bit_length())]
 
     shape = (size_x, size_y, size_z)
     odd, even, tile_even, tile_odd, *own = pl.pallas_call(
@@ -429,7 +411,9 @@
         return pltpu.VMEM((size_x + extra, wide, size_z), jnp.float32)
 
     energy = call(energy_part, f32(8, size_z), [room(2)])(x_odd, x_even, y_odd, y_even, own[0], own[1], own[4])
-    mine, other = doubling(energy, y_bits[1:])
+    devices = lax.axis_size("gx") * lax.axis_size("gy")
+    spread = jnp.broadcast_to(energy[None], (devices, 8, size_z))
+    energies = lax.all_to_all(spread, ("gx", "gy"), 0, 0)
     face = f32(FILTER_SWEEPS, size_y, size_z)
     raw = call(
         adjoint_part,
@@ -438,17 +422,13 @@
         cost=10000000,
     )(x_odd, x_even, y_odd, y_even, corner_odd, corner_even, *own)
 
-    even, odd, energy = call(pack_raw_x, (face, face, f32(8, size_z)))(raw, mine, other)
+    even, odd = call(pack_raw_x, (face, face))(raw)
     x_even = swap_even(even, "gx")
     x_odd = swap_odd(odd, "gx")
-    mine, other = doubling(energy, x_bits)
     _, rows = segments((FILTER_SWEEPS,), size_x)
-    even, odd, energy = call(pack_raw_y, (f32(rows + 8, size_z), f32(rows, size_z), f32(8, size_z)))(
-        x_odd, x_even, raw, mine, other)
+    even, odd = call(pack_raw_y, (f32(rows, size_z), f32(rows, size_z)))(x_odd, x_even, raw)
     y_even = swap_even(even, "gy")
     y_odd = swap_odd(odd, "gy")
-    energy = energy + y_even[rows:rows + 8]
-    mine, other = doubling(energy, y_bits[:1] + [("gx", 1)])
     padded = f32(size_x + 2 * FILTER_SWEEPS, wide, size_z)
     raw, filtered = call(
         filter_first,
@@ -462,7 +442,7 @@
         out_specs=(pl.BlockSpec(memory_space=pl.ANY), pl.BlockSpec(memory_space=pltpu.SMEM)),
         scratch_shapes=[pltpu.VMEM(shape, jnp.float32), pltpu.SemaphoreType.DMA((2,))],
         compiler_params=pltpu.CompilerParams(vmem_limit_bytes=VMEM_LIMIT),
-    )(raw, filtered, own[1], mine, other)
+    )(raw, filtered, own[1], energies)
     return (sensitivity, mean_energy[0, 0])
 
 

time: 38.8 us -> 45.6 us (1.18)
  starting transfers between devices: 21.8 us -> 29.2 us
  waiting for transfers between devices: 8.82 us -> 7.55 us
  local copies, waits for them, and re-layouts: 0 us -> 0.66 us
    ppermute x4 -> x0, waiting for transfers between devices: 6.38 us -> none  [partner(): lax.ppermute(value, axis, [(i, i ^ bit) for i in range(lax.axis_size(axis...]
    ppermute x5, starting transfers between devices: 15.4 us -> 20.9 us  [swap_even(): lax.ppermute(value, axis, [(i, i ^ 1) for i in range(lax.axis_size(axis))])]
    ppermute x5, waiting for transfers between devices: 2.43 us -> 7.54 us  [swap_even(): lax.ppermute(value, axis, [(i, i ^ 1) for i in range(lax.axis_size(axis))])]
    all_to_all x0 -> x1, starting transfers between devices: none -> 4.93 us  [shards(): energies = lax.all_to_all(spread, ('gx', 'gy'), 0, 0)]
    ppermute x4 -> x0, starting transfers between devices: 3.01 us -> none  [partner(): lax.ppermute(value, axis, [(i, i ^ bit) for i in range(lax.axis_size(axis...]
    broadcast_in_dim x0 -> x1, local copies, waits for them, and re-layouts: none -> 0.66 us  [shards(): spread = jnp.broadcast_to(energy[None], (devices, 8, size_z))]
  transfers between devices with their start and end apart: 14 -> 11, of which waited for: 4 -> 4; matrix products, arithmetic and copies ran while one was open for 0% -> 0% of each run, Pallas kernels for 11% -> 8%
where the time goes in v9:
time: 45.6 us; the launch traced here: 45.3 us
  starting transfers between devices  29.2 us (64%)
  waiting for transfers between devices  7.55 us (17%)
  Pallas kernels  7.17 us (16%)
  between operations  0.74 us (2%)
  local copies, waits for them, and re-layouts  0.66 us (1%)
    ppermute x5, starting transfers between devices, swap_even(): lax.ppermute(value, axis, [(i, i ^ 1) for i in range(lax.axis_size(axis))])  20.9 us
    ppermute x5, waiting for transfers between devices, swap_even(): lax.ppermute(value, axis, [(i, i ^ 1) for i in range(lax.axis_size(axis))])  7.54 us
    all_to_all x1, starting transfers between devices, shards(): energies = lax.all_to_all(spread, ('gx', 'gy'), 0, 0)  4.93 us
    ppermute x5, starting transfers between devices, swap_odd(): return lax.ppermute(value, axis, up + [(b, a) for a, b in up])  3.31 us
    pallas_call x1, Pallas kernels, shards(): call(adjoint_part, f32(*shape), [room(6), room(6), room(4), room(2), room...  2.38 us
    pallas_call x1, Pallas kernels, shards(): pl.pallas_call(filter_last, out_shape=(f32(*shape), f32(1, 1)), out_specs...  1.45 us
    pallas_call x1, Pallas kernels, shards(): pl.pallas_call(pack_own, out_shape=(f32(planes, size_y, size_z),) * 2 + (...  1.41 us
    pallas_call x1, Pallas kernels, shards(): call(filter_first, (padded, padded), [pltpu.VMEM(padded.shape, jnp.float3...  1.17 us
  transfers between devices with their start and end apart: 11, of which 4 were waited for; matrix products, arithmetic and copies ran while one was open for 0% of the time, Pallas kernels for 8%

profile of v9, /device:TPU:0, one launch (start us, length us, event | category | flops | bytes accessed | tf_op | source)
XLA Modules:
  0.0 45.3 jit_solution(880307376741248684)
XLA Ops:
  0.6 1.4 %shard_map.68 = (f32[9,32,128]{2,1,0:T(8,128)S(1)}, f32[9,32,128]{2,1,0:T(8,128)S(1)}, f32[144,128]{1,0:T(8,128)S(1)}, f32[144,128]{1,0:T(8,128)S(1)}, f32[16,32...) custom-call(f32[16,32,128]{2,1,0:T(8,128)} %refs_0_.1, ...), custom_call_target="tpu_custom_call" | custom-call | tf_op jit(solution)/shard_map/pallas_call | solution.py:392
  2.0 0.7 %collective-permute-start = (f32[9,32,128]{2,1,0:T(8,128)S(1)}, f32[9,32,128]{2,1,0:T(8,128)S(1)}, u32[]{:S(2)}, u32[]{:S(2)}) collective-permute-start(f32[9,32,128]{2,1,0:T(8,128)S(1)} %get-tuple-element.21), channel_id=1, source_target_pairs={{8,16},{16,8},{9,17},{17,9},{10,18},{18,10},{11,19},{19,11},{12,20... | collective-permute-start | bytes 442376 | tf_op jit(solution)/shard_map/ppermute | solution.py:378
  2.7 4.4 %collective-permute-start.1 = (f32[9,32,128]{2,1,0:T(8,128)S(1)}, f32[9,32,128]{2,1,0:T(8,128)S(1)}, u32[]{:S(2)}, u32[]{:S(2)}) collective-permute-start(f32[9,32,128]{2,1,0:T(8,128)S(1)} %get-tuple-element.22), channel_id=1, source_target_pairs={{0,8},{8,0},{16,24},{24,16},{1,9},{9,1},{17,25},{25,17},{2,10},{10... | collective-permute-start | bytes 442376 | tf_op jit(solution)/shard_map/ppermute | solution.py:372
  7.1 0.7 %collective-permute-start.2 = (f32[144,128]{1,0:T(8,128)S(1)}, f32[144,128]{1,0:T(8,128)S(1)}, u32[]{:S(2)}, u32[]{:S(2)}) collective-permute-start(f32[144,128]{1,0:T(8,128)S(1)} %get-tuple-element.23), channel_id=1, source_target_pairs={{1,2},{3,4},{5,6},{2,1},{4,3},{6,5},{9,10},{11,12},{13,14},{10,9},... | collective-permute-start | bytes 221192 | tf_op jit(solution)/shard_map/ppermute | solution.py:378
  7.7 4.3 %collective-permute-start.3 = (f32[144,128]{1,0:T(8,128)S(1)}, f32[144,128]{1,0:T(8,128)S(1)}, u32[]{:S(2)}, u32[]{:S(2)}) collective-permute-start(f32[144,128]{1,0:T(8,128)S(1)} %get-tuple-element.24), channel_id=1, source_target_pairs={{0,1},{1,0},{2,3},{3,2},{4,5},{5,4},{6,7},{7,6},{8,9},{9,8},{10,11... | collective-permute-start | bytes 221192 | tf_op jit(solution)/shard_map/ppermute | solution.py:372
  12.1 0.0 collective-permute-done.2.y_odd
  12.1 2.6 %collective-permute-done.3.y_even = f32[144,128]{1,0:T(8,128)S(1)} collective-permute-done((f32[144,128]{1,0:T(8,128)S(1)}, f32[144,128]{1,0:T(8,128)S(1)}, u32[]{:S(2)}, u32[]{:S(2)}) %collective-permute-start.3) | collective-permute-done | bytes 73760 | tf_op jit(solution)/shard_map/ppermute | solution.py:372
  14.7 0.0 collective-permute-done.x_odd
  14.7 0.0 collective-permute-done.1.x_even
  14.7 0.7 %shard_map.74 = f32[8,128]{1,0:T(8,128)S(1)} custom-call(f32[9,32,128]{2,1,0:T(8,128)S(1)} %collective-permute-done.x_odd, f32[9,32,128]{2,1,0:T(8,128)S(1)} %collective-permute-done.1.x_even, f32[144,128]{1,0:T(8,128)S(1)} %collective-permute-done.2.y_odd, f32[144,128]{1,0:T(8,128)S(1)} %collective-permute-done.3.y_even, ...), custom_call_target="tpu_custom_call" | custom-call | flops 10000 | bytes 10000 | tf_op jit(solution)/shard_map/pallas_call | solution.py:413
  15.4 0.7 %broadcast_in_dim.2 = f32[32,8,128]{2,1,0:T(8,128)} broadcast(f32[8,128]{1,0:T(8,128)S(1)} %shard_map.74), dimensions={1,2} | broadcast | bytes 135168 | tf_op jit(solution)/shard_map/broadcast_in_dim | solution.py:415
  16.0 4.9 %all-to-all-start = ((f32[32,8,128]{2,1,0:T(8,128)}), f32[32,8,128]{2,1,0:T(8,128)S(1)}, u32[]{:S(2)}, u32[]{:S(2)}) async-start(f32[32,8,128]{2,1,0:T(8,128)} %broadcast_in_dim.2), calls=%async_computation | async-start | bytes 262144 | tf_op jit(solution)/shard_map/all_to_all | solution.py:416
  21.0 0.7 %collective-permute-start.4 = (f32[16,128]{1,0:T(8,128)S(1)}, f32[16,128]{1,0:T(8,128)S(1)}, u32[]{:S(2)}, u32[]{:S(2)}) collective-permute-start(f32[16,128]{1,0:T(8,128)S(1)} %get-tuple-element.25), channel_id=1, source_target_pairs={{1,2},{3,4},{5,6},{2,1},{4,3},{6,5},{9,10},{11,12},{13,14},{10,9},... | collective-permute-start | bytes 24584 | tf_op jit(solution)/shard_map/ppermute | solution.py:378
  21.7 4.5 %collective-permute-start.5 = (f32[16,128]{1,0:T(8,128)S(1)}, f32[16,128]{1,0:T(8,128)S(1)}, u32[]{:S(2)}, u32[]{:S(2)}) collective-permute-start(f32[16,128]{1,0:T(8,128)S(1)} %get-tuple-element.26), channel_id=1, source_target_pairs={{0,1},{1,0},{2,3},{3,2},{4,5},{5,4},{6,7},{7,6},{8,9},{9,8},{10,11... | collective-permute-start | bytes 24584 | tf_op jit(solution)/shard_map/ppermute | solution.py:372
  26.2 0.0 collective-permute-done.4.corner_odd
  26.2 1.6 %collective-permute-done.5.corner_even = f32[16,128]{1,0:T(8,128)S(1)} collective-permute-done((f32[16,128]{1,0:T(8,128)S(1)}, f32[16,128]{1,0:T(8,128)S(1)}, u32[]{:S(2)}, u32[]{:S(2)}) %collective-permute-start.5) | collective-permute-done | bytes 8224 | tf_op jit(solution)/shard_map/ppermute | solution.py:372
  27.9 2.4 %shard_map.70.raw.raw_in = f32[16,32,128]{2,1,0:T(8,128)S(1)} custom-call(f32[9,32,128]{2,1,0:T(8,128)S(1)} %collective-permute-done.x_odd, f32[9,32,128]{2,1,0:T(8,128)S(1)} %collective-permute-done.1.x_even, f32[144,128]{1,0:T(8,128)S(1)} %collective-permute-done.2.y_odd, f32[144,128]{1,0:T(8,128)S(1)} %collective-permute-done.3.y_even, ...), custom_call_target="tpu_custom_call" | custom-call | flops 10000000 | bytes 10000000 | tf_op jit(solution)/shard_map/pallas_call | solution.py:418
  30.3 0.7 %collective-permute-start.6 = (f32[4,32,128]{2,1,0:T(8,128)S(1)}, f32[4,32,128]{2,1,0:T(8,128)S(1)}, u32[]{:S(2)}, u32[]{:S(2)}) collective-permute-start(f32[4,32,128]{2,1,0:T(8,128)S(1)} %get-tuple-element.32), channel_id=1, source_target_pairs={{8,16},{16,8},{9,17},{17,9},{10,18},{18,10},{11,19},{19,11},{12,20... | collective-permute-start | bytes 196616 | tf_op jit(solution)/shard_map/ppermute | solution.py:378
  31.0 2.9 %collective-permute-start.7 = (f32[4,32,128]{2,1,0:T(8,128)S(1)}, f32[4,32,128]{2,1,0:T(8,128)S(1)}, u32[]{:S(2)}, u32[]{:S(2)}) collective-permute-start(f32[4,32,128]{2,1,0:T(8,128)S(1)} %get-tuple-element.33), channel_id=1, source_target_pairs={{0,8},{8,0},{16,24},{24,16},{1,9},{9,1},{17,25},{25,17},{2,10},{10... | collective-permute-start | bytes 196616 | tf_op jit(solution)/shard_map/ppermute | solution.py:372
  33.9 0.0 collective-permute-done.6.x_odd
  33.9 0.9 %collective-permute-done.7.x_even = f32[4,32,128]{2,1,0:T(8,128)S(1)} collective-permute-done((f32[4,32,128]{2,1,0:T(8,128)S(1)}, f32[4,32,128]{2,1,0:T(8,128)S(1)}, u32[]{:S(2)}, u32[]{:S(2)}) %collective-permute-start.7) | collective-permute-done | bytes 65568 | tf_op jit(solution)/shard_map/ppermute | solution.py:372
  34.8 0.7 %collective-permute-start.8 = (f32[80,128]{1,0:T(8,128)S(1)}, f32[80,128]{1,0:T(8,128)S(1)}, u32[]{:S(2)}, u32[]{:S(2)}) collective-permute-start(f32[80,128]{1,0:T(8,128)S(1)} %get-tuple-element.34), channel_id=1, source_target_pairs={{1,2},{3,4},{5,6},{2,1},{4,3},{6,5},{9,10},{11,12},{13,14},{10,9},... | collective-permute-start | bytes 122888 | tf_op jit(solution)/shard_map/ppermute | solution.py:378
  35.5 4.7 %collective-permute-start.9 = (f32[80,128]{1,0:T(8,128)S(1)}, f32[80,128]{1,0:T(8,128)S(1)}, u32[]{:S(2)}, u32[]{:S(2)}) collective-permute-start(f32[80,128]{1,0:T(8,128)S(1)} %get-tuple-element.35), channel_id=1, source_target_pairs={{0,1},{1,0},{2,3},{3,2},{4,5},{5,4},{6,7},{7,6},{8,9},{9,8},{10,11... | collective-permute-start | bytes 122888 | tf_op jit(solution)/shard_map/ppermute | solution.py:372
  40.2 0.0 collective-permute-done.8.y_odd
  40.2 2.4 %collective-permute-done.9.y_even = f32[80,128]{1,0:T(8,128)S(1)} collective-permute-done((f32[80,128]{1,0:T(8,128)S(1)}, f32[80,128]{1,0:T(8,128)S(1)}, u32[]{:S(2)}, u32[]{:S(2)}) %collective-permute-start.9) | collective-permute-done | bytes 40992 | tf_op jit(solution)/shard_map/ppermute | solution.py:372
  42.7 1.2 %shard_map.73 = (f32[24,40,128]{2,1,0:T(8,128)S(1)}, f32[24,40,128]{2,1,0:T(8,128)S(1)}) custom-call(f32[4,32,128]{2,1,0:T(8,128)S(1)} %collective-permute-done.6.x_odd, f32[4,32,128]{2,1,0:T(8,128)S(1)} %collective-permute-done.7.x_even, f32[80,128]{1,0:T(8,128)S(1)} %collective-permute-done.8.y_odd, f32[80,128]{1,0:T(8,128)S(1)} %collective-permute-done.9.y_even, ...), custom_call_target="tpu_custom_call" | custom-call | flops 10000000 | bytes 10000000 | tf_op jit(solution)/shard_map/pallas_call | solution.py:433
  43.8 0.0 all-to-all-done.energies
  43.8 1.5 %shard_map.75 = (f32[16,32,128]{2,1,0:T(8,128)}, f32[1,1]{1,0:T(1,128)}) custom-call(f32[24,40,128]{2,1,0:T(8,128)S(1)} %get-tuple-element.36.raw, f32[24,40,128]{2,1,0:T(8,128)S(1)} %get-tuple-element.37.src, s32[16,32,128]{2,1,0:T(8,128)S(1)} %get-tuple-element.28.labels, f32[32,8,128]{2,1,0:T(8,128)S(1)} %all-to-all-done.energies), custom_call_target="tpu_custom_call" | custom-call | tf_op jit(solution)/shard_map/pallas_call | solution.py:439
  (3 shorter events, 0.1 us)
Async XLA Ops:
  2.0 12.6 %collective-permute-start = (f32[9,32,128]{2,1,0:T(8,128)S(1)}, f32[9,32,128]{2,1,0:T(8,128)S(1)}, u32[]{:S(2)}, u32[]{:S(2)}) collective-permute-start(f32[9,32,128]{2,1,0:T(8,128)S(1)} %get-tuple-element.21), channel_id=1, source_target_pairs={{8,16},{16,8},{9,17},{17,9},{10,18},{18,10},{11,19},{19,11},{12,20... | collective-permute-start | bytes 442376 | tf_op jit(solution)/shard_map/ppermute | solution.py:378
  2.7 12.0 %collective-permute-start.1 = (f32[9,32,128]{2,1,0:T(8,128)S(1)}, f32[9,32,128]{2,1,0:T(8,128)S(1)}, u32[]{:S(2)}, u32[]{:S(2)}) collective-permute-start(f32[9,32,128]{2,1,0:T(8,128)S(1)} %get-tuple-element.22), channel_id=1, source_target_pairs={{0,8},{8,0},{16,24},{24,16},{1,9},{9,1},{17,25},{25,17},{2,10},{10... | collective-permute-start | bytes 442376 | tf_op jit(solution)/shard_map/ppermute | solution.py:372
  7.1 5.0 %collective-permute-start.2 = (f32[144,128]{1,0:T(8,128)S(1)}, f32[144,128]{1,0:T(8,128)S(1)}, u32[]{:S(2)}, u32[]{:S(2)}) collective-permute-start(f32[144,128]{1,0:T(8,128)S(1)} %get-tuple-element.23), channel_id=1, source_target_pairs={{1,2},{3,4},{5,6},{2,1},{4,3},{6,5},{9,10},{11,12},{13,14},{10,9},... | collective-permute-start | bytes 221192 | tf_op jit(solution)/shard_map/ppermute | solution.py:378
  7.7 6.9 %collective-permute-start.3 = (f32[144,128]{1,0:T(8,128)S(1)}, f32[144,128]{1,0:T(8,128)S(1)}, u32[]{:S(2)}, u32[]{:S(2)}) collective-permute-start(f32[144,128]{1,0:T(8,128)S(1)} %get-tuple-element.24), channel_id=1, source_target_pairs={{0,1},{1,0},{2,3},{3,2},{4,5},{5,4},{6,7},{7,6},{8,9},{9,8},{10,11... | collective-permute-start | bytes 221192 | tf_op jit(solution)/shard_map/ppermute | solution.py:372
  16.0 27.8 %all-to-all-start = ((f32[32,8,128]{2,1,0:T(8,128)}), f32[32,8,128]{2,1,0:T(8,128)S(1)}, u32[]{:S(2)}, u32[]{:S(2)}) async-start(f32[32,8,128]{2,1,0:T(8,128)} %broadcast_in_dim.2), calls=%async_computation | async-start | bytes 262144 | tf_op jit(solution)/shard_map/all_to_all | solution.py:416
  21.0 5.2 %collective-permute-start.4 = (f32[16,128]{1,0:T(8,128)S(1)}, f32[16,128]{1,0:T(8,128)S(1)}, u32[]{:S(2)}, u32[]{:S(2)}) collective-permute-start(f32[16,128]{1,0:T(8,128)S(1)} %get-tuple-element.25), channel_id=1, source_target_pairs={{1,2},{3,4},{5,6},{2,1},{4,3},{6,5},{9,10},{11,12},{13,14},{10,9},... | collective-permute-start | bytes 24584 | tf_op jit(solution)/shard_map/ppermute | solution.py:378
  21.7 6.2 %collective-permute-start.5 = (f32[16,128]{1,0:T(8,128)S(1)}, f32[16,128]{1,0:T(8,128)S(1)}, u32[]{:S(2)}, u32[]{:S(2)}) collective-permute-start(f32[16,128]{1,0:T(8,128)S(1)} %get-tuple-element.26), channel_id=1, source_target_pairs={{0,1},{1,0},{2,3},{3,2},{4,5},{5,4},{6,7},{7,6},{8,9},{9,8},{10,11... | collective-permute-start | bytes 24584 | tf_op jit(solution)/shard_map/ppermute | solution.py:372
  30.3 3.6 %collective-permute-start.6 = (f32[4,32,128]{2,1,0:T(8,128)S(1)}, f32[4,32,128]{2,1,0:T(8,128)S(1)}, u32[]{:S(2)}, u32[]{:S(2)}) collective-permute-start(f32[4,32,128]{2,1,0:T(8,128)S(1)} %get-tuple-element.32), channel_id=1, source_target_pairs={{8,16},{16,8},{9,17},{17,9},{10,18},{18,10},{11,19},{19,11},{12,20... | collective-permute-start | bytes 196616 | tf_op jit(solution)/shard_map/ppermute | solution.py:378
  31.0 3.8 %collective-permute-start.7 = (f32[4,32,128]{2,1,0:T(8,128)S(1)}, f32[4,32,128]{2,1,0:T(8,128)S(1)}, u32[]{:S(2)}, u32[]{:S(2)}) collective-permute-start(f32[4,32,128]{2,1,0:T(8,128)S(1)} %get-tuple-element.33), channel_id=1, source_target_pairs={{0,8},{8,0},{16,24},{24,16},{1,9},{9,1},{17,25},{25,17},{2,10},{10... | collective-permute-start | bytes 196616 | tf_op jit(solution)/shard_map/ppermute | solution.py:372
  34.8 5.4 %collective-permute-start.8 = (f32[80,128]{1,0:T(8,128)S(1)}, f32[80,128]{1,0:T(8,128)S(1)}, u32[]{:S(2)}, u32[]{:S(2)}) collective-permute-start(f32[80,128]{1,0:T(8,128)S(1)} %get-tuple-element.34), channel_id=1, source_target_pairs={{1,2},{3,4},{5,6},{2,1},{4,3},{6,5},{9,10},{11,12},{13,14},{10,9},... | collective-permute-start | bytes 122888 | tf_op jit(solution)/shard_map/ppermute | solution.py:378
  35.5 7.1 %collective-permute-start.9 = (f32[80,128]{1,0:T(8,128)S(1)}, f32[80,128]{1,0:T(8,128)S(1)}, u32[]{:S(2)}, u32[]{:S(2)}) collective-permute-start(f32[80,128]{1,0:T(8,128)S(1)} %get-tuple-element.35), channel_id=1, source_target_pairs={{0,1},{1,0},{2,3},{3,2},{4,5},{5,4},{6,7},{7,6},{8,9},{9,8},{10,11... | collective-permute-start | bytes 122888 | tf_op jit(solution)/shard_map/ppermute | solution.py:372

commit v10 on v8

--- a/solution.py
+++ b/solution.py
@@ -75,28 +75,28 @@
     copies = [pltpu.make_async_copy(a, b, sem.at[k]) for k, (a, b) in enumerate(zip(inputs, held))]
     for copy in copies:
         copy.start()
-    for copy in copies:
-        copy.wait()
-    low_first = odd_place("gx")
-    for out, low in ((x_even_out, low_first), (x_odd_out, jnp.logical_not(low_first))):
-        for field, width in enumerate(WIDTHS):
+    copies[0].wait()
+    low_first, y_swap = odd_place("gx"), odd_place("gy")
+    found, _ = segments(WIDTHS, size_x, beyond=False)
+    for field, width in enumerate(WIDTHS):
+        copies[field + 1].wait()
+        for out, low in ((x_even_out, low_first), (x_odd_out, jnp.logical_not(low_first))):
             span = pl.ds(jnp.where(low, 0, size_x - width), width)
             if field == 0:
                 face = material(density[span], labels[span])
             else:
                 face = (adjoint, source, potential)[field - 1][span]
             out[pl.ds(starts[field], width)] = face
-    y_swap = odd_place("gy")
-    for field, x, rows, at in segments(WIDTHS, size_x, beyond=False)[0]:
-        faces = []
-        for rim in (slice(0, rows), slice(size_y - rows, size_y)):
-            if field == 0:
-                faces.append(material(density[x, rim], labels[x, rim]))
-            else:
-                faces.append((adjoint, source, potential)[field - 1][x, rim])
-        low, high = faces
-        y_even_out[at:at + rows] = jnp.where(y_swap, low, high)
-        y_odd_out[at:at + rows] = jnp.where(y_swap, high, low)
+        for _, x, rows, at in (part for part in found if part[0] == field):
+            faces = []
+            for rim in (slice(0, rows), slice(size_y - rows, size_y)):
+                if field == 0:
+                    faces.append(material(density[x, rim], labels[x, rim]))
+                else:
+                    faces.append((adjoint, source, potential)[field - 1][x, rim])
+            low, high = faces
+            y_even_out[at:at + rows] = jnp.where(y_swap, low, high)
+            y_odd_out[at:at + rows] = jnp.where(y_swap, high, low)
 
 
 def pack_corners(size_x, x_odd, x_even, even_out, odd_out):
@@ -263,12 +263,17 @@
     planes_loop(0, size_x, 8, finish)
 
 
-def pack_raw_x(raw, mine, other, even_out, odd_out, energy_out):
-    size_x = raw.shape[0]
+def pack_raw_x(raw, out, low):
+    out[...] = raw[pl.ds(jnp.where(low, 0, raw.shape[0] - FILTER_SWEEPS), FILTER_SWEEPS)]
+
+
+def pack_raw_x_odd(raw, out):
+    pack_raw_x(raw, out, jnp.logical_not(odd_place("gx")))
+
+
+def pack_raw_x_even(raw, mine, other, out, energy_out):
     energy_out[...] = mine[...] + other[...]
-    low_first = odd_place("gx")
-    for out, low in ((even_out, low_first), (odd_out, jnp.logical_not(low_first))):
-        out[...] = raw[pl.ds(jnp.where(low, 0, size_x - FILTER_SWEEPS), FILTER_SWEEPS)]
+    pack_raw_x(raw, out, odd_place("gx"))
 
 
 def pack_raw_y(x_odd, x_even, raw, mine, other, even_out, odd_out, energy_out):
@@ -438,9 +443,9 @@
         cost=10000000,
     )(x_odd, x_even, y_odd, y_even, corner_odd, corner_even, *own)
 
-    even, odd, energy = call(pack_raw_x, (face, face, f32(8, size_z)))(raw, mine, other)
+    x_odd = swap_odd(call(pack_raw_x_odd, face)(raw), "gx")
+    even, energy = call(pack_raw_x_even, (face, f32(8, size_z)))(raw, mine, other)
     x_even = swap_even(even, "gx")
-    x_odd = swap_odd(odd, "gx")
     mine, other = doubling(energy, x_bits)
     _, rows = segments((FILTER_SWEEPS,), size_x)
     even, odd, energy = call(pack_raw_y, (f32(rows + 8, size_z), f32(rows, size_z), f32(8, size_z)))(

time: 38.8 us -> 38.6 us (level)
  waiting for transfers between devices: 8.82 us -> 8.14 us
  starting transfers between devices: 21.8 us -> 22.4 us
    ppermute x5, starting transfers between devices: 15.4 us -> 16.1 us  [swap_even(): lax.ppermute(value, axis, [(i, i ^ 1) for i in range(lax.axis_size(axis))])]
    ppermute x4, waiting for transfers between devices: 6.38 us -> 5.77 us  [partner(): lax.ppermute(value, axis, [(i, i ^ bit) for i in range(lax.axis_size(axis...]
where the time goes in v10:
time: 38.6 us; the launch traced here: 38.4 us
  starting transfers between devices  22.4 us (58%)
  waiting for transfers between devices  8.14 us (21%)
  Pallas kernels  7.09 us (18%)
  between operations  0.75 us (2%)
    ppermute x5, starting transfers between devices, swap_even(): lax.ppermute(value, axis, [(i, i ^ 1) for i in range(lax.axis_size(axis))])  16.1 us
    ppermute x4, waiting for transfers between devices, partner(): lax.ppermute(value, axis, [(i, i ^ bit) for i in range(lax.axis_size(axis...  5.77 us
    ppermute x5, starting transfers between devices, swap_odd(): return lax.ppermute(value, axis, up + [(b, a) for a, b in up])  3.3 us
    ppermute x4, starting transfers between devices, partner(): lax.ppermute(value, axis, [(i, i ^ bit) for i in range(lax.axis_size(axis...  2.93 us
    pallas_call x1, Pallas kernels, shards(): call(adjoint_part, f32(*shape), [room(6), room(6), room(4), room(2), room...  2.38 us
    ppermute x5, waiting for transfers between devices, swap_even(): lax.ppermute(value, axis, [(i, i ^ 1) for i in range(lax.axis_size(axis))])  2.36 us
    pallas_call x1, Pallas kernels, shards(): pl.pallas_call(filter_last, out_shape=(f32(*shape), f32(1, 1)), out_specs...  1.45 us
    pallas_call x1, Pallas kernels, shards(): pl.pallas_call(pack_own, out_shape=(f32(planes, size_y, size_z),) * 2 + (...  1.33 us
  transfers between devices with their start and end apart: 14, of which 4 were waited for; matrix products, arithmetic and copies ran while one was open for 0% of the time, Pallas kernels for 11%

profile of v10, /device:TPU:0, one launch (start us, length us, event | category | flops | bytes accessed | tf_op | source)
XLA Modules:
  0.0 38.4 jit_solution(7581312443619303527)
XLA Ops:
  0.6 1.3 %shard_map.68 = (f32[9,32,128]{2,1,0:T(8,128)S(1)}, f32[9,32,128]{2,1,0:T(8,128)S(1)}, f32[144,128]{1,0:T(8,128)S(1)}, f32[144,128]{1,0:T(8,128)S(1)}, f32[16,32...) custom-call(f32[16,32,128]{2,1,0:T(8,128)} %refs_0_.1, ...), custom_call_target="tpu_custom_call" | custom-call | tf_op jit(solution)/shard_map/pallas_call | solution.py:415
  2.0 0.7 %collective-permute-start = (f32[9,32,128]{2,1,0:T(8,128)S(1)}, f32[9,32,128]{2,1,0:T(8,128)S(1)}, u32[]{:S(2)}, u32[]{:S(2)}) collective-permute-start(f32[9,32,128]{2,1,0:T(8,128)S(1)} %get-tuple-element.22), channel_id=1, source_target_pairs={{8,16},{16,8},{9,17},{17,9},{10,18},{18,10},{11,19},{19,11},{12,20... | collective-permute-start | bytes 442376 | tf_op jit(solution)/shard_map/ppermute | solution.py:387
  2.6 4.4 %collective-permute-start.1 = (f32[9,32,128]{2,1,0:T(8,128)S(1)}, f32[9,32,128]{2,1,0:T(8,128)S(1)}, u32[]{:S(2)}, u32[]{:S(2)}) collective-permute-start(f32[9,32,128]{2,1,0:T(8,128)S(1)} %get-tuple-element.23), channel_id=1, source_target_pairs={{0,8},{8,0},{16,24},{24,16},{1,9},{9,1},{17,25},{25,17},{2,10},{10... | collective-permute-start | bytes 442376 | tf_op jit(solution)/shard_map/ppermute | solution.py:381
  7.0 0.7 %collective-permute-start.2 = (f32[144,128]{1,0:T(8,128)S(1)}, f32[144,128]{1,0:T(8,128)S(1)}, u32[]{:S(2)}, u32[]{:S(2)}) collective-permute-start(f32[144,128]{1,0:T(8,128)S(1)} %get-tuple-element.24), channel_id=1, source_target_pairs={{1,2},{3,4},{5,6},{2,1},{4,3},{6,5},{9,10},{11,12},{13,14},{10,9},... | collective-permute-start | bytes 221192 | tf_op jit(solution)/shard_map/ppermute | solution.py:387
  7.7 4.3 %collective-permute-start.3 = (f32[144,128]{1,0:T(8,128)S(1)}, f32[144,128]{1,0:T(8,128)S(1)}, u32[]{:S(2)}, u32[]{:S(2)}) collective-permute-start(f32[144,128]{1,0:T(8,128)S(1)} %get-tuple-element.25), channel_id=1, source_target_pairs={{0,1},{1,0},{2,3},{3,2},{4,5},{5,4},{6,7},{7,6},{8,9},{9,8},{10,11... | collective-permute-start | bytes 221192 | tf_op jit(solution)/shard_map/ppermute | solution.py:381
  12.0 0.0 collective-permute-done.x_odd
  12.0 0.0 collective-permute-done.1.x_even
  12.0 0.7 %collective-permute-start.4 = (f32[16,128]{1,0:T(8,128)S(1)}, f32[16,128]{1,0:T(8,128)S(1)}, u32[]{:S(2)}, u32[]{:S(2)}) collective-permute-start(f32[16,128]{1,0:T(8,128)S(1)} %get-tuple-element.26), channel_id=1, source_target_pairs={{1,2},{3,4},{5,6},{2,1},{4,3},{6,5},{9,10},{11,12},{13,14},{10,9},... | collective-permute-start | bytes 24584 | tf_op jit(solution)/shard_map/ppermute | solution.py:387
  12.7 4.4 %collective-permute-start.5 = (f32[16,128]{1,0:T(8,128)S(1)}, f32[16,128]{1,0:T(8,128)S(1)}, u32[]{:S(2)}, u32[]{:S(2)}) collective-permute-start(f32[16,128]{1,0:T(8,128)S(1)} %get-tuple-element.27), channel_id=1, source_target_pairs={{0,1},{1,0},{2,3},{3,2},{4,5},{5,4},{6,7},{7,6},{8,9},{9,8},{10,11... | collective-permute-start | bytes 24584 | tf_op jit(solution)/shard_map/ppermute | solution.py:381
  17.1 0.0 collective-permute-done.2.y_odd
  17.1 0.0 collective-permute-done.3.y_even
  17.1 0.7 %shard_map.72.mine = f32[8,128]{1,0:T(8,128)S(1)} custom-call(f32[9,32,128]{2,1,0:T(8,128)S(1)} %collective-permute-done.x_odd, f32[9,32,128]{2,1,0:T(8,128)S(1)} %collective-permute-done.1.x_even, f32[144,128]{1,0:T(8,128)S(1)} %collective-permute-done.2.y_odd, f32[144,128]{1,0:T(8,128)S(1)} %collective-permute-done.3.y_even, ...), custom_call_target="tpu_custom_call" | custom-call | flops 10000 | bytes 10000 | tf_op jit(solution)/shard_map/pallas_call | solution.py:436
  17.8 1.1 %collective-permute-start.7 = (f32[8,128]{1,0:T(8,128)S(1)}, f32[8,128]{1,0:T(8,128)S(1)}, u32[]{:S(2)}, u32[]{:S(2)}) collective-permute-start(f32[8,128]{1,0:T(8,128)S(1)} %shard_map.72.mine), channel_id=1, source_target_pairs={{0,4},{1,5},{2,6},{3,7},{4,0},{5,1},{6,2},{7,3},{8,12},{9,13},{10,... | collective-permute-start | bytes 12296 | tf_op jit(solution)/shard_map/ppermute | solution.py:391
  18.9 0.0 collective-permute-done.4.corner_odd
  18.9 0.0 collective-permute-done.5.corner_even
  18.9 2.4 %shard_map.70.raw.raw_in = f32[16,32,128]{2,1,0:T(8,128)S(1)} custom-call(f32[9,32,128]{2,1,0:T(8,128)S(1)} %collective-permute-done.x_odd, f32[9,32,128]{2,1,0:T(8,128)S(1)} %collective-permute-done.1.x_even, f32[144,128]{1,0:T(8,128)S(1)} %collective-permute-done.2.y_odd, f32[144,128]{1,0:T(8,128)S(1)} %collective-permute-done.3.y_even, ...), custom_call_target="tpu_custom_call" | custom-call | flops 10000000 | bytes 10000000 | tf_op jit(solution)/shard_map/pallas_call | solution.py:439
  21.3 0.7 %collective-permute-start.6 = (f32[4,32,128]{2,1,0:T(8,128)S(1)}, f32[4,32,128]{2,1,0:T(8,128)S(1)}, u32[]{:S(2)}, u32[]{:S(2)}) collective-permute-start(f32[4,32,128]{2,1,0:T(8,128)S(1)} %shard_map.71), channel_id=1, source_target_pairs={{8,16},{16,8},{9,17},{17,9},{10,18},{18,10},{11,19},{19,11},{12,20... | collective-permute-start | bytes 196616 | tf_op jit(solution)/shard_map/ppermute | solution.py:387
  22.0 0.3 collective-permute-done.7.other
  22.3 2.0 %collective-permute-start.8 = (f32[4,32,128]{2,1,0:T(8,128)S(1)}, f32[4,32,128]{2,1,0:T(8,128)S(1)}, u32[]{:S(2)}, u32[]{:S(2)}) collective-permute-start(f32[4,32,128]{2,1,0:T(8,128)S(1)} %get-tuple-element.33), channel_id=1, source_target_pairs={{0,8},{8,0},{16,24},{24,16},{1,9},{9,1},{17,25},{25,17},{2,10},{10... | collective-permute-start | bytes 196616 | tf_op jit(solution)/shard_map/ppermute | solution.py:381
  24.3 0.4 collective-permute-start.9
  24.7 3.3 %collective-permute-done.9.other = f32[8,128]{1,0:T(8,128)S(1)} collective-permute-done((f32[8,128]{1,0:T(8,128)S(1)}, f32[8,128]{1,0:T(8,128)S(1)}, u32[]{:S(2)}, u32[]{:S(2)}) %collective-permute-start.9) | collective-permute-done | bytes 4128 | tf_op jit(solution)/shard_map/ppermute | solution.py:391
  27.9 0.0 collective-permute-done.6.x_odd
  27.9 0.0 collective-permute-done.8.x_even
  28.0 1.1 %collective-permute-start.11 = (f32[88,128]{1,0:T(8,128)S(1)}, f32[88,128]{1,0:T(8,128)S(1)}, u32[]{:S(2)}, u32[]{:S(2)}) collective-permute-start(f32[88,128]{1,0:T(8,128)S(1)} %get-tuple-element.36), channel_id=1, source_target_pairs={{0,1},{1,0},{2,3},{3,2},{4,5},{5,4},{6,7},{7,6},{8,9},{9,8},{10,11... | collective-permute-start | bytes 135176 | tf_op jit(solution)/shard_map/ppermute | solution.py:381
  29.1 0.7 %collective-permute-start.10 = (f32[80,128]{1,0:T(8,128)S(1)}, f32[80,128]{1,0:T(8,128)S(1)}, u32[]{:S(2)}, u32[]{:S(2)}) collective-permute-start(f32[80,128]{1,0:T(8,128)S(1)} %get-tuple-element.35), channel_id=1, source_target_pairs={{1,2},{3,4},{5,6},{2,1},{4,3},{6,5},{9,10},{11,12},{13,14},{10,9},... | collective-permute-start | bytes 122888 | tf_op jit(solution)/shard_map/ppermute | solution.py:387
  29.7 2.4 %collective-permute-done.11.y_even = f32[88,128]{1,0:T(8,128)S(1)} collective-permute-done((f32[88,128]{1,0:T(8,128)S(1)}, f32[88,128]{1,0:T(8,128)S(1)}, u32[]{:S(2)}, u32[]{:S(2)}) %collective-permute-start.11) | collective-permute-done | bytes 45088 | tf_op jit(solution)/shard_map/ppermute | solution.py:381
  32.1 1.4 %collective-permute-start.12 = (f32[8,128]{1,0:T(8,128)S(1)}, f32[8,128]{1,0:T(8,128)S(1)}, u32[]{:S(2)}, u32[]{:S(2)}) collective-permute-start(f32[8,128]{1,0:T(8,128)S(1)} %slice_add_fusion), channel_id=1, source_target_pairs={{0,2},{1,3},{2,0},{3,1},{4,6},{5,7},{6,4},{7,5},{8,10},{9,11},{10,... | collective-permute-start | bytes 12296 | tf_op jit(solution)/shard_map/ppermute | solution.py:391
  33.5 2.2 %collective-permute-done.12 = f32[8,128]{1,0:T(8,128)S(1)} collective-permute-done((f32[8,128]{1,0:T(8,128)S(1)}, f32[8,128]{1,0:T(8,128)S(1)}, u32[]{:S(2)}, u32[]{:S(2)}) %collective-permute-start.12) | collective-permute-done | bytes 4128 | tf_op jit(solution)/shard_map/ppermute | solution.py:391
  35.7 0.0 collective-permute-start.13
  35.7 0.0 collective-permute-done.10.y_odd
  35.7 1.2 %shard_map.75 = (f32[24,40,128]{2,1,0:T(8,128)S(1)}, f32[24,40,128]{2,1,0:T(8,128)S(1)}) custom-call(f32[4,32,128]{2,1,0:T(8,128)S(1)} %collective-permute-done.6.x_odd, f32[4,32,128]{2,1,0:T(8,128)S(1)} %collective-permute-done.8.x_even, f32[80,128]{1,0:T(8,128)S(1)} %collective-permute-done.10.y_odd, f32[88,128]{1,0:T(8,128)S(1)} %collective-permute-done.11.y_even, ...), custom_call_target="tpu_custom_call" | custom-call | flops 10000000 | bytes 10000000 | tf_op jit(solution)/shard_map/pallas_call | solution.py:458
  36.9 0.0 collective-permute-done.13.other
  36.9 1.5 %shard_map.76 = (f32[16,32,128]{2,1,0:T(8,128)}, f32[1,1]{1,0:T(1,128)}) custom-call(f32[24,40,128]{2,1,0:T(8,128)S(1)} %get-tuple-element.37.raw, f32[24,40,128]{2,1,0:T(8,128)S(1)} %get-tuple-element.38.src, s32[16,32,128]{2,1,0:T(8,128)S(1)} %get-tuple-element.29.labels, f32[8,128]{1,0:T(8,128)S(1)} %add.7.mine, f32[8,128]{1,0:T(8,128)S(1)} %collective-permute-done.13.other), custom_call_target="tpu_custom_call" | custom-call | tf_op jit(solution)/shard_map/pallas_call | solution.py:464
  (6 shorter events, 0.1 us)
Async XLA Ops:
  2.0 10.0 %collective-permute-start = (f32[9,32,128]{2,1,0:T(8,128)S(1)}, f32[9,32,128]{2,1,0:T(8,128)S(1)}, u32[]{:S(2)}, u32[]{:S(2)}) collective-permute-start(f32[9,32,128]{2,1,0:T(8,128)S(1)} %get-tuple-element.22), channel_id=1, source_target_pairs={{8,16},{16,8},{9,17},{17,9},{10,18},{18,10},{11,19},{19,11},{12,20... | collective-permute-start | bytes 442376 | tf_op jit(solution)/shard_map/ppermute | solution.py:387
  2.6 9.4 %collective-permute-start.1 = (f32[9,32,128]{2,1,0:T(8,128)S(1)}, f32[9,32,128]{2,1,0:T(8,128)S(1)}, u32[]{:S(2)}, u32[]{:S(2)}) collective-permute-start(f32[9,32,128]{2,1,0:T(8,128)S(1)} %get-tuple-element.23), channel_id=1, source_target_pairs={{0,8},{8,0},{16,24},{24,16},{1,9},{9,1},{17,25},{25,17},{2,10},{10... | collective-permute-start | bytes 442376 | tf_op jit(solution)/shard_map/ppermute | solution.py:381
  7.0 10.1 %collective-permute-start.2 = (f32[144,128]{1,0:T(8,128)S(1)}, f32[144,128]{1,0:T(8,128)S(1)}, u32[]{:S(2)}, u32[]{:S(2)}) collective-permute-start(f32[144,128]{1,0:T(8,128)S(1)} %get-tuple-element.24), channel_id=1, source_target_pairs={{1,2},{3,4},{5,6},{2,1},{4,3},{6,5},{9,10},{11,12},{13,14},{10,9},... | collective-permute-start | bytes 221192 | tf_op jit(solution)/shard_map/ppermute | solution.py:387
  7.7 9.4 %collective-permute-start.3 = (f32[144,128]{1,0:T(8,128)S(1)}, f32[144,128]{1,0:T(8,128)S(1)}, u32[]{:S(2)}, u32[]{:S(2)}) collective-permute-start(f32[144,128]{1,0:T(8,128)S(1)} %get-tuple-element.25), channel_id=1, source_target_pairs={{0,1},{1,0},{2,3},{3,2},{4,5},{5,4},{6,7},{7,6},{8,9},{9,8},{10,11... | collective-permute-start | bytes 221192 | tf_op jit(solution)/shard_map/ppermute | solution.py:381
  12.0 6.9 %collective-permute-start.4 = (f32[16,128]{1,0:T(8,128)S(1)}, f32[16,128]{1,0:T(8,128)S(1)}, u32[]{:S(2)}, u32[]{:S(2)}) collective-permute-start(f32[16,128]{1,0:T(8,128)S(1)} %get-tuple-element.26), channel_id=1, source_target_pairs={{1,2},{3,4},{5,6},{2,1},{4,3},{6,5},{9,10},{11,12},{13,14},{10,9},... | collective-permute-start | bytes 24584 | tf_op jit(solution)/shard_map/ppermute | solution.py:387
  12.7 6.2 %collective-permute-start.5 = (f32[16,128]{1,0:T(8,128)S(1)}, f32[16,128]{1,0:T(8,128)S(1)}, u32[]{:S(2)}, u32[]{:S(2)}) collective-permute-start(f32[16,128]{1,0:T(8,128)S(1)} %get-tuple-element.27), channel_id=1, source_target_pairs={{0,1},{1,0},{2,3},{3,2},{4,5},{5,4},{6,7},{7,6},{8,9},{9,8},{10,11... | collective-permute-start | bytes 24584 | tf_op jit(solution)/shard_map/ppermute | solution.py:381
  17.8 4.6 %collective-permute-start.7 = (f32[8,128]{1,0:T(8,128)S(1)}, f32[8,128]{1,0:T(8,128)S(1)}, u32[]{:S(2)}, u32[]{:S(2)}) collective-permute-start(f32[8,128]{1,0:T(8,128)S(1)} %shard_map.72.mine), channel_id=1, source_target_pairs={{0,4},{1,5},{2,6},{3,7},{4,0},{5,1},{6,2},{7,3},{8,12},{9,13},{10,... | collective-permute-start | bytes 12296 | tf_op jit(solution)/shard_map/ppermute | solution.py:391
  21.3 6.6 %collective-permute-start.6 = (f32[4,32,128]{2,1,0:T(8,128)S(1)}, f32[4,32,128]{2,1,0:T(8,128)S(1)}, u32[]{:S(2)}, u32[]{:S(2)}) collective-permute-start(f32[4,32,128]{2,1,0:T(8,128)S(1)} %shard_map.71), channel_id=1, source_target_pairs={{8,16},{16,8},{9,17},{17,9},{10,18},{18,10},{11,19},{19,11},{12,20... | collective-permute-start | bytes 196616 | tf_op jit(solution)/shard_map/ppermute | solution.py:387
  22.3 5.6 %collective-permute-start.8 = (f32[4,32,128]{2,1,0:T(8,128)S(1)}, f32[4,32,128]{2,1,0:T(8,128)S(1)}, u32[]{:S(2)}, u32[]{:S(2)}) collective-permute-start(f32[4,32,128]{2,1,0:T(8,128)S(1)} %get-tuple-element.33), channel_id=1, source_target_pairs={{0,8},{8,0},{16,24},{24,16},{1,9},{9,1},{17,25},{25,17},{2,10},{10... | collective-permute-start | bytes 196616 | tf_op jit(solution)/shard_map/ppermute | solution.py:381
  24.3 3.6 %collective-permute-start.9 = (f32[8,128]{1,0:T(8,128)S(1)}, f32[8,128]{1,0:T(8,128)S(1)}, u32[]{:S(2)}, u32[]{:S(2)}) collective-permute-start(f32[8,128]{1,0:T(8,128)S(1)} %get-tuple-element.34.mine), channel_id=1, source_target_pairs={{0,16},{8,24},{16,0},{24,8},{1,17},{9,25},{17,1},{25,9},{2,18},{10... | collective-permute-start | bytes 12296 | tf_op jit(solution)/shard_map/ppermute | solution.py:391
  28.0 4.1 %collective-permute-start.11 = (f32[88,128]{1,0:T(8,128)S(1)}, f32[88,128]{1,0:T(8,128)S(1)}, u32[]{:S(2)}, u32[]{:S(2)}) collective-permute-start(f32[88,128]{1,0:T(8,128)S(1)} %get-tuple-element.36), channel_id=1, source_target_pairs={{0,1},{1,0},{2,3},{3,2},{4,5},{5,4},{6,7},{7,6},{8,9},{9,8},{10,11... | collective-permute-start | bytes 135176 | tf_op jit(solution)/shard_map/ppermute | solution.py:381
  29.1 6.6 %collective-permute-start.10 = (f32[80,128]{1,0:T(8,128)S(1)}, f32[80,128]{1,0:T(8,128)S(1)}, u32[]{:S(2)}, u32[]{:S(2)}) collective-permute-start(f32[80,128]{1,0:T(8,128)S(1)} %get-tuple-element.35), channel_id=1, source_target_pairs={{1,2},{3,4},{5,6},{2,1},{4,3},{6,5},{9,10},{11,12},{13,14},{10,9},... | collective-permute-start | bytes 122888 | tf_op jit(solution)/shard_map/ppermute | solution.py:387
  32.1 3.6 %collective-permute-start.12 = (f32[8,128]{1,0:T(8,128)S(1)}, f32[8,128]{1,0:T(8,128)S(1)}, u32[]{:S(2)}, u32[]{:S(2)}) collective-permute-start(f32[8,128]{1,0:T(8,128)S(1)} %slice_add_fusion), channel_id=1, source_target_pairs={{0,2},{1,3},{2,0},{3,1},{4,6},{5,7},{6,4},{7,5},{8,10},{9,11},{10,... | collective-permute-start | bytes 12296 | tf_op jit(solution)/shard_map/ppermute | solution.py:391
  35.7 1.2 %collective-permute-start.13 = (f32[8,128]{1,0:T(8,128)S(1)}, f32[8,128]{1,0:T(8,128)S(1)}, u32[]{:S(2)}, u32[]{:S(2)}) collective-permute-start(f32[8,128]{1,0:T(8,128)S(1)} %add.7.mine), channel_id=1, source_target_pairs={{0,8},{8,0},{16,24},{24,16},{1,9},{9,1},{17,25},{25,17},{2,10},{10... | collective-permute-start | bytes 12296 | tf_op jit(solution)/shard_map/ppermute | solution.py:391

commit v11 on v10

--- a/solution.py
+++ b/solution.py
@@ -209,8 +209,12 @@
     is_first = lane == 0
     is_last = lane == size_z - 1
 
+    def inverted(d):
+        first_guess = pl.reciprocal(d, approx=True)
+        return first_guess * (2.0 - d * first_guess)
+
     def harmonic(a, b):
-        return 2.0 * a * b / jnp.maximum(a + b, 0.25)
+        return 2.0 * a * b * inverted(jnp.maximum(a + b, 0.25))
 
     def faces_x(x, n):
         face_x[pl.ds(x, n)] = harmonic(permit[pl.ds(x, n)], permit[pl.ds(x + 1, n)])
@@ -225,9 +229,9 @@
         face_y[span] = fy
         face_z[span] = fz
         total = screen + face_x[span] + face_x[pl.ds(x + 1, n)] + fy + shift(fy, 1, 1) + fz + shift(fz, 1, 2)
-        inverse[span] = jnp.where(p > 20.0, 0.0, 1.0 / total)
-
-    planes_loop(0, size_x + 4, 5, weigh)
+        inverse[span] = jnp.where(p > 20.0, 0.0, inverted(total))
+
+    planes_loop(0, size_x + 4, 10, weigh)
 
     def relax(x, n, a, a_low, a_high):
         span = pl.ds(x, n)
@@ -335,7 +339,7 @@
     return relax
 
 
-def filter_first(x_odd, x_even, y_odd, y_even, raw_in, raw, odd, even):
+def filter_part(x_odd, x_even, y_odd, y_even, raw_in, labels, out, raw, odd, even):
     size_x, size_y, size_z = raw_in.shape
     width = FILTER_SWEEPS
     tile = pl.ds(0, size_y)
@@ -349,7 +353,7 @@
     relax = relaxation(raw, size_x, size_y, size_z)
     src = raw
     for sweep in range(FILTER_SWEEPS - 1):
-        dst = (odd, even)[(FILTER_SWEEPS - sweep) % 2]
+        dst = (odd, even)[sweep % 2]
 
         def step(x, n, src=src, dst=dst):
             dst[pl.ds(x, n)] = relax(src, x, n)
@@ -357,20 +361,24 @@
         planes_loop(sweep + 1, size_x + 2 * width - sweep - 1, 11, step)
         src = dst
 
-
-def filter_last(raw, src, labels, mine, other, out, mean_out, held, sem):
-    size_x, size_y, size_z = labels.shape
-    relax = relaxation(raw, size_x, size_y, size_z)
+    def last(x, n):
+        f = relax(src, x + width, n)[:, :size_y]
+        out[pl.ds(x, n)] = jnp.where(labels[pl.ds(x, n)] == 1, f, 0.0)
+
+    planes_loop(0, size_x, 8, last)
+
+
+def rescale(filtered, mine, other, out, mean_out, held, sem):
+    size_x, size_y, size_z = filtered.shape
     voxels = lax.axis_size("gx") * size_x * lax.axis_size("gy") * size_y * size_z
     mean = 0.5 * jnp.sum(mine[...] + other[...]) / voxels + epsilon_mean
     mean_out[0, 0] = mean
     inverse = 1.0 / jnp.full((1, 1, size_z), mean, jnp.float32)
-    block = size_x // 2
+    block = size_x // 4
     copies = []
-    for k in range(2):
+    for k in range(4):
         span = pl.ds(k * block, block)
-        f = relax(src, k * block + FILTER_SWEEPS, block)[:, :size_y]
-        held[span] = jnp.where(labels[span] == 1, f * inverse, 0.0)
+        held[span] = filtered[span] * inverse
         copies.append(pltpu.make_async_copy(held.at[span], out.at[span], sem.at[k]))
         copies[k].start()
     for copy in copies:
@@ -454,20 +462,19 @@
     y_odd = swap_odd(odd, "gy")
     energy = energy + y_even[rows:rows + 8]
     mine, other = doubling(energy, y_bits[:1] + [("gx", 1)])
-    padded = f32(size_x + 2 * FILTER_SWEEPS, wide, size_z)
-    raw, filtered = call(
-        filter_first,
-        (padded, padded),
-        [pltpu.VMEM(padded.shape, jnp.float32)],
+    filtered = call(
+        filter_part,
+        f32(*shape),
+        [room(2 * FILTER_SWEEPS)] * 3,
         cost=10000000,
-    )(x_odd, x_even, y_odd, y_even, raw)
+    )(x_odd, x_even, y_odd, y_even, raw, own[1])
     sensitivity, mean_energy = pl.pallas_call(
-        filter_last,
+        rescale,
         out_shape=(f32(*shape), f32(1, 1)),
         out_specs=(pl.BlockSpec(memory_space=pl.ANY), pl.BlockSpec(memory_space=pltpu.SMEM)),
-        scratch_shapes=[pltpu.VMEM(shape, jnp.float32), pltpu.SemaphoreType.DMA((2,))],
+        scratch_shapes=[pltpu.VMEM(shape, jnp.float32), pltpu.SemaphoreType.DMA((4,))],
         compiler_params=pltpu.CompilerParams(vmem_limit_bytes=VMEM_LIMIT),
-    )(raw, filtered, own[1], mine, other)
+    )(filtered, mine, other)
     return (sensitivity, mean_energy[0, 0])
 
 

time: 38.6 us -> 38.7 us (level)
  transfers between devices with their start and end apart: 14 -> 14, of which waited for: 4 -> 4; matrix products, arithmetic and copies ran while one was open for 0% -> 0% of each run, Pallas kernels for 11% -> 12%
where the time goes in v11:
time: 38.7 us; the launch traced here: 38.4 us
  starting transfers between devices  22.2 us (57%)
  waiting for transfers between devices  8.29 us (21%)
  Pallas kernels  7.15 us (18%)
  between operations  0.75 us (2%)
    ppermute x5, starting transfers between devices, swap_even(): lax.ppermute(value, axis, [(i, i ^ 1) for i in range(lax.axis_size(axis))])  16 us
    ppermute x4, waiting for transfers between devices, partner(): lax.ppermute(value, axis, [(i, i ^ bit) for i in range(lax.axis_size(axis...  5.92 us
    ppermute x5, starting transfers between devices, swap_odd(): return lax.ppermute(value, axis, up + [(b, a) for a, b in up])  3.3 us
    ppermute x4, starting transfers between devices, partner(): lax.ppermute(value, axis, [(i, i ^ bit) for i in range(lax.axis_size(axis...  2.93 us
    ppermute x5, waiting for transfers between devices, swap_even(): lax.ppermute(value, axis, [(i, i ^ 1) for i in range(lax.axis_size(axis))])  2.36 us
    pallas_call x1, Pallas kernels, shards(): call(adjoint_part, f32(*shape), [room(6), room(6), room(4), room(2), room...  2.23 us
    pallas_call x1, Pallas kernels, shards(): call(filter_part, f32(*shape), [room(2 * FILTER_SWEEPS)] * 3, cost=10000000)  1.46 us
    pallas_call x1, Pallas kernels, shards(): pl.pallas_call(rescale, out_shape=(f32(*shape), f32(1, 1)), out_specs=(pl...  1.38 us
  transfers between devices with their start and end apart: 14, of which 4 were waited for; matrix products, arithmetic and copies ran while one was open for 0% of the time, Pallas kernels for 12%

profile of v11, /device:TPU:0, one launch (start us, length us, event | category | flops | bytes accessed | tf_op | source)
XLA Modules:
  0.0 38.4 jit_solution(563027954698472455)
XLA Ops:
  0.6 1.3 %shard_map.68 = (f32[9,32,128]{2,1,0:T(8,128)S(1)}, f32[9,32,128]{2,1,0:T(8,128)S(1)}, f32[144,128]{1,0:T(8,128)S(1)}, f32[144,128]{1,0:T(8,128)S(1)}, f32[16,32...) custom-call(f32[16,32,128]{2,1,0:T(8,128)} %refs_0_.1, ...), custom_call_target="tpu_custom_call" | custom-call | tf_op jit(solution)/shard_map/pallas_call | solution.py:423
  2.0 0.7 %collective-permute-start = (f32[9,32,128]{2,1,0:T(8,128)S(1)}, f32[9,32,128]{2,1,0:T(8,128)S(1)}, u32[]{:S(2)}, u32[]{:S(2)}) collective-permute-start(f32[9,32,128]{2,1,0:T(8,128)S(1)} %get-tuple-element.20), channel_id=1, source_target_pairs={{8,16},{16,8},{9,17},{17,9},{10,18},{18,10},{11,19},{19,11},{12,20... | collective-permute-start | bytes 442376 | tf_op jit(solution)/shard_map/ppermute | solution.py:395
  2.6 4.4 %collective-permute-start.1 = (f32[9,32,128]{2,1,0:T(8,128)S(1)}, f32[9,32,128]{2,1,0:T(8,128)S(1)}, u32[]{:S(2)}, u32[]{:S(2)}) collective-permute-start(f32[9,32,128]{2,1,0:T(8,128)S(1)} %get-tuple-element.21), channel_id=1, source_target_pairs={{0,8},{8,0},{16,24},{24,16},{1,9},{9,1},{17,25},{25,17},{2,10},{10... | collective-permute-start | bytes 442376 | tf_op jit(solution)/shard_map/ppermute | solution.py:389
  7.0 0.7 %collective-permute-start.2 = (f32[144,128]{1,0:T(8,128)S(1)}, f32[144,128]{1,0:T(8,128)S(1)}, u32[]{:S(2)}, u32[]{:S(2)}) collective-permute-start(f32[144,128]{1,0:T(8,128)S(1)} %get-tuple-element.22), channel_id=1, source_target_pairs={{1,2},{3,4},{5,6},{2,1},{4,3},{6,5},{9,10},{11,12},{13,14},{10,9},... | collective-permute-start | bytes 221192 | tf_op jit(solution)/shard_map/ppermute | solution.py:395
  7.7 4.3 %collective-permute-start.3 = (f32[144,128]{1,0:T(8,128)S(1)}, f32[144,128]{1,0:T(8,128)S(1)}, u32[]{:S(2)}, u32[]{:S(2)}) collective-permute-start(f32[144,128]{1,0:T(8,128)S(1)} %get-tuple-element.23), channel_id=1, source_target_pairs={{0,1},{1,0},{2,3},{3,2},{4,5},{5,4},{6,7},{7,6},{8,9},{9,8},{10,11... | collective-permute-start | bytes 221192 | tf_op jit(solution)/shard_map/ppermute | solution.py:389
  12.0 0.0 collective-permute-done.x_odd
  12.0 0.0 collective-permute-done.1.x_even
  12.0 0.7 %collective-permute-start.4 = (f32[16,128]{1,0:T(8,128)S(1)}, f32[16,128]{1,0:T(8,128)S(1)}, u32[]{:S(2)}, u32[]{:S(2)}) collective-permute-start(f32[16,128]{1,0:T(8,128)S(1)} %get-tuple-element.24), channel_id=1, source_target_pairs={{1,2},{3,4},{5,6},{2,1},{4,3},{6,5},{9,10},{11,12},{13,14},{10,9},... | collective-permute-start | bytes 24584 | tf_op jit(solution)/shard_map/ppermute | solution.py:395
  12.7 4.4 %collective-permute-start.5 = (f32[16,128]{1,0:T(8,128)S(1)}, f32[16,128]{1,0:T(8,128)S(1)}, u32[]{:S(2)}, u32[]{:S(2)}) collective-permute-start(f32[16,128]{1,0:T(8,128)S(1)} %get-tuple-element.25), channel_id=1, source_target_pairs={{0,1},{1,0},{2,3},{3,2},{4,5},{5,4},{6,7},{7,6},{8,9},{9,8},{10,11... | collective-permute-start | bytes 24584 | tf_op jit(solution)/shard_map/ppermute | solution.py:389
  17.1 0.0 collective-permute-done.2.y_odd
  17.1 0.0 collective-permute-done.3.y_even
  17.1 0.7 %shard_map.72.mine = f32[8,128]{1,0:T(8,128)S(1)} custom-call(f32[9,32,128]{2,1,0:T(8,128)S(1)} %collective-permute-done.x_odd, f32[9,32,128]{2,1,0:T(8,128)S(1)} %collective-permute-done.1.x_even, f32[144,128]{1,0:T(8,128)S(1)} %collective-permute-done.2.y_odd, f32[144,128]{1,0:T(8,128)S(1)} %collective-permute-done.3.y_even, ...), custom_call_target="tpu_custom_call" | custom-call | flops 10000 | bytes 10000 | tf_op jit(solution)/shard_map/pallas_call | solution.py:444
  17.8 1.1 %collective-permute-start.7 = (f32[8,128]{1,0:T(8,128)S(1)}, f32[8,128]{1,0:T(8,128)S(1)}, u32[]{:S(2)}, u32[]{:S(2)}) collective-permute-start(f32[8,128]{1,0:T(8,128)S(1)} %shard_map.72.mine), channel_id=1, source_target_pairs={{0,4},{1,5},{2,6},{3,7},{4,0},{5,1},{6,2},{7,3},{8,12},{9,13},{10,... | collective-permute-start | bytes 12296 | tf_op jit(solution)/shard_map/ppermute | solution.py:399
  18.9 0.0 collective-permute-done.4.corner_odd
  18.9 0.0 collective-permute-done.5.corner_even
  18.9 2.2 %shard_map.70.raw.raw_in = f32[16,32,128]{2,1,0:T(8,128)S(1)} custom-call(f32[9,32,128]{2,1,0:T(8,128)S(1)} %collective-permute-done.x_odd, f32[9,32,128]{2,1,0:T(8,128)S(1)} %collective-permute-done.1.x_even, f32[144,128]{1,0:T(8,128)S(1)} %collective-permute-done.2.y_odd, f32[144,128]{1,0:T(8,128)S(1)} %collective-permute-done.3.y_even, ...), custom_call_target="tpu_custom_call" | custom-call | flops 10000000 | bytes 10000000 | tf_op jit(solution)/shard_map/pallas_call | solution.py:447
  21.2 0.7 %collective-permute-start.6 = (f32[4,32,128]{2,1,0:T(8,128)S(1)}, f32[4,32,128]{2,1,0:T(8,128)S(1)}, u32[]{:S(2)}, u32[]{:S(2)}) collective-permute-start(f32[4,32,128]{2,1,0:T(8,128)S(1)} %shard_map.71), channel_id=1, source_target_pairs={{8,16},{16,8},{9,17},{17,9},{10,18},{18,10},{11,19},{19,11},{12,20... | collective-permute-start | bytes 196616 | tf_op jit(solution)/shard_map/ppermute | solution.py:395
  21.8 0.5 %collective-permute-done.7.other = f32[8,128]{1,0:T(8,128)S(1)} collective-permute-done((f32[8,128]{1,0:T(8,128)S(1)}, f32[8,128]{1,0:T(8,128)S(1)}, u32[]{:S(2)}, u32[]{:S(2)}) %collective-permute-start.7) | collective-permute-done | bytes 4128 | tf_op jit(solution)/shard_map/ppermute | solution.py:399
  22.3 1.8 %collective-permute-start.8 = (f32[4,32,128]{2,1,0:T(8,128)S(1)}, f32[4,32,128]{2,1,0:T(8,128)S(1)}, u32[]{:S(2)}, u32[]{:S(2)}) collective-permute-start(f32[4,32,128]{2,1,0:T(8,128)S(1)} %get-tuple-element.31), channel_id=1, source_target_pairs={{0,8},{8,0},{16,24},{24,16},{1,9},{9,1},{17,25},{25,17},{2,10},{10... | collective-permute-start | bytes 196616 | tf_op jit(solution)/shard_map/ppermute | solution.py:389
  24.2 0.4 collective-permute-start.9
  24.5 3.3 %collective-permute-done.9.other = f32[8,128]{1,0:T(8,128)S(1)} collective-permute-done((f32[8,128]{1,0:T(8,128)S(1)}, f32[8,128]{1,0:T(8,128)S(1)}, u32[]{:S(2)}, u32[]{:S(2)}) %collective-permute-start.9) | collective-permute-done | bytes 4128 | tf_op jit(solution)/shard_map/ppermute | solution.py:399
  27.8 0.0 collective-permute-done.6.x_odd
  27.8 0.0 collective-permute-done.8.x_even
  27.8 1.1 %collective-permute-start.11 = (f32[88,128]{1,0:T(8,128)S(1)}, f32[88,128]{1,0:T(8,128)S(1)}, u32[]{:S(2)}, u32[]{:S(2)}) collective-permute-start(f32[88,128]{1,0:T(8,128)S(1)} %get-tuple-element.34), channel_id=1, source_target_pairs={{0,1},{1,0},{2,3},{3,2},{4,5},{5,4},{6,7},{7,6},{8,9},{9,8},{10,11... | collective-permute-start | bytes 135176 | tf_op jit(solution)/shard_map/ppermute | solution.py:389
  28.9 0.7 %collective-permute-start.10 = (f32[80,128]{1,0:T(8,128)S(1)}, f32[80,128]{1,0:T(8,128)S(1)}, u32[]{:S(2)}, u32[]{:S(2)}) collective-permute-start(f32[80,128]{1,0:T(8,128)S(1)} %get-tuple-element.33), channel_id=1, source_target_pairs={{1,2},{3,4},{5,6},{2,1},{4,3},{6,5},{9,10},{11,12},{13,14},{10,9},... | collective-permute-start | bytes 122888 | tf_op jit(solution)/shard_map/ppermute | solution.py:395
  29.6 2.4 %collective-permute-done.11.y_even = f32[88,128]{1,0:T(8,128)S(1)} collective-permute-done((f32[88,128]{1,0:T(8,128)S(1)}, f32[88,128]{1,0:T(8,128)S(1)}, u32[]{:S(2)}, u32[]{:S(2)}) %collective-permute-start.11) | collective-permute-done | bytes 45088 | tf_op jit(solution)/shard_map/ppermute | solution.py:389
  31.9 1.4 %collective-permute-start.12 = (f32[8,128]{1,0:T(8,128)S(1)}, f32[8,128]{1,0:T(8,128)S(1)}, u32[]{:S(2)}, u32[]{:S(2)}) collective-permute-start(f32[8,128]{1,0:T(8,128)S(1)} %slice_add_fusion), channel_id=1, source_target_pairs={{0,2},{1,3},{2,0},{3,1},{4,6},{5,7},{6,4},{7,5},{8,10},{9,11},{10,... | collective-permute-start | bytes 12296 | tf_op jit(solution)/shard_map/ppermute | solution.py:399
  33.4 2.2 %collective-permute-done.12 = f32[8,128]{1,0:T(8,128)S(1)} collective-permute-done((f32[8,128]{1,0:T(8,128)S(1)}, f32[8,128]{1,0:T(8,128)S(1)}, u32[]{:S(2)}, u32[]{:S(2)}) %collective-permute-start.12) | collective-permute-done | bytes 4128 | tf_op jit(solution)/shard_map/ppermute | solution.py:399
  35.5 0.0 collective-permute-start.13
  35.6 0.0 collective-permute-done.10.y_odd
  35.6 1.5 %shard_map.75.filtered = f32[16,32,128]{2,1,0:T(8,128)S(1)} custom-call(f32[4,32,128]{2,1,0:T(8,128)S(1)} %collective-permute-done.6.x_odd, f32[4,32,128]{2,1,0:T(8,128)S(1)} %collective-permute-done.8.x_even, f32[80,128]{1,0:T(8,128)S(1)} %collective-permute-done.10.y_odd, f32[88,128]{1,0:T(8,128)S(1)} %collective-permute-done.11.y_even, ...), custom_call_target="tpu_custom_call" | custom-call | flops 10000000 | bytes 10000000 | tf_op jit(solution)/shard_map/pallas_call | solution.py:465
  37.0 0.0 collective-permute-done.13.other
  37.0 1.4 %shard_map.76 = (f32[16,32,128]{2,1,0:T(8,128)}, f32[1,1]{1,0:T(1,128)}) custom-call(f32[16,32,128]{2,1,0:T(8,128)S(1)} %shard_map.75.filtered, f32[8,128]{1,0:T(8,128)S(1)} %add.7.mine, f32[8,128]{1,0:T(8,128)S(1)} %collective-permute-done.13.other), custom_call_target="tpu_custom_call" | custom-call | tf_op jit(solution)/shard_map/pallas_call | solution.py:471
  (6 shorter events, 0.1 us)
Async XLA Ops:
  2.0 10.0 %collective-permute-start = (f32[9,32,128]{2,1,0:T(8,128)S(1)}, f32[9,32,128]{2,1,0:T(8,128)S(1)}, u32[]{:S(2)}, u32[]{:S(2)}) collective-permute-start(f32[9,32,128]{2,1,0:T(8,128)S(1)} %get-tuple-element.20), channel_id=1, source_target_pairs={{8,16},{16,8},{9,17},{17,9},{10,18},{18,10},{11,19},{19,11},{12,20... | collective-permute-start | bytes 442376 | tf_op jit(solution)/shard_map/ppermute | solution.py:395
  2.6 9.4 %collective-permute-start.1 = (f32[9,32,128]{2,1,0:T(8,128)S(1)}, f32[9,32,128]{2,1,0:T(8,128)S(1)}, u32[]{:S(2)}, u32[]{:S(2)}) collective-permute-start(f32[9,32,128]{2,1,0:T(8,128)S(1)} %get-tuple-element.21), channel_id=1, source_target_pairs={{0,8},{8,0},{16,24},{24,16},{1,9},{9,1},{17,25},{25,17},{2,10},{10... | collective-permute-start | bytes 442376 | tf_op jit(solution)/shard_map/ppermute | solution.py:389
  7.0 10.1 %collective-permute-start.2 = (f32[144,128]{1,0:T(8,128)S(1)}, f32[144,128]{1,0:T(8,128)S(1)}, u32[]{:S(2)}, u32[]{:S(2)}) collective-permute-start(f32[144,128]{1,0:T(8,128)S(1)} %get-tuple-element.22), channel_id=1, source_target_pairs={{1,2},{3,4},{5,6},{2,1},{4,3},{6,5},{9,10},{11,12},{13,14},{10,9},... | collective-permute-start | bytes 221192 | tf_op jit(solution)/shard_map/ppermute | solution.py:395
  7.7 9.4 %collective-permute-start.3 = (f32[144,128]{1,0:T(8,128)S(1)}, f32[144,128]{1,0:T(8,128)S(1)}, u32[]{:S(2)}, u32[]{:S(2)}) collective-permute-start(f32[144,128]{1,0:T(8,128)S(1)} %get-tuple-element.23), channel_id=1, source_target_pairs={{0,1},{1,0},{2,3},{3,2},{4,5},{5,4},{6,7},{7,6},{8,9},{9,8},{10,11... | collective-permute-start | bytes 221192 | tf_op jit(solution)/shard_map/ppermute | solution.py:389
  12.0 6.9 %collective-permute-start.4 = (f32[16,128]{1,0:T(8,128)S(1)}, f32[16,128]{1,0:T(8,128)S(1)}, u32[]{:S(2)}, u32[]{:S(2)}) collective-permute-start(f32[16,128]{1,0:T(8,128)S(1)} %get-tuple-element.24), channel_id=1, source_target_pairs={{1,2},{3,4},{5,6},{2,1},{4,3},{6,5},{9,10},{11,12},{13,14},{10,9},... | collective-permute-start | bytes 24584 | tf_op jit(solution)/shard_map/ppermute | solution.py:395
  12.7 6.2 %collective-permute-start.5 = (f32[16,128]{1,0:T(8,128)S(1)}, f32[16,128]{1,0:T(8,128)S(1)}, u32[]{:S(2)}, u32[]{:S(2)}) collective-permute-start(f32[16,128]{1,0:T(8,128)S(1)} %get-tuple-element.25), channel_id=1, source_target_pairs={{0,1},{1,0},{2,3},{3,2},{4,5},{5,4},{6,7},{7,6},{8,9},{9,8},{10,11... | collective-permute-start | bytes 24584 | tf_op jit(solution)/shard_map/ppermute | solution.py:389
  17.8 4.6 %collective-permute-start.7 = (f32[8,128]{1,0:T(8,128)S(1)}, f32[8,128]{1,0:T(8,128)S(1)}, u32[]{:S(2)}, u32[]{:S(2)}) collective-permute-start(f32[8,128]{1,0:T(8,128)S(1)} %shard_map.72.mine), channel_id=1, source_target_pairs={{0,4},{1,5},{2,6},{3,7},{4,0},{5,1},{6,2},{7,3},{8,12},{9,13},{10,... | collective-permute-start | bytes 12296 | tf_op jit(solution)/shard_map/ppermute | solution.py:399
  21.2 6.6 %collective-permute-start.6 = (f32[4,32,128]{2,1,0:T(8,128)S(1)}, f32[4,32,128]{2,1,0:T(8,128)S(1)}, u32[]{:S(2)}, u32[]{:S(2)}) collective-permute-start(f32[4,32,128]{2,1,0:T(8,128)S(1)} %shard_map.71), channel_id=1, source_target_pairs={{8,16},{16,8},{9,17},{17,9},{10,18},{18,10},{11,19},{19,11},{12,20... | collective-permute-start | bytes 196616 | tf_op jit(solution)/shard_map/ppermute | solution.py:395
  22.3 5.4 %collective-permute-start.8 = (f32[4,32,128]{2,1,0:T(8,128)S(1)}, f32[4,32,128]{2,1,0:T(8,128)S(1)}, u32[]{:S(2)}, u32[]{:S(2)}) collective-permute-start(f32[4,32,128]{2,1,0:T(8,128)S(1)} %get-tuple-element.31), channel_id=1, source_target_pairs={{0,8},{8,0},{16,24},{24,16},{1,9},{9,1},{17,25},{25,17},{2,10},{10... | collective-permute-start | bytes 196616 | tf_op jit(solution)/shard_map/ppermute | solution.py:389
  24.2 3.6 %collective-permute-start.9 = (f32[8,128]{1,0:T(8,128)S(1)}, f32[8,128]{1,0:T(8,128)S(1)}, u32[]{:S(2)}, u32[]{:S(2)}) collective-permute-start(f32[8,128]{1,0:T(8,128)S(1)} %get-tuple-element.32.mine), channel_id=1, source_target_pairs={{0,16},{8,24},{16,0},{24,8},{1,17},{9,25},{17,1},{25,9},{2,18},{10... | collective-permute-start | bytes 12296 | tf_op jit(solution)/shard_map/ppermute | solution.py:399
  27.8 4.1 %collective-permute-start.11 = (f32[88,128]{1,0:T(8,128)S(1)}, f32[88,128]{1,0:T(8,128)S(1)}, u32[]{:S(2)}, u32[]{:S(2)}) collective-permute-start(f32[88,128]{1,0:T(8,128)S(1)} %get-tuple-element.34), channel_id=1, source_target_pairs={{0,1},{1,0},{2,3},{3,2},{4,5},{5,4},{6,7},{7,6},{8,9},{9,8},{10,11... | collective-permute-start | bytes 135176 | tf_op jit(solution)/shard_map/ppermute | solution.py:389
  28.9 6.6 %collective-permute-start.10 = (f32[80,128]{1,0:T(8,128)S(1)}, f32[80,128]{1,0:T(8,128)S(1)}, u32[]{:S(2)}, u32[]{:S(2)}) collective-permute-start(f32[80,128]{1,0:T(8,128)S(1)} %get-tuple-element.33), channel_id=1, source_target_pairs={{1,2},{3,4},{5,6},{2,1},{4,3},{6,5},{9,10},{11,12},{13,14},{10,9},... | collective-permute-start | bytes 122888 | tf_op jit(solution)/shard_map/ppermute | solution.py:395
  31.9 3.6 %collective-permute-start.12 = (f32[8,128]{1,0:T(8,128)S(1)}, f32[8,128]{1,0:T(8,128)S(1)}, u32[]{:S(2)}, u32[]{:S(2)}) collective-permute-start(f32[8,128]{1,0:T(8,128)S(1)} %slice_add_fusion), channel_id=1, source_target_pairs={{0,2},{1,3},{2,0},{3,1},{4,6},{5,7},{6,4},{7,5},{8,10},{9,11},{10,... | collective-permute-start | bytes 12296 | tf_op jit(solution)/shard_map/ppermute | solution.py:399
  35.5 1.5 %collective-permute-start.13 = (f32[8,128]{1,0:T(8,128)S(1)}, f32[8,128]{1,0:T(8,128)S(1)}, u32[]{:S(2)}, u32[]{:S(2)}) collective-permute-start(f32[8,128]{1,0:T(8,128)S(1)} %add.7.mine), channel_id=1, source_target_pairs={{0,8},{8,0},{16,24},{24,16},{1,9},{9,1},{17,25},{25,17},{2,10},{10... | collective-permute-start | bytes 12296 | tf_op jit(solution)/shard_map/ppermute | solution.py:399

commit v12 on v11

--- a/solution.py
+++ b/solution.py
@@ -368,21 +368,12 @@
     planes_loop(0, size_x, 8, last)
 
 
-def rescale(filtered, mine, other, out, mean_out, held, sem):
+def rescale(filtered, mine, other, out, mean_out):
     size_x, size_y, size_z = filtered.shape
     voxels = lax.axis_size("gx") * size_x * lax.axis_size("gy") * size_y * size_z
     mean = 0.5 * jnp.sum(mine[...] + other[...]) / voxels + epsilon_mean
     mean_out[0, 0] = mean
-    inverse = 1.0 / jnp.full((1, 1, size_z), mean, jnp.float32)
-    block = size_x // 4
-    copies = []
-    for k in range(4):
-        span = pl.ds(k * block, block)
-        held[span] = filtered[span] * inverse
-        copies.append(pltpu.make_async_copy(held.at[span], out.at[span], sem.at[k]))
-        copies[k].start()
-    for copy in copies:
-        copy.wait()
+    out[...] = filtered[...] * (1.0 / jnp.full((1, 1, size_z), mean, jnp.float32))
 
 
 def swap_even(value, axis):
@@ -471,8 +462,7 @@
     sensitivity, mean_energy = pl.pallas_call(
         rescale,
         out_shape=(f32(*shape), f32(1, 1)),
-        out_specs=(pl.BlockSpec(memory_space=pl.ANY), pl.BlockSpec(memory_space=pltpu.SMEM)),
-        scratch_shapes=[pltpu.VMEM(shape, jnp.float32), pltpu.SemaphoreType.DMA((4,))],
+        out_specs=(pl.BlockSpec(memory_space=pltpu.VMEM), pl.BlockSpec(memory_space=pltpu.SMEM)),
         compiler_params=pltpu.CompilerParams(vmem_limit_bytes=VMEM_LIMIT),
     )(filtered, mine, other)
     return (sensitivity, mean_energy[0, 0])

time: 38.7 us -> 38.2 us (0.987)
  Pallas kernels: 7.15 us -> 6.63 us
    pallas_call x1, Pallas kernels: 1.38 us -> 0.86 us  [shards(): pl.pallas_call(rescale, out_shape=(f32(*shape), f32(1, 1)), out_specs=(pl...]
where the time goes in v12:
time: 38.2 us; the launch traced here: 37.9 us
  starting transfers between devices  22.2 us (58%)
  waiting for transfers between devices  8.29 us (22%)
  Pallas kernels  6.63 us (17%)
  between operations  0.75 us (2%)
    ppermute x5, starting transfers between devices, swap_even(): lax.ppermute(value, axis, [(i, i ^ 1) for i in range(lax.axis_size(axis))])  16 us
    ppermute x4, waiting for transfers between devices, partner(): lax.ppermute(value, axis, [(i, i ^ bit) for i in range(lax.axis_size(axis...  5.92 us
    ppermute x5, starting transfers between devices, swap_odd(): return lax.ppermute(value, axis, up + [(b, a) for a, b in up])  3.3 us
    ppermute x4, starting transfers between devices, partner(): lax.ppermute(value, axis, [(i, i ^ bit) for i in range(lax.axis_size(axis...  2.93 us
    ppermute x5, waiting for transfers between devices, swap_even(): lax.ppermute(value, axis, [(i, i ^ 1) for i in range(lax.axis_size(axis))])  2.36 us
    pallas_call x1, Pallas kernels, shards(): call(adjoint_part, f32(*shape), [room(6), room(6), room(4), room(2), room...  2.23 us
    pallas_call x1, Pallas kernels, shards(): call(filter_part, f32(*shape), [room(2 * FILTER_SWEEPS)] * 3, cost=10000000)  1.46 us
    pallas_call x1, Pallas kernels, shards(): pl.pallas_call(pack_own, out_shape=(f32(planes, size_y, size_z),) * 2 + (...  1.33 us
  transfers between devices with their start and end apart: 14, of which 4 were waited for; matrix products, arithmetic and copies ran while one was open for 0% of the time, Pallas kernels for 12%

profile of v12, /device:TPU:0, one launch (start us, length us, event | category | flops | bytes accessed | tf_op | source)
XLA Modules:
  0.0 37.9 jit_solution(13511498918251603028)
XLA Ops:
  0.6 1.3 %shard_map.68 = (f32[9,32,128]{2,1,0:T(8,128)S(1)}, f32[9,32,128]{2,1,0:T(8,128)S(1)}, f32[144,128]{1,0:T(8,128)S(1)}, f32[144,128]{1,0:T(8,128)S(1)}, f32[16,32...) custom-call(f32[16,32,128]{2,1,0:T(8,128)} %refs_0_.1, ...), custom_call_target="tpu_custom_call" | custom-call | tf_op jit(solution)/shard_map/pallas_call | solution.py:414
  2.0 0.7 %collective-permute-start = (f32[9,32,128]{2,1,0:T(8,128)S(1)}, f32[9,32,128]{2,1,0:T(8,128)S(1)}, u32[]{:S(2)}, u32[]{:S(2)}) collective-permute-start(f32[9,32,128]{2,1,0:T(8,128)S(1)} %get-tuple-element.20), channel_id=1, source_target_pairs={{8,16},{16,8},{9,17},{17,9},{10,18},{18,10},{11,19},{19,11},{12,20... | collective-permute-start | bytes 442376 | tf_op jit(solution)/shard_map/ppermute | solution.py:386
  2.6 4.4 %collective-permute-start.1 = (f32[9,32,128]{2,1,0:T(8,128)S(1)}, f32[9,32,128]{2,1,0:T(8,128)S(1)}, u32[]{:S(2)}, u32[]{:S(2)}) collective-permute-start(f32[9,32,128]{2,1,0:T(8,128)S(1)} %get-tuple-element.21), channel_id=1, source_target_pairs={{0,8},{8,0},{16,24},{24,16},{1,9},{9,1},{17,25},{25,17},{2,10},{10... | collective-permute-start | bytes 442376 | tf_op jit(solution)/shard_map/ppermute | solution.py:380
  7.0 0.7 %collective-permute-start.2 = (f32[144,128]{1,0:T(8,128)S(1)}, f32[144,128]{1,0:T(8,128)S(1)}, u32[]{:S(2)}, u32[]{:S(2)}) collective-permute-start(f32[144,128]{1,0:T(8,128)S(1)} %get-tuple-element.22), channel_id=1, source_target_pairs={{1,2},{3,4},{5,6},{2,1},{4,3},{6,5},{9,10},{11,12},{13,14},{10,9},... | collective-permute-start | bytes 221192 | tf_op jit(solution)/shard_map/ppermute | solution.py:386
  7.7 4.3 %collective-permute-start.3 = (f32[144,128]{1,0:T(8,128)S(1)}, f32[144,128]{1,0:T(8,128)S(1)}, u32[]{:S(2)}, u32[]{:S(2)}) collective-permute-start(f32[144,128]{1,0:T(8,128)S(1)} %get-tuple-element.23), channel_id=1, source_target_pairs={{0,1},{1,0},{2,3},{3,2},{4,5},{5,4},{6,7},{7,6},{8,9},{9,8},{10,11... | collective-permute-start | bytes 221192 | tf_op jit(solution)/shard_map/ppermute | solution.py:380
  12.0 0.0 collective-permute-done.x_odd
  12.0 0.0 collective-permute-done.1.x_even
  12.0 0.7 %collective-permute-start.4 = (f32[16,128]{1,0:T(8,128)S(1)}, f32[16,128]{1,0:T(8,128)S(1)}, u32[]{:S(2)}, u32[]{:S(2)}) collective-permute-start(f32[16,128]{1,0:T(8,128)S(1)} %get-tuple-element.24), channel_id=1, source_target_pairs={{1,2},{3,4},{5,6},{2,1},{4,3},{6,5},{9,10},{11,12},{13,14},{10,9},... | collective-permute-start | bytes 24584 | tf_op jit(solution)/shard_map/ppermute | solution.py:386
  12.7 4.4 %collective-permute-start.5 = (f32[16,128]{1,0:T(8,128)S(1)}, f32[16,128]{1,0:T(8,128)S(1)}, u32[]{:S(2)}, u32[]{:S(2)}) collective-permute-start(f32[16,128]{1,0:T(8,128)S(1)} %get-tuple-element.25), channel_id=1, source_target_pairs={{0,1},{1,0},{2,3},{3,2},{4,5},{5,4},{6,7},{7,6},{8,9},{9,8},{10,11... | collective-permute-start | bytes 24584 | tf_op jit(solution)/shard_map/ppermute | solution.py:380
  17.1 0.0 collective-permute-done.2.y_odd
  17.1 0.0 collective-permute-done.3.y_even
  17.1 0.7 %shard_map.72.mine = f32[8,128]{1,0:T(8,128)S(1)} custom-call(f32[9,32,128]{2,1,0:T(8,128)S(1)} %collective-permute-done.x_odd, f32[9,32,128]{2,1,0:T(8,128)S(1)} %collective-permute-done.1.x_even, f32[144,128]{1,0:T(8,128)S(1)} %collective-permute-done.2.y_odd, f32[144,128]{1,0:T(8,128)S(1)} %collective-permute-done.3.y_even, ...), custom_call_target="tpu_custom_call" | custom-call | flops 10000 | bytes 10000 | tf_op jit(solution)/shard_map/pallas_call | solution.py:435
  17.8 1.1 %collective-permute-start.7 = (f32[8,128]{1,0:T(8,128)S(1)}, f32[8,128]{1,0:T(8,128)S(1)}, u32[]{:S(2)}, u32[]{:S(2)}) collective-permute-start(f32[8,128]{1,0:T(8,128)S(1)} %shard_map.72.mine), channel_id=1, source_target_pairs={{0,4},{1,5},{2,6},{3,7},{4,0},{5,1},{6,2},{7,3},{8,12},{9,13},{10,... | collective-permute-start | bytes 12296 | tf_op jit(solution)/shard_map/ppermute | solution.py:390
  18.9 0.0 collective-permute-done.4.corner_odd
  18.9 0.0 collective-permute-done.5.corner_even
  18.9 2.2 %shard_map.70.raw.raw_in = f32[16,32,128]{2,1,0:T(8,128)S(1)} custom-call(f32[9,32,128]{2,1,0:T(8,128)S(1)} %collective-permute-done.x_odd, f32[9,32,128]{2,1,0:T(8,128)S(1)} %collective-permute-done.1.x_even, f32[144,128]{1,0:T(8,128)S(1)} %collective-permute-done.2.y_odd, f32[144,128]{1,0:T(8,128)S(1)} %collective-permute-done.3.y_even, ...), custom_call_target="tpu_custom_call" | custom-call | flops 10000000 | bytes 10000000 | tf_op jit(solution)/shard_map/pallas_call | solution.py:438
  21.2 0.7 %collective-permute-start.6 = (f32[4,32,128]{2,1,0:T(8,128)S(1)}, f32[4,32,128]{2,1,0:T(8,128)S(1)}, u32[]{:S(2)}, u32[]{:S(2)}) collective-permute-start(f32[4,32,128]{2,1,0:T(8,128)S(1)} %shard_map.71), channel_id=1, source_target_pairs={{8,16},{16,8},{9,17},{17,9},{10,18},{18,10},{11,19},{19,11},{12,20... | collective-permute-start | bytes 196616 | tf_op jit(solution)/shard_map/ppermute | solution.py:386
  21.8 0.5 %collective-permute-done.7.other = f32[8,128]{1,0:T(8,128)S(1)} collective-permute-done((f32[8,128]{1,0:T(8,128)S(1)}, f32[8,128]{1,0:T(8,128)S(1)}, u32[]{:S(2)}, u32[]{:S(2)}) %collective-permute-start.7) | collective-permute-done | bytes 4128 | tf_op jit(solution)/shard_map/ppermute | solution.py:390
  22.3 1.8 %collective-permute-start.8 = (f32[4,32,128]{2,1,0:T(8,128)S(1)}, f32[4,32,128]{2,1,0:T(8,128)S(1)}, u32[]{:S(2)}, u32[]{:S(2)}) collective-permute-start(f32[4,32,128]{2,1,0:T(8,128)S(1)} %get-tuple-element.31), channel_id=1, source_target_pairs={{0,8},{8,0},{16,24},{24,16},{1,9},{9,1},{17,25},{25,17},{2,10},{10... | collective-permute-start | bytes 196616 | tf_op jit(solution)/shard_map/ppermute | solution.py:380
  24.2 0.4 collective-permute-start.9
  24.5 3.3 %collective-permute-done.9.other = f32[8,128]{1,0:T(8,128)S(1)} collective-permute-done((f32[8,128]{1,0:T(8,128)S(1)}, f32[8,128]{1,0:T(8,128)S(1)}, u32[]{:S(2)}, u32[]{:S(2)}) %collective-permute-start.9) | collective-permute-done | bytes 4128 | tf_op jit(solution)/shard_map/ppermute | solution.py:390
  27.8 0.0 collective-permute-done.6.x_odd
  27.8 0.0 collective-permute-done.8.x_even
  27.8 1.1 %collective-permute-start.11 = (f32[88,128]{1,0:T(8,128)S(1)}, f32[88,128]{1,0:T(8,128)S(1)}, u32[]{:S(2)}, u32[]{:S(2)}) collective-permute-start(f32[88,128]{1,0:T(8,128)S(1)} %get-tuple-element.34), channel_id=1, source_target_pairs={{0,1},{1,0},{2,3},{3,2},{4,5},{5,4},{6,7},{7,6},{8,9},{9,8},{10,11... | collective-permute-start | bytes 135176 | tf_op jit(solution)/shard_map/ppermute | solution.py:380
  28.9 0.7 %collective-permute-start.10 = (f32[80,128]{1,0:T(8,128)S(1)}, f32[80,128]{1,0:T(8,128)S(1)}, u32[]{:S(2)}, u32[]{:S(2)}) collective-permute-start(f32[80,128]{1,0:T(8,128)S(1)} %get-tuple-element.33), channel_id=1, source_target_pairs={{1,2},{3,4},{5,6},{2,1},{4,3},{6,5},{9,10},{11,12},{13,14},{10,9},... | collective-permute-start | bytes 122888 | tf_op jit(solution)/shard_map/ppermute | solution.py:386
  29.6 2.4 %collective-permute-done.11.y_even = f32[88,128]{1,0:T(8,128)S(1)} collective-permute-done((f32[88,128]{1,0:T(8,128)S(1)}, f32[88,128]{1,0:T(8,128)S(1)}, u32[]{:S(2)}, u32[]{:S(2)}) %collective-permute-start.11) | collective-permute-done | bytes 45088 | tf_op jit(solution)/shard_map/ppermute | solution.py:380
  31.9 1.4 %collective-permute-start.12 = (f32[8,128]{1,0:T(8,128)S(1)}, f32[8,128]{1,0:T(8,128)S(1)}, u32[]{:S(2)}, u32[]{:S(2)}) collective-permute-start(f32[8,128]{1,0:T(8,128)S(1)} %slice_add_fusion), channel_id=1, source_target_pairs={{0,2},{1,3},{2,0},{3,1},{4,6},{5,7},{6,4},{7,5},{8,10},{9,11},{10,... | collective-permute-start | bytes 12296 | tf_op jit(solution)/shard_map/ppermute | solution.py:390
  33.4 2.2 %collective-permute-done.12 = f32[8,128]{1,0:T(8,128)S(1)} collective-permute-done((f32[8,128]{1,0:T(8,128)S(1)}, f32[8,128]{1,0:T(8,128)S(1)}, u32[]{:S(2)}, u32[]{:S(2)}) %collective-permute-start.12) | collective-permute-done | bytes 4128 | tf_op jit(solution)/shard_map/ppermute | solution.py:390
  35.5 0.0 collective-permute-start.13
  35.6 0.0 collective-permute-done.10.y_odd
  35.6 1.5 %shard_map.75.filtered = f32[16,32,128]{2,1,0:T(8,128)S(1)} custom-call(f32[4,32,128]{2,1,0:T(8,128)S(1)} %collective-permute-done.6.x_odd, f32[4,32,128]{2,1,0:T(8,128)S(1)} %collective-permute-done.8.x_even, f32[80,128]{1,0:T(8,128)S(1)} %collective-permute-done.10.y_odd, f32[88,128]{1,0:T(8,128)S(1)} %collective-permute-done.11.y_even, ...), custom_call_target="tpu_custom_call" | custom-call | flops 10000000 | bytes 10000000 | tf_op jit(solution)/shard_map/pallas_call | solution.py:456
  37.0 0.0 collective-permute-done.13.other
  37.0 0.9 %shard_map.76 = (f32[16,32,128]{2,1,0:T(8,128)}, f32[1,1]{1,0:T(1,128)}) custom-call(f32[16,32,128]{2,1,0:T(8,128)S(1)} %shard_map.75.filtered, f32[8,128]{1,0:T(8,128)S(1)} %add.7.mine, f32[8,128]{1,0:T(8,128)S(1)} %collective-permute-done.13.other), custom_call_target="tpu_custom_call" | custom-call | tf_op jit(solution)/shard_map/pallas_call | solution.py:462
  (6 shorter events, 0.1 us)
Async XLA Ops:
  2.0 10.0 %collective-permute-start = (f32[9,32,128]{2,1,0:T(8,128)S(1)}, f32[9,32,128]{2,1,0:T(8,128)S(1)}, u32[]{:S(2)}, u32[]{:S(2)}) collective-permute-start(f32[9,32,128]{2,1,0:T(8,128)S(1)} %get-tuple-element.20), channel_id=1, source_target_pairs={{8,16},{16,8},{9,17},{17,9},{10,18},{18,10},{11,19},{19,11},{12,20... | collective-permute-start | bytes 442376 | tf_op jit(solution)/shard_map/ppermute | solution.py:386
  2.6 9.4 %collective-permute-start.1 = (f32[9,32,128]{2,1,0:T(8,128)S(1)}, f32[9,32,128]{2,1,0:T(8,128)S(1)}, u32[]{:S(2)}, u32[]{:S(2)}) collective-permute-start(f32[9,32,128]{2,1,0:T(8,128)S(1)} %get-tuple-element.21), channel_id=1, source_target_pairs={{0,8},{8,0},{16,24},{24,16},{1,9},{9,1},{17,25},{25,17},{2,10},{10... | collective-permute-start | bytes 442376 | tf_op jit(solution)/shard_map/ppermute | solution.py:380
  7.0 10.1 %collective-permute-start.2 = (f32[144,128]{1,0:T(8,128)S(1)}, f32[144,128]{1,0:T(8,128)S(1)}, u32[]{:S(2)}, u32[]{:S(2)}) collective-permute-start(f32[144,128]{1,0:T(8,128)S(1)} %get-tuple-element.22), channel_id=1, source_target_pairs={{1,2},{3,4},{5,6},{2,1},{4,3},{6,5},{9,10},{11,12},{13,14},{10,9},... | collective-permute-start | bytes 221192 | tf_op jit(solution)/shard_map/ppermute | solution.py:386
  7.7 9.4 %collective-permute-start.3 = (f32[144,128]{1,0:T(8,128)S(1)}, f32[144,128]{1,0:T(8,128)S(1)}, u32[]{:S(2)}, u32[]{:S(2)}) collective-permute-start(f32[144,128]{1,0:T(8,128)S(1)} %get-tuple-element.23), channel_id=1, source_target_pairs={{0,1},{1,0},{2,3},{3,2},{4,5},{5,4},{6,7},{7,6},{8,9},{9,8},{10,11... | collective-permute-start | bytes 221192 | tf_op jit(solution)/shard_map/ppermute | solution.py:380
  12.0 6.9 %collective-permute-start.4 = (f32[16,128]{1,0:T(8,128)S(1)}, f32[16,128]{1,0:T(8,128)S(1)}, u32[]{:S(2)}, u32[]{:S(2)}) collective-permute-start(f32[16,128]{1,0:T(8,128)S(1)} %get-tuple-element.24), channel_id=1, source_target_pairs={{1,2},{3,4},{5,6},{2,1},{4,3},{6,5},{9,10},{11,12},{13,14},{10,9},... | collective-permute-start | bytes 24584 | tf_op jit(solution)/shard_map/ppermute | solution.py:386
  12.7 6.2 %collective-permute-start.5 = (f32[16,128]{1,0:T(8,128)S(1)}, f32[16,128]{1,0:T(8,128)S(1)}, u32[]{:S(2)}, u32[]{:S(2)}) collective-permute-start(f32[16,128]{1,0:T(8,128)S(1)} %get-tuple-element.25), channel_id=1, source_target_pairs={{0,1},{1,0},{2,3},{3,2},{4,5},{5,4},{6,7},{7,6},{8,9},{9,8},{10,11... | collective-permute-start | bytes 24584 | tf_op jit(solution)/shard_map/ppermute | solution.py:380
  17.8 4.6 %collective-permute-start.7 = (f32[8,128]{1,0:T(8,128)S(1)}, f32[8,128]{1,0:T(8,128)S(1)}, u32[]{:S(2)}, u32[]{:S(2)}) collective-permute-start(f32[8,128]{1,0:T(8,128)S(1)} %shard_map.72.mine), channel_id=1, source_target_pairs={{0,4},{1,5},{2,6},{3,7},{4,0},{5,1},{6,2},{7,3},{8,12},{9,13},{10,... | collective-permute-start | bytes 12296 | tf_op jit(solution)/shard_map/ppermute | solution.py:390
  21.2 6.6 %collective-permute-start.6 = (f32[4,32,128]{2,1,0:T(8,128)S(1)}, f32[4,32,128]{2,1,0:T(8,128)S(1)}, u32[]{:S(2)}, u32[]{:S(2)}) collective-permute-start(f32[4,32,128]{2,1,0:T(8,128)S(1)} %shard_map.71), channel_id=1, source_target_pairs={{8,16},{16,8},{9,17},{17,9},{10,18},{18,10},{11,19},{19,11},{12,20... | collective-permute-start | bytes 196616 | tf_op jit(solution)/shard_map/ppermute | solution.py:386
  22.3 5.4 %collective-permute-start.8 = (f32[4,32,128]{2,1,0:T(8,128)S(1)}, f32[4,32,128]{2,1,0:T(8,128)S(1)}, u32[]{:S(2)}, u32[]{:S(2)}) collective-permute-start(f32[4,32,128]{2,1,0:T(8,128)S(1)} %get-tuple-element.31), channel_id=1, source_target_pairs={{0,8},{8,0},{16,24},{24,16},{1,9},{9,1},{17,25},{25,17},{2,10},{10... | collective-permute-start | bytes 196616 | tf_op jit(solution)/shard_map/ppermute | solution.py:380
  24.2 3.6 %collective-permute-start.9 = (f32[8,128]{1,0:T(8,128)S(1)}, f32[8,128]{1,0:T(8,128)S(1)}, u32[]{:S(2)}, u32[]{:S(2)}) collective-permute-start(f32[8,128]{1,0:T(8,128)S(1)} %get-tuple-element.32.mine), channel_id=1, source_target_pairs={{0,16},{8,24},{16,0},{24,8},{1,17},{9,25},{17,1},{25,9},{2,18},{10... | collective-permute-start | bytes 12296 | tf_op jit(solution)/shard_map/ppermute | solution.py:390
  27.8 4.1 %collective-permute-start.11 = (f32[88,128]{1,0:T(8,128)S(1)}, f32[88,128]{1,0:T(8,128)S(1)}, u32[]{:S(2)}, u32[]{:S(2)}) collective-permute-start(f32[88,128]{1,0:T(8,128)S(1)} %get-tuple-element.34), channel_id=1, source_target_pairs={{0,1},{1,0},{2,3},{3,2},{4,5},{5,4},{6,7},{7,6},{8,9},{9,8},{10,11... | collective-permute-start | bytes 135176 | tf_op jit(solution)/shard_map/ppermute | solution.py:380
  28.9 6.6 %collective-permute-start.10 = (f32[80,128]{1,0:T(8,128)S(1)}, f32[80,128]{1,0:T(8,128)S(1)}, u32[]{:S(2)}, u32[]{:S(2)}) collective-permute-start(f32[80,128]{1,0:T(8,128)S(1)} %get-tuple-element.33), channel_id=1, source_target_pairs={{1,2},{3,4},{5,6},{2,1},{4,3},{6,5},{9,10},{11,12},{13,14},{10,9},... | collective-permute-start | bytes 122888 | tf_op jit(solution)/shard_map/ppermute | solution.py:386
  31.9 3.6 %collective-permute-start.12 = (f32[8,128]{1,0:T(8,128)S(1)}, f32[8,128]{1,0:T(8,128)S(1)}, u32[]{:S(2)}, u32[]{:S(2)}) collective-permute-start(f32[8,128]{1,0:T(8,128)S(1)} %slice_add_fusion), channel_id=1, source_target_pairs={{0,2},{1,3},{2,0},{3,1},{4,6},{5,7},{6,4},{7,5},{8,10},{9,11},{10,... | collective-permute-start | bytes 12296 | tf_op jit(solution)/shard_map/ppermute | solution.py:390
  35.5 1.5 %collective-permute-start.13 = (f32[8,128]{1,0:T(8,128)S(1)}, f32[8,128]{1,0:T(8,128)S(1)}, u32[]{:S(2)}, u32[]{:S(2)}) collective-permute-start(f32[8,128]{1,0:T(8,128)S(1)} %add.7.mine), channel_id=1, source_target_pairs={{0,8},{8,0},{16,24},{24,16},{1,9},{9,1},{17,25},{25,17},{2,10},{10... | collective-permute-start | bytes 12296 | tf_op jit(solution)/shard_map/ppermute | solution.py:390

commit v13 on v12

--- a/solution.py
+++ b/solution.py
@@ -182,9 +182,47 @@
     planes_loop(0, size_x, 4, step)
 
 
+def inverted(d):
+    first_guess = pl.reciprocal(d, approx=True)
+    return first_guess * (2.0 - d * first_guess)
+
+
+def harmonic(a, b):
+    return 2.0 * a * b * inverted(jnp.maximum(a + b, 0.25))
+
+
+def weigh(permit, face_x, face_y, face_z, inverse, x, k, n):
+    p = permit[pl.ds(x, n)]
+    span = pl.ds(k, n)
+    is_last = lax.broadcasted_iota(jnp.int32, (1,) + p.shape[1:], 2) == p.shape[2] - 1
+    fy = harmonic(p, shift(p, -1, 1))
+    fz = jnp.where(is_last, 0.0, harmonic(p, shift(p, -1, 2)))
+    face_y[span] = fy
+    face_z[span] = fz
+    total = screen + face_x[span] + face_x[pl.ds(k + 1, n)] + fy + shift(fy, 1, 1) + fz + shift(fz, 1, 2)
+    inverse[span] = jnp.where(p > 20.0, 0.0, inverted(total))
+
+
+def inner_weights(y_odd, y_even, density, labels, face_x, face_y, face_z, inverse, permit):
+    size_x, size_y, _ = density.shape
+
+    def fill(x, n):
+        permit[pl.ds(x, n), pl.ds(0, size_y)] = material(density[pl.ds(x, n)], labels[pl.ds(x, n)])
+
+    planes_loop(0, size_x, 8, fill)
+    found = [part for part in segments(WIDTHS, size_x, beyond=False)[0] if part[0] == 0]
+    unpack_rows((permit,), (0,), found, y_even, y_odd, size_y)
+
+    def faces(x, n):
+        face_x[pl.ds(x, n)] = harmonic(permit[pl.ds(x, n)], permit[pl.ds(x + 1, n)])
+
+    planes_loop(0, size_x - 1, 5, faces)
+    planes_loop(0, size_x - 2, 7, lambda k, n: weigh(permit, face_x, face_y, face_z, inverse, k + 1, k, n))
+
+
 def adjoint_part(x_odd, x_even, y_odd, y_even, corner_odd, corner_even, density, labels, adjoint_start, adjoint_source, potential,
-                 raw_out,
-                 permit, start, source, poten, face_x, face_y, face_z, inverse, first, second):
+                 inner_x, inner_y, inner_z, inner_inverse, raw_out,
+                 permit, start, source, poten, edge_x, edge_y, edge_z, edge_inverse, first, second):
     size_x, size_y, size_z = density.shape
     starts, _ = plane_starts(WIDTHS)
     fields = (permit, start, source, poten)
@@ -209,47 +247,40 @@
     is_first = lane == 0
     is_last = lane == size_z - 1
 
-    def inverted(d):
-        first_guess = pl.reciprocal(d, approx=True)
-        return first_guess * (2.0 - d * first_guess)
-
-    def harmonic(a, b):
-        return 2.0 * a * b * inverted(jnp.maximum(a + b, 0.25))
-
-    def faces_x(x, n):
-        face_x[pl.ds(x, n)] = harmonic(permit[pl.ds(x, n)], permit[pl.ds(x + 1, n)])
-
-    planes_loop(0, size_x + 5, 7, faces_x)
-
-    def weigh(x, n):
-        span = pl.ds(x, n)
-        p = permit[pl.ds(x + 1, n)]
-        fy = harmonic(p, shift(p, -1, 1))
-        fz = jnp.where(is_last, 0.0, harmonic(p, shift(p, -1, 2)))
-        face_y[span] = fy
-        face_z[span] = fz
-        total = screen + face_x[span] + face_x[pl.ds(x + 1, n)] + fy + shift(fy, 1, 1) + fz + shift(fz, 1, 2)
-        inverse[span] = jnp.where(p > 20.0, 0.0, inverted(total))
-
-    planes_loop(0, size_x + 4, 10, weigh)
-
-    def relax(x, n, a, a_low, a_high):
-        span = pl.ds(x, n)
+    top = size_x + 1
+    for side, x in ((0, 0), (1, top)):
+        edge_x[side] = harmonic(permit[pl.ds(x, 4)], permit[pl.ds(x + 1, 4)])
+        weigh(permit, edge_x.at[side], edge_y.at[side], edge_z.at[side], edge_inverse.at[side], x + 1, 0, 3)
+    inner = (inner_x, inner_y, inner_z, inner_inverse)
+    low_edge, high_edge = (
+        tuple(ref.at[side] for ref in (edge_x, edge_y, edge_z, edge_inverse)) for side in (0, 1)
+    )
+
+    def relax(x, n, field, at, weights, base):
+        face_x, face_y, face_z, inverse = weights
+        a = field[pl.ds(at, n)]
+        k = x - base
+        span = pl.ds(k, n)
         fy, fz = face_y[span], face_z[span]
-        total = source[span] + face_x[pl.ds(x + 1, n)] * a_high + face_x[span] * a_low
+        total = source[pl.ds(x, n)] + face_x[pl.ds(k + 1, n)] * field[pl.ds(at + 1, n)]
+        total = total + face_x[span] * field[pl.ds(at - 1, n)]
         total = total + fy * shift(a, -1, 1) + shift(fy * a, 1, 1)
         total = total + fz * shift(a, -1, 2) + shift(fz * a, 1, 2)
         return total * inverse[span]
 
-    def sweep_one(x, n):
-        first[pl.ds(x, n)] = relax(x, n, start[pl.ds(x + 1, n)], start[pl.ds(x, n)], start[pl.ds(x + 2, n)])
-
-    planes_loop(0, size_x + 4, 10, sweep_one)
-
-    def sweep_two(x, n):
-        second[pl.ds(x, n)] = relax(x + 1, n, first[pl.ds(x + 1, n)], first[pl.ds(x, n)], first[pl.ds(x + 2, n)])
-
-    planes_loop(0, size_x + 2, 9, sweep_two)
+    def sweep(out, field, by, skip):
+        def step(weights, base):
+            def put(x, n):
+                out[pl.ds(x - skip, n)] = relax(x, n, field, x + by, weights, base)
+
+            return put
+
+        step(low_edge, 0)(skip, 3 - skip)
+        planes_loop(3, top, 7, step(inner, 3))
+        step(high_edge, top)(top, 3 - skip)
+
+    sweep(first, start, 1, 0)
+    sweep(second, first, 0, 1)
 
     def finish(x, n):
         span = pl.ds(x, n)
@@ -435,12 +466,21 @@
     energy = call(energy_part, f32(8, size_z), [room(2)])(x_odd, x_even, y_odd, y_even, own[0], own[1], own[4])
     mine, other = doubling(energy, y_bits[1:])
     face = f32(FILTER_SWEEPS, size_y, size_z)
+    inner = call(
+        inner_weights,
+        (f32(size_x - 1, wide, size_z),) + (f32(size_x - 2, wide, size_z),) * 3,
+        [room(0)],
+    )(y_odd, y_even, own[0], own[1])
+
+    def edges(planes):
+        return pltpu.VMEM((2, planes, wide, size_z), jnp.float32)
+
     raw = call(
         adjoint_part,
         f32(*shape),
-        [room(6), room(6), room(4), room(2), room(5), room(4), room(4), room(4), room(4), room(2)],
+        [room(6), room(6), room(4), room(2), edges(4), edges(3), edges(3), edges(3), room(4), room(2)],
         cost=10000000,
-    )(x_odd, x_even, y_odd, y_even, corner_odd, corner_even, *own)
+    )(x_odd, x_even, y_odd, y_even, corner_odd, corner_even, *own, *inner)
 
     x_odd = swap_odd(call(pack_raw_x_odd, face)(raw), "gx")
     even, energy = call(pack_raw_x_even, (face, f32(8, size_z)))(raw, mine, other)

time: 38.2 us -> 38.4 us (level)
    pallas_call x1 -> x2, Pallas kernels: 2.23 us -> 2.39 us  [the longest x1 1.77 us: shards(): call(adjoint_part, f32(*shape), [room(6), room(6), room(4), room(2), edge...]
where the time goes in v13:
time: 38.4 us; the launch traced here: 38.1 us
  starting transfers between devices  22.4 us (58%)
  waiting for transfers between devices  8.11 us (21%)
  Pallas kernels  6.81 us (18%)
  between operations  0.77 us (2%)
    ppermute x5, starting transfers between devices, swap_even(): lax.ppermute(value, axis, [(i, i ^ 1) for i in range(lax.axis_size(axis))])  16.2 us
    ppermute x4, waiting for transfers between devices, partner(): lax.ppermute(value, axis, [(i, i ^ bit) for i in range(lax.axis_size(axis...  5.73 us
    ppermute x5, starting transfers between devices, swap_odd(): return lax.ppermute(value, axis, up + [(b, a) for a, b in up])  3.3 us
    ppermute x4, starting transfers between devices, partner(): lax.ppermute(value, axis, [(i, i ^ bit) for i in range(lax.axis_size(axis...  2.93 us
    ppermute x5, waiting for transfers between devices, swap_even(): lax.ppermute(value, axis, [(i, i ^ 1) for i in range(lax.axis_size(axis))])  2.36 us
    pallas_call x1, Pallas kernels, shards(): call(adjoint_part, f32(*shape), [room(6), room(6), room(4), room(2), edge...  1.77 us
    pallas_call x1, Pallas kernels, shards(): call(filter_part, f32(*shape), [room(2 * FILTER_SWEEPS)] * 3, cost=10000000)  1.47 us
    pallas_call x1, Pallas kernels, shards(): pl.pallas_call(pack_own, out_shape=(f32(planes, size_y, size_z),) * 2 + (...  1.33 us
  transfers between devices with their start and end apart: 14, of which 4 were waited for; matrix products, arithmetic and copies ran while one was open for 0% of the time, Pallas kernels for 12%

profile of v13, /device:TPU:0, one launch (start us, length us, event | category | flops | bytes accessed | tf_op | source)
XLA Modules:
  0.0 38.1 jit_solution(9486607326700877574)
XLA Ops:
  0.6 1.3 %shard_map.68 = (f32[9,32,128]{2,1,0:T(8,128)S(1)}, f32[9,32,128]{2,1,0:T(8,128)S(1)}, f32[144,128]{1,0:T(8,128)S(1)}, f32[144,128]{1,0:T(8,128)S(1)}, f32[16,32...) custom-call(f32[16,32,128]{2,1,0:T(8,128)} %refs_0_.1, ...), custom_call_target="tpu_custom_call" | custom-call | tf_op jit(solution)/shard_map/pallas_call | solution.py:445
  2.0 0.7 %collective-permute-start = (f32[9,32,128]{2,1,0:T(8,128)S(1)}, f32[9,32,128]{2,1,0:T(8,128)S(1)}, u32[]{:S(2)}, u32[]{:S(2)}) collective-permute-start(f32[9,32,128]{2,1,0:T(8,128)S(1)} %get-tuple-element.24), channel_id=1, source_target_pairs={{8,16},{16,8},{9,17},{17,9},{10,18},{18,10},{11,19},{19,11},{12,20... | collective-permute-start | bytes 442376 | tf_op jit(solution)/shard_map/ppermute | solution.py:417
  2.6 4.4 %collective-permute-start.1 = (f32[9,32,128]{2,1,0:T(8,128)S(1)}, f32[9,32,128]{2,1,0:T(8,128)S(1)}, u32[]{:S(2)}, u32[]{:S(2)}) collective-permute-start(f32[9,32,128]{2,1,0:T(8,128)S(1)} %get-tuple-element.25), channel_id=1, source_target_pairs={{0,8},{8,0},{16,24},{24,16},{1,9},{9,1},{17,25},{25,17},{2,10},{10... | collective-permute-start | bytes 442376 | tf_op jit(solution)/shard_map/ppermute | solution.py:411
  7.0 0.7 %collective-permute-start.2 = (f32[144,128]{1,0:T(8,128)S(1)}, f32[144,128]{1,0:T(8,128)S(1)}, u32[]{:S(2)}, u32[]{:S(2)}) collective-permute-start(f32[144,128]{1,0:T(8,128)S(1)} %get-tuple-element.26), channel_id=1, source_target_pairs={{1,2},{3,4},{5,6},{2,1},{4,3},{6,5},{9,10},{11,12},{13,14},{10,9},... | collective-permute-start | bytes 221192 | tf_op jit(solution)/shard_map/ppermute | solution.py:417
  7.7 4.3 %collective-permute-start.3 = (f32[144,128]{1,0:T(8,128)S(1)}, f32[144,128]{1,0:T(8,128)S(1)}, u32[]{:S(2)}, u32[]{:S(2)}) collective-permute-start(f32[144,128]{1,0:T(8,128)S(1)} %get-tuple-element.27), channel_id=1, source_target_pairs={{0,1},{1,0},{2,3},{3,2},{4,5},{5,4},{6,7},{7,6},{8,9},{9,8},{10,11... | collective-permute-start | bytes 221192 | tf_op jit(solution)/shard_map/ppermute | solution.py:411
  12.0 0.0 collective-permute-done.x_odd
  12.0 0.0 collective-permute-done.1.x_even
  12.0 0.7 %collective-permute-start.4 = (f32[16,128]{1,0:T(8,128)S(1)}, f32[16,128]{1,0:T(8,128)S(1)}, u32[]{:S(2)}, u32[]{:S(2)}) collective-permute-start(f32[16,128]{1,0:T(8,128)S(1)} %get-tuple-element.28), channel_id=1, source_target_pairs={{1,2},{3,4},{5,6},{2,1},{4,3},{6,5},{9,10},{11,12},{13,14},{10,9},... | collective-permute-start | bytes 24584 | tf_op jit(solution)/shard_map/ppermute | solution.py:417
  12.7 4.4 %collective-permute-start.5 = (f32[16,128]{1,0:T(8,128)S(1)}, f32[16,128]{1,0:T(8,128)S(1)}, u32[]{:S(2)}, u32[]{:S(2)}) collective-permute-start(f32[16,128]{1,0:T(8,128)S(1)} %get-tuple-element.29), channel_id=1, source_target_pairs={{0,1},{1,0},{2,3},{3,2},{4,5},{5,4},{6,7},{7,6},{8,9},{9,8},{10,11... | collective-permute-start | bytes 24584 | tf_op jit(solution)/shard_map/ppermute | solution.py:411
  17.1 0.0 collective-permute-done.2.y_odd
  17.1 0.0 collective-permute-done.3.y_even
  17.1 0.7 %shard_map.73.mine = f32[8,128]{1,0:T(8,128)S(1)} custom-call(f32[9,32,128]{2,1,0:T(8,128)S(1)} %collective-permute-done.x_odd, f32[9,32,128]{2,1,0:T(8,128)S(1)} %collective-permute-done.1.x_even, f32[144,128]{1,0:T(8,128)S(1)} %collective-permute-done.2.y_odd, f32[144,128]{1,0:T(8,128)S(1)} %collective-permute-done.3.y_even, ...), custom_call_target="tpu_custom_call" | custom-call | flops 10000 | bytes 10000 | tf_op jit(solution)/shard_map/pallas_call | solution.py:466
  17.8 1.1 %collective-permute-start.7 = (f32[8,128]{1,0:T(8,128)S(1)}, f32[8,128]{1,0:T(8,128)S(1)}, u32[]{:S(2)}, u32[]{:S(2)}) collective-permute-start(f32[8,128]{1,0:T(8,128)S(1)} %shard_map.73.mine), channel_id=1, source_target_pairs={{0,4},{1,5},{2,6},{3,7},{4,0},{5,1},{6,2},{7,3},{8,12},{9,13},{10,... | collective-permute-start | bytes 12296 | tf_op jit(solution)/shard_map/ppermute | solution.py:421
  18.9 0.6 %shard_map.70 = (f32[15,40,128]{2,1,0:T(8,128)S(1)}, f32[14,40,128]{2,1,0:T(8,128)S(1)}, f32[14,40,128]{2,1,0:T(8,128)S(1)}, f32[14,40,128]{2,1,0:T(8,128)S(1)}) custom-call(f32[144,128]{1,0:T(8,128)S(1)} %collective-permute-done.2.y_odd, f32[144,128]{1,0:T(8,128)S(1)} %collective-permute-done.3.y_even, f32[16,32,128]{2,1,0:T(8,128)S(1)} %get-tuple-element.30.density, ...), custom_call_target="tpu_custom_call" | custom-call | flops 10000 | bytes 10000 | tf_op jit(solution)/shard_map/pallas_call | solution.py:469
  19.5 0.0 collective-permute-done.4.corner_odd
  19.5 0.0 collective-permute-done.5.corner_even
  19.6 1.8 %shard_map.71.raw.raw_in = f32[16,32,128]{2,1,0:T(8,128)S(1)} custom-call(f32[9,32,128]{2,1,0:T(8,128)S(1)} %collective-permute-done.x_odd, f32[9,32,128]{2,1,0:T(8,128)S(1)} %collective-permute-done.1.x_even, f32[144,128]{1,0:T(8,128)S(1)} %collective-permute-done.2.y_odd, f32[144,128]{1,0:T(8,128)S(1)} %collective-permute-done.3.y_even, ...), custom_call_target="tpu_custom_call" | custom-call | flops 10000000 | bytes 10000000 | tf_op jit(solution)/shard_map/pallas_call | solution.py:478
  21.4 0.7 %collective-permute-start.6 = (f32[4,32,128]{2,1,0:T(8,128)S(1)}, f32[4,32,128]{2,1,0:T(8,128)S(1)}, u32[]{:S(2)}, u32[]{:S(2)}) collective-permute-start(f32[4,32,128]{2,1,0:T(8,128)S(1)} %shard_map.72), channel_id=1, source_target_pairs={{8,16},{16,8},{9,17},{17,9},{10,18},{18,10},{11,19},{19,11},{12,20... | collective-permute-start | bytes 196616 | tf_op jit(solution)/shard_map/ppermute | solution.py:417
  22.0 0.3 collective-permute-done.7.other
  22.3 2.0 %collective-permute-start.8 = (f32[4,32,128]{2,1,0:T(8,128)S(1)}, f32[4,32,128]{2,1,0:T(8,128)S(1)}, u32[]{:S(2)}, u32[]{:S(2)}) collective-permute-start(f32[4,32,128]{2,1,0:T(8,128)S(1)} %get-tuple-element.39), channel_id=1, source_target_pairs={{0,8},{8,0},{16,24},{24,16},{1,9},{9,1},{17,25},{25,17},{2,10},{10... | collective-permute-start | bytes 196616 | tf_op jit(solution)/shard_map/ppermute | solution.py:411
  24.4 0.4 collective-permute-start.9
  24.7 3.3 %collective-permute-done.9.other = f32[8,128]{1,0:T(8,128)S(1)} collective-permute-done((f32[8,128]{1,0:T(8,128)S(1)}, f32[8,128]{1,0:T(8,128)S(1)}, u32[]{:S(2)}, u32[]{:S(2)}) %collective-permute-start.9) | collective-permute-done | bytes 4128 | tf_op jit(solution)/shard_map/ppermute | solution.py:421
  28.0 0.0 collective-permute-done.6.x_odd
  28.0 0.0 collective-permute-done.8.x_even
  28.0 1.1 %collective-permute-start.11 = (f32[88,128]{1,0:T(8,128)S(1)}, f32[88,128]{1,0:T(8,128)S(1)}, u32[]{:S(2)}, u32[]{:S(2)}) collective-permute-start(f32[88,128]{1,0:T(8,128)S(1)} %get-tuple-element.42), channel_id=1, source_target_pairs={{0,1},{1,0},{2,3},{3,2},{4,5},{5,4},{6,7},{7,6},{8,9},{9,8},{10,11... | collective-permute-start | bytes 135176 | tf_op jit(solution)/shard_map/ppermute | solution.py:411
  29.1 0.7 %collective-permute-start.10 = (f32[80,128]{1,0:T(8,128)S(1)}, f32[80,128]{1,0:T(8,128)S(1)}, u32[]{:S(2)}, u32[]{:S(2)}) collective-permute-start(f32[80,128]{1,0:T(8,128)S(1)} %get-tuple-element.41), channel_id=1, source_target_pairs={{1,2},{3,4},{5,6},{2,1},{4,3},{6,5},{9,10},{11,12},{13,14},{10,9},... | collective-permute-start | bytes 122888 | tf_op jit(solution)/shard_map/ppermute | solution.py:417
  29.8 2.4 %collective-permute-done.11.y_even = f32[88,128]{1,0:T(8,128)S(1)} collective-permute-done((f32[88,128]{1,0:T(8,128)S(1)}, f32[88,128]{1,0:T(8,128)S(1)}, u32[]{:S(2)}, u32[]{:S(2)}) %collective-permute-start.11) | collective-permute-done | bytes 45088 | tf_op jit(solution)/shard_map/ppermute | solution.py:411
  32.1 1.4 %collective-permute-start.12 = (f32[8,128]{1,0:T(8,128)S(1)}, f32[8,128]{1,0:T(8,128)S(1)}, u32[]{:S(2)}, u32[]{:S(2)}) collective-permute-start(f32[8,128]{1,0:T(8,128)S(1)} %slice_add_fusion), channel_id=1, source_target_pairs={{0,2},{1,3},{2,0},{3,1},{4,6},{5,7},{6,4},{7,5},{8,10},{9,11},{10,... | collective-permute-start | bytes 12296 | tf_op jit(solution)/shard_map/ppermute | solution.py:421
  33.6 2.2 %collective-permute-done.12 = f32[8,128]{1,0:T(8,128)S(1)} collective-permute-done((f32[8,128]{1,0:T(8,128)S(1)}, f32[8,128]{1,0:T(8,128)S(1)}, u32[]{:S(2)}, u32[]{:S(2)}) %collective-permute-start.12) | collective-permute-done | bytes 4128 | tf_op jit(solution)/shard_map/ppermute | solution.py:421
  35.7 0.0 collective-permute-start.13
  35.7 0.0 collective-permute-done.10.y_odd
  35.7 1.5 %shard_map.76.filtered = f32[16,32,128]{2,1,0:T(8,128)S(1)} custom-call(f32[4,32,128]{2,1,0:T(8,128)S(1)} %collective-permute-done.6.x_odd, f32[4,32,128]{2,1,0:T(8,128)S(1)} %collective-permute-done.8.x_even, f32[80,128]{1,0:T(8,128)S(1)} %collective-permute-done.10.y_odd, f32[88,128]{1,0:T(8,128)S(1)} %collective-permute-done.11.y_even, ...), custom_call_target="tpu_custom_call" | custom-call | flops 10000000 | bytes 10000000 | tf_op jit(solution)/shard_map/pallas_call | solution.py:496
  37.2 0.0 collective-permute-done.13.other
  37.2 0.9 %shard_map.77 = (f32[16,32,128]{2,1,0:T(8,128)}, f32[1,1]{1,0:T(1,128)}) custom-call(f32[16,32,128]{2,1,0:T(8,128)S(1)} %shard_map.76.filtered, f32[8,128]{1,0:T(8,128)S(1)} %add.7.mine, f32[8,128]{1,0:T(8,128)S(1)} %collective-permute-done.13.other), custom_call_target="tpu_custom_call" | custom-call | tf_op jit(solution)/shard_map/pallas_call | solution.py:502
  (6 shorter events, 0.1 us)
Async XLA Ops:
  2.0 10.0 %collective-permute-start = (f32[9,32,128]{2,1,0:T(8,128)S(1)}, f32[9,32,128]{2,1,0:T(8,128)S(1)}, u32[]{:S(2)}, u32[]{:S(2)}) collective-permute-start(f32[9,32,128]{2,1,0:T(8,128)S(1)} %get-tuple-element.24), channel_id=1, source_target_pairs={{8,16},{16,8},{9,17},{17,9},{10,18},{18,10},{11,19},{19,11},{12,20... | collective-permute-start | bytes 442376 | tf_op jit(solution)/shard_map/ppermute | solution.py:417
  2.6 9.4 %collective-permute-start.1 = (f32[9,32,128]{2,1,0:T(8,128)S(1)}, f32[9,32,128]{2,1,0:T(8,128)S(1)}, u32[]{:S(2)}, u32[]{:S(2)}) collective-permute-start(f32[9,32,128]{2,1,0:T(8,128)S(1)} %get-tuple-element.25), channel_id=1, source_target_pairs={{0,8},{8,0},{16,24},{24,16},{1,9},{9,1},{17,25},{25,17},{2,10},{10... | collective-permute-start | bytes 442376 | tf_op jit(solution)/shard_map/ppermute | solution.py:411
  7.0 10.1 %collective-permute-start.2 = (f32[144,128]{1,0:T(8,128)S(1)}, f32[144,128]{1,0:T(8,128)S(1)}, u32[]{:S(2)}, u32[]{:S(2)}) collective-permute-start(f32[144,128]{1,0:T(8,128)S(1)} %get-tuple-element.26), channel_id=1, source_target_pairs={{1,2},{3,4},{5,6},{2,1},{4,3},{6,5},{9,10},{11,12},{13,14},{10,9},... | collective-permute-start | bytes 221192 | tf_op jit(solution)/shard_map/ppermute | solution.py:417
  7.7 9.4 %collective-permute-start.3 = (f32[144,128]{1,0:T(8,128)S(1)}, f32[144,128]{1,0:T(8,128)S(1)}, u32[]{:S(2)}, u32[]{:S(2)}) collective-permute-start(f32[144,128]{1,0:T(8,128)S(1)} %get-tuple-element.27), channel_id=1, source_target_pairs={{0,1},{1,0},{2,3},{3,2},{4,5},{5,4},{6,7},{7,6},{8,9},{9,8},{10,11... | collective-permute-start | bytes 221192 | tf_op jit(solution)/shard_map/ppermute | solution.py:411
  12.0 7.5 %collective-permute-start.4 = (f32[16,128]{1,0:T(8,128)S(1)}, f32[16,128]{1,0:T(8,128)S(1)}, u32[]{:S(2)}, u32[]{:S(2)}) collective-permute-start(f32[16,128]{1,0:T(8,128)S(1)} %get-tuple-element.28), channel_id=1, source_target_pairs={{1,2},{3,4},{5,6},{2,1},{4,3},{6,5},{9,10},{11,12},{13,14},{10,9},... | collective-permute-start | bytes 24584 | tf_op jit(solution)/shard_map/ppermute | solution.py:417
  12.7 6.8 %collective-permute-start.5 = (f32[16,128]{1,0:T(8,128)S(1)}, f32[16,128]{1,0:T(8,128)S(1)}, u32[]{:S(2)}, u32[]{:S(2)}) collective-permute-start(f32[16,128]{1,0:T(8,128)S(1)} %get-tuple-element.29), channel_id=1, source_target_pairs={{0,1},{1,0},{2,3},{3,2},{4,5},{5,4},{6,7},{7,6},{8,9},{9,8},{10,11... | collective-permute-start | bytes 24584 | tf_op jit(solution)/shard_map/ppermute | solution.py:411
  17.8 4.6 %collective-permute-start.7 = (f32[8,128]{1,0:T(8,128)S(1)}, f32[8,128]{1,0:T(8,128)S(1)}, u32[]{:S(2)}, u32[]{:S(2)}) collective-permute-start(f32[8,128]{1,0:T(8,128)S(1)} %shard_map.73.mine), channel_id=1, source_target_pairs={{0,4},{1,5},{2,6},{3,7},{4,0},{5,1},{6,2},{7,3},{8,12},{9,13},{10,... | collective-permute-start | bytes 12296 | tf_op jit(solution)/shard_map/ppermute | solution.py:421
  21.4 6.6 %collective-permute-start.6 = (f32[4,32,128]{2,1,0:T(8,128)S(1)}, f32[4,32,128]{2,1,0:T(8,128)S(1)}, u32[]{:S(2)}, u32[]{:S(2)}) collective-permute-start(f32[4,32,128]{2,1,0:T(8,128)S(1)} %shard_map.72), channel_id=1, source_target_pairs={{8,16},{16,8},{9,17},{17,9},{10,18},{18,10},{11,19},{19,11},{12,20... | collective-permute-start | bytes 196616 | tf_op jit(solution)/shard_map/ppermute | solution.py:417
  22.3 5.6 %collective-permute-start.8 = (f32[4,32,128]{2,1,0:T(8,128)S(1)}, f32[4,32,128]{2,1,0:T(8,128)S(1)}, u32[]{:S(2)}, u32[]{:S(2)}) collective-permute-start(f32[4,32,128]{2,1,0:T(8,128)S(1)} %get-tuple-element.39), channel_id=1, source_target_pairs={{0,8},{8,0},{16,24},{24,16},{1,9},{9,1},{17,25},{25,17},{2,10},{10... | collective-permute-start | bytes 196616 | tf_op jit(solution)/shard_map/ppermute | solution.py:411
  24.4 3.6 %collective-permute-start.9 = (f32[8,128]{1,0:T(8,128)S(1)}, f32[8,128]{1,0:T(8,128)S(1)}, u32[]{:S(2)}, u32[]{:S(2)}) collective-permute-start(f32[8,128]{1,0:T(8,128)S(1)} %get-tuple-element.40.mine), channel_id=1, source_target_pairs={{0,16},{8,24},{16,0},{24,8},{1,17},{9,25},{17,1},{25,9},{2,18},{10... | collective-permute-start | bytes 12296 | tf_op jit(solution)/shard_map/ppermute | solution.py:421
  28.0 4.1 %collective-permute-start.11 = (f32[88,128]{1,0:T(8,128)S(1)}, f32[88,128]{1,0:T(8,128)S(1)}, u32[]{:S(2)}, u32[]{:S(2)}) collective-permute-start(f32[88,128]{1,0:T(8,128)S(1)} %get-tuple-element.42), channel_id=1, source_target_pairs={{0,1},{1,0},{2,3},{3,2},{4,5},{5,4},{6,7},{7,6},{8,9},{9,8},{10,11... | collective-permute-start | bytes 135176 | tf_op jit(solution)/shard_map/ppermute | solution.py:411
  29.1 6.6 %collective-permute-start.10 = (f32[80,128]{1,0:T(8,128)S(1)}, f32[80,128]{1,0:T(8,128)S(1)}, u32[]{:S(2)}, u32[]{:S(2)}) collective-permute-start(f32[80,128]{1,0:T(8,128)S(1)} %get-tuple-element.41), channel_id=1, source_target_pairs={{1,2},{3,4},{5,6},{2,1},{4,3},{6,5},{9,10},{11,12},{13,14},{10,9},... | collective-permute-start | bytes 122888 | tf_op jit(solution)/shard_map/ppermute | solution.py:417
  32.1 3.6 %collective-permute-start.12 = (f32[8,128]{1,0:T(8,128)S(1)}, f32[8,128]{1,0:T(8,128)S(1)}, u32[]{:S(2)}, u32[]{:S(2)}) collective-permute-start(f32[8,128]{1,0:T(8,128)S(1)} %slice_add_fusion), channel_id=1, source_target_pairs={{0,2},{1,3},{2,0},{3,1},{4,6},{5,7},{6,4},{7,5},{8,10},{9,11},{10,... | collective-permute-start | bytes 12296 | tf_op jit(solution)/shard_map/ppermute | solution.py:421
  35.7 1.5 %collective-permute-start.13 = (f32[8,128]{1,0:T(8,128)S(1)}, f32[8,128]{1,0:T(8,128)S(1)}, u32[]{:S(2)}, u32[]{:S(2)}) collective-permute-start(f32[8,128]{1,0:T(8,128)S(1)} %add.7.mine), channel_id=1, source_target_pairs={{0,8},{8,0},{16,24},{24,16},{1,9},{9,1},{17,25},{25,17},{2,10},{10... | collective-permute-start | bytes 12296 | tf_op jit(solution)/shard_map/ppermute | solution.py:421

commit v14 on v12

--- a/solution.py
+++ b/solution.py
@@ -151,7 +151,7 @@
     field[pl.ds(width + size_x, width), tile] = jnp.where(swap, odd, even)
 
 
-def energy_part(x_odd, x_even, y_odd, y_even, density, labels, potential, energy_out, poten):
+def energy_part(x_odd, x_even, y_even, y_odd, density, labels, potential, energy_out, poten):
     size_x, size_y, size_z = density.shape
     starts, planes = plane_starts(WIDTHS)
     planes_loop(0, size_x, 4, lambda x, n: poten.__setitem__((pl.ds(x + 1, n), pl.ds(0, size_y)), potential[pl.ds(x, n)]))
@@ -182,7 +182,7 @@
     planes_loop(0, size_x, 4, step)
 
 
-def adjoint_part(x_odd, x_even, y_odd, y_even, corner_odd, corner_even, density, labels, adjoint_start, adjoint_source, potential,
+def adjoint_part(x_odd, x_even, y_even, y_odd, corner_odd, corner_even, density, labels, adjoint_start, adjoint_source, potential,
                  raw_out,
                  permit, start, source, poten, face_x, face_y, face_z, inverse, first, second):
     size_x, size_y, size_z = density.shape
@@ -432,7 +432,7 @@
     def room(extra):
         return pltpu.VMEM((size_x + extra, wide, size_z), jnp.float32)
 
-    energy = call(energy_part, f32(8, size_z), [room(2)])(x_odd, x_even, y_odd, y_even, own[0], own[1], own[4])
+    energy = call(energy_part, f32(8, size_z), [room(2)])(x_odd, x_even, y_even, y_odd, own[0], own[1], own[4])
     mine, other = doubling(energy, y_bits[1:])
     face = f32(FILTER_SWEEPS, size_y, size_z)
     raw = call(
@@ -440,7 +440,7 @@
         f32(*shape),
         [room(6), room(6), room(4), room(2), room(5), room(4), room(4), room(4), room(4), room(2)],
         cost=10000000,
-    )(x_odd, x_even, y_odd, y_even, corner_odd, corner_even, *own)
+    )(x_odd, x_even, y_even, y_odd, corner_odd, corner_even, *own)
 
     x_odd = swap_odd(call(pack_raw_x_odd, face)(raw), "gx")
     even, energy = call(pack_raw_x_even, (face, f32(8, size_z)))(raw, mine, other)

time: 38.2 us -> 38.2 us (level)
    ppermute x4, starting transfers between devices: 2.93 us -> 4.09 us  [partner(): lax.ppermute(value, axis, [(i, i ^ bit) for i in range(lax.axis_size(axis...]
    ppermute x5, starting transfers between devices: 16 us -> 14.8 us  [swap_even(): lax.ppermute(value, axis, [(i, i ^ 1) for i in range(lax.axis_size(axis))])]
  transfers between devices with their start and end apart: 14 -> 14, of which waited for: 4 -> 3; matrix products, arithmetic and copies ran while one was open for 0% -> 0% of each run, Pallas kernels for 12% -> 12%
where the time goes in v14:
time: 38.2 us; the launch traced here: 37.9 us
  starting transfers between devices  22.2 us (58%)
  waiting for transfers between devices  8.23 us (22%)
  Pallas kernels  6.65 us (17%)
  between operations  0.77 us (2%)
    ppermute x5, starting transfers between devices, swap_even(): lax.ppermute(value, axis, [(i, i ^ 1) for i in range(lax.axis_size(axis))])  14.8 us
    ppermute x4, waiting for transfers between devices, partner(): lax.ppermute(value, axis, [(i, i ^ bit) for i in range(lax.axis_size(axis...  5.79 us
    ppermute x4, starting transfers between devices, partner(): lax.ppermute(value, axis, [(i, i ^ bit) for i in range(lax.axis_size(axis...  4.09 us
    ppermute x5, starting transfers between devices, swap_odd(): return lax.ppermute(value, axis, up + [(b, a) for a, b in up])  3.3 us
    ppermute x5, waiting for transfers between devices, swap_even(): lax.ppermute(value, axis, [(i, i ^ 1) for i in range(lax.axis_size(axis))])  2.43 us
    pallas_call x1, Pallas kernels, shards(): call(adjoint_part, f32(*shape), [room(6), room(6), room(4), room(2), room...  2.23 us
    pallas_call x1, Pallas kernels, shards(): call(filter_part, f32(*shape), [room(2 * FILTER_SWEEPS)] * 3, cost=10000000)  1.46 us
    pallas_call x1, Pallas kernels, shards(): pl.pallas_call(pack_own, out_shape=(f32(planes, size_y, size_z),) * 2 + (...  1.33 us
  transfers between devices with their start and end apart: 14, of which 3 were waited for; matrix products, arithmetic and copies ran while one was open for 0% of the time, Pallas kernels for 12%

profile of v14, /device:TPU:0, one launch (start us, length us, event | category | flops | bytes accessed | tf_op | source)
XLA Modules:
  0.0 37.9 jit_solution(3365823569131772157)
XLA Ops:
  0.6 1.3 %shard_map.68 = (f32[9,32,128]{2,1,0:T(8,128)S(1)}, f32[9,32,128]{2,1,0:T(8,128)S(1)}, f32[144,128]{1,0:T(8,128)S(1)}, f32[144,128]{1,0:T(8,128)S(1)}, f32[16,32...) custom-call(f32[16,32,128]{2,1,0:T(8,128)} %refs_0_.1, ...), custom_call_target="tpu_custom_call" | custom-call | tf_op jit(solution)/shard_map/pallas_call | solution.py:414
  2.0 0.7 %collective-permute-start = (f32[9,32,128]{2,1,0:T(8,128)S(1)}, f32[9,32,128]{2,1,0:T(8,128)S(1)}, u32[]{:S(2)}, u32[]{:S(2)}) collective-permute-start(f32[9,32,128]{2,1,0:T(8,128)S(1)} %get-tuple-element.20), channel_id=1, source_target_pairs={{8,16},{16,8},{9,17},{17,9},{10,18},{18,10},{11,19},{19,11},{12,20... | collective-permute-start | bytes 442376 | tf_op jit(solution)/shard_map/ppermute | solution.py:386
  2.6 4.4 %collective-permute-start.1 = (f32[9,32,128]{2,1,0:T(8,128)S(1)}, f32[9,32,128]{2,1,0:T(8,128)S(1)}, u32[]{:S(2)}, u32[]{:S(2)}) collective-permute-start(f32[9,32,128]{2,1,0:T(8,128)S(1)} %get-tuple-element.21), channel_id=1, source_target_pairs={{0,8},{8,0},{16,24},{24,16},{1,9},{9,1},{17,25},{25,17},{2,10},{10... | collective-permute-start | bytes 442376 | tf_op jit(solution)/shard_map/ppermute | solution.py:380
  7.0 1.5 %collective-permute-start.2 = (f32[144,128]{1,0:T(8,128)S(1)}, f32[144,128]{1,0:T(8,128)S(1)}, u32[]{:S(2)}, u32[]{:S(2)}) collective-permute-start(f32[144,128]{1,0:T(8,128)S(1)} %get-tuple-element.22), channel_id=1, source_target_pairs={{0,1},{1,0},{2,3},{3,2},{4,5},{5,4},{6,7},{7,6},{8,9},{9,8},{10,11... | collective-permute-start | bytes 221192 | tf_op jit(solution)/shard_map/ppermute | solution.py:380
  8.5 0.7 %collective-permute-start.3 = (f32[144,128]{1,0:T(8,128)S(1)}, f32[144,128]{1,0:T(8,128)S(1)}, u32[]{:S(2)}, u32[]{:S(2)}) collective-permute-start(f32[144,128]{1,0:T(8,128)S(1)} %get-tuple-element.23), channel_id=1, source_target_pairs={{1,2},{3,4},{5,6},{2,1},{4,3},{6,5},{9,10},{11,12},{13,14},{10,9},... | collective-permute-start | bytes 221192 | tf_op jit(solution)/shard_map/ppermute | solution.py:386
  9.2 0.0 collective-permute-done.x_odd
  9.2 0.0 collective-permute-done.1.x_even
  9.2 0.7 %collective-permute-start.4 = (f32[16,128]{1,0:T(8,128)S(1)}, f32[16,128]{1,0:T(8,128)S(1)}, u32[]{:S(2)}, u32[]{:S(2)}) collective-permute-start(f32[16,128]{1,0:T(8,128)S(1)} %get-tuple-element.24), channel_id=1, source_target_pairs={{1,2},{3,4},{5,6},{2,1},{4,3},{6,5},{9,10},{11,12},{13,14},{10,9},... | collective-permute-start | bytes 24584 | tf_op jit(solution)/shard_map/ppermute | solution.py:386
  9.9 6.0 %collective-permute-start.5 = (f32[16,128]{1,0:T(8,128)S(1)}, f32[16,128]{1,0:T(8,128)S(1)}, u32[]{:S(2)}, u32[]{:S(2)}) collective-permute-start(f32[16,128]{1,0:T(8,128)S(1)} %get-tuple-element.25), channel_id=1, source_target_pairs={{0,1},{1,0},{2,3},{3,2},{4,5},{5,4},{6,7},{7,6},{8,9},{9,8},{10,11... | collective-permute-start | bytes 24584 | tf_op jit(solution)/shard_map/ppermute | solution.py:380
  15.9 0.0 collective-permute-done.2.y_even
  15.9 0.0 collective-permute-done.3.y_odd
  15.9 0.7 %shard_map.72.mine = f32[8,128]{1,0:T(8,128)S(1)} custom-call(f32[9,32,128]{2,1,0:T(8,128)S(1)} %collective-permute-done.x_odd, f32[9,32,128]{2,1,0:T(8,128)S(1)} %collective-permute-done.1.x_even, f32[144,128]{1,0:T(8,128)S(1)} %collective-permute-done.2.y_even, f32[144,128]{1,0:T(8,128)S(1)} %collective-permute-done.3.y_odd, ...), custom_call_target="tpu_custom_call" | custom-call | flops 10000 | bytes 10000 | tf_op jit(solution)/shard_map/pallas_call | solution.py:435
  16.6 2.7 %collective-permute-start.7 = (f32[8,128]{1,0:T(8,128)S(1)}, f32[8,128]{1,0:T(8,128)S(1)}, u32[]{:S(2)}, u32[]{:S(2)}) collective-permute-start(f32[8,128]{1,0:T(8,128)S(1)} %shard_map.72.mine), channel_id=1, source_target_pairs={{0,4},{1,5},{2,6},{3,7},{4,0},{5,1},{6,2},{7,3},{8,12},{9,13},{10,... | collective-permute-start | bytes 12296 | tf_op jit(solution)/shard_map/ppermute | solution.py:390
  19.2 0.0 collective-permute-done.4.corner_odd
  19.2 0.0 collective-permute-done.5.corner_even
  19.2 2.2 %shard_map.70.raw.raw_in = f32[16,32,128]{2,1,0:T(8,128)S(1)} custom-call(f32[9,32,128]{2,1,0:T(8,128)S(1)} %collective-permute-done.x_odd, f32[9,32,128]{2,1,0:T(8,128)S(1)} %collective-permute-done.1.x_even, f32[144,128]{1,0:T(8,128)S(1)} %collective-permute-done.2.y_even, f32[144,128]{1,0:T(8,128)S(1)} %collective-permute-done.3.y_odd, ...), custom_call_target="tpu_custom_call" | custom-call | flops 10000000 | bytes 10000000 | tf_op jit(solution)/shard_map/pallas_call | solution.py:438
  21.5 0.7 %collective-permute-start.6 = (f32[4,32,128]{2,1,0:T(8,128)S(1)}, f32[4,32,128]{2,1,0:T(8,128)S(1)}, u32[]{:S(2)}, u32[]{:S(2)}) collective-permute-start(f32[4,32,128]{2,1,0:T(8,128)S(1)} %shard_map.71), channel_id=1, source_target_pairs={{8,16},{16,8},{9,17},{17,9},{10,18},{18,10},{11,19},{19,11},{12,20... | collective-permute-start | bytes 196616 | tf_op jit(solution)/shard_map/ppermute | solution.py:386
  22.2 0.0 collective-permute-done.7.other
  22.2 2.0 %collective-permute-start.8 = (f32[4,32,128]{2,1,0:T(8,128)S(1)}, f32[4,32,128]{2,1,0:T(8,128)S(1)}, u32[]{:S(2)}, u32[]{:S(2)}) collective-permute-start(f32[4,32,128]{2,1,0:T(8,128)S(1)} %get-tuple-element.31), channel_id=1, source_target_pairs={{0,8},{8,0},{16,24},{24,16},{1,9},{9,1},{17,25},{25,17},{2,10},{10... | collective-permute-start | bytes 196616 | tf_op jit(solution)/shard_map/ppermute | solution.py:380
  24.2 0.0 collective-permute-start.9
  24.2 3.6 %collective-permute-done.9.other = f32[8,128]{1,0:T(8,128)S(1)} collective-permute-done((f32[8,128]{1,0:T(8,128)S(1)}, f32[8,128]{1,0:T(8,128)S(1)}, u32[]{:S(2)}, u32[]{:S(2)}) %collective-permute-start.9) | collective-permute-done | bytes 4128 | tf_op jit(solution)/shard_map/ppermute | solution.py:390
  27.8 0.0 collective-permute-done.6.x_odd
  27.8 0.0 collective-permute-done.8.x_even
  27.8 1.0 %collective-permute-start.11 = (f32[88,128]{1,0:T(8,128)S(1)}, f32[88,128]{1,0:T(8,128)S(1)}, u32[]{:S(2)}, u32[]{:S(2)}) collective-permute-start(f32[88,128]{1,0:T(8,128)S(1)} %get-tuple-element.34), channel_id=1, source_target_pairs={{0,1},{1,0},{2,3},{3,2},{4,5},{5,4},{6,7},{7,6},{8,9},{9,8},{10,11... | collective-permute-start | bytes 135176 | tf_op jit(solution)/shard_map/ppermute | solution.py:380
  28.9 0.7 %collective-permute-start.10 = (f32[80,128]{1,0:T(8,128)S(1)}, f32[80,128]{1,0:T(8,128)S(1)}, u32[]{:S(2)}, u32[]{:S(2)}) collective-permute-start(f32[80,128]{1,0:T(8,128)S(1)} %get-tuple-element.33), channel_id=1, source_target_pairs={{1,2},{3,4},{5,6},{2,1},{4,3},{6,5},{9,10},{11,12},{13,14},{10,9},... | collective-permute-start | bytes 122888 | tf_op jit(solution)/shard_map/ppermute | solution.py:386
  29.5 2.4 %collective-permute-done.11.y_even = f32[88,128]{1,0:T(8,128)S(1)} collective-permute-done((f32[88,128]{1,0:T(8,128)S(1)}, f32[88,128]{1,0:T(8,128)S(1)}, u32[]{:S(2)}, u32[]{:S(2)}) %collective-permute-start.11) | collective-permute-done | bytes 45088 | tf_op jit(solution)/shard_map/ppermute | solution.py:380
  31.9 1.4 %collective-permute-start.12 = (f32[8,128]{1,0:T(8,128)S(1)}, f32[8,128]{1,0:T(8,128)S(1)}, u32[]{:S(2)}, u32[]{:S(2)}) collective-permute-start(f32[8,128]{1,0:T(8,128)S(1)} %slice_add_fusion), channel_id=1, source_target_pairs={{0,2},{1,3},{2,0},{3,1},{4,6},{5,7},{6,4},{7,5},{8,10},{9,11},{10,... | collective-permute-start | bytes 12296 | tf_op jit(solution)/shard_map/ppermute | solution.py:390
  33.4 2.2 %collective-permute-done.12 = f32[8,128]{1,0:T(8,128)S(1)} collective-permute-done((f32[8,128]{1,0:T(8,128)S(1)}, f32[8,128]{1,0:T(8,128)S(1)}, u32[]{:S(2)}, u32[]{:S(2)}) %collective-permute-start.12) | collective-permute-done | bytes 4128 | tf_op jit(solution)/shard_map/ppermute | solution.py:390
  35.5 0.0 collective-permute-start.13
  35.6 0.0 collective-permute-done.10.y_odd
  35.6 1.5 %shard_map.75.filtered = f32[16,32,128]{2,1,0:T(8,128)S(1)} custom-call(f32[4,32,128]{2,1,0:T(8,128)S(1)} %collective-permute-done.6.x_odd, f32[4,32,128]{2,1,0:T(8,128)S(1)} %collective-permute-done.8.x_even, f32[80,128]{1,0:T(8,128)S(1)} %collective-permute-done.10.y_odd, f32[88,128]{1,0:T(8,128)S(1)} %collective-permute-done.11.y_even, ...), custom_call_target="tpu_custom_call" | custom-call | flops 10000000 | bytes 10000000 | tf_op jit(solution)/shard_map/pallas_call | solution.py:456
  37.0 0.0 collective-permute-done.13.other
  37.0 0.9 %shard_map.76 = (f32[16,32,128]{2,1,0:T(8,128)}, f32[1,1]{1,0:T(1,128)}) custom-call(f32[16,32,128]{2,1,0:T(8,128)S(1)} %shard_map.75.filtered, f32[8,128]{1,0:T(8,128)S(1)} %add.7.mine, f32[8,128]{1,0:T(8,128)S(1)} %collective-permute-done.13.other), custom_call_target="tpu_custom_call" | custom-call | tf_op jit(solution)/shard_map/pallas_call | solution.py:462
  (6 shorter events, 0.1 us)
Async XLA Ops:
  2.0 7.2 %collective-permute-start = (f32[9,32,128]{2,1,0:T(8,128)S(1)}, f32[9,32,128]{2,1,0:T(8,128)S(1)}, u32[]{:S(2)}, u32[]{:S(2)}) collective-permute-start(f32[9,32,128]{2,1,0:T(8,128)S(1)} %get-tuple-element.20), channel_id=1, source_target_pairs={{8,16},{16,8},{9,17},{17,9},{10,18},{18,10},{11,19},{19,11},{12,20... | collective-permute-start | bytes 442376 | tf_op jit(solution)/shard_map/ppermute | solution.py:386
  2.6 6.6 %collective-permute-start.1 = (f32[9,32,128]{2,1,0:T(8,128)S(1)}, f32[9,32,128]{2,1,0:T(8,128)S(1)}, u32[]{:S(2)}, u32[]{:S(2)}) collective-permute-start(f32[9,32,128]{2,1,0:T(8,128)S(1)} %get-tuple-element.21), channel_id=1, source_target_pairs={{0,8},{8,0},{16,24},{24,16},{1,9},{9,1},{17,25},{25,17},{2,10},{10... | collective-permute-start | bytes 442376 | tf_op jit(solution)/shard_map/ppermute | solution.py:380
  7.0 8.9 %collective-permute-start.2 = (f32[144,128]{1,0:T(8,128)S(1)}, f32[144,128]{1,0:T(8,128)S(1)}, u32[]{:S(2)}, u32[]{:S(2)}) collective-permute-start(f32[144,128]{1,0:T(8,128)S(1)} %get-tuple-element.22), channel_id=1, source_target_pairs={{0,1},{1,0},{2,3},{3,2},{4,5},{5,4},{6,7},{7,6},{8,9},{9,8},{10,11... | collective-permute-start | bytes 221192 | tf_op jit(solution)/shard_map/ppermute | solution.py:380
  8.5 7.4 %collective-permute-start.3 = (f32[144,128]{1,0:T(8,128)S(1)}, f32[144,128]{1,0:T(8,128)S(1)}, u32[]{:S(2)}, u32[]{:S(2)}) collective-permute-start(f32[144,128]{1,0:T(8,128)S(1)} %get-tuple-element.23), channel_id=1, source_target_pairs={{1,2},{3,4},{5,6},{2,1},{4,3},{6,5},{9,10},{11,12},{13,14},{10,9},... | collective-permute-start | bytes 221192 | tf_op jit(solution)/shard_map/ppermute | solution.py:386
  9.2 10.0 %collective-permute-start.4 = (f32[16,128]{1,0:T(8,128)S(1)}, f32[16,128]{1,0:T(8,128)S(1)}, u32[]{:S(2)}, u32[]{:S(2)}) collective-permute-start(f32[16,128]{1,0:T(8,128)S(1)} %get-tuple-element.24), channel_id=1, source_target_pairs={{1,2},{3,4},{5,6},{2,1},{4,3},{6,5},{9,10},{11,12},{13,14},{10,9},... | collective-permute-start | bytes 24584 | tf_op jit(solution)/shard_map/ppermute | solution.py:386
  9.9 9.3 %collective-permute-start.5 = (f32[16,128]{1,0:T(8,128)S(1)}, f32[16,128]{1,0:T(8,128)S(1)}, u32[]{:S(2)}, u32[]{:S(2)}) collective-permute-start(f32[16,128]{1,0:T(8,128)S(1)} %get-tuple-element.25), channel_id=1, source_target_pairs={{0,1},{1,0},{2,3},{3,2},{4,5},{5,4},{6,7},{7,6},{8,9},{9,8},{10,11... | collective-permute-start | bytes 24584 | tf_op jit(solution)/shard_map/ppermute | solution.py:380
  16.6 5.6 %collective-permute-start.7 = (f32[8,128]{1,0:T(8,128)S(1)}, f32[8,128]{1,0:T(8,128)S(1)}, u32[]{:S(2)}, u32[]{:S(2)}) collective-permute-start(f32[8,128]{1,0:T(8,128)S(1)} %shard_map.72.mine), channel_id=1, source_target_pairs={{0,4},{1,5},{2,6},{3,7},{4,0},{5,1},{6,2},{7,3},{8,12},{9,13},{10,... | collective-permute-start | bytes 12296 | tf_op jit(solution)/shard_map/ppermute | solution.py:390
  21.5 6.3 %collective-permute-start.6 = (f32[4,32,128]{2,1,0:T(8,128)S(1)}, f32[4,32,128]{2,1,0:T(8,128)S(1)}, u32[]{:S(2)}, u32[]{:S(2)}) collective-permute-start(f32[4,32,128]{2,1,0:T(8,128)S(1)} %shard_map.71), channel_id=1, source_target_pairs={{8,16},{16,8},{9,17},{17,9},{10,18},{18,10},{11,19},{19,11},{12,20... | collective-permute-start | bytes 196616 | tf_op jit(solution)/shard_map/ppermute | solution.py:386
  22.2 5.6 %collective-permute-start.8 = (f32[4,32,128]{2,1,0:T(8,128)S(1)}, f32[4,32,128]{2,1,0:T(8,128)S(1)}, u32[]{:S(2)}, u32[]{:S(2)}) collective-permute-start(f32[4,32,128]{2,1,0:T(8,128)S(1)} %get-tuple-element.31), channel_id=1, source_target_pairs={{0,8},{8,0},{16,24},{24,16},{1,9},{9,1},{17,25},{25,17},{2,10},{10... | collective-permute-start | bytes 196616 | tf_op jit(solution)/shard_map/ppermute | solution.py:380
  24.2 3.6 %collective-permute-start.9 = (f32[8,128]{1,0:T(8,128)S(1)}, f32[8,128]{1,0:T(8,128)S(1)}, u32[]{:S(2)}, u32[]{:S(2)}) collective-permute-start(f32[8,128]{1,0:T(8,128)S(1)} %get-tuple-element.32.mine), channel_id=1, source_target_pairs={{0,16},{8,24},{16,0},{24,8},{1,17},{9,25},{17,1},{25,9},{2,18},{10... | collective-permute-start | bytes 12296 | tf_op jit(solution)/shard_map/ppermute | solution.py:390
  27.8 4.1 %collective-permute-start.11 = (f32[88,128]{1,0:T(8,128)S(1)}, f32[88,128]{1,0:T(8,128)S(1)}, u32[]{:S(2)}, u32[]{:S(2)}) collective-permute-start(f32[88,128]{1,0:T(8,128)S(1)} %get-tuple-element.34), channel_id=1, source_target_pairs={{0,1},{1,0},{2,3},{3,2},{4,5},{5,4},{6,7},{7,6},{8,9},{9,8},{10,11... | collective-permute-start | bytes 135176 | tf_op jit(solution)/shard_map/ppermute | solution.py:380
  28.9 6.7 %collective-permute-start.10 = (f32[80,128]{1,0:T(8,128)S(1)}, f32[80,128]{1,0:T(8,128)S(1)}, u32[]{:S(2)}, u32[]{:S(2)}) collective-permute-start(f32[80,128]{1,0:T(8,128)S(1)} %get-tuple-element.33), channel_id=1, source_target_pairs={{1,2},{3,4},{5,6},{2,1},{4,3},{6,5},{9,10},{11,12},{13,14},{10,9},... | collective-permute-start | bytes 122888 | tf_op jit(solution)/shard_map/ppermute | solution.py:386
  31.9 3.6 %collective-permute-start.12 = (f32[8,128]{1,0:T(8,128)S(1)}, f32[8,128]{1,0:T(8,128)S(1)}, u32[]{:S(2)}, u32[]{:S(2)}) collective-permute-start(f32[8,128]{1,0:T(8,128)S(1)} %slice_add_fusion), channel_id=1, source_target_pairs={{0,2},{1,3},{2,0},{3,1},{4,6},{5,7},{6,4},{7,5},{8,10},{9,11},{10,... | collective-permute-start | bytes 12296 | tf_op jit(solution)/shard_map/ppermute | solution.py:390
  35.5 1.5 %collective-permute-start.13 = (f32[8,128]{1,0:T(8,128)S(1)}, f32[8,128]{1,0:T(8,128)S(1)}, u32[]{:S(2)}, u32[]{:S(2)}) collective-permute-start(f32[8,128]{1,0:T(8,128)S(1)} %add.7.mine), channel_id=1, source_target_pairs={{0,8},{8,0},{16,24},{24,16},{1,9},{9,1},{17,25},{25,17},{2,10},{10... | collective-permute-start | bytes 12296 | tf_op jit(solution)/shard_map/ppermute | solution.py:390

commit v15 on v13

--- a/solution.py
+++ b/solution.py
@@ -151,7 +151,7 @@
     field[pl.ds(width + size_x, width), tile] = jnp.where(swap, odd, even)
 
 
-def energy_part(x_odd, x_even, y_odd, y_even, density, labels, potential, energy_out, poten):
+def energy_part(x_odd, x_even, y_even, y_odd, density, labels, potential, energy_out, poten):
     size_x, size_y, size_z = density.shape
     starts, planes = plane_starts(WIDTHS)
     planes_loop(0, size_x, 4, lambda x, n: poten.__setitem__((pl.ds(x + 1, n), pl.ds(0, size_y)), potential[pl.ds(x, n)]))
@@ -203,7 +203,7 @@
     inverse[span] = jnp.where(p > 20.0, 0.0, inverted(total))
 
 
-def inner_weights(y_odd, y_even, density, labels, face_x, face_y, face_z, inverse, permit):
+def inner_weights(y_even, y_odd, density, labels, face_x, face_y, face_z, inverse, permit):
     size_x, size_y, _ = density.shape
 
     def fill(x, n):
@@ -220,7 +220,7 @@
     planes_loop(0, size_x - 2, 7, lambda k, n: weigh(permit, face_x, face_y, face_z, inverse, k + 1, k, n))
 
 
-def adjoint_part(x_odd, x_even, y_odd, y_even, corner_odd, corner_even, density, labels, adjoint_start, adjoint_source, potential,
+def adjoint_part(x_odd, x_even, y_even, y_odd, corner_odd, corner_even, density, labels, adjoint_start, adjoint_source, potential,
                  inner_x, inner_y, inner_z, inner_inverse, raw_out,
                  permit, start, source, poten, edge_x, edge_y, edge_z, edge_inverse, first, second):
     size_x, size_y, size_z = density.shape
@@ -463,14 +463,14 @@
     def room(extra):
         return pltpu.VMEM((size_x + extra, wide, size_z), jnp.float32)
 
-    energy = call(energy_part, f32(8, size_z), [room(2)])(x_odd, x_even, y_odd, y_even, own[0], own[1], own[4])
+    energy = call(energy_part, f32(8, size_z), [room(2)])(x_odd, x_even, y_even, y_odd, own[0], own[1], own[4])
     mine, other = doubling(energy, y_bits[1:])
     face = f32(FILTER_SWEEPS, size_y, size_z)
     inner = call(
         inner_weights,
         (f32(size_x - 1, wide, size_z),) + (f32(size_x - 2, wide, size_z),) * 3,
         [room(0)],
-    )(y_odd, y_even, own[0], own[1])
+    )(y_even, y_odd, own[0], own[1])
 
     def edges(planes):
         return pltpu.VMEM((2, planes, wide, size_z), jnp.float32)
@@ -480,7 +480,7 @@
         f32(*shape),
         [room(6), room(6), room(4), room(2), edges(4), edges(3), edges(3), edges(3), room(4), room(2)],
         cost=10000000,
-    )(x_odd, x_even, y_odd, y_even, corner_odd, corner_even, *own, *inner)
+    )(x_odd, x_even, y_even, y_odd, corner_odd, corner_even, *own, *inner)
 
     x_odd = swap_odd(call(pack_raw_x_odd, face)(raw), "gx")
     even, energy = call(pack_raw_x_even, (face, f32(8, size_z)))(raw, mine, other)

time: 38.4 us -> 38.4 us (level)
    ppermute x5, starting transfers between devices: 16.2 us -> 14.8 us  [swap_even(): lax.ppermute(value, axis, [(i, i ^ 1) for i in range(lax.axis_size(axis))])]
    ppermute x4, starting transfers between devices: 2.93 us -> 4.09 us  [partner(): lax.ppermute(value, axis, [(i, i ^ bit) for i in range(lax.axis_size(axis...]
  transfers between devices with their start and end apart: 14 -> 14, of which waited for: 4 -> 3; matrix products, arithmetic and copies ran while one was open for 0% -> 0% of each run, Pallas kernels for 12% -> 12%
where the time goes in v15:
time: 38.4 us; the launch traced here: 38.1 us
  starting transfers between devices  22.2 us (58%)
  waiting for transfers between devices  8.23 us (21%)
  Pallas kernels  6.83 us (18%)
  between operations  0.79 us (2%)
    ppermute x5, starting transfers between devices, swap_even(): lax.ppermute(value, axis, [(i, i ^ 1) for i in range(lax.axis_size(axis))])  14.8 us
    ppermute x4, waiting for transfers between devices, partner(): lax.ppermute(value, axis, [(i, i ^ bit) for i in range(lax.axis_size(axis...  5.79 us
    ppermute x4, starting transfers between devices, partner(): lax.ppermute(value, axis, [(i, i ^ bit) for i in range(lax.axis_size(axis...  4.09 us
    ppermute x5, starting transfers between devices, swap_odd(): return lax.ppermute(value, axis, up + [(b, a) for a, b in up])  3.3 us
    ppermute x5, waiting for transfers between devices, swap_even(): lax.ppermute(value, axis, [(i, i ^ 1) for i in range(lax.axis_size(axis))])  2.43 us
    pallas_call x1, Pallas kernels, shards(): call(adjoint_part, f32(*shape), [room(6), room(6), room(4), room(2), edge...  1.77 us
    pallas_call x1, Pallas kernels, shards(): call(filter_part, f32(*shape), [room(2 * FILTER_SWEEPS)] * 3, cost=10000000)  1.47 us
    pallas_call x1, Pallas kernels, shards(): pl.pallas_call(pack_own, out_shape=(f32(planes, size_y, size_z),) * 2 + (...  1.33 us
  transfers between devices with their start and end apart: 14, of which 3 were waited for; matrix products, arithmetic and copies ran while one was open for 0% of the time, Pallas kernels for 12%

profile of v15, /device:TPU:0, one launch (start us, length us, event | category | flops | bytes accessed | tf_op | source)
XLA Modules:
  0.0 38.1 jit_solution(1643200890462288269)
XLA Ops:
  0.6 1.3 %shard_map.68 = (f32[9,32,128]{2,1,0:T(8,128)S(1)}, f32[9,32,128]{2,1,0:T(8,128)S(1)}, f32[144,128]{1,0:T(8,128)S(1)}, f32[144,128]{1,0:T(8,128)S(1)}, f32[16,32...) custom-call(f32[16,32,128]{2,1,0:T(8,128)} %refs_0_.1, ...), custom_call_target="tpu_custom_call" | custom-call | tf_op jit(solution)/shard_map/pallas_call | solution.py:445
  2.0 0.7 %collective-permute-start = (f32[9,32,128]{2,1,0:T(8,128)S(1)}, f32[9,32,128]{2,1,0:T(8,128)S(1)}, u32[]{:S(2)}, u32[]{:S(2)}) collective-permute-start(f32[9,32,128]{2,1,0:T(8,128)S(1)} %get-tuple-element.24), channel_id=1, source_target_pairs={{8,16},{16,8},{9,17},{17,9},{10,18},{18,10},{11,19},{19,11},{12,20... | collective-permute-start | bytes 442376 | tf_op jit(solution)/shard_map/ppermute | solution.py:417
  2.6 4.4 %collective-permute-start.1 = (f32[9,32,128]{2,1,0:T(8,128)S(1)}, f32[9,32,128]{2,1,0:T(8,128)S(1)}, u32[]{:S(2)}, u32[]{:S(2)}) collective-permute-start(f32[9,32,128]{2,1,0:T(8,128)S(1)} %get-tuple-element.25), channel_id=1, source_target_pairs={{0,8},{8,0},{16,24},{24,16},{1,9},{9,1},{17,25},{25,17},{2,10},{10... | collective-permute-start | bytes 442376 | tf_op jit(solution)/shard_map/ppermute | solution.py:411
  7.0 1.5 %collective-permute-start.2 = (f32[144,128]{1,0:T(8,128)S(1)}, f32[144,128]{1,0:T(8,128)S(1)}, u32[]{:S(2)}, u32[]{:S(2)}) collective-permute-start(f32[144,128]{1,0:T(8,128)S(1)} %get-tuple-element.26), channel_id=1, source_target_pairs={{0,1},{1,0},{2,3},{3,2},{4,5},{5,4},{6,7},{7,6},{8,9},{9,8},{10,11... | collective-permute-start | bytes 221192 | tf_op jit(solution)/shard_map/ppermute | solution.py:411
  8.5 0.7 %collective-permute-start.3 = (f32[144,128]{1,0:T(8,128)S(1)}, f32[144,128]{1,0:T(8,128)S(1)}, u32[]{:S(2)}, u32[]{:S(2)}) collective-permute-start(f32[144,128]{1,0:T(8,128)S(1)} %get-tuple-element.27), channel_id=1, source_target_pairs={{1,2},{3,4},{5,6},{2,1},{4,3},{6,5},{9,10},{11,12},{13,14},{10,9},... | collective-permute-start | bytes 221192 | tf_op jit(solution)/shard_map/ppermute | solution.py:417
  9.2 0.0 collective-permute-done.x_odd
  9.2 0.0 collective-permute-done.1.x_even
  9.2 0.7 %collective-permute-start.4 = (f32[16,128]{1,0:T(8,128)S(1)}, f32[16,128]{1,0:T(8,128)S(1)}, u32[]{:S(2)}, u32[]{:S(2)}) collective-permute-start(f32[16,128]{1,0:T(8,128)S(1)} %get-tuple-element.28), channel_id=1, source_target_pairs={{1,2},{3,4},{5,6},{2,1},{4,3},{6,5},{9,10},{11,12},{13,14},{10,9},... | collective-permute-start | bytes 24584 | tf_op jit(solution)/shard_map/ppermute | solution.py:417
  9.9 6.0 %collective-permute-start.5 = (f32[16,128]{1,0:T(8,128)S(1)}, f32[16,128]{1,0:T(8,128)S(1)}, u32[]{:S(2)}, u32[]{:S(2)}) collective-permute-start(f32[16,128]{1,0:T(8,128)S(1)} %get-tuple-element.29), channel_id=1, source_target_pairs={{0,1},{1,0},{2,3},{3,2},{4,5},{5,4},{6,7},{7,6},{8,9},{9,8},{10,11... | collective-permute-start | bytes 24584 | tf_op jit(solution)/shard_map/ppermute | solution.py:411
  15.9 0.0 collective-permute-done.2.y_even
  15.9 0.0 collective-permute-done.3.y_odd
  15.9 0.7 %shard_map.73.mine = f32[8,128]{1,0:T(8,128)S(1)} custom-call(f32[9,32,128]{2,1,0:T(8,128)S(1)} %collective-permute-done.x_odd, f32[9,32,128]{2,1,0:T(8,128)S(1)} %collective-permute-done.1.x_even, f32[144,128]{1,0:T(8,128)S(1)} %collective-permute-done.2.y_even, f32[144,128]{1,0:T(8,128)S(1)} %collective-permute-done.3.y_odd, ...), custom_call_target="tpu_custom_call" | custom-call | flops 10000 | bytes 10000 | tf_op jit(solution)/shard_map/pallas_call | solution.py:466
  16.6 2.7 %collective-permute-start.7 = (f32[8,128]{1,0:T(8,128)S(1)}, f32[8,128]{1,0:T(8,128)S(1)}, u32[]{:S(2)}, u32[]{:S(2)}) collective-permute-start(f32[8,128]{1,0:T(8,128)S(1)} %shard_map.73.mine), channel_id=1, source_target_pairs={{0,4},{1,5},{2,6},{3,7},{4,0},{5,1},{6,2},{7,3},{8,12},{9,13},{10,... | collective-permute-start | bytes 12296 | tf_op jit(solution)/shard_map/ppermute | solution.py:421
  19.2 0.6 %shard_map.70 = (f32[15,40,128]{2,1,0:T(8,128)S(1)}, f32[14,40,128]{2,1,0:T(8,128)S(1)}, f32[14,40,128]{2,1,0:T(8,128)S(1)}, f32[14,40,128]{2,1,0:T(8,128)S(1)}) custom-call(f32[144,128]{1,0:T(8,128)S(1)} %collective-permute-done.2.y_even, f32[144,128]{1,0:T(8,128)S(1)} %collective-permute-done.3.y_odd, f32[16,32,128]{2,1,0:T(8,128)S(1)} %get-tuple-element.30.density, ...), custom_call_target="tpu_custom_call" | custom-call | flops 10000 | bytes 10000 | tf_op jit(solution)/shard_map/pallas_call | solution.py:469
  19.9 0.0 collective-permute-done.4.corner_odd
  19.9 0.0 collective-permute-done.5.corner_even
  19.9 1.8 %shard_map.71.raw.raw_in = f32[16,32,128]{2,1,0:T(8,128)S(1)} custom-call(f32[9,32,128]{2,1,0:T(8,128)S(1)} %collective-permute-done.x_odd, f32[9,32,128]{2,1,0:T(8,128)S(1)} %collective-permute-done.1.x_even, f32[144,128]{1,0:T(8,128)S(1)} %collective-permute-done.2.y_even, f32[144,128]{1,0:T(8,128)S(1)} %collective-permute-done.3.y_odd, ...), custom_call_target="tpu_custom_call" | custom-call | flops 10000000 | bytes 10000000 | tf_op jit(solution)/shard_map/pallas_call | solution.py:478
  21.7 0.7 %collective-permute-start.6 = (f32[4,32,128]{2,1,0:T(8,128)S(1)}, f32[4,32,128]{2,1,0:T(8,128)S(1)}, u32[]{:S(2)}, u32[]{:S(2)}) collective-permute-start(f32[4,32,128]{2,1,0:T(8,128)S(1)} %shard_map.72), channel_id=1, source_target_pairs={{8,16},{16,8},{9,17},{17,9},{10,18},{18,10},{11,19},{19,11},{12,20... | collective-permute-start | bytes 196616 | tf_op jit(solution)/shard_map/ppermute | solution.py:417
  22.4 0.0 collective-permute-done.7.other
  22.4 2.0 %collective-permute-start.8 = (f32[4,32,128]{2,1,0:T(8,128)S(1)}, f32[4,32,128]{2,1,0:T(8,128)S(1)}, u32[]{:S(2)}, u32[]{:S(2)}) collective-permute-start(f32[4,32,128]{2,1,0:T(8,128)S(1)} %get-tuple-element.39), channel_id=1, source_target_pairs={{0,8},{8,0},{16,24},{24,16},{1,9},{9,1},{17,25},{25,17},{2,10},{10... | collective-permute-start | bytes 196616 | tf_op jit(solution)/shard_map/ppermute | solution.py:411
  24.4 0.0 collective-permute-start.9
  24.4 3.6 %collective-permute-done.9.other = f32[8,128]{1,0:T(8,128)S(1)} collective-permute-done((f32[8,128]{1,0:T(8,128)S(1)}, f32[8,128]{1,0:T(8,128)S(1)}, u32[]{:S(2)}, u32[]{:S(2)}) %collective-permute-start.9) | collective-permute-done | bytes 4128 | tf_op jit(solution)/shard_map/ppermute | solution.py:421
  28.0 0.0 collective-permute-done.6.x_odd
  28.0 0.0 collective-permute-done.8.x_even
  28.0 1.0 %collective-permute-start.11 = (f32[88,128]{1,0:T(8,128)S(1)}, f32[88,128]{1,0:T(8,128)S(1)}, u32[]{:S(2)}, u32[]{:S(2)}) collective-permute-start(f32[88,128]{1,0:T(8,128)S(1)} %get-tuple-element.42), channel_id=1, source_target_pairs={{0,1},{1,0},{2,3},{3,2},{4,5},{5,4},{6,7},{7,6},{8,9},{9,8},{10,11... | collective-permute-start | bytes 135176 | tf_op jit(solution)/shard_map/ppermute | solution.py:411
  29.0 0.7 %collective-permute-start.10 = (f32[80,128]{1,0:T(8,128)S(1)}, f32[80,128]{1,0:T(8,128)S(1)}, u32[]{:S(2)}, u32[]{:S(2)}) collective-permute-start(f32[80,128]{1,0:T(8,128)S(1)} %get-tuple-element.41), channel_id=1, source_target_pairs={{1,2},{3,4},{5,6},{2,1},{4,3},{6,5},{9,10},{11,12},{13,14},{10,9},... | collective-permute-start | bytes 122888 | tf_op jit(solution)/shard_map/ppermute | solution.py:417
  29.7 2.4 %collective-permute-done.11.y_even = f32[88,128]{1,0:T(8,128)S(1)} collective-permute-done((f32[88,128]{1,0:T(8,128)S(1)}, f32[88,128]{1,0:T(8,128)S(1)}, u32[]{:S(2)}, u32[]{:S(2)}) %collective-permute-start.11) | collective-permute-done | bytes 45088 | tf_op jit(solution)/shard_map/ppermute | solution.py:411
  32.1 1.4 %collective-permute-start.12 = (f32[8,128]{1,0:T(8,128)S(1)}, f32[8,128]{1,0:T(8,128)S(1)}, u32[]{:S(2)}, u32[]{:S(2)}) collective-permute-start(f32[8,128]{1,0:T(8,128)S(1)} %slice_add_fusion), channel_id=1, source_target_pairs={{0,2},{1,3},{2,0},{3,1},{4,6},{5,7},{6,4},{7,5},{8,10},{9,11},{10,... | collective-permute-start | bytes 12296 | tf_op jit(solution)/shard_map/ppermute | solution.py:421
  33.6 2.2 %collective-permute-done.12 = f32[8,128]{1,0:T(8,128)S(1)} collective-permute-done((f32[8,128]{1,0:T(8,128)S(1)}, f32[8,128]{1,0:T(8,128)S(1)}, u32[]{:S(2)}, u32[]{:S(2)}) %collective-permute-start.12) | collective-permute-done | bytes 4128 | tf_op jit(solution)/shard_map/ppermute | solution.py:421
  35.7 0.0 collective-permute-start.13
  35.7 0.0 collective-permute-done.10.y_odd
  35.7 1.5 %shard_map.76.filtered = f32[16,32,128]{2,1,0:T(8,128)S(1)} custom-call(f32[4,32,128]{2,1,0:T(8,128)S(1)} %collective-permute-done.6.x_odd, f32[4,32,128]{2,1,0:T(8,128)S(1)} %collective-permute-done.8.x_even, f32[80,128]{1,0:T(8,128)S(1)} %collective-permute-done.10.y_odd, f32[88,128]{1,0:T(8,128)S(1)} %collective-permute-done.11.y_even, ...), custom_call_target="tpu_custom_call" | custom-call | flops 10000000 | bytes 10000000 | tf_op jit(solution)/shard_map/pallas_call | solution.py:496
  37.2 0.0 collective-permute-done.13.other
  37.2 0.9 %shard_map.77 = (f32[16,32,128]{2,1,0:T(8,128)}, f32[1,1]{1,0:T(1,128)}) custom-call(f32[16,32,128]{2,1,0:T(8,128)S(1)} %shard_map.76.filtered, f32[8,128]{1,0:T(8,128)S(1)} %add.7.mine, f32[8,128]{1,0:T(8,128)S(1)} %collective-permute-done.13.other), custom_call_target="tpu_custom_call" | custom-call | tf_op jit(solution)/shard_map/pallas_call | solution.py:502
  (6 shorter events, 0.1 us)
Async XLA Ops:
  2.0 7.2 %collective-permute-start = (f32[9,32,128]{2,1,0:T(8,128)S(1)}, f32[9,32,128]{2,1,0:T(8,128)S(1)}, u32[]{:S(2)}, u32[]{:S(2)}) collective-permute-start(f32[9,32,128]{2,1,0:T(8,128)S(1)} %get-tuple-element.24), channel_id=1, source_target_pairs={{8,16},{16,8},{9,17},{17,9},{10,18},{18,10},{11,19},{19,11},{12,20... | collective-permute-start | bytes 442376 | tf_op jit(solution)/shard_map/ppermute | solution.py:417
  2.6 6.6 %collective-permute-start.1 = (f32[9,32,128]{2,1,0:T(8,128)S(1)}, f32[9,32,128]{2,1,0:T(8,128)S(1)}, u32[]{:S(2)}, u32[]{:S(2)}) collective-permute-start(f32[9,32,128]{2,1,0:T(8,128)S(1)} %get-tuple-element.25), channel_id=1, source_target_pairs={{0,8},{8,0},{16,24},{24,16},{1,9},{9,1},{17,25},{25,17},{2,10},{10... | collective-permute-start | bytes 442376 | tf_op jit(solution)/shard_map/ppermute | solution.py:411
  7.0 8.9 %collective-permute-start.2 = (f32[144,128]{1,0:T(8,128)S(1)}, f32[144,128]{1,0:T(8,128)S(1)}, u32[]{:S(2)}, u32[]{:S(2)}) collective-permute-start(f32[144,128]{1,0:T(8,128)S(1)} %get-tuple-element.26), channel_id=1, source_target_pairs={{0,1},{1,0},{2,3},{3,2},{4,5},{5,4},{6,7},{7,6},{8,9},{9,8},{10,11... | collective-permute-start | bytes 221192 | tf_op jit(solution)/shard_map/ppermute | solution.py:411
  8.5 7.4 %collective-permute-start.3 = (f32[144,128]{1,0:T(8,128)S(1)}, f32[144,128]{1,0:T(8,128)S(1)}, u32[]{:S(2)}, u32[]{:S(2)}) collective-permute-start(f32[144,128]{1,0:T(8,128)S(1)} %get-tuple-element.27), channel_id=1, source_target_pairs={{1,2},{3,4},{5,6},{2,1},{4,3},{6,5},{9,10},{11,12},{13,14},{10,9},... | collective-permute-start | bytes 221192 | tf_op jit(solution)/shard_map/ppermute | solution.py:417
  9.2 10.6 %collective-permute-start.4 = (f32[16,128]{1,0:T(8,128)S(1)}, f32[16,128]{1,0:T(8,128)S(1)}, u32[]{:S(2)}, u32[]{:S(2)}) collective-permute-start(f32[16,128]{1,0:T(8,128)S(1)} %get-tuple-element.28), channel_id=1, source_target_pairs={{1,2},{3,4},{5,6},{2,1},{4,3},{6,5},{9,10},{11,12},{13,14},{10,9},... | collective-permute-start | bytes 24584 | tf_op jit(solution)/shard_map/ppermute | solution.py:417
  9.9 10.0 %collective-permute-start.5 = (f32[16,128]{1,0:T(8,128)S(1)}, f32[16,128]{1,0:T(8,128)S(1)}, u32[]{:S(2)}, u32[]{:S(2)}) collective-permute-start(f32[16,128]{1,0:T(8,128)S(1)} %get-tuple-element.29), channel_id=1, source_target_pairs={{0,1},{1,0},{2,3},{3,2},{4,5},{5,4},{6,7},{7,6},{8,9},{9,8},{10,11... | collective-permute-start | bytes 24584 | tf_op jit(solution)/shard_map/ppermute | solution.py:411
  16.6 5.8 %collective-permute-start.7 = (f32[8,128]{1,0:T(8,128)S(1)}, f32[8,128]{1,0:T(8,128)S(1)}, u32[]{:S(2)}, u32[]{:S(2)}) collective-permute-start(f32[8,128]{1,0:T(8,128)S(1)} %shard_map.73.mine), channel_id=1, source_target_pairs={{0,4},{1,5},{2,6},{3,7},{4,0},{5,1},{6,2},{7,3},{8,12},{9,13},{10,... | collective-permute-start | bytes 12296 | tf_op jit(solution)/shard_map/ppermute | solution.py:421
  21.7 6.3 %collective-permute-start.6 = (f32[4,32,128]{2,1,0:T(8,128)S(1)}, f32[4,32,128]{2,1,0:T(8,128)S(1)}, u32[]{:S(2)}, u32[]{:S(2)}) collective-permute-start(f32[4,32,128]{2,1,0:T(8,128)S(1)} %shard_map.72), channel_id=1, source_target_pairs={{8,16},{16,8},{9,17},{17,9},{10,18},{18,10},{11,19},{19,11},{12,20... | collective-permute-start | bytes 196616 | tf_op jit(solution)/shard_map/ppermute | solution.py:417
  22.4 5.6 %collective-permute-start.8 = (f32[4,32,128]{2,1,0:T(8,128)S(1)}, f32[4,32,128]{2,1,0:T(8,128)S(1)}, u32[]{:S(2)}, u32[]{:S(2)}) collective-permute-start(f32[4,32,128]{2,1,0:T(8,128)S(1)} %get-tuple-element.39), channel_id=1, source_target_pairs={{0,8},{8,0},{16,24},{24,16},{1,9},{9,1},{17,25},{25,17},{2,10},{10... | collective-permute-start | bytes 196616 | tf_op jit(solution)/shard_map/ppermute | solution.py:411
  24.4 3.6 %collective-permute-start.9 = (f32[8,128]{1,0:T(8,128)S(1)}, f32[8,128]{1,0:T(8,128)S(1)}, u32[]{:S(2)}, u32[]{:S(2)}) collective-permute-start(f32[8,128]{1,0:T(8,128)S(1)} %get-tuple-element.40.mine), channel_id=1, source_target_pairs={{0,16},{8,24},{16,0},{24,8},{1,17},{9,25},{17,1},{25,9},{2,18},{10... | collective-permute-start | bytes 12296 | tf_op jit(solution)/shard_map/ppermute | solution.py:421
  28.0 4.1 %collective-permute-start.11 = (f32[88,128]{1,0:T(8,128)S(1)}, f32[88,128]{1,0:T(8,128)S(1)}, u32[]{:S(2)}, u32[]{:S(2)}) collective-permute-start(f32[88,128]{1,0:T(8,128)S(1)} %get-tuple-element.42), channel_id=1, source_target_pairs={{0,1},{1,0},{2,3},{3,2},{4,5},{5,4},{6,7},{7,6},{8,9},{9,8},{10,11... | collective-permute-start | bytes 135176 | tf_op jit(solution)/shard_map/ppermute | solution.py:411
  29.0 6.7 %collective-permute-start.10 = (f32[80,128]{1,0:T(8,128)S(1)}, f32[80,128]{1,0:T(8,128)S(1)}, u32[]{:S(2)}, u32[]{:S(2)}) collective-permute-start(f32[80,128]{1,0:T(8,128)S(1)} %get-tuple-element.41), channel_id=1, source_target_pairs={{1,2},{3,4},{5,6},{2,1},{4,3},{6,5},{9,10},{11,12},{13,14},{10,9},... | collective-permute-start | bytes 122888 | tf_op jit(solution)/shard_map/ppermute | solution.py:417
  32.1 3.6 %collective-permute-start.12 = (f32[8,128]{1,0:T(8,128)S(1)}, f32[8,128]{1,0:T(8,128)S(1)}, u32[]{:S(2)}, u32[]{:S(2)}) collective-permute-start(f32[8,128]{1,0:T(8,128)S(1)} %slice_add_fusion), channel_id=1, source_target_pairs={{0,2},{1,3},{2,0},{3,1},{4,6},{5,7},{6,4},{7,5},{8,10},{9,11},{10,... | collective-permute-start | bytes 12296 | tf_op jit(solution)/shard_map/ppermute | solution.py:421
  35.7 1.5 %collective-permute-start.13 = (f32[8,128]{1,0:T(8,128)S(1)}, f32[8,128]{1,0:T(8,128)S(1)}, u32[]{:S(2)}, u32[]{:S(2)}) collective-permute-start(f32[8,128]{1,0:T(8,128)S(1)} %add.7.mine), channel_id=1, source_target_pairs={{0,8},{8,0},{16,24},{24,16},{1,9},{9,1},{17,25},{25,17},{2,10},{10... | collective-permute-start | bytes 12296 | tf_op jit(solution)/shard_map/ppermute | solution.py:421

commit v16 on v12

--- a/solution.py
+++ b/solution.py
@@ -303,7 +303,7 @@
         odd_out[at:at + rows] = jnp.where(y_swap, high, low)
 
 
-def relaxation(raw, size_x, size_y, size_z):
+def relaxation(raw, scales, size_x, size_y, size_z):
     width = FILTER_SWEEPS
     wide = size_y + 2 * RIM
     extent_x = lax.axis_size("gx") * size_x
@@ -319,8 +319,9 @@
 
     count = edges(place, extent_y) + edges(lane, size_z)
     inside = (place >= 0) & (place < extent_y)
-    scale_two = jnp.where(inside, 1.0 / (1.0 + radius_sq * (count + 2.0)), 0.0)
-    scale_one = jnp.where(inside, 1.0 / (1.0 + radius_sq * (count + 1.0)), 0.0)
+    scales[pl.ds(0, 1)] = jnp.zeros((1, wide, size_z), jnp.float32)
+    scales[pl.ds(1, 1)] = jnp.where(inside, 1.0 / (1.0 + radius_sq * (count + 1.0)), 0.0)
+    scales[pl.ds(2, 1)] = jnp.where(inside, 1.0 / (1.0 + radius_sq * (count + 2.0)), 0.0)
 
     def relax(src, x, n):
         f = src[pl.ds(x, n)]
@@ -332,14 +333,14 @@
             at = base_x + x + k
             outside = (at < 0) | (at >= extent_x)
             border = (at == 0) | (at == extent_x - 1)
-            scale = jnp.where(outside, 0.0, jnp.where(border, scale_one, scale_two))
-            scaled.append(total[k:k + 1] * scale)
+            which = jnp.where(outside, 0, jnp.where(border, 1, 2))
+            scaled.append(total[k:k + 1] * scales[pl.ds(which, 1)])
         return jnp.concatenate(scaled, axis=0)
 
     return relax
 
 
-def filter_part(x_odd, x_even, y_odd, y_even, raw_in, labels, out, raw, odd, even):
+def filter_part(x_odd, x_even, y_odd, y_even, raw_in, labels, out, raw, odd, even, scales):
     size_x, size_y, size_z = raw_in.shape
     width = FILTER_SWEEPS
     tile = pl.ds(0, size_y)
@@ -350,7 +351,7 @@
     planes_loop(0, size_x, 4, fill)
     unpack_planes(raw, width, x_even[...], x_odd[...], size_x, size_y)
     unpack_rows((raw,), (width,), segments((width,), size_x)[0], y_even, y_odd, size_y)
-    relax = relaxation(raw, size_x, size_y, size_z)
+    relax = relaxation(raw, scales, size_x, size_y, size_z)
     src = raw
     for sweep in range(FILTER_SWEEPS - 1):
         dst = (odd, even)[sweep % 2]
@@ -456,7 +457,7 @@
     filtered = call(
         filter_part,
         f32(*shape),
-        [room(2 * FILTER_SWEEPS)] * 3,
+        [room(2 * FILTER_SWEEPS)] * 3 + [pltpu.VMEM((3, wide, size_z), jnp.float32)],
         cost=10000000,
     )(x_odd, x_even, y_odd, y_even, raw, own[1])
     sensitivity, mean_energy = pl.pallas_call(

time: 38.2 us -> 38.2 us (level)
  no operation moved by 1% of the time
where the time goes in v16:
time: 38.2 us; the launch traced here: 37.9 us
  starting transfers between devices  22.2 us (58%)
  waiting for transfers between devices  8.29 us (22%)
  Pallas kernels  6.68 us (17%)
  between operations  0.75 us (2%)
    ppermute x5, starting transfers between devices, swap_even(): lax.ppermute(value, axis, [(i, i ^ 1) for i in range(lax.axis_size(axis))])  16 us
    ppermute x4, waiting for transfers between devices, partner(): lax.ppermute(value, axis, [(i, i ^ bit) for i in range(lax.axis_size(axis...  5.92 us
    ppermute x5, starting transfers between devices, swap_odd(): return lax.ppermute(value, axis, up + [(b, a) for a, b in up])  3.3 us
    ppermute x4, starting transfers between devices, partner(): lax.ppermute(value, axis, [(i, i ^ bit) for i in range(lax.axis_size(axis...  2.93 us
    ppermute x5, waiting for transfers between devices, swap_even(): lax.ppermute(value, axis, [(i, i ^ 1) for i in range(lax.axis_size(axis))])  2.36 us
    pallas_call x1, Pallas kernels, shards(): call(adjoint_part, f32(*shape), [room(6), room(6), room(4), room(2), room...  2.23 us
    pallas_call x1, Pallas kernels, shards(): call(filter_part, f32(*shape), [room(2 * FILTER_SWEEPS)] * 3 + [pltpu.VME...  1.51 us
    pallas_call x1, Pallas kernels, shards(): pl.pallas_call(pack_own, out_shape=(f32(planes, size_y, size_z),) * 2 + (...  1.33 us
  transfers between devices with their start and end apart: 14, of which 4 were waited for; matrix products, arithmetic and copies ran while one was open for 0% of the time, Pallas kernels for 12%

profile of v16, /device:TPU:0, one launch (start us, length us, event | category | flops | bytes accessed | tf_op | source)
XLA Modules:
  0.0 37.9 jit_solution(10840519038913781511)
XLA Ops:
  0.6 1.3 %shard_map.68 = (f32[9,32,128]{2,1,0:T(8,128)S(1)}, f32[9,32,128]{2,1,0:T(8,128)S(1)}, f32[144,128]{1,0:T(8,128)S(1)}, f32[144,128]{1,0:T(8,128)S(1)}, f32[16,32...) custom-call(f32[16,32,128]{2,1,0:T(8,128)} %refs_0_.1, ...), custom_call_target="tpu_custom_call" | custom-call | tf_op jit(solution)/shard_map/pallas_call | solution.py:415
  2.0 0.7 %collective-permute-start = (f32[9,32,128]{2,1,0:T(8,128)S(1)}, f32[9,32,128]{2,1,0:T(8,128)S(1)}, u32[]{:S(2)}, u32[]{:S(2)}) collective-permute-start(f32[9,32,128]{2,1,0:T(8,128)S(1)} %get-tuple-element.20), channel_id=1, source_target_pairs={{8,16},{16,8},{9,17},{17,9},{10,18},{18,10},{11,19},{19,11},{12,20... | collective-permute-start | bytes 442376 | tf_op jit(solution)/shard_map/ppermute | solution.py:387
  2.6 4.4 %collective-permute-start.1 = (f32[9,32,128]{2,1,0:T(8,128)S(1)}, f32[9,32,128]{2,1,0:T(8,128)S(1)}, u32[]{:S(2)}, u32[]{:S(2)}) collective-permute-start(f32[9,32,128]{2,1,0:T(8,128)S(1)} %get-tuple-element.21), channel_id=1, source_target_pairs={{0,8},{8,0},{16,24},{24,16},{1,9},{9,1},{17,25},{25,17},{2,10},{10... | collective-permute-start | bytes 442376 | tf_op jit(solution)/shard_map/ppermute | solution.py:381
  7.0 0.7 %collective-permute-start.2 = (f32[144,128]{1,0:T(8,128)S(1)}, f32[144,128]{1,0:T(8,128)S(1)}, u32[]{:S(2)}, u32[]{:S(2)}) collective-permute-start(f32[144,128]{1,0:T(8,128)S(1)} %get-tuple-element.22), channel_id=1, source_target_pairs={{1,2},{3,4},{5,6},{2,1},{4,3},{6,5},{9,10},{11,12},{13,14},{10,9},... | collective-permute-start | bytes 221192 | tf_op jit(solution)/shard_map/ppermute | solution.py:387
  7.7 4.3 %collective-permute-start.3 = (f32[144,128]{1,0:T(8,128)S(1)}, f32[144,128]{1,0:T(8,128)S(1)}, u32[]{:S(2)}, u32[]{:S(2)}) collective-permute-start(f32[144,128]{1,0:T(8,128)S(1)} %get-tuple-element.23), channel_id=1, source_target_pairs={{0,1},{1,0},{2,3},{3,2},{4,5},{5,4},{6,7},{7,6},{8,9},{9,8},{10,11... | collective-permute-start | bytes 221192 | tf_op jit(solution)/shard_map/ppermute | solution.py:381
  12.0 0.0 collective-permute-done.x_odd
  12.0 0.0 collective-permute-done.1.x_even
  12.0 0.7 %collective-permute-start.4 = (f32[16,128]{1,0:T(8,128)S(1)}, f32[16,128]{1,0:T(8,128)S(1)}, u32[]{:S(2)}, u32[]{:S(2)}) collective-permute-start(f32[16,128]{1,0:T(8,128)S(1)} %get-tuple-element.24), channel_id=1, source_target_pairs={{1,2},{3,4},{5,6},{2,1},{4,3},{6,5},{9,10},{11,12},{13,14},{10,9},... | collective-permute-start | bytes 24584 | tf_op jit(solution)/shard_map/ppermute | solution.py:387
  12.7 4.4 %collective-permute-start.5 = (f32[16,128]{1,0:T(8,128)S(1)}, f32[16,128]{1,0:T(8,128)S(1)}, u32[]{:S(2)}, u32[]{:S(2)}) collective-permute-start(f32[16,128]{1,0:T(8,128)S(1)} %get-tuple-element.25), channel_id=1, source_target_pairs={{0,1},{1,0},{2,3},{3,2},{4,5},{5,4},{6,7},{7,6},{8,9},{9,8},{10,11... | collective-permute-start | bytes 24584 | tf_op jit(solution)/shard_map/ppermute | solution.py:381
  17.1 0.0 collective-permute-done.2.y_odd
  17.1 0.0 collective-permute-done.3.y_even
  17.1 0.7 %shard_map.72.mine = f32[8,128]{1,0:T(8,128)S(1)} custom-call(f32[9,32,128]{2,1,0:T(8,128)S(1)} %collective-permute-done.x_odd, f32[9,32,128]{2,1,0:T(8,128)S(1)} %collective-permute-done.1.x_even, f32[144,128]{1,0:T(8,128)S(1)} %collective-permute-done.2.y_odd, f32[144,128]{1,0:T(8,128)S(1)} %collective-permute-done.3.y_even, ...), custom_call_target="tpu_custom_call" | custom-call | flops 10000 | bytes 10000 | tf_op jit(solution)/shard_map/pallas_call | solution.py:436
  17.8 1.1 %collective-permute-start.7 = (f32[8,128]{1,0:T(8,128)S(1)}, f32[8,128]{1,0:T(8,128)S(1)}, u32[]{:S(2)}, u32[]{:S(2)}) collective-permute-start(f32[8,128]{1,0:T(8,128)S(1)} %shard_map.72.mine), channel_id=1, source_target_pairs={{0,4},{1,5},{2,6},{3,7},{4,0},{5,1},{6,2},{7,3},{8,12},{9,13},{10,... | collective-permute-start | bytes 12296 | tf_op jit(solution)/shard_map/ppermute | solution.py:391
  18.9 0.0 collective-permute-done.4.corner_odd
  18.9 0.0 collective-permute-done.5.corner_even
  18.9 2.2 %shard_map.70.raw.raw_in = f32[16,32,128]{2,1,0:T(8,128)S(1)} custom-call(f32[9,32,128]{2,1,0:T(8,128)S(1)} %collective-permute-done.x_odd, f32[9,32,128]{2,1,0:T(8,128)S(1)} %collective-permute-done.1.x_even, f32[144,128]{1,0:T(8,128)S(1)} %collective-permute-done.2.y_odd, f32[144,128]{1,0:T(8,128)S(1)} %collective-permute-done.3.y_even, ...), custom_call_target="tpu_custom_call" | custom-call | flops 10000000 | bytes 10000000 | tf_op jit(solution)/shard_map/pallas_call | solution.py:439
  21.2 0.7 %collective-permute-start.6 = (f32[4,32,128]{2,1,0:T(8,128)S(1)}, f32[4,32,128]{2,1,0:T(8,128)S(1)}, u32[]{:S(2)}, u32[]{:S(2)}) collective-permute-start(f32[4,32,128]{2,1,0:T(8,128)S(1)} %shard_map.71), channel_id=1, source_target_pairs={{8,16},{16,8},{9,17},{17,9},{10,18},{18,10},{11,19},{19,11},{12,20... | collective-permute-start | bytes 196616 | tf_op jit(solution)/shard_map/ppermute | solution.py:387
  21.8 0.5 %collective-permute-done.7.other = f32[8,128]{1,0:T(8,128)S(1)} collective-permute-done((f32[8,128]{1,0:T(8,128)S(1)}, f32[8,128]{1,0:T(8,128)S(1)}, u32[]{:S(2)}, u32[]{:S(2)}) %collective-permute-start.7) | collective-permute-done | bytes 4128 | tf_op jit(solution)/shard_map/ppermute | solution.py:391
  22.3 1.8 %collective-permute-start.8 = (f32[4,32,128]{2,1,0:T(8,128)S(1)}, f32[4,32,128]{2,1,0:T(8,128)S(1)}, u32[]{:S(2)}, u32[]{:S(2)}) collective-permute-start(f32[4,32,128]{2,1,0:T(8,128)S(1)} %get-tuple-element.31), channel_id=1, source_target_pairs={{0,8},{8,0},{16,24},{24,16},{1,9},{9,1},{17,25},{25,17},{2,10},{10... | collective-permute-start | bytes 196616 | tf_op jit(solution)/shard_map/ppermute | solution.py:381
  24.2 0.4 collective-permute-start.9
  24.5 3.3 %collective-permute-done.9.other = f32[8,128]{1,0:T(8,128)S(1)} collective-permute-done((f32[8,128]{1,0:T(8,128)S(1)}, f32[8,128]{1,0:T(8,128)S(1)}, u32[]{:S(2)}, u32[]{:S(2)}) %collective-permute-start.9) | collective-permute-done | bytes 4128 | tf_op jit(solution)/shard_map/ppermute | solution.py:391
  27.8 0.0 collective-permute-done.6.x_odd
  27.8 0.0 collective-permute-done.8.x_even
  27.8 1.1 %collective-permute-start.11 = (f32[88,128]{1,0:T(8,128)S(1)}, f32[88,128]{1,0:T(8,128)S(1)}, u32[]{:S(2)}, u32[]{:S(2)}) collective-permute-start(f32[88,128]{1,0:T(8,128)S(1)} %get-tuple-element.34), channel_id=1, source_target_pairs={{0,1},{1,0},{2,3},{3,2},{4,5},{5,4},{6,7},{7,6},{8,9},{9,8},{10,11... | collective-permute-start | bytes 135176 | tf_op jit(solution)/shard_map/ppermute | solution.py:381
  28.9 0.7 %collective-permute-start.10 = (f32[80,128]{1,0:T(8,128)S(1)}, f32[80,128]{1,0:T(8,128)S(1)}, u32[]{:S(2)}, u32[]{:S(2)}) collective-permute-start(f32[80,128]{1,0:T(8,128)S(1)} %get-tuple-element.33), channel_id=1, source_target_pairs={{1,2},{3,4},{5,6},{2,1},{4,3},{6,5},{9,10},{11,12},{13,14},{10,9},... | collective-permute-start | bytes 122888 | tf_op jit(solution)/shard_map/ppermute | solution.py:387
  29.6 2.4 %collective-permute-done.11.y_even = f32[88,128]{1,0:T(8,128)S(1)} collective-permute-done((f32[88,128]{1,0:T(8,128)S(1)}, f32[88,128]{1,0:T(8,128)S(1)}, u32[]{:S(2)}, u32[]{:S(2)}) %collective-permute-start.11) | collective-permute-done | bytes 45088 | tf_op jit(solution)/shard_map/ppermute | solution.py:381
  31.9 1.4 %collective-permute-start.12 = (f32[8,128]{1,0:T(8,128)S(1)}, f32[8,128]{1,0:T(8,128)S(1)}, u32[]{:S(2)}, u32[]{:S(2)}) collective-permute-start(f32[8,128]{1,0:T(8,128)S(1)} %slice_add_fusion), channel_id=1, source_target_pairs={{0,2},{1,3},{2,0},{3,1},{4,6},{5,7},{6,4},{7,5},{8,10},{9,11},{10,... | collective-permute-start | bytes 12296 | tf_op jit(solution)/shard_map/ppermute | solution.py:391
  33.4 2.2 %collective-permute-done.12 = f32[8,128]{1,0:T(8,128)S(1)} collective-permute-done((f32[8,128]{1,0:T(8,128)S(1)}, f32[8,128]{1,0:T(8,128)S(1)}, u32[]{:S(2)}, u32[]{:S(2)}) %collective-permute-start.12) | collective-permute-done | bytes 4128 | tf_op jit(solution)/shard_map/ppermute | solution.py:391
  35.5 0.0 collective-permute-start.13
  35.6 0.0 collective-permute-done.10.y_odd
  35.6 1.5 %shard_map.75.filtered = f32[16,32,128]{2,1,0:T(8,128)S(1)} custom-call(f32[4,32,128]{2,1,0:T(8,128)S(1)} %collective-permute-done.6.x_odd, f32[4,32,128]{2,1,0:T(8,128)S(1)} %collective-permute-done.8.x_even, f32[80,128]{1,0:T(8,128)S(1)} %collective-permute-done.10.y_odd, f32[88,128]{1,0:T(8,128)S(1)} %collective-permute-done.11.y_even, ...), custom_call_target="tpu_custom_call" | custom-call | flops 10000000 | bytes 10000000 | tf_op jit(solution)/shard_map/pallas_call | solution.py:457
  37.1 0.0 collective-permute-done.13.other
  37.1 0.9 %shard_map.76 = (f32[16,32,128]{2,1,0:T(8,128)}, f32[1,1]{1,0:T(1,128)}) custom-call(f32[16,32,128]{2,1,0:T(8,128)S(1)} %shard_map.75.filtered, f32[8,128]{1,0:T(8,128)S(1)} %add.7.mine, f32[8,128]{1,0:T(8,128)S(1)} %collective-permute-done.13.other), custom_call_target="tpu_custom_call" | custom-call | tf_op jit(solution)/shard_map/pallas_call | solution.py:463
  (6 shorter events, 0.1 us)
Async XLA Ops:
  2.0 10.0 %collective-permute-start = (f32[9,32,128]{2,1,0:T(8,128)S(1)}, f32[9,32,128]{2,1,0:T(8,128)S(1)}, u32[]{:S(2)}, u32[]{:S(2)}) collective-permute-start(f32[9,32,128]{2,1,0:T(8,128)S(1)} %get-tuple-element.20), channel_id=1, source_target_pairs={{8,16},{16,8},{9,17},{17,9},{10,18},{18,10},{11,19},{19,11},{12,20... | collective-permute-start | bytes 442376 | tf_op jit(solution)/shard_map/ppermute | solution.py:387
  2.6 9.4 %collective-permute-start.1 = (f32[9,32,128]{2,1,0:T(8,128)S(1)}, f32[9,32,128]{2,1,0:T(8,128)S(1)}, u32[]{:S(2)}, u32[]{:S(2)}) collective-permute-start(f32[9,32,128]{2,1,0:T(8,128)S(1)} %get-tuple-element.21), channel_id=1, source_target_pairs={{0,8},{8,0},{16,24},{24,16},{1,9},{9,1},{17,25},{25,17},{2,10},{10... | collective-permute-start | bytes 442376 | tf_op jit(solution)/shard_map/ppermute | solution.py:381
  7.0 10.1 %collective-permute-start.2 = (f32[144,128]{1,0:T(8,128)S(1)}, f32[144,128]{1,0:T(8,128)S(1)}, u32[]{:S(2)}, u32[]{:S(2)}) collective-permute-start(f32[144,128]{1,0:T(8,128)S(1)} %get-tuple-element.22), channel_id=1, source_target_pairs={{1,2},{3,4},{5,6},{2,1},{4,3},{6,5},{9,10},{11,12},{13,14},{10,9},... | collective-permute-start | bytes 221192 | tf_op jit(solution)/shard_map/ppermute | solution.py:387
  7.7 9.4 %collective-permute-start.3 = (f32[144,128]{1,0:T(8,128)S(1)}, f32[144,128]{1,0:T(8,128)S(1)}, u32[]{:S(2)}, u32[]{:S(2)}) collective-permute-start(f32[144,128]{1,0:T(8,128)S(1)} %get-tuple-element.23), channel_id=1, source_target_pairs={{0,1},{1,0},{2,3},{3,2},{4,5},{5,4},{6,7},{7,6},{8,9},{9,8},{10,11... | collective-permute-start | bytes 221192 | tf_op jit(solution)/shard_map/ppermute | solution.py:381
  12.0 6.9 %collective-permute-start.4 = (f32[16,128]{1,0:T(8,128)S(1)}, f32[16,128]{1,0:T(8,128)S(1)}, u32[]{:S(2)}, u32[]{:S(2)}) collective-permute-start(f32[16,128]{1,0:T(8,128)S(1)} %get-tuple-element.24), channel_id=1, source_target_pairs={{1,2},{3,4},{5,6},{2,1},{4,3},{6,5},{9,10},{11,12},{13,14},{10,9},... | collective-permute-start | bytes 24584 | tf_op jit(solution)/shard_map/ppermute | solution.py:387
  12.7 6.2 %collective-permute-start.5 = (f32[16,128]{1,0:T(8,128)S(1)}, f32[16,128]{1,0:T(8,128)S(1)}, u32[]{:S(2)}, u32[]{:S(2)}) collective-permute-start(f32[16,128]{1,0:T(8,128)S(1)} %get-tuple-element.25), channel_id=1, source_target_pairs={{0,1},{1,0},{2,3},{3,2},{4,5},{5,4},{6,7},{7,6},{8,9},{9,8},{10,11... | collective-permute-start | bytes 24584 | tf_op jit(solution)/shard_map/ppermute | solution.py:381
  17.8 4.6 %collective-permute-start.7 = (f32[8,128]{1,0:T(8,128)S(1)}, f32[8,128]{1,0:T(8,128)S(1)}, u32[]{:S(2)}, u32[]{:S(2)}) collective-permute-start(f32[8,128]{1,0:T(8,128)S(1)} %shard_map.72.mine), channel_id=1, source_target_pairs={{0,4},{1,5},{2,6},{3,7},{4,0},{5,1},{6,2},{7,3},{8,12},{9,13},{10,... | collective-permute-start | bytes 12296 | tf_op jit(solution)/shard_map/ppermute | solution.py:391
  21.2 6.6 %collective-permute-start.6 = (f32[4,32,128]{2,1,0:T(8,128)S(1)}, f32[4,32,128]{2,1,0:T(8,128)S(1)}, u32[]{:S(2)}, u32[]{:S(2)}) collective-permute-start(f32[4,32,128]{2,1,0:T(8,128)S(1)} %shard_map.71), channel_id=1, source_target_pairs={{8,16},{16,8},{9,17},{17,9},{10,18},{18,10},{11,19},{19,11},{12,20... | collective-permute-start | bytes 196616 | tf_op jit(solution)/shard_map/ppermute | solution.py:387
  22.3 5.4 %collective-permute-start.8 = (f32[4,32,128]{2,1,0:T(8,128)S(1)}, f32[4,32,128]{2,1,0:T(8,128)S(1)}, u32[]{:S(2)}, u32[]{:S(2)}) collective-permute-start(f32[4,32,128]{2,1,0:T(8,128)S(1)} %get-tuple-element.31), channel_id=1, source_target_pairs={{0,8},{8,0},{16,24},{24,16},{1,9},{9,1},{17,25},{25,17},{2,10},{10... | collective-permute-start | bytes 196616 | tf_op jit(solution)/shard_map/ppermute | solution.py:381
  24.2 3.6 %collective-permute-start.9 = (f32[8,128]{1,0:T(8,128)S(1)}, f32[8,128]{1,0:T(8,128)S(1)}, u32[]{:S(2)}, u32[]{:S(2)}) collective-permute-start(f32[8,128]{1,0:T(8,128)S(1)} %get-tuple-element.32.mine), channel_id=1, source_target_pairs={{0,16},{8,24},{16,0},{24,8},{1,17},{9,25},{17,1},{25,9},{2,18},{10... | collective-permute-start | bytes 12296 | tf_op jit(solution)/shard_map/ppermute | solution.py:391
  27.8 4.1 %collective-permute-start.11 = (f32[88,128]{1,0:T(8,128)S(1)}, f32[88,128]{1,0:T(8,128)S(1)}, u32[]{:S(2)}, u32[]{:S(2)}) collective-permute-start(f32[88,128]{1,0:T(8,128)S(1)} %get-tuple-element.34), channel_id=1, source_target_pairs={{0,1},{1,0},{2,3},{3,2},{4,5},{5,4},{6,7},{7,6},{8,9},{9,8},{10,11... | collective-permute-start | bytes 135176 | tf_op jit(solution)/shard_map/ppermute | solution.py:381
  28.9 6.6 %collective-permute-start.10 = (f32[80,128]{1,0:T(8,128)S(1)}, f32[80,128]{1,0:T(8,128)S(1)}, u32[]{:S(2)}, u32[]{:S(2)}) collective-permute-start(f32[80,128]{1,0:T(8,128)S(1)} %get-tuple-element.33), channel_id=1, source_target_pairs={{1,2},{3,4},{5,6},{2,1},{4,3},{6,5},{9,10},{11,12},{13,14},{10,9},... | collective-permute-start | bytes 122888 | tf_op jit(solution)/shard_map/ppermute | solution.py:387
  31.9 3.6 %collective-permute-start.12 = (f32[8,128]{1,0:T(8,128)S(1)}, f32[8,128]{1,0:T(8,128)S(1)}, u32[]{:S(2)}, u32[]{:S(2)}) collective-permute-start(f32[8,128]{1,0:T(8,128)S(1)} %slice_add_fusion), channel_id=1, source_target_pairs={{0,2},{1,3},{2,0},{3,1},{4,6},{5,7},{6,4},{7,5},{8,10},{9,11},{10,... | collective-permute-start | bytes 12296 | tf_op jit(solution)/shard_map/ppermute | solution.py:391
  35.5 1.5 %collective-permute-start.13 = (f32[8,128]{1,0:T(8,128)S(1)}, f32[8,128]{1,0:T(8,128)S(1)}, u32[]{:S(2)}, u32[]{:S(2)}) collective-permute-start(f32[8,128]{1,0:T(8,128)S(1)} %add.7.mine), channel_id=1, source_target_pairs={{0,8},{8,0},{16,24},{24,16},{1,9},{9,1},{17,25},{25,17},{2,10},{10... | collective-permute-start | bytes 12296 | tf_op jit(solution)/shard_map/ppermute | solution.py:391

commit v17 on v12

--- a/solution.py
+++ b/solution.py
@@ -219,7 +219,7 @@
     def faces_x(x, n):
         face_x[pl.ds(x, n)] = harmonic(permit[pl.ds(x, n)], permit[pl.ds(x + 1, n)])
 
-    planes_loop(0, size_x + 5, 7, faces_x)
+    planes_loop(0, size_x + 5, 21, faces_x)
 
     def weigh(x, n):
         span = pl.ds(x, n)
@@ -231,7 +231,7 @@
         total = screen + face_x[span] + face_x[pl.ds(x + 1, n)] + fy + shift(fy, 1, 1) + fz + shift(fz, 1, 2)
         inverse[span] = jnp.where(p > 20.0, 0.0, inverted(total))
 
-    planes_loop(0, size_x + 4, 10, weigh)
+    planes_loop(0, size_x + 4, 20, weigh)
 
     def relax(x, n, a, a_low, a_high):
         span = pl.ds(x, n)
@@ -244,12 +244,12 @@
     def sweep_one(x, n):
         first[pl.ds(x, n)] = relax(x, n, start[pl.ds(x + 1, n)], start[pl.ds(x, n)], start[pl.ds(x + 2, n)])
 
-    planes_loop(0, size_x + 4, 10, sweep_one)
+    planes_loop(0, size_x + 4, 20, sweep_one)
 
     def sweep_two(x, n):
         second[pl.ds(x, n)] = relax(x + 1, n, first[pl.ds(x + 1, n)], first[pl.ds(x, n)], first[pl.ds(x + 2, n)])
 
-    planes_loop(0, size_x + 2, 9, sweep_two)
+    planes_loop(0, size_x + 2, 18, sweep_two)
 
     def finish(x, n):
         span = pl.ds(x, n)
@@ -264,7 +264,7 @@
         gain = jnp.where(labels[span] == 1, -1.5 * (eps_solid - eps_void) * d * d, 0.0)
         raw_out[span] = gain * product[:, :size_y]
 
-    planes_loop(0, size_x, 8, finish)
+    planes_loop(0, size_x, 16, finish)
 
 
 def pack_raw_x(raw, out, low):
@@ -358,14 +358,14 @@
         def step(x, n, src=src, dst=dst):
             dst[pl.ds(x, n)] = relax(src, x, n)
 
-        planes_loop(sweep + 1, size_x + 2 * width - sweep - 1, 11, step)
+        planes_loop(sweep + 1, size_x + 2 * width - sweep - 1, 22, step)
         src = dst
 
     def last(x, n):
         f = relax(src, x + width, n)[:, :size_y]
         out[pl.ds(x, n)] = jnp.where(labels[pl.ds(x, n)] == 1, f, 0.0)
 
-    planes_loop(0, size_x, 8, last)
+    planes_loop(0, size_x, 16, last)
 
 
 def rescale(filtered, mine, other, out, mean_out):

time: 38.2 us -> 37.2 us (0.974)
  Pallas kernels: 6.63 us -> 5.51 us
  waiting for transfers between devices: 8.29 us -> 9.1 us
  starting transfers between devices: 22.2 us -> 21.6 us
    ppermute x4, waiting for transfers between devices: 5.92 us -> 6.72 us  [partner(): lax.ppermute(value, axis, [(i, i ^ bit) for i in range(lax.axis_size(axis...]
    ppermute x5, starting transfers between devices: 16 us -> 15.4 us  [swap_even(): lax.ppermute(value, axis, [(i, i ^ 1) for i in range(lax.axis_size(axis))])]
    pallas_call x1, Pallas kernels: 2.23 us -> 1.66 us  [shards(): call(adjoint_part, f32(*shape), [room(6), room(6), room(4), room(2), room...]
    pallas_call x1, Pallas kernels: 1.46 us -> 0.91 us  [shards(): call(filter_part, f32(*shape), [room(2 * FILTER_SWEEPS)] * 3, cost=10000000)]
  transfers between devices with their start and end apart: 14 -> 14, of which waited for: 4 -> 5; matrix products, arithmetic and copies ran while one was open for 0% -> 0% of each run, Pallas kernels for 12% -> 9%
where the time goes in v17:
time: 37.2 us; the launch traced here: 37 us
  starting transfers between devices  21.6 us (58%)
  waiting for transfers between devices  9.1 us (24%)
  Pallas kernels  5.51 us (15%)
  between operations  0.74 us (2%)
    ppermute x5, starting transfers between devices, swap_even(): lax.ppermute(value, axis, [(i, i ^ 1) for i in range(lax.axis_size(axis))])  15.4 us
    ppermute x4, waiting for transfers between devices, partner(): lax.ppermute(value, axis, [(i, i ^ bit) for i in range(lax.axis_size(axis...  6.72 us
    ppermute x5, starting transfers between devices, swap_odd(): return lax.ppermute(value, axis, up + [(b, a) for a, b in up])  3.3 us
    ppermute x4, starting transfers between devices, partner(): lax.ppermute(value, axis, [(i, i ^ bit) for i in range(lax.axis_size(axis...  2.93 us
    ppermute x5, waiting for transfers between devices, swap_even(): lax.ppermute(value, axis, [(i, i ^ 1) for i in range(lax.axis_size(axis))])  2.36 us
    pallas_call x1, Pallas kernels, shards(): call(adjoint_part, f32(*shape), [room(6), room(6), room(4), room(2), room...  1.66 us
    pallas_call x1, Pallas kernels, shards(): pl.pallas_call(pack_own, out_shape=(f32(planes, size_y, size_z),) * 2 + (...  1.33 us
    pallas_call x1, Pallas kernels, shards(): call(filter_part, f32(*shape), [room(2 * FILTER_SWEEPS)] * 3, cost=10000000)  0.91 us
  transfers between devices with their start and end apart: 14, of which 5 were waited for; matrix products, arithmetic and copies ran while one was open for 0% of the time, Pallas kernels for 9%

profile of v17, /device:TPU:0, one launch (start us, length us, event | category | flops | bytes accessed | tf_op | source)
XLA Modules:
  0.0 37.0 jit_solution(959407113660343161)
XLA Ops:
  0.6 1.3 %shard_map.68 = (f32[9,32,128]{2,1,0:T(8,128)S(1)}, f32[9,32,128]{2,1,0:T(8,128)S(1)}, f32[144,128]{1,0:T(8,128)S(1)}, f32[144,128]{1,0:T(8,128)S(1)}, f32[16,32...) custom-call(f32[16,32,128]{2,1,0:T(8,128)} %refs_0_.1, ...), custom_call_target="tpu_custom_call" | custom-call | tf_op jit(solution)/shard_map/pallas_call | solution.py:414
  2.0 0.7 %collective-permute-start = (f32[9,32,128]{2,1,0:T(8,128)S(1)}, f32[9,32,128]{2,1,0:T(8,128)S(1)}, u32[]{:S(2)}, u32[]{:S(2)}) collective-permute-start(f32[9,32,128]{2,1,0:T(8,128)S(1)} %get-tuple-element.20), channel_id=1, source_target_pairs={{8,16},{16,8},{9,17},{17,9},{10,18},{18,10},{11,19},{19,11},{12,20... | collective-permute-start | bytes 442376 | tf_op jit(solution)/shard_map/ppermute | solution.py:386
  2.6 4.4 %collective-permute-start.1 = (f32[9,32,128]{2,1,0:T(8,128)S(1)}, f32[9,32,128]{2,1,0:T(8,128)S(1)}, u32[]{:S(2)}, u32[]{:S(2)}) collective-permute-start(f32[9,32,128]{2,1,0:T(8,128)S(1)} %get-tuple-element.21), channel_id=1, source_target_pairs={{0,8},{8,0},{16,24},{24,16},{1,9},{9,1},{17,25},{25,17},{2,10},{10... | collective-permute-start | bytes 442376 | tf_op jit(solution)/shard_map/ppermute | solution.py:380
  7.0 0.7 %collective-permute-start.2 = (f32[144,128]{1,0:T(8,128)S(1)}, f32[144,128]{1,0:T(8,128)S(1)}, u32[]{:S(2)}, u32[]{:S(2)}) collective-permute-start(f32[144,128]{1,0:T(8,128)S(1)} %get-tuple-element.22), channel_id=1, source_target_pairs={{1,2},{3,4},{5,6},{2,1},{4,3},{6,5},{9,10},{11,12},{13,14},{10,9},... | collective-permute-start | bytes 221192 | tf_op jit(solution)/shard_map/ppermute | solution.py:386
  7.7 4.3 %collective-permute-start.3 = (f32[144,128]{1,0:T(8,128)S(1)}, f32[144,128]{1,0:T(8,128)S(1)}, u32[]{:S(2)}, u32[]{:S(2)}) collective-permute-start(f32[144,128]{1,0:T(8,128)S(1)} %get-tuple-element.23), channel_id=1, source_target_pairs={{0,1},{1,0},{2,3},{3,2},{4,5},{5,4},{6,7},{7,6},{8,9},{9,8},{10,11... | collective-permute-start | bytes 221192 | tf_op jit(solution)/shard_map/ppermute | solution.py:380
  12.0 0.0 collective-permute-done.x_odd
  12.0 0.0 collective-permute-done.1.x_even
  12.0 0.7 %collective-permute-start.4 = (f32[16,128]{1,0:T(8,128)S(1)}, f32[16,128]{1,0:T(8,128)S(1)}, u32[]{:S(2)}, u32[]{:S(2)}) collective-permute-start(f32[16,128]{1,0:T(8,128)S(1)} %get-tuple-element.24), channel_id=1, source_target_pairs={{1,2},{3,4},{5,6},{2,1},{4,3},{6,5},{9,10},{11,12},{13,14},{10,9},... | collective-permute-start | bytes 24584 | tf_op jit(solution)/shard_map/ppermute | solution.py:386
  12.7 4.4 %collective-permute-start.5 = (f32[16,128]{1,0:T(8,128)S(1)}, f32[16,128]{1,0:T(8,128)S(1)}, u32[]{:S(2)}, u32[]{:S(2)}) collective-permute-start(f32[16,128]{1,0:T(8,128)S(1)} %get-tuple-element.25), channel_id=1, source_target_pairs={{0,1},{1,0},{2,3},{3,2},{4,5},{5,4},{6,7},{7,6},{8,9},{9,8},{10,11... | collective-permute-start | bytes 24584 | tf_op jit(solution)/shard_map/ppermute | solution.py:380
  17.1 0.0 collective-permute-done.2.y_odd
  17.1 0.0 collective-permute-done.3.y_even
  17.1 0.7 %shard_map.72.mine = f32[8,128]{1,0:T(8,128)S(1)} custom-call(f32[9,32,128]{2,1,0:T(8,128)S(1)} %collective-permute-done.x_odd, f32[9,32,128]{2,1,0:T(8,128)S(1)} %collective-permute-done.1.x_even, f32[144,128]{1,0:T(8,128)S(1)} %collective-permute-done.2.y_odd, f32[144,128]{1,0:T(8,128)S(1)} %collective-permute-done.3.y_even, ...), custom_call_target="tpu_custom_call" | custom-call | flops 10000 | bytes 10000 | tf_op jit(solution)/shard_map/pallas_call | solution.py:435
  17.8 1.1 %collective-permute-start.7 = (f32[8,128]{1,0:T(8,128)S(1)}, f32[8,128]{1,0:T(8,128)S(1)}, u32[]{:S(2)}, u32[]{:S(2)}) collective-permute-start(f32[8,128]{1,0:T(8,128)S(1)} %shard_map.72.mine), channel_id=1, source_target_pairs={{0,4},{1,5},{2,6},{3,7},{4,0},{5,1},{6,2},{7,3},{8,12},{9,13},{10,... | collective-permute-start | bytes 12296 | tf_op jit(solution)/shard_map/ppermute | solution.py:390
  18.9 0.0 collective-permute-done.4.corner_odd
  18.9 0.0 collective-permute-done.5.corner_even
  18.9 1.7 %shard_map.70.raw.raw_in = f32[16,32,128]{2,1,0:T(8,128)S(1)} custom-call(f32[9,32,128]{2,1,0:T(8,128)S(1)} %collective-permute-done.x_odd, f32[9,32,128]{2,1,0:T(8,128)S(1)} %collective-permute-done.1.x_even, f32[144,128]{1,0:T(8,128)S(1)} %collective-permute-done.2.y_odd, f32[144,128]{1,0:T(8,128)S(1)} %collective-permute-done.3.y_even, ...), custom_call_target="tpu_custom_call" | custom-call | flops 10000000 | bytes 10000000 | tf_op jit(solution)/shard_map/pallas_call | solution.py:438
  20.6 0.7 %collective-permute-start.6 = (f32[4,32,128]{2,1,0:T(8,128)S(1)}, f32[4,32,128]{2,1,0:T(8,128)S(1)}, u32[]{:S(2)}, u32[]{:S(2)}) collective-permute-start(f32[4,32,128]{2,1,0:T(8,128)S(1)} %shard_map.71), channel_id=1, source_target_pairs={{8,16},{16,8},{9,17},{17,9},{10,18},{18,10},{11,19},{19,11},{12,20... | collective-permute-start | bytes 196616 | tf_op jit(solution)/shard_map/ppermute | solution.py:386
  21.3 1.1 %collective-permute-done.7.other = f32[8,128]{1,0:T(8,128)S(1)} collective-permute-done((f32[8,128]{1,0:T(8,128)S(1)}, f32[8,128]{1,0:T(8,128)S(1)}, u32[]{:S(2)}, u32[]{:S(2)}) %collective-permute-start.7) | collective-permute-done | bytes 4128 | tf_op jit(solution)/shard_map/ppermute | solution.py:390
  22.3 1.3 %collective-permute-start.8 = (f32[4,32,128]{2,1,0:T(8,128)S(1)}, f32[4,32,128]{2,1,0:T(8,128)S(1)}, u32[]{:S(2)}, u32[]{:S(2)}) collective-permute-start(f32[4,32,128]{2,1,0:T(8,128)S(1)} %get-tuple-element.31), channel_id=1, source_target_pairs={{0,8},{8,0},{16,24},{24,16},{1,9},{9,1},{17,25},{25,17},{2,10},{10... | collective-permute-start | bytes 196616 | tf_op jit(solution)/shard_map/ppermute | solution.py:380
  23.6 0.4 collective-permute-start.9
  24.0 3.3 %collective-permute-done.9.other = f32[8,128]{1,0:T(8,128)S(1)} collective-permute-done((f32[8,128]{1,0:T(8,128)S(1)}, f32[8,128]{1,0:T(8,128)S(1)}, u32[]{:S(2)}, u32[]{:S(2)}) %collective-permute-start.9) | collective-permute-done | bytes 4128 | tf_op jit(solution)/shard_map/ppermute | solution.py:390
  27.2 0.0 collective-permute-done.6.x_odd
  27.2 0.0 collective-permute-done.8.x_even
  27.3 1.1 %collective-permute-start.11 = (f32[88,128]{1,0:T(8,128)S(1)}, f32[88,128]{1,0:T(8,128)S(1)}, u32[]{:S(2)}, u32[]{:S(2)}) collective-permute-start(f32[88,128]{1,0:T(8,128)S(1)} %get-tuple-element.34), channel_id=1, source_target_pairs={{0,1},{1,0},{2,3},{3,2},{4,5},{5,4},{6,7},{7,6},{8,9},{9,8},{10,11... | collective-permute-start | bytes 135176 | tf_op jit(solution)/shard_map/ppermute | solution.py:380
  28.4 0.7 %collective-permute-start.10 = (f32[80,128]{1,0:T(8,128)S(1)}, f32[80,128]{1,0:T(8,128)S(1)}, u32[]{:S(2)}, u32[]{:S(2)}) collective-permute-start(f32[80,128]{1,0:T(8,128)S(1)} %get-tuple-element.33), channel_id=1, source_target_pairs={{1,2},{3,4},{5,6},{2,1},{4,3},{6,5},{9,10},{11,12},{13,14},{10,9},... | collective-permute-start | bytes 122888 | tf_op jit(solution)/shard_map/ppermute | solution.py:386
  29.0 2.4 %collective-permute-done.11.y_even = f32[88,128]{1,0:T(8,128)S(1)} collective-permute-done((f32[88,128]{1,0:T(8,128)S(1)}, f32[88,128]{1,0:T(8,128)S(1)}, u32[]{:S(2)}, u32[]{:S(2)}) %collective-permute-start.11) | collective-permute-done | bytes 45088 | tf_op jit(solution)/shard_map/ppermute | solution.py:380
  31.4 1.4 %collective-permute-start.12 = (f32[8,128]{1,0:T(8,128)S(1)}, f32[8,128]{1,0:T(8,128)S(1)}, u32[]{:S(2)}, u32[]{:S(2)}) collective-permute-start(f32[8,128]{1,0:T(8,128)S(1)} %slice_add_fusion), channel_id=1, source_target_pairs={{0,2},{1,3},{2,0},{3,1},{4,6},{5,7},{6,4},{7,5},{8,10},{9,11},{10,... | collective-permute-start | bytes 12296 | tf_op jit(solution)/shard_map/ppermute | solution.py:390
  32.8 2.2 %collective-permute-done.12 = f32[8,128]{1,0:T(8,128)S(1)} collective-permute-done((f32[8,128]{1,0:T(8,128)S(1)}, f32[8,128]{1,0:T(8,128)S(1)}, u32[]{:S(2)}, u32[]{:S(2)}) %collective-permute-start.12) | collective-permute-done | bytes 4128 | tf_op jit(solution)/shard_map/ppermute | solution.py:390
  35.0 0.0 collective-permute-start.13
  35.0 0.0 collective-permute-done.10.y_odd
  35.0 0.9 %shard_map.75.filtered = f32[16,32,128]{2,1,0:T(8,128)S(1)} custom-call(f32[4,32,128]{2,1,0:T(8,128)S(1)} %collective-permute-done.6.x_odd, f32[4,32,128]{2,1,0:T(8,128)S(1)} %collective-permute-done.8.x_even, f32[80,128]{1,0:T(8,128)S(1)} %collective-permute-done.10.y_odd, f32[88,128]{1,0:T(8,128)S(1)} %collective-permute-done.11.y_even, ...), custom_call_target="tpu_custom_call" | custom-call | flops 10000000 | bytes 10000000 | tf_op jit(solution)/shard_map/pallas_call | solution.py:456
  35.9 0.2 collective-permute-done.13.other
  36.1 0.9 %shard_map.76 = (f32[16,32,128]{2,1,0:T(8,128)}, f32[1,1]{1,0:T(1,128)}) custom-call(f32[16,32,128]{2,1,0:T(8,128)S(1)} %shard_map.75.filtered, f32[8,128]{1,0:T(8,128)S(1)} %add.7.mine, f32[8,128]{1,0:T(8,128)S(1)} %collective-permute-done.13.other), custom_call_target="tpu_custom_call" | custom-call | tf_op jit(solution)/shard_map/pallas_call | solution.py:462
  (6 shorter events, 0.1 us)
Async XLA Ops:
  2.0 10.0 %collective-permute-start = (f32[9,32,128]{2,1,0:T(8,128)S(1)}, f32[9,32,128]{2,1,0:T(8,128)S(1)}, u32[]{:S(2)}, u32[]{:S(2)}) collective-permute-start(f32[9,32,128]{2,1,0:T(8,128)S(1)} %get-tuple-element.20), channel_id=1, source_target_pairs={{8,16},{16,8},{9,17},{17,9},{10,18},{18,10},{11,19},{19,11},{12,20... | collective-permute-start | bytes 442376 | tf_op jit(solution)/shard_map/ppermute | solution.py:386
  2.6 9.4 %collective-permute-start.1 = (f32[9,32,128]{2,1,0:T(8,128)S(1)}, f32[9,32,128]{2,1,0:T(8,128)S(1)}, u32[]{:S(2)}, u32[]{:S(2)}) collective-permute-start(f32[9,32,128]{2,1,0:T(8,128)S(1)} %get-tuple-element.21), channel_id=1, source_target_pairs={{0,8},{8,0},{16,24},{24,16},{1,9},{9,1},{17,25},{25,17},{2,10},{10... | collective-permute-start | bytes 442376 | tf_op jit(solution)/shard_map/ppermute | solution.py:380
  7.0 10.1 %collective-permute-start.2 = (f32[144,128]{1,0:T(8,128)S(1)}, f32[144,128]{1,0:T(8,128)S(1)}, u32[]{:S(2)}, u32[]{:S(2)}) collective-permute-start(f32[144,128]{1,0:T(8,128)S(1)} %get-tuple-element.22), channel_id=1, source_target_pairs={{1,2},{3,4},{5,6},{2,1},{4,3},{6,5},{9,10},{11,12},{13,14},{10,9},... | collective-permute-start | bytes 221192 | tf_op jit(solution)/shard_map/ppermute | solution.py:386
  7.7 9.4 %collective-permute-start.3 = (f32[144,128]{1,0:T(8,128)S(1)}, f32[144,128]{1,0:T(8,128)S(1)}, u32[]{:S(2)}, u32[]{:S(2)}) collective-permute-start(f32[144,128]{1,0:T(8,128)S(1)} %get-tuple-element.23), channel_id=1, source_target_pairs={{0,1},{1,0},{2,3},{3,2},{4,5},{5,4},{6,7},{7,6},{8,9},{9,8},{10,11... | collective-permute-start | bytes 221192 | tf_op jit(solution)/shard_map/ppermute | solution.py:380
  12.0 6.9 %collective-permute-start.4 = (f32[16,128]{1,0:T(8,128)S(1)}, f32[16,128]{1,0:T(8,128)S(1)}, u32[]{:S(2)}, u32[]{:S(2)}) collective-permute-start(f32[16,128]{1,0:T(8,128)S(1)} %get-tuple-element.24), channel_id=1, source_target_pairs={{1,2},{3,4},{5,6},{2,1},{4,3},{6,5},{9,10},{11,12},{13,14},{10,9},... | collective-permute-start | bytes 24584 | tf_op jit(solution)/shard_map/ppermute | solution.py:386
  12.7 6.2 %collective-permute-start.5 = (f32[16,128]{1,0:T(8,128)S(1)}, f32[16,128]{1,0:T(8,128)S(1)}, u32[]{:S(2)}, u32[]{:S(2)}) collective-permute-start(f32[16,128]{1,0:T(8,128)S(1)} %get-tuple-element.25), channel_id=1, source_target_pairs={{0,1},{1,0},{2,3},{3,2},{4,5},{5,4},{6,7},{7,6},{8,9},{9,8},{10,11... | collective-permute-start | bytes 24584 | tf_op jit(solution)/shard_map/ppermute | solution.py:380
  17.8 4.6 %collective-permute-start.7 = (f32[8,128]{1,0:T(8,128)S(1)}, f32[8,128]{1,0:T(8,128)S(1)}, u32[]{:S(2)}, u32[]{:S(2)}) collective-permute-start(f32[8,128]{1,0:T(8,128)S(1)} %shard_map.72.mine), channel_id=1, source_target_pairs={{0,4},{1,5},{2,6},{3,7},{4,0},{5,1},{6,2},{7,3},{8,12},{9,13},{10,... | collective-permute-start | bytes 12296 | tf_op jit(solution)/shard_map/ppermute | solution.py:390
  20.6 6.6 %collective-permute-start.6 = (f32[4,32,128]{2,1,0:T(8,128)S(1)}, f32[4,32,128]{2,1,0:T(8,128)S(1)}, u32[]{:S(2)}, u32[]{:S(2)}) collective-permute-start(f32[4,32,128]{2,1,0:T(8,128)S(1)} %shard_map.71), channel_id=1, source_target_pairs={{8,16},{16,8},{9,17},{17,9},{10,18},{18,10},{11,19},{19,11},{12,20... | collective-permute-start | bytes 196616 | tf_op jit(solution)/shard_map/ppermute | solution.py:386
  22.3 4.9 %collective-permute-start.8 = (f32[4,32,128]{2,1,0:T(8,128)S(1)}, f32[4,32,128]{2,1,0:T(8,128)S(1)}, u32[]{:S(2)}, u32[]{:S(2)}) collective-permute-start(f32[4,32,128]{2,1,0:T(8,128)S(1)} %get-tuple-element.31), channel_id=1, source_target_pairs={{0,8},{8,0},{16,24},{24,16},{1,9},{9,1},{17,25},{25,17},{2,10},{10... | collective-permute-start | bytes 196616 | tf_op jit(solution)/shard_map/ppermute | solution.py:380
  23.6 3.6 %collective-permute-start.9 = (f32[8,128]{1,0:T(8,128)S(1)}, f32[8,128]{1,0:T(8,128)S(1)}, u32[]{:S(2)}, u32[]{:S(2)}) collective-permute-start(f32[8,128]{1,0:T(8,128)S(1)} %get-tuple-element.32.mine), channel_id=1, source_target_pairs={{0,16},{8,24},{16,0},{24,8},{1,17},{9,25},{17,1},{25,9},{2,18},{10... | collective-permute-start | bytes 12296 | tf_op jit(solution)/shard_map/ppermute | solution.py:390
  27.3 4.1 %collective-permute-start.11 = (f32[88,128]{1,0:T(8,128)S(1)}, f32[88,128]{1,0:T(8,128)S(1)}, u32[]{:S(2)}, u32[]{:S(2)}) collective-permute-start(f32[88,128]{1,0:T(8,128)S(1)} %get-tuple-element.34), channel_id=1, source_target_pairs={{0,1},{1,0},{2,3},{3,2},{4,5},{5,4},{6,7},{7,6},{8,9},{9,8},{10,11... | collective-permute-start | bytes 135176 | tf_op jit(solution)/shard_map/ppermute | solution.py:380
  28.4 6.6 %collective-permute-start.10 = (f32[80,128]{1,0:T(8,128)S(1)}, f32[80,128]{1,0:T(8,128)S(1)}, u32[]{:S(2)}, u32[]{:S(2)}) collective-permute-start(f32[80,128]{1,0:T(8,128)S(1)} %get-tuple-element.33), channel_id=1, source_target_pairs={{1,2},{3,4},{5,6},{2,1},{4,3},{6,5},{9,10},{11,12},{13,14},{10,9},... | collective-permute-start | bytes 122888 | tf_op jit(solution)/shard_map/ppermute | solution.py:386
  31.4 3.6 %collective-permute-start.12 = (f32[8,128]{1,0:T(8,128)S(1)}, f32[8,128]{1,0:T(8,128)S(1)}, u32[]{:S(2)}, u32[]{:S(2)}) collective-permute-start(f32[8,128]{1,0:T(8,128)S(1)} %slice_add_fusion), channel_id=1, source_target_pairs={{0,2},{1,3},{2,0},{3,1},{4,6},{5,7},{6,4},{7,5},{8,10},{9,11},{10,... | collective-permute-start | bytes 12296 | tf_op jit(solution)/shard_map/ppermute | solution.py:390
  35.0 1.2 %collective-permute-start.13 = (f32[8,128]{1,0:T(8,128)S(1)}, f32[8,128]{1,0:T(8,128)S(1)}, u32[]{:S(2)}, u32[]{:S(2)}) collective-permute-start(f32[8,128]{1,0:T(8,128)S(1)} %add.7.mine), channel_id=1, source_target_pairs={{0,8},{8,0},{16,24},{24,16},{1,9},{9,1},{17,25},{25,17},{2,10},{10... | collective-permute-start | bytes 12296 | tf_op jit(solution)/shard_map/ppermute | solution.py:390

commit v18 on v17

--- a/solution.py
+++ b/solution.py
@@ -154,7 +154,7 @@
 def energy_part(x_odd, x_even, y_odd, y_even, density, labels, potential, energy_out, poten):
     size_x, size_y, size_z = density.shape
     starts, planes = plane_starts(WIDTHS)
-    planes_loop(0, size_x, 4, lambda x, n: poten.__setitem__((pl.ds(x + 1, n), pl.ds(0, size_y)), potential[pl.ds(x, n)]))
+    planes_loop(0, size_x, 16, lambda x, n: poten.__setitem__((pl.ds(x + 1, n), pl.ds(0, size_y)), potential[pl.ds(x, n)]))
     span = pl.ds(starts[3], 1)
     unpack_planes(poten, 1, x_even[span], x_odd[span], size_x, size_y)
     found, _ = segments(WIDTHS, size_x, beyond=False)
@@ -179,7 +179,7 @@
         energy = material(density[span], labels[span]) * squares[:, :size_y]
         energy_out[...] += jnp.sum(energy.reshape(-1, 8, size_z), axis=0)
 
-    planes_loop(0, size_x, 4, step)
+    planes_loop(0, size_x, 16, step)
 
 
 def adjoint_part(x_odd, x_even, y_odd, y_even, corner_odd, corner_even, density, labels, adjoint_start, adjoint_source, potential,
@@ -197,7 +197,7 @@
         source[pl.ds(x + WIDTHS[2], n), tile] = adjoint_source[span]
         poten[pl.ds(x + WIDTHS[3], n), tile] = potential[span]
 
-    planes_loop(0, size_x, 4, fill)
+    planes_loop(0, size_x, 16, fill)
     for field, width in enumerate(WIDTHS):
         span = pl.ds(starts[field], width)
         unpack_planes(fields[field], width, x_even[span], x_odd[span], size_x, size_y)
@@ -347,7 +347,7 @@
     def fill(x, n):
         raw[pl.ds(x + width, n), tile] = raw_in[pl.ds(x, n)]
 
-    planes_loop(0, size_x, 4, fill)
+    planes_loop(0, size_x, 16, fill)
     unpack_planes(raw, width, x_even[...], x_odd[...], size_x, size_y)
     unpack_rows((raw,), (width,), segments((width,), size_x)[0], y_even, y_odd, size_y)
     relax = relaxation(raw, size_x, size_y, size_z)

time: 37.2 us -> 36.9 us (level)
  Pallas kernels: 5.51 us -> 5.12 us
  transfers between devices with their start and end apart: 14 -> 14, of which waited for: 5 -> 6; matrix products, arithmetic and copies ran while one was open for 0% -> 0% of each run, Pallas kernels for 9% -> 8%
where the time goes in v18:
time: 36.9 us; the launch traced here: 36.6 us
  starting transfers between devices  21.8 us (59%)
  waiting for transfers between devices  8.93 us (24%)
  Pallas kernels  5.12 us (14%)
  between operations  0.74 us (2%)
    ppermute x5, starting transfers between devices, swap_even(): lax.ppermute(value, axis, [(i, i ^ 1) for i in range(lax.axis_size(axis))])  15.6 us
    ppermute x4, waiting for transfers between devices, partner(): lax.ppermute(value, axis, [(i, i ^ bit) for i in range(lax.axis_size(axis...  6.6 us
    ppermute x5, starting transfers between devices, swap_odd(): return lax.ppermute(value, axis, up + [(b, a) for a, b in up])  3.3 us
    ppermute x4, starting transfers between devices, partner(): lax.ppermute(value, axis, [(i, i ^ bit) for i in range(lax.axis_size(axis...  2.93 us
    ppermute x5, waiting for transfers between devices, swap_even(): lax.ppermute(value, axis, [(i, i ^ 1) for i in range(lax.axis_size(axis))])  2.32 us
    pallas_call x1, Pallas kernels, shards(): call(adjoint_part, f32(*shape), [room(6), room(6), room(4), room(2), room...  1.64 us
    pallas_call x1, Pallas kernels, shards(): pl.pallas_call(pack_own, out_shape=(f32(planes, size_y, size_z),) * 2 + (...  1.33 us
    pallas_call x1, Pallas kernels, shards(): call(filter_part, f32(*shape), [room(2 * FILTER_SWEEPS)] * 3, cost=10000000)  0.91 us
  transfers between devices with their start and end apart: 14, of which 6 were waited for; matrix products, arithmetic and copies ran while one was open for 0% of the time, Pallas kernels for 8%

profile of v18, /device:TPU:0, one launch (start us, length us, event | category | flops | bytes accessed | tf_op | source)
XLA Modules:
  0.0 36.6 jit_solution(15064838794506684437)
XLA Ops:
  0.6 1.3 %shard_map.68 = (f32[9,32,128]{2,1,0:T(8,128)S(1)}, f32[9,32,128]{2,1,0:T(8,128)S(1)}, f32[144,128]{1,0:T(8,128)S(1)}, f32[144,128]{1,0:T(8,128)S(1)}, f32[16,32...) custom-call(f32[16,32,128]{2,1,0:T(8,128)} %refs_0_.1, ...), custom_call_target="tpu_custom_call" | custom-call | tf_op jit(solution)/shard_map/pallas_call | solution.py:414
  2.0 0.7 %collective-permute-start = (f32[9,32,128]{2,1,0:T(8,128)S(1)}, f32[9,32,128]{2,1,0:T(8,128)S(1)}, u32[]{:S(2)}, u32[]{:S(2)}) collective-permute-start(f32[9,32,128]{2,1,0:T(8,128)S(1)} %get-tuple-element.20), channel_id=1, source_target_pairs={{8,16},{16,8},{9,17},{17,9},{10,18},{18,10},{11,19},{19,11},{12,20... | collective-permute-start | bytes 442376 | tf_op jit(solution)/shard_map/ppermute | solution.py:386
  2.6 4.4 %collective-permute-start.1 = (f32[9,32,128]{2,1,0:T(8,128)S(1)}, f32[9,32,128]{2,1,0:T(8,128)S(1)}, u32[]{:S(2)}, u32[]{:S(2)}) collective-permute-start(f32[9,32,128]{2,1,0:T(8,128)S(1)} %get-tuple-element.21), channel_id=1, source_target_pairs={{0,8},{8,0},{16,24},{24,16},{1,9},{9,1},{17,25},{25,17},{2,10},{10... | collective-permute-start | bytes 442376 | tf_op jit(solution)/shard_map/ppermute | solution.py:380
  7.0 0.7 %collective-permute-start.2 = (f32[144,128]{1,0:T(8,128)S(1)}, f32[144,128]{1,0:T(8,128)S(1)}, u32[]{:S(2)}, u32[]{:S(2)}) collective-permute-start(f32[144,128]{1,0:T(8,128)S(1)} %get-tuple-element.22), channel_id=1, source_target_pairs={{1,2},{3,4},{5,6},{2,1},{4,3},{6,5},{9,10},{11,12},{13,14},{10,9},... | collective-permute-start | bytes 221192 | tf_op jit(solution)/shard_map/ppermute | solution.py:386
  7.7 4.3 %collective-permute-start.3 = (f32[144,128]{1,0:T(8,128)S(1)}, f32[144,128]{1,0:T(8,128)S(1)}, u32[]{:S(2)}, u32[]{:S(2)}) collective-permute-start(f32[144,128]{1,0:T(8,128)S(1)} %get-tuple-element.23), channel_id=1, source_target_pairs={{0,1},{1,0},{2,3},{3,2},{4,5},{5,4},{6,7},{7,6},{8,9},{9,8},{10,11... | collective-permute-start | bytes 221192 | tf_op jit(solution)/shard_map/ppermute | solution.py:380
  12.0 0.0 collective-permute-done.x_odd
  12.0 0.0 collective-permute-done.1.x_even
  12.0 0.7 %collective-permute-start.4 = (f32[16,128]{1,0:T(8,128)S(1)}, f32[16,128]{1,0:T(8,128)S(1)}, u32[]{:S(2)}, u32[]{:S(2)}) collective-permute-start(f32[16,128]{1,0:T(8,128)S(1)} %get-tuple-element.24), channel_id=1, source_target_pairs={{1,2},{3,4},{5,6},{2,1},{4,3},{6,5},{9,10},{11,12},{13,14},{10,9},... | collective-permute-start | bytes 24584 | tf_op jit(solution)/shard_map/ppermute | solution.py:386
  12.7 4.4 %collective-permute-start.5 = (f32[16,128]{1,0:T(8,128)S(1)}, f32[16,128]{1,0:T(8,128)S(1)}, u32[]{:S(2)}, u32[]{:S(2)}) collective-permute-start(f32[16,128]{1,0:T(8,128)S(1)} %get-tuple-element.25), channel_id=1, source_target_pairs={{0,1},{1,0},{2,3},{3,2},{4,5},{5,4},{6,7},{7,6},{8,9},{9,8},{10,11... | collective-permute-start | bytes 24584 | tf_op jit(solution)/shard_map/ppermute | solution.py:380
  17.1 0.0 collective-permute-done.2.y_odd
  17.1 0.0 collective-permute-done.3.y_even
  17.1 0.3 shard_map.72.mine
  17.4 1.1 %collective-permute-start.7 = (f32[8,128]{1,0:T(8,128)S(1)}, f32[8,128]{1,0:T(8,128)S(1)}, u32[]{:S(2)}, u32[]{:S(2)}) collective-permute-start(f32[8,128]{1,0:T(8,128)S(1)} %shard_map.72.mine), channel_id=1, source_target_pairs={{0,4},{1,5},{2,6},{3,7},{4,0},{5,1},{6,2},{7,3},{8,12},{9,13},{10,... | collective-permute-start | bytes 12296 | tf_op jit(solution)/shard_map/ppermute | solution.py:390
  18.5 0.0 collective-permute-done.4.corner_odd
  18.5 0.2 collective-permute-done.5.corner_even
  18.7 1.6 %shard_map.70.raw.raw_in = f32[16,32,128]{2,1,0:T(8,128)S(1)} custom-call(f32[9,32,128]{2,1,0:T(8,128)S(1)} %collective-permute-done.x_odd, f32[9,32,128]{2,1,0:T(8,128)S(1)} %collective-permute-done.1.x_even, f32[144,128]{1,0:T(8,128)S(1)} %collective-permute-done.2.y_odd, f32[144,128]{1,0:T(8,128)S(1)} %collective-permute-done.3.y_even, ...), custom_call_target="tpu_custom_call" | custom-call | flops 10000000 | bytes 10000000 | tf_op jit(solution)/shard_map/pallas_call | solution.py:438
  20.4 0.7 %collective-permute-start.6 = (f32[4,32,128]{2,1,0:T(8,128)S(1)}, f32[4,32,128]{2,1,0:T(8,128)S(1)}, u32[]{:S(2)}, u32[]{:S(2)}) collective-permute-start(f32[4,32,128]{2,1,0:T(8,128)S(1)} %shard_map.71), channel_id=1, source_target_pairs={{8,16},{16,8},{9,17},{17,9},{10,18},{18,10},{11,19},{19,11},{12,20... | collective-permute-start | bytes 196616 | tf_op jit(solution)/shard_map/ppermute | solution.py:386
  21.0 0.9 %collective-permute-done.7.other = f32[8,128]{1,0:T(8,128)S(1)} collective-permute-done((f32[8,128]{1,0:T(8,128)S(1)}, f32[8,128]{1,0:T(8,128)S(1)}, u32[]{:S(2)}, u32[]{:S(2)}) %collective-permute-start.7) | collective-permute-done | bytes 4128 | tf_op jit(solution)/shard_map/ppermute | solution.py:390
  22.0 1.2 %collective-permute-start.8 = (f32[4,32,128]{2,1,0:T(8,128)S(1)}, f32[4,32,128]{2,1,0:T(8,128)S(1)}, u32[]{:S(2)}, u32[]{:S(2)}) collective-permute-start(f32[4,32,128]{2,1,0:T(8,128)S(1)} %get-tuple-element.31), channel_id=1, source_target_pairs={{0,8},{8,0},{16,24},{24,16},{1,9},{9,1},{17,25},{25,17},{2,10},{10... | collective-permute-start | bytes 196616 | tf_op jit(solution)/shard_map/ppermute | solution.py:380
  23.2 0.4 collective-permute-start.9
  23.6 3.3 %collective-permute-done.9.other = f32[8,128]{1,0:T(8,128)S(1)} collective-permute-done((f32[8,128]{1,0:T(8,128)S(1)}, f32[8,128]{1,0:T(8,128)S(1)}, u32[]{:S(2)}, u32[]{:S(2)}) %collective-permute-start.9) | collective-permute-done | bytes 4128 | tf_op jit(solution)/shard_map/ppermute | solution.py:390
  26.8 0.0 collective-permute-done.6.x_odd
  26.8 0.0 collective-permute-done.8.x_even
  26.9 1.3 %collective-permute-start.11 = (f32[88,128]{1,0:T(8,128)S(1)}, f32[88,128]{1,0:T(8,128)S(1)}, u32[]{:S(2)}, u32[]{:S(2)}) collective-permute-start(f32[88,128]{1,0:T(8,128)S(1)} %get-tuple-element.34), channel_id=1, source_target_pairs={{0,1},{1,0},{2,3},{3,2},{4,5},{5,4},{6,7},{7,6},{8,9},{9,8},{10,11... | collective-permute-start | bytes 135176 | tf_op jit(solution)/shard_map/ppermute | solution.py:380
  28.2 0.7 %collective-permute-start.10 = (f32[80,128]{1,0:T(8,128)S(1)}, f32[80,128]{1,0:T(8,128)S(1)}, u32[]{:S(2)}, u32[]{:S(2)}) collective-permute-start(f32[80,128]{1,0:T(8,128)S(1)} %get-tuple-element.33), channel_id=1, source_target_pairs={{1,2},{3,4},{5,6},{2,1},{4,3},{6,5},{9,10},{11,12},{13,14},{10,9},... | collective-permute-start | bytes 122888 | tf_op jit(solution)/shard_map/ppermute | solution.py:386
  28.8 2.2 %collective-permute-done.11.y_even = f32[88,128]{1,0:T(8,128)S(1)} collective-permute-done((f32[88,128]{1,0:T(8,128)S(1)}, f32[88,128]{1,0:T(8,128)S(1)}, u32[]{:S(2)}, u32[]{:S(2)}) %collective-permute-start.11) | collective-permute-done | bytes 45088 | tf_op jit(solution)/shard_map/ppermute | solution.py:380
  31.0 1.4 %collective-permute-start.12 = (f32[8,128]{1,0:T(8,128)S(1)}, f32[8,128]{1,0:T(8,128)S(1)}, u32[]{:S(2)}, u32[]{:S(2)}) collective-permute-start(f32[8,128]{1,0:T(8,128)S(1)} %slice_add_fusion), channel_id=1, source_target_pairs={{0,2},{1,3},{2,0},{3,1},{4,6},{5,7},{6,4},{7,5},{8,10},{9,11},{10,... | collective-permute-start | bytes 12296 | tf_op jit(solution)/shard_map/ppermute | solution.py:390
  32.4 2.2 %collective-permute-done.12 = f32[8,128]{1,0:T(8,128)S(1)} collective-permute-done((f32[8,128]{1,0:T(8,128)S(1)}, f32[8,128]{1,0:T(8,128)S(1)}, u32[]{:S(2)}, u32[]{:S(2)}) %collective-permute-start.12) | collective-permute-done | bytes 4128 | tf_op jit(solution)/shard_map/ppermute | solution.py:390
  34.6 0.0 collective-permute-start.13
  34.6 0.0 collective-permute-done.10.y_odd
  34.6 0.9 %shard_map.75.filtered = f32[16,32,128]{2,1,0:T(8,128)S(1)} custom-call(f32[4,32,128]{2,1,0:T(8,128)S(1)} %collective-permute-done.6.x_odd, f32[4,32,128]{2,1,0:T(8,128)S(1)} %collective-permute-done.8.x_even, f32[80,128]{1,0:T(8,128)S(1)} %collective-permute-done.10.y_odd, f32[88,128]{1,0:T(8,128)S(1)} %collective-permute-done.11.y_even, ...), custom_call_target="tpu_custom_call" | custom-call | flops 10000000 | bytes 10000000 | tf_op jit(solution)/shard_map/pallas_call | solution.py:456
  35.5 0.2 collective-permute-done.13.other
  35.8 0.9 %shard_map.76 = (f32[16,32,128]{2,1,0:T(8,128)}, f32[1,1]{1,0:T(1,128)}) custom-call(f32[16,32,128]{2,1,0:T(8,128)S(1)} %shard_map.75.filtered, f32[8,128]{1,0:T(8,128)S(1)} %add.7.mine, f32[8,128]{1,0:T(8,128)S(1)} %collective-permute-done.13.other), custom_call_target="tpu_custom_call" | custom-call | tf_op jit(solution)/shard_map/pallas_call | solution.py:462
  (6 shorter events, 0.1 us)
Async XLA Ops:
  2.0 10.0 %collective-permute-start = (f32[9,32,128]{2,1,0:T(8,128)S(1)}, f32[9,32,128]{2,1,0:T(8,128)S(1)}, u32[]{:S(2)}, u32[]{:S(2)}) collective-permute-start(f32[9,32,128]{2,1,0:T(8,128)S(1)} %get-tuple-element.20), channel_id=1, source_target_pairs={{8,16},{16,8},{9,17},{17,9},{10,18},{18,10},{11,19},{19,11},{12,20... | collective-permute-start | bytes 442376 | tf_op jit(solution)/shard_map/ppermute | solution.py:386
  2.6 9.4 %collective-permute-start.1 = (f32[9,32,128]{2,1,0:T(8,128)S(1)}, f32[9,32,128]{2,1,0:T(8,128)S(1)}, u32[]{:S(2)}, u32[]{:S(2)}) collective-permute-start(f32[9,32,128]{2,1,0:T(8,128)S(1)} %get-tuple-element.21), channel_id=1, source_target_pairs={{0,8},{8,0},{16,24},{24,16},{1,9},{9,1},{17,25},{25,17},{2,10},{10... | collective-permute-start | bytes 442376 | tf_op jit(solution)/shard_map/ppermute | solution.py:380
  7.0 10.1 %collective-permute-start.2 = (f32[144,128]{1,0:T(8,128)S(1)}, f32[144,128]{1,0:T(8,128)S(1)}, u32[]{:S(2)}, u32[]{:S(2)}) collective-permute-start(f32[144,128]{1,0:T(8,128)S(1)} %get-tuple-element.22), channel_id=1, source_target_pairs={{1,2},{3,4},{5,6},{2,1},{4,3},{6,5},{9,10},{11,12},{13,14},{10,9},... | collective-permute-start | bytes 221192 | tf_op jit(solution)/shard_map/ppermute | solution.py:386
  7.7 9.4 %collective-permute-start.3 = (f32[144,128]{1,0:T(8,128)S(1)}, f32[144,128]{1,0:T(8,128)S(1)}, u32[]{:S(2)}, u32[]{:S(2)}) collective-permute-start(f32[144,128]{1,0:T(8,128)S(1)} %get-tuple-element.23), channel_id=1, source_target_pairs={{0,1},{1,0},{2,3},{3,2},{4,5},{5,4},{6,7},{7,6},{8,9},{9,8},{10,11... | collective-permute-start | bytes 221192 | tf_op jit(solution)/shard_map/ppermute | solution.py:380
  12.0 6.5 %collective-permute-start.4 = (f32[16,128]{1,0:T(8,128)S(1)}, f32[16,128]{1,0:T(8,128)S(1)}, u32[]{:S(2)}, u32[]{:S(2)}) collective-permute-start(f32[16,128]{1,0:T(8,128)S(1)} %get-tuple-element.24), channel_id=1, source_target_pairs={{1,2},{3,4},{5,6},{2,1},{4,3},{6,5},{9,10},{11,12},{13,14},{10,9},... | collective-permute-start | bytes 24584 | tf_op jit(solution)/shard_map/ppermute | solution.py:386
  12.7 6.0 %collective-permute-start.5 = (f32[16,128]{1,0:T(8,128)S(1)}, f32[16,128]{1,0:T(8,128)S(1)}, u32[]{:S(2)}, u32[]{:S(2)}) collective-permute-start(f32[16,128]{1,0:T(8,128)S(1)} %get-tuple-element.25), channel_id=1, source_target_pairs={{0,1},{1,0},{2,3},{3,2},{4,5},{5,4},{6,7},{7,6},{8,9},{9,8},{10,11... | collective-permute-start | bytes 24584 | tf_op jit(solution)/shard_map/ppermute | solution.py:380
  17.4 4.6 %collective-permute-start.7 = (f32[8,128]{1,0:T(8,128)S(1)}, f32[8,128]{1,0:T(8,128)S(1)}, u32[]{:S(2)}, u32[]{:S(2)}) collective-permute-start(f32[8,128]{1,0:T(8,128)S(1)} %shard_map.72.mine), channel_id=1, source_target_pairs={{0,4},{1,5},{2,6},{3,7},{4,0},{5,1},{6,2},{7,3},{8,12},{9,13},{10,... | collective-permute-start | bytes 12296 | tf_op jit(solution)/shard_map/ppermute | solution.py:390
  20.4 6.5 %collective-permute-start.6 = (f32[4,32,128]{2,1,0:T(8,128)S(1)}, f32[4,32,128]{2,1,0:T(8,128)S(1)}, u32[]{:S(2)}, u32[]{:S(2)}) collective-permute-start(f32[4,32,128]{2,1,0:T(8,128)S(1)} %shard_map.71), channel_id=1, source_target_pairs={{8,16},{16,8},{9,17},{17,9},{10,18},{18,10},{11,19},{19,11},{12,20... | collective-permute-start | bytes 196616 | tf_op jit(solution)/shard_map/ppermute | solution.py:386
  22.0 4.9 %collective-permute-start.8 = (f32[4,32,128]{2,1,0:T(8,128)S(1)}, f32[4,32,128]{2,1,0:T(8,128)S(1)}, u32[]{:S(2)}, u32[]{:S(2)}) collective-permute-start(f32[4,32,128]{2,1,0:T(8,128)S(1)} %get-tuple-element.31), channel_id=1, source_target_pairs={{0,8},{8,0},{16,24},{24,16},{1,9},{9,1},{17,25},{25,17},{2,10},{10... | collective-permute-start | bytes 196616 | tf_op jit(solution)/shard_map/ppermute | solution.py:380
  23.2 3.6 %collective-permute-start.9 = (f32[8,128]{1,0:T(8,128)S(1)}, f32[8,128]{1,0:T(8,128)S(1)}, u32[]{:S(2)}, u32[]{:S(2)}) collective-permute-start(f32[8,128]{1,0:T(8,128)S(1)} %get-tuple-element.32.mine), channel_id=1, source_target_pairs={{0,16},{8,24},{16,0},{24,8},{1,17},{9,25},{17,1},{25,9},{2,18},{10... | collective-permute-start | bytes 12296 | tf_op jit(solution)/shard_map/ppermute | solution.py:390
  26.9 4.1 %collective-permute-start.11 = (f32[88,128]{1,0:T(8,128)S(1)}, f32[88,128]{1,0:T(8,128)S(1)}, u32[]{:S(2)}, u32[]{:S(2)}) collective-permute-start(f32[88,128]{1,0:T(8,128)S(1)} %get-tuple-element.34), channel_id=1, source_target_pairs={{0,1},{1,0},{2,3},{3,2},{4,5},{5,4},{6,7},{7,6},{8,9},{9,8},{10,11... | collective-permute-start | bytes 135176 | tf_op jit(solution)/shard_map/ppermute | solution.py:380
  28.2 6.4 %collective-permute-start.10 = (f32[80,128]{1,0:T(8,128)S(1)}, f32[80,128]{1,0:T(8,128)S(1)}, u32[]{:S(2)}, u32[]{:S(2)}) collective-permute-start(f32[80,128]{1,0:T(8,128)S(1)} %get-tuple-element.33), channel_id=1, source_target_pairs={{1,2},{3,4},{5,6},{2,1},{4,3},{6,5},{9,10},{11,12},{13,14},{10,9},... | collective-permute-start | bytes 122888 | tf_op jit(solution)/shard_map/ppermute | solution.py:386
  31.0 3.6 %collective-permute-start.12 = (f32[8,128]{1,0:T(8,128)S(1)}, f32[8,128]{1,0:T(8,128)S(1)}, u32[]{:S(2)}, u32[]{:S(2)}) collective-permute-start(f32[8,128]{1,0:T(8,128)S(1)} %slice_add_fusion), channel_id=1, source_target_pairs={{0,2},{1,3},{2,0},{3,1},{4,6},{5,7},{6,4},{7,5},{8,10},{9,11},{10,... | collective-permute-start | bytes 12296 | tf_op jit(solution)/shard_map/ppermute | solution.py:390
  34.6 1.2 %collective-permute-start.13 = (f32[8,128]{1,0:T(8,128)S(1)}, f32[8,128]{1,0:T(8,128)S(1)}, u32[]{:S(2)}, u32[]{:S(2)}) collective-permute-start(f32[8,128]{1,0:T(8,128)S(1)} %add.7.mine), channel_id=1, source_target_pairs={{0,8},{8,0},{16,24},{24,16},{1,9},{9,1},{17,25},{25,17},{2,10},{10... | collective-permute-start | bytes 12296 | tf_op jit(solution)/shard_map/ppermute | solution.py:390
